TPU v7x, 256 devices: a whole 4x4x8 slice. The times are simulated.
256 devices in a mesh: dp: 64 (over z_lo, x, y, core), tensor: 4 (over z_hi).
Axes of the slice: x: 4, y: 4, z: 8 (z_hi: 4, z_lo: 2; z = z_hi * 2 + z_lo), core: 2. Of those that a mesh axis runs over, the one named last changes fastest.
Arguments:
- activations: bfloat16 [2, 2, 32768, 5120], P(None, None, ('dp', 'tensor')), may hold values from -60 to 60
- grad_qkv: bfloat16 [2, 15360, 5120], P(None, 'dp', 'tensor'), may hold values from -60 to 60
- grad_up: bfloat16 [2, 20480, 5120], P(None, 'dp', 'tensor'), may hold values from -60 to 60
- newton_steps: int32 [2, 2, 8], replicated, may hold values from 2 to 4, as said below
Outputs:
- precond_qkv: bfloat16 [2, 15360, 5120], P(None, 'dp', 'tensor')
- precond_up: bfloat16 [2, 20480, 5120], P(None, 'dp', 'tensor')
Inputs may be any that keep to these rules, and one draw needn't show every extreme that they name: `newton_steps`: one count for each diagonal block; some block takes all 4 iterations.
All inputs are finite; a program needn't handle non-finite values.
Results may differ from a plain program's by a relative error of at most 0.0051.
Values may be sent and summed in bfloat16 or wider, within the bound.
No kernel may reach another device: no remote copies, remote signals or barrier semaphores. Data moves between devices by JAX's collectives and lax.ppermute only.
A program may use at most 128 MiB of HBM per device.

v0:
```python
import jax
import jax.numpy as jnp
from jax import lax
from jax.sharding import PartitionSpec as P

ITERS = 4


damping = 0.05


def partner_2(array, axis, bit):
    return lax.ppermute(array, axis, [(i, i ^ 1 << bit) for i in range(lax.axis_size(axis))])


def doubling_gather(local_rows, mover, levels, position):
    joined = local_rows
    for bit_index in range(levels):
        partner = mover(joined, bit_index)
        upper = position >> bit_index & 1 == 1
        joined = jnp.where(
            upper, jnp.concatenate([partner, joined], 0), jnp.concatenate([joined, partner], 0)
        )
    return joined


def pair_total(operand, mover, levels):
    running = operand
    for bit_index in range(levels):
        running = running + mover(running, bit_index)
    return running


def local(activations, grad_qkv, grad_up, newton_steps):
    dp_count = lax.axis_size("dp")
    tp_count = lax.axis_size("tensor")
    dp_index = lax.axis_index("dp")
    tp_index = lax.axis_index("tensor")
    layer_count, factor_kinds, tok_rows, feature_width = activations.shape
    block_width = feature_width // (2 * tp_count)
    pair_count = layer_count * factor_kinds
    group_size = dp_count // (pair_count * 2)
    levels = group_size.bit_length() - 1
    member_rows = block_width // group_size
    tokens_all = tok_rows * dp_count * tp_count
    block_slot = dp_index // group_size
    member = dp_index % group_size
    flattened = activations.reshape(pair_count, tok_rows, feature_width)
    eye_block = jnp.eye(block_width, dtype=jnp.float32)
    row_numbers = member * member_rows + lax.iota(jnp.int32, member_rows)
    diag_rows = (row_numbers[:, None] == lax.iota(jnp.int32, block_width)[None, :]).astype(
        jnp.float32
    )
    received = lax.all_to_all(flattened, "tensor", split_axis=2, concat_axis=1, tiled=True)
    item_count = received.shape[0]
    halves = received.reshape(item_count, received.shape[1], 2, block_width)
    partial_terms = jnp.einsum(
        "ntjp,ntjq->njpq", halves, halves, preferred_element_type=jnp.float32
    )
    summed = lax.psum_scatter(
        partial_terms.reshape(pair_count * 2 * block_width, block_width),
        "dp",
        scatter_dimension=0,
        tiled=True,
    )
    factor_rows = summed / tokens_all + damping * diag_rows
    pair_index = block_slot // 2
    block_half = block_slot % 2
    steps_flat = newton_steps.reshape(-1)
    step_count = lax.dynamic_index_in_dim(
        steps_flat, pair_index * (2 * tp_count) + tp_index * 2 + block_half, 0, keepdims=False
    )
    square_sum = pair_total(
        jnp.sum(factor_rows * factor_rows),
        lambda piece_rows, bit_index: partner_2(piece_rows, "dp", bit_index),
        levels,
    )
    norm_scale = jnp.sqrt(square_sum)

    def newton_turn(turn_index, state_pair):
        inverse, mixed = state_pair
        whole_rows = doubling_gather(
            mixed,
            lambda piece_rows, bit_index: partner_2(
                piece_rows.astype(jnp.bfloat16), "dp", bit_index
            ).astype(piece_rows.dtype),
            levels,
            member,
        )
        reflect = 2.0 * eye_block - whole_rows
        new_inverse = jnp.dot(inverse, reflect, precision=lax.Precision.HIGHEST)
        new_mixed = jnp.dot(mixed, reflect, precision=lax.Precision.HIGHEST)
        active_turn = turn_index < step_count
        return (
            jnp.where(active_turn, new_inverse, inverse),
            jnp.where(active_turn, new_mixed, mixed),
        )

    inverse_rows, mixed_rows = lax.fori_loop(
        0, ITERS, newton_turn, (diag_rows / norm_scale, factor_rows / norm_scale)
    )
    gathered = lax.all_gather(inverse_rows.astype(jnp.bfloat16), "dp", axis=0, tiled=True)
    inverses = gathered.reshape(layer_count, factor_kinds, 2, block_width, block_width)

    def precondition(gradient, kind_index):
        grad_rows = gradient.shape[1]
        halves = gradient.reshape(layer_count, grad_rows, 2, block_width)
        product = jnp.einsum(
            "lrjp,ljpq->lrjq", halves, inverses[:, kind_index], preferred_element_type=jnp.float32
        )
        return product.reshape(layer_count, grad_rows, 2 * block_width).astype(jnp.bfloat16)

    return (precondition(grad_qkv, 0), precondition(grad_up, 1))


def solution(mesh):
    placed = (
        P(None, None, ("dp", "tensor"), None),
        P(None, "dp", "tensor"),
        P(None, "dp", "tensor"),
        P(),
    )
    return jax.shard_map(
        local,
        mesh=mesh,
        in_specs=placed,
        out_specs=(P(None, "dp", "tensor"), P(None, "dp", "tensor")),
        check_vma=False,
    )
```

profile of v0, /device:TPU:1, one launch (start us, length us, event | category | flops | bytes accessed | tf_op | source)
XLA Modules:
  0.0 723.8 jit_solution(12856241570361824255)
XLA Ops:
  7.2 13.6 %copy.27 = bf16[2,2,128,5120]{2,1,0,3:T(2,128)(2,1)} copy(bf16[2,2,128,5120]{3,2,1,0:T(8,128)(2,1)} %param.6) | data formatting | bytes 10485760 | tf_op args[0]
  20.8 125.9 %all_to_all.15 = bf16[4,128,5120]{1,0,2:T(4,128)(2,1)S(1)} all-to-all(bf16[4,128,5120]{1,0,2:T(4,128)(2,1)} %bitcast.64), channel_id=1, replica_groups=mesh['dp'=64,'tensor'=4] {'tensor'}, dimensions={2} | all-to-all | bytes 10485760 | tf_op jit(solution)/shard_map/all_to_all | solution.py:54
  146.7 3.0 copy.28
  149.7 7.8 %copy.29 = bf16[4,4,128,1280]{3,2,1,0:T(8,128)(2,1)} copy(bf16[4,4,128,1280]{2,3,1,0:T(8,128)(2,1)} %bitcast.63) | data formatting | bytes 10485760 | tf_op jit(solution)/shard_map/all_to_all | solution.py:54
  157.5 10.8 %reshape.35 = bf16[4,512,2,640]{3,2,1,0:T(2,128)(2,1)} reshape(bf16[4,4,128,1280]{3,2,1,0:T(8,128)(2,1)} %copy.29) | data formatting | bytes 10485760 | tf_op jit(solution)/shard_map/reshape | solution.py:56
  168.4 13.0 %fusion.13 = f32[4,2,640,640]{3,2,1,0:T(8,128)} fusion(bf16[4,512,2,640]{3,2,1,0:T(2,128)(2,1)} %reshape.35), kind=kOutput, calls=%fused_computation.16 | convolution fusion | flops 3355443200 | bytes 18350080 | tf_op jit(solution)/shard_map/ntjp,ntjq->njpq/dot_general | solution.py:57
  181.5 0.6 copy-done
  182.1 0.1 reshape.37
  182.1 0.6 dynamic_slice.4
  182.7 300.8 %reduce-scatter.2.cloned.1.call-done = f32[80,640]{1,0:T(8,128)} async-done(((f32[5120,640]{1,0:T(8,128)}), f32[80,640]{1,0:T(8,128)}) %reduce-scatter.2.cloned.1.call-update) | async-done | bytes 204816 | tf_op jit(solution)/shard_map/reduce_scatter | solution.py:60
  483.6 1.7 multiply_reduce_fusion
  485.2 6.3 collective-permute-start.3
  491.6 1.1 collective-permute-done.3
  493.8 0.8 collective-permute-start.4
  494.7 1.6 collective-permute-done.4
  496.8 1.0 collective-permute-start.5
  497.8 3.1 collective-permute-done.5
  501.6 1.0 fusion.28
  502.7 96.5 %while.18 = (s32[]{:T(128)}, f32[80,640]{1,0:T(8,128)S(1)}, f32[80,640]{1,0:T(8,128)S(1)}, s32[]{:T(128)}, pred[]{:T(512)}, /*index=5*/pred[]{:T(512)}, pred[]{:T(512)}, s32[]{:T(128)}) while((s32[]{:T(128)}, f32[80,640]{1,0:T(8,128)S(1)}, f32[80,640]{1,0:T(8,128)S(1)}, s32[]{:T(128)}, pred[]{:T(512)}, /*index=5*/pred[]{:T(512)}, ...), condition=%wide.region_3.4_spmd.clone, body=%wide.region_2.3_spmd.clone.sunk | while | flops 793088000 | bytes 13312228 | solution.py:99
  502.7 3.0 collective-permute-start
  505.7 0.9 collective-permute-done
  506.7 0.1 collective-permute-start.1
  506.8 6.3 collective-permute-done.1
  513.2 0.1 fusion.46
  513.3 0.1 collective-permute-start.2
  513.9 10.7 %collective-permute-done.2 = bf16[320,640]{1,0:T(8,128)(2,1)S(1)} collective-permute-done((bf16[320,640]{1,0:T(8,128)(2,1)S(1)}, bf16[320,640]{1,0:T(8,128)(2,1)S(1)}, u32[]{:S(2)}, u32[]{:S(2)}) %collective-permute-start.2) | collective-permute-done | bytes 409632 | tf_op jit(solution)/shard_map/while/body/eval_jaxpr/ppermute | solution.py:13
  524.6 0.1 convert_element_type.116
  524.7 1.3 fusion.48
  526.0 1.3 fusion.47
  527.4 2.2 collective-permute-start
  529.6 0.9 collective-permute-done
  530.7 0.4 collective-permute-start.1
  531.1 6.0 collective-permute-done.1
  537.1 0.1 fusion.46
  537.2 0.1 collective-permute-start.2
  537.8 10.7 %collective-permute-done.2 = bf16[320,640]{1,0:T(8,128)(2,1)S(1)} collective-permute-done((bf16[320,640]{1,0:T(8,128)(2,1)S(1)}, bf16[320,640]{1,0:T(8,128)(2,1)S(1)}, u32[]{:S(2)}, u32[]{:S(2)}) %collective-permute-start.2) | collective-permute-done | bytes 409632 | tf_op jit(solution)/shard_map/while/body/eval_jaxpr/ppermute | solution.py:13
  548.5 0.1 convert_element_type.116
  548.6 1.3 fusion.48
  549.9 1.3 fusion.47
  551.4 2.2 collective-permute-start
  553.6 0.9 collective-permute-done
  554.6 0.4 collective-permute-start.1
  555.0 6.0 collective-permute-done.1
  561.0 0.1 fusion.46
  561.1 0.1 collective-permute-start.2
  561.8 10.7 %collective-permute-done.2 = bf16[320,640]{1,0:T(8,128)(2,1)S(1)} collective-permute-done((bf16[320,640]{1,0:T(8,128)(2,1)S(1)}, bf16[320,640]{1,0:T(8,128)(2,1)S(1)}, u32[]{:S(2)}, u32[]{:S(2)}) %collective-permute-start.2) | collective-permute-done | bytes 409632 | tf_op jit(solution)/shard_map/while/body/eval_jaxpr/ppermute | solution.py:13
  572.5 1.3 fusion.48
  573.9 1.3 fusion.47
  575.3 2.2 collective-permute-start
  577.5 0.9 collective-permute-done
  578.5 0.4 collective-permute-start.1
  578.9 6.0 collective-permute-done.1
  584.9 0.1 fusion.46
  585.0 0.1 collective-permute-start.2
  585.7 10.7 %collective-permute-done.2 = bf16[320,640]{1,0:T(8,128)(2,1)S(1)} collective-permute-done((bf16[320,640]{1,0:T(8,128)(2,1)S(1)}, bf16[320,640]{1,0:T(8,128)(2,1)S(1)}, u32[]{:S(2)}, u32[]{:S(2)}) %collective-permute-start.2) | collective-permute-done | bytes 409632 | tf_op jit(solution)/shard_map/while/body/eval_jaxpr/ppermute | solution.py:13
  596.4 1.3 fusion.48
  597.8 1.3 fusion.47
  599.2 0.7 convert_element_type.80
  599.8 108.4 %all-gather.2.cloned.1.call-done = bf16[5120,640]{1,0:T(8,128)(2,1)} async-done(((bf16[80,640]{1,0:T(8,128)(2,1)}), bf16[5120,640]{1,0:T(8,128)(2,1)}) %all-gather.2.cloned.1.call-update) | async-done | bytes 6553616 | tf_op jit(solution)/shard_map/all_gather | solution.py:102
  708.3 3.8 fusion.24
  712.0 1.1 copy.42
  713.2 0.8 copy-done.2
  714.0 1.6 fusion.21
  715.6 1.3 copy.43
  (35 shorter events, 0.8 us)
Async XLA Ops:
  7.2 476.4 %reduce-scatter.2.cloned.1.call-start = ((), (), s32[]{:S(2)}) async-start(), calls=%async_computation.2 | async-start | bytes 13312000 | tf_op jit(solution)/shard_map/reduce_scatter | solution.py:60
  181.4 0.7 copy-start
  181.4 526.9 %all-gather.2.cloned.1.call-start = ((), (), s32[]{:S(2)}) async-start(), calls=%async_computation.3 | async-start | bytes 6656000 | tf_op jit(solution)/shard_map/all_gather | solution.py:102
  485.2 7.4 %collective-permute-start.3 = (f32[]{:T(128)}, f32[]{:T(128)}, u32[]{:S(2)}, u32[]{:S(2)}) collective-permute-start(f32[]{:T(128)} %multiply_reduce_fusion), channel_id=1, source_target_pairs={{0,4},{4,0},{8,12},{12,8},{16,20},{20,16},{24,28},{28,24},{32,36},... | collective-permute-start | bytes 20 | tf_op jit(solution)/shard_map/ppermute | solution.py:13
  493.8 2.4 collective-permute-start.4
  496.8 4.1 collective-permute-start.5
  502.7 3.9 collective-permute-start
  506.7 6.4 collective-permute-start.1
  513.3 11.4 %collective-permute-start.2 = (bf16[320,640]{1,0:T(8,128)(2,1)S(1)}, bf16[320,640]{1,0:T(8,128)(2,1)S(1)}, u32[]{:S(2)}, u32[]{:S(2)}) collective-permute-start(bf16[320,640]{1,0:T(8,128)(2,1)S(1)} %get-tuple-element.254), channel_id=1, source_target_pairs={{0,16},{4,20},{8,24},{12,28},{16,0},{20,4},{24,8},{28,12},{32,48},... | collective-permute-start | bytes 1228808 | tf_op jit(solution)/shard_map/while/body/eval_jaxpr/ppermute | solution.py:13
  527.4 3.1 collective-permute-start
  530.7 6.4 collective-permute-start.1
  537.2 11.4 %collective-permute-start.2 = (bf16[320,640]{1,0:T(8,128)(2,1)S(1)}, bf16[320,640]{1,0:T(8,128)(2,1)S(1)}, u32[]{:S(2)}, u32[]{:S(2)}) collective-permute-start(bf16[320,640]{1,0:T(8,128)(2,1)S(1)} %get-tuple-element.254), channel_id=1, source_target_pairs={{0,16},{4,20},{8,24},{12,28},{16,0},{20,4},{24,8},{28,12},{32,48},... | collective-permute-start | bytes 1228808 | tf_op jit(solution)/shard_map/while/body/eval_jaxpr/ppermute | solution.py:13
  551.4 3.1 collective-permute-start
  554.6 6.4 collective-permute-start.1
  561.1 11.4 %collective-permute-start.2 = (bf16[320,640]{1,0:T(8,128)(2,1)S(1)}, bf16[320,640]{1,0:T(8,128)(2,1)S(1)}, u32[]{:S(2)}, u32[]{:S(2)}) collective-permute-start(bf16[320,640]{1,0:T(8,128)(2,1)S(1)} %get-tuple-element.254), channel_id=1, source_target_pairs={{0,16},{4,20},{8,24},{12,28},{16,0},{20,4},{24,8},{28,12},{32,48},... | collective-permute-start | bytes 1228808 | tf_op jit(solution)/shard_map/while/body/eval_jaxpr/ppermute | solution.py:13
  575.3 3.1 collective-permute-start
  578.5 6.4 collective-permute-start.1
  585.0 11.4 %collective-permute-start.2 = (bf16[320,640]{1,0:T(8,128)(2,1)S(1)}, bf16[320,640]{1,0:T(8,128)(2,1)S(1)}, u32[]{:S(2)}, u32[]{:S(2)}) collective-permute-start(bf16[320,640]{1,0:T(8,128)(2,1)S(1)} %get-tuple-element.254), channel_id=1, source_target_pairs={{0,16},{4,20},{8,24},{12,28},{16,0},{20,4},{24,8},{28,12},{32,48},... | collective-permute-start | bytes 1228808 | tf_op jit(solution)/shard_map/while/body/eval_jaxpr/ppermute | solution.py:13
  708.3 4.9 copy-start.1
  712.0 2.0 copy-start.2
Sparse Core Ops, SparseCore 0:
  181.5 301.9 reduce-scatter.1
  600.0 108.2 all-gather.1
where the time goes:
time: 725 us; the launch traced here: 724 us
  waiting for transfers between devices  486 us (67%)
  blocking collectives  126 us (17%)
  local copies, waits for them, and re-layouts  39.9 us (6%)
  matrix products  29.1 us (4%)
  starting transfers between devices  19.5 us (3%)
  between operations  16.5 us (2%)
    reduce_scatter x1, waiting for transfers between devices, local(): lax.psum_scatter(partial_terms.reshape(pair_count * 2 * block_width, bloc...  301 us
    all_to_all x1, blocking collectives, local(): lax.all_to_all(flattened, 'tensor', split_axis=2, concat_axis=1, tiled=True)  126 us
    all_gather x1, waiting for transfers between devices, local(): lax.all_gather(inverse_rows.astype(jnp.bfloat16), 'dp', axis=0, tiled=True)  108 us
    ppermute x15, waiting for transfers between devices, partner_2(): lax.ppermute(array, axis, [(i, i ^ 1 << bit) for i in range(lax.axis_size...  76.6 us
    ppermute x15, starting transfers between devices, partner_2(): lax.ppermute(array, axis, [(i, i ^ 1 << bit) for i in range(lax.axis_size...  19.4 us
    unnamed x7, local copies, waits for them, and re-layouts  15 us
  transfers between devices with their start and end apart: 17, of which 17 were waited for; matrix products, arithmetic and copies ran while one was open for 0% of the time, Pallas kernels for 0%

commit v1 on v0

v1 whole, which is shorter than its diff:
```python
import functools

import jax
import jax.numpy as jnp
from jax import lax
from jax.experimental import pallas as pl
from jax.experimental.pallas import tpu as pltpu
from jax.sharding import PartitionSpec as P

DAMPING = 0.05
BLOCK = 640
TILE = 128
PACK = 384
PANELS = ((0, 0), (128, 0), (256, 0), (256, 384), (128, 512))
RING = 4
SLABS = 4
CHUNK = PACK // RING
PIECE = CHUNK // 2
AXES = ("dp", "tensor")
PARAMS = pltpu.CompilerParams(vmem_limit_bytes=48 * 1024 * 1024)
SMEM = pl.BlockSpec(memory_space=pltpu.SMEM)
VMEM = pl.BlockSpec(memory_space=pltpu.VMEM)
ANY = pl.BlockSpec(memory_space=pl.ANY)


def place_of(device):
    dp, t = device // 4, device % 4
    return dp // 32, dp // 8 % 4, dp // 2 % 4, dp % 2, t


def groups_by(key):
    found = {}
    for device in range(256):
        group, rank = key(*place_of(device))
        found.setdefault(group, []).append((rank, device))
    return [[device for _, device in sorted(found[group])] for group in sorted(found)]


def along_place(zl, x, y, c, t):
    return ((c, zl, y, t), x) if c == 0 else ((c, zl, x, t), y)


def across_place(zl, x, y, c, t):
    return ((c, zl, x, t), y) if c == 0 else ((c, zl, y, t), x)


def along_z(zl, x, y, c, t):
    return (x, y, c), 2 * t + zl


def sharing_block(zl, x, y, c, t):
    return ((c, x, t), 2 * y + zl) if c == 0 else ((c, y, t), 2 * x + zl)


def exchange(array, key):
    return lax.all_to_all(array, AXES, 0, 0, axis_index_groups=groups_by(key), tiled=True)


def to_other_core(array):
    return lax.ppermute(array, "dp", [(i, i ^ 1) for i in range(64)])


def pack_kernel(dev, act, own, sent, sem):
    core = dev[0] // 4 % 2
    copies = []
    for side, out in enumerate((sent, own)):
        for place in range(RING):
            for slab in range(SLABS):
                start = (2 * slab + place % 2) * BLOCK
                copies.append(
                    pltpu.make_async_copy(
                        act.at[core ^ (1 - side), place // 2, :, start : start + BLOCK],
                        out.at[place, slab],
                        sem.at[len(copies)],
                    )
                )
                copies[-1].start()
    for copy in copies:
        copy.wait()


def gram_kernel(own, other, out, tri):
    count = own.shape[0] * own.shape[2]
    for slab in range(SLABS):

        def product(low, high):
            def side(start, stop):
                return jnp.concatenate(
                    [
                        ref[:, slab, :, start:stop].reshape(count, stop - start)
                        for ref in (own, other)
                    ]
                )

            return lax.dot_general(
                side(low, high),
                side(low, BLOCK),
                (((0,), (0,)), ((), ())),
                preferred_element_type=jnp.float32,
            )

        top = product(0, 256)
        tri[0:128, :] = top[0:128]
        tri[128:256, 0:512] = top[128:256, 128:]
        middle = product(256, 512)
        tri[256:384, 0:384] = middle[0:128]
        tri[256:384, 384:640] = middle[128:256, 128:]
        tri[128:256, 512:640] = product(512, 640)
        for place in range(RING):
            rows = tri[place * CHUNK : (place + 1) * CHUNK, :]
            out[place, slab] = rows.astype(out.dtype)


def newton_kernel(tokens_all, dev, newton_steps, total, out, mixed, gap, mixed_half):
    dp, t = dev[0] // 4, dev[0] % 4
    core = dp % 2
    place = jnp.where(core == 0, dp // 8 % 4, dp // 2 % 4)
    steps = newton_steps[core, place // 2, 2 * t + place % 2]
    for i, (row, col) in enumerate(PANELS):
        low = TILE * i
        panel = total[row : row + TILE, col : col + BLOCK - low].astype(jnp.float32)
        mixed[low : low + TILE, low:] = panel
        if i < 4:
            mixed[low + TILE :, low : low + TILE] = panel[:, TILE:].T
    eye = (
        lax.broadcasted_iota(jnp.int32, (BLOCK, BLOCK), 0)
        == lax.broadcasted_iota(jnp.int32, (BLOCK, BLOCK), 1)
    ).astype(jnp.float32)
    factor = mixed[...] * (1.0 / tokens_all) + DAMPING * eye
    norm_scale = jnp.sqrt(jnp.sum(factor * factor))
    mixed[...] = factor / norm_scale

    def dot(a, b):
        return jnp.dot(a.astype(jnp.bfloat16), b, preferred_element_type=jnp.float32)

    gap[...] = mixed[...]
    power = 2.0
    for turn in range(1, 4):
        half = mixed[...].astype(jnp.bfloat16)
        mixed_half[...] = half
        mixed[...] = 2.0 * mixed[...] - dot(half, mixed_half[...])
        mixed_half[...] = mixed[...].astype(jnp.bfloat16)
        new_gap = 2.0 * gap[...] + power * mixed[...] - dot(gap[...], mixed_half[...])
        gap[...] = jnp.where(turn < steps, new_gap, gap[...])
        power = 2.0 * power
    reach = jnp.where(steps <= 1, 2.0, jnp.where(steps == 2, 4.0, jnp.where(steps == 3, 8.0, 16.0)))
    scale = 1.0 / norm_scale
    for i, (row, col) in enumerate(PANELS):
        low = TILE * i
        value = (reach * eye[low : low + TILE, low:] - gap[low : low + TILE, low:]) * scale
        for copy in range(RING):
            out[copy, row : row + TILE, col : col + BLOCK - low] = value.astype(jnp.bfloat16)


def apply_kernel(side, dev, blocks, grad_qkv, grad_up, *refs):
    outs, ins_here, outs_here = refs[-8:-6], refs[-6:-4], refs[-4:-2]
    whole, sem = refs[-2:]
    layer = (dev[0] // 4 % 2) ^ side
    loads = [
        pltpu.make_async_copy(grad.at[layer], here, sem.at[kind])
        for kind, (grad, here) in enumerate(zip((grad_qkv, grad_up), ins_here))
    ]
    stores = [
        pltpu.make_async_copy(here, out.at[layer], sem.at[2 + kind])
        for kind, (out, here) in enumerate(zip(outs, outs_here))
    ]
    for load in loads:
        load.start()
    for place in range(RING):
        kind, j = place // 2, place % 2
        for i, (row, col) in enumerate(PANELS):
            low = TILE * i
            panel = blocks[place, row : row + TILE, col : col + BLOCK - low]
            whole[place, low : low + TILE, low:] = panel
            if i < 4:
                whole[place, low + TILE :, low : low + TILE] = panel[:, TILE:].T
        if j == 0:
            loads[kind].wait()
        columns = slice(j * BLOCK, (j + 1) * BLOCK)
        outs_here[kind][:, columns] = jnp.dot(
            ins_here[kind][:, columns], whole[place], preferred_element_type=jnp.float32
        ).astype(jnp.bfloat16)
        if j == 1:
            stores[kind].start()
    for store in stores:
        store.wait()


def local(activations, grad_qkv, grad_up, newton_steps):
    half = jnp.bfloat16
    dev = (lax.axis_index("dp") * 4 + lax.axis_index("tensor")).astype(jnp.int32).reshape(1)
    rows = activations.shape[2]
    tokens_all = rows * 256

    def shape(*dims):
        return jax.ShapeDtypeStruct(dims, half)

    own, sent = pl.pallas_call(
        pack_kernel,
        out_shape=[shape(RING, SLABS, rows, BLOCK)] * 2,
        in_specs=[SMEM, ANY],
        out_specs=[ANY] * 2,
        scratch_shapes=[pltpu.SemaphoreType.DMA((2 * RING * SLABS,))],
        compiler_params=PARAMS,
        name="pack",
    )(dev, activations)
    other = to_other_core(sent)
    own = exchange(own, along_place)
    other = exchange(other, along_place)

    chunks = pl.pallas_call(
        gram_kernel,
        out_shape=shape(RING, SLABS, CHUNK, BLOCK),
        in_specs=[VMEM] * 2,
        out_specs=VMEM,
        scratch_shapes=[pltpu.VMEM((PACK, BLOCK), jnp.float32)],
        compiler_params=PARAMS,
        name="gram",
    )(own, other)
    chunks = exchange(chunks, across_place)
    pieces = jnp.sum(chunks.astype(jnp.float32), axis=0).astype(half)
    pieces = exchange(pieces.reshape(2 * SLABS, PIECE, BLOCK), along_z)
    piece = jnp.sum(pieces.astype(jnp.float32), axis=0).astype(half)
    members = jnp.broadcast_to(piece[None], (2 * RING, PIECE, BLOCK))
    total = exchange(members, sharing_block).reshape(PACK, BLOCK)

    inverse = pl.pallas_call(
        functools.partial(newton_kernel, tokens_all),
        out_shape=shape(RING, PACK, BLOCK),
        in_specs=[SMEM, SMEM, VMEM],
        out_specs=VMEM,
        scratch_shapes=[
            pltpu.VMEM((BLOCK, BLOCK), jnp.float32),
            pltpu.VMEM((BLOCK, BLOCK), jnp.float32),
            pltpu.VMEM((BLOCK, BLOCK), half),
        ],
        compiler_params=PARAMS,
        name="newton",
    )(dev, newton_steps, total)
    mine = exchange(inverse, along_place)
    others = to_other_core(mine)

    def apply(side, blocks, before):
        kinds = (grad_qkv.shape, grad_up.shape)
        here = [pltpu.VMEM(dims[1:], half) for dims in kinds]
        return pl.pallas_call(
            functools.partial(apply_kernel, side),
            out_shape=[shape(*dims) for dims in kinds],
            in_specs=[SMEM, VMEM] + [ANY] * (2 + len(before)),
            out_specs=[ANY] * 2,
            input_output_aliases={4: 0, 5: 1} if before else {},
            scratch_shapes=here
            + here
            + [pltpu.VMEM((RING, BLOCK, BLOCK), half), pltpu.SemaphoreType.DMA((4,))],
            compiler_params=PARAMS,
            name="apply",
        )(dev, blocks, grad_qkv, grad_up, *before)

    return tuple(apply(1, others, apply(0, mine, ())))


def solution(mesh):
    placed = (
        P(None, None, ("dp", "tensor"), None),
        P(None, "dp", "tensor"),
        P(None, "dp", "tensor"),
        P(),
    )
    return jax.shard_map(
        local,
        mesh=mesh,
        in_specs=placed,
        out_specs=(P(None, "dp", "tensor"), P(None, "dp", "tensor")),
        check_vma=False,
    )
```

time: 725 us -> 141 us (0.19)
  waiting for transfers between devices: 486 us -> 0.6 us
  local copies, waits for them, and re-layouts: 39.9 us -> 0.06 us
  matrix products: 29.1 us -> 0 us
  Pallas kernels: 0 us -> 19.8 us
  blocking collectives: 126 us -> 108 us
  between operations: 16.5 us -> 0.87 us
  starting transfers between devices: 19.5 us -> 11 us
    reduce_scatter x1 -> x0, waiting for transfers between devices: 301 us -> none  [local(): lax.psum_scatter(partial_terms.reshape(pair_count * 2 * block_width, bloc...]
    all_gather x1 -> x0, waiting for transfers between devices: 108 us -> none  [local(): lax.all_gather(inverse_rows.astype(jnp.bfloat16), 'dp', axis=0, tiled=True)]
    ppermute x15 -> x2, waiting for transfers between devices: 76.6 us -> 0.6 us  [to_other_core(): return lax.ppermute(array, 'dp', [(i, i ^ 1) for i in range(64)])]
    dot_general x11 -> x0, matrix products: 29.1 us -> none  [the longest x1 13 us: local(): jnp.einsum('ntjp,ntjq->njpq', halves, halves, preferred_element_type=jnp....]
    pallas_call x0 -> x5, Pallas kernels: none -> 19.8 us  [the longest x1 6.04 us: local(): pl.pallas_call(functools.partial(newton_kernel, tokens_all), out_shape=sh...]
    all_to_all x1 -> x6, blocking collectives: 126 us -> 108 us  [exchange(): lax.all_to_all(array, AXES, 0, 0, axis_index_groups=groups_by(key), tiled...]
    unnamed x7 -> x6, local copies, waits for them, and re-layouts: 15 us -> 0.02 us
    reshape x2 -> x0, local copies, waits for them, and re-layouts: 10.9 us -> none  [the longest x1 10.8 us: local(): halves = received.reshape(item_count, received.shape[1], 2, block_width)]
  transfers between devices with their start and end apart: 17 -> 2, of which waited for: 17 -> 1; matrix products, arithmetic and copies ran while one was open for 0% -> 0% of each run, Pallas kernels for 0% -> 2%
where the time goes in v1:
time: 141 us
  blocking collectives  108 us (77%)
  Pallas kernels  19.8 us (14%)
  starting transfers between devices  11 us (8%)
    all_to_all x6, blocking collectives, exchange(): lax.all_to_all(array, AXES, 0, 0, axis_index_groups=groups_by(key), tiled...  108 us
    ppermute x2, starting transfers between devices, to_other_core(): return lax.ppermute(array, 'dp', [(i, i ^ 1) for i in range(64)])  11 us
    pallas_call x1, Pallas kernels, local(): pl.pallas_call(functools.partial(newton_kernel, tokens_all), out_shape=sh...  6.04 us
    pallas_call x2, Pallas kernels, apply(): pl.pallas_call(functools.partial(apply_kernel, side), out_shape=[shape(*d...  5.98 us
    pallas_call x1, Pallas kernels, local(): pl.pallas_call(gram_kernel, out_shape=shape(RING, SLABS, CHUNK, BLOCK), i...  4.93 us
    pallas_call x1, Pallas kernels, local(): pl.pallas_call(pack_kernel, out_shape=[shape(RING, SLABS, rows, BLOCK)] *...  2.9 us
  transfers between devices with their start and end apart: 2, of which 1 were waited for; matrix products, arithmetic and copies ran while one was open for 0% of the time, Pallas kernels for 2%

profile of v1, /device:TPU:1, one launch (start us, length us, event | category | flops | bytes accessed | tf_op | source)
XLA Modules:
  0.0 141.1 jit_solution(5357181471827631549)
XLA Ops:
  0.6 2.9 %pack.1 = (bf16[4,4,128,640]{3,2,1,0:T(8,128)(2,1)S(1)}, bf16[4,4,128,640]{3,2,1,0:T(8,128)(2,1)S(1)}) custom-call(s32[1]{0:T(128)} %bitcast.dev, bf16[2,2,128,5120]{3,2,1,0:T(8,128)(2,1)} %act.1), custom_call_target="tpu_custom_call" | custom-call | tf_op jit(solution)/shard_map/pack/pallas_call | solution.py:198
  3.5 3.3 %collective-permute-start = (bf16[4,4,128,640]{3,2,1,0:T(8,128)(2,1)S(1)}, bf16[4,4,128,640]{3,2,1,0:T(8,128)(2,1)S(1)}, u32[]{:S(2)}, u32[]{:S(2)}) collective-permute-start(bf16[4,4,128,640]{3,2,1,0:T(8,128)(2,1)S(1)} %get-tuple-element.7), channel_id=1, source_target_pairs={{0,4},{4,0},{8,12},{12,8},{16,20},{20,16},{24,28},{28,24},{32,36},... | collective-permute-start | bytes 7864328 | tf_op jit(solution)/shard_map/ppermute | solution.py:60
  6.9 20.7 %all_to_all.30.own = bf16[4,4,128,640]{3,2,1,0:T(8,128)(2,1)S(1)} all-to-all(bf16[4,4,128,640]{3,2,1,0:T(8,128)(2,1)S(1)} %get-tuple-element.6), channel_id=1, replica_groups={{0,32,64,96},{1,33,65,97},{2,34,66,98},{3,35,67,99},{8,40,72,104},{9,41..., dimensions={0} | all-to-all | bytes 5242880 | tf_op jit(solution)/shard_map/all_to_all | solution.py:56
  27.6 0.0 collective-permute-done
  27.6 21.7 %all_to_all.31.other = bf16[4,4,128,640]{3,2,1,0:T(8,128)(2,1)} all-to-all(bf16[4,4,128,640]{3,2,1,0:T(8,128)(2,1)S(1)} %collective-permute-done), channel_id=1, replica_groups={{0,32,64,96},{1,33,65,97},{2,34,66,98},{3,35,67,99},{8,40,72,104},{9,41..., dimensions={0} | all-to-all | bytes 5242880 | tf_op jit(solution)/shard_map/all_to_all | solution.py:56
  49.3 4.9 %gram.1 = bf16[4,4,96,640]{3,2,1,0:T(8,128)(2,1)S(1)} custom-call(bf16[4,4,128,640]{3,2,1,0:T(8,128)(2,1)S(1)} %all_to_all.30.own, bf16[4,4,128,640]{3,2,1,0:T(8,128)(2,1)} %all_to_all.31.other), custom_call_target="tpu_custom_call" | custom-call | tf_op jit(solution)/shard_map/gram/pallas_call | solution.py:211
  54.3 18.0 %all_to_all.32 = bf16[4,4,96,640]{3,2,1,0:T(8,128)(2,1)S(1)} all-to-all(bf16[4,4,96,640]{3,2,1,0:T(8,128)(2,1)S(1)} %gram.1), channel_id=1, replica_groups={{0,8,16,24},{1,9,17,25},{2,10,18,26},{3,11,19,27},{32,40,48,56},{33,41,..., dimensions={0} | all-to-all | bytes 3932160 | tf_op jit(solution)/shard_map/all_to_all | solution.py:56
  72.3 0.5 reduce_sum.24
  72.8 0.0 copy-start.2
  72.8 20.2 %all_to_all.33 = bf16[8,48,640]{2,1,0:T(8,128)(2,1)S(1)} all-to-all(bf16[8,48,640]{2,1,0:T(8,128)(2,1)S(1)} %bitcast.4), channel_id=1, replica_groups={{0,128,1,129,2,130,3,131},{4,132,5,133,6,134,7,135},{8,136,9,137,10,138..., dimensions={0} | all-to-all | bytes 983040 | tf_op jit(solution)/shard_map/all_to_all | solution.py:56
  93.0 0.1 reduce_sum.25
  93.2 9.8 %all_to_all.34 = bf16[8,48,640]{2,1,0:T(8,128)(2,1)S(1)} all-to-all(bf16[8,48,640]{2,1,0:T(8,128)(2,1)S(1)} %broadcast_in_dim.2), channel_id=1, replica_groups={{0,128,8,136,16,144,24,152},{1,129,9,137,17,145,25,153},{2,130,10,138,1..., dimensions={0} | all-to-all | bytes 983040 | tf_op jit(solution)/shard_map/all_to_all | solution.py:56
  102.9 0.0 copy-done.2
  102.9 6.0 %newton.1 = bf16[4,384,640]{2,1,0:T(8,128)(2,1)S(1)} custom-call(s32[1]{0:T(128)} %bitcast.dev, s32[2,2,8]{2,1,0:T(2,128)S(1)} %copy-done.2, bf16[384,640]{1,0:T(8,128)(2,1)S(1)} %bitcast.3), custom_call_target="tpu_custom_call" | custom-call | tf_op jit(solution)/shard_map/newton/pallas_call | solution.py:227
  109.0 0.0 copy-start
  109.0 0.0 copy-start.1
  109.0 17.7 %all_to_all.35.blocks = bf16[4,384,640]{2,1,0:T(8,128)(2,1)S(1)} all-to-all(bf16[4,384,640]{2,1,0:T(8,128)(2,1)S(1)} %newton.1), channel_id=1, replica_groups={{0,32,64,96},{1,33,65,97},{2,34,66,98},{3,35,67,99},{8,40,72,104},{9,41..., dimensions={0} | all-to-all | bytes 3932160 | tf_op jit(solution)/shard_map/all_to_all | solution.py:56
  126.7 7.7 %collective-permute-start.1 = (bf16[4,384,640]{2,1,0:T(8,128)(2,1)S(1)}, bf16[4,384,640]{2,1,0:T(8,128)(2,1)S(1)}, u32[]{:S(2)}, u32[]{:S(2)}) collective-permute-start(bf16[4,384,640]{2,1,0:T(8,128)(2,1)S(1)} %all_to_all.35.blocks), channel_id=1, source_target_pairs={{0,4},{4,0},{8,12},{12,8},{16,20},{20,16},{24,28},{28,24},{32,36},... | collective-permute-start | bytes 5898248 | tf_op jit(solution)/shard_map/ppermute | solution.py:60
  134.4 0.0 copy-done
  134.4 0.0 copy-done.1
  134.4 3.0 %apply.2 = (bf16[2,240,1280]{2,1,0:T(8,128)(2,1)}, bf16[2,320,1280]{2,1,0:T(8,128)(2,1)}) custom-call(s32[1]{0:T(128)} %bitcast.dev, bf16[4,384,640]{2,1,0:T(8,128)(2,1)S(1)} %all_to_all.35.blocks, bf16[2,240,1280]{2,1,0:T(8,128)(2,1)S(1)} %copy-done.1, bf16[2,320,1280]{2,1,0:T(8,128)(2,1)S(1)} %copy-done), custom_call_target="tpu_custom_call" | custom-call | tf_op jit(solution)/shard_map/apply/pallas_call | solution.py:246
  137.4 0.6 collective-permute-done.1.blocks
  138.0 3.0 %apply.3 = (bf16[2,240,1280]{2,1,0:T(8,128)(2,1)}, bf16[2,320,1280]{2,1,0:T(8,128)(2,1)}) custom-call(s32[1]{0:T(128)} %bitcast.dev, bf16[4,384,640]{2,1,0:T(8,128)(2,1)S(1)} %collective-permute-done.1.blocks, bf16[2,240,1280]{2,1,0:T(8,128)(2,1)S(1)} %copy-done.1, bf16[2,320,1280]{2,1,0:T(8,128)(2,1)S(1)} %copy-done, ...), custom_call_target="tpu_custom_call", output_to_operand_aliasing={{0}: (4, {}), {1}: (5, {})} | custom-call | tf_op jit(solution)/shard_map/apply/pallas_call | solution.py:246
  (1 shorter events, 0.0 us)
Async XLA Ops:
  3.5 24.1 %collective-permute-start = (bf16[4,4,128,640]{3,2,1,0:T(8,128)(2,1)S(1)}, bf16[4,4,128,640]{3,2,1,0:T(8,128)(2,1)S(1)}, u32[]{:S(2)}, u32[]{:S(2)}) collective-permute-start(bf16[4,4,128,640]{3,2,1,0:T(8,128)(2,1)S(1)} %get-tuple-element.7), channel_id=1, source_target_pairs={{0,4},{4,0},{8,12},{12,8},{16,20},{20,16},{24,28},{28,24},{32,36},... | collective-permute-start | bytes 7864328 | tf_op jit(solution)/shard_map/ppermute | solution.py:60
  72.8 30.1 %copy-start.2 = (s32[2,2,8]{2,1,0:T(2,128)S(1)}, s32[2,2,8]{2,1,0:T(2,128)}, u32[]{:S(2)}) copy-start(s32[2,2,8]{2,1,0:T(2,128)} %newton_steps.1) | copy-start | bytes 388
  109.0 25.4 %copy-start = (bf16[2,320,1280]{2,1,0:T(8,128)(2,1)S(1)}, bf16[2,320,1280]{2,1,0:T(8,128)(2,1)}, u32[]{:S(2)}) copy-start(bf16[2,320,1280]{2,1,0:T(8,128)(2,1)} %grad_up.3) | copy-start | bytes 4915204
  109.0 25.4 %copy-start.1 = (bf16[2,240,1280]{2,1,0:T(8,128)(2,1)S(1)}, bf16[2,240,1280]{2,1,0:T(8,128)(2,1)}, u32[]{:S(2)}) copy-start(bf16[2,240,1280]{2,1,0:T(8,128)(2,1)} %grad_qkv.3) | copy-start | bytes 3686404
  126.7 11.3 %collective-permute-start.1 = (bf16[4,384,640]{2,1,0:T(8,128)(2,1)S(1)}, bf16[4,384,640]{2,1,0:T(8,128)(2,1)S(1)}, u32[]{:S(2)}, u32[]{:S(2)}) collective-permute-start(bf16[4,384,640]{2,1,0:T(8,128)(2,1)S(1)} %all_to_all.35.blocks), channel_id=1, source_target_pairs={{0,4},{4,0},{8,12},{12,8},{16,20},{20,16},{24,28},{28,24},{32,36},... | collective-permute-start | bytes 5898248 | tf_op jit(solution)/shard_map/ppermute | solution.py:60

commit v2 on v1

--- a/solution.py
+++ b/solution.py
@@ -23,25 +23,40 @@
 ANY = pl.BlockSpec(memory_space=pl.ANY)
 
 
-def place_of(device):
+def bit_a(i):
+    return (i + 1) // 2 % 2
+
+
+def bit_b(i):
+    return i // 2
+
+
+def device_at(device):
     dp, t = device // 4, device % 4
     return dp // 32, dp // 8 % 4, dp // 2 % 4, dp % 2, t
+
+
+def squares(x, y, c):
+    a, b = 2 * bit_a(x) + bit_a(y), 2 * bit_b(x) + bit_b(y)
+    return (a, b) if c == 0 else (b, a)
 
 
 def groups_by(key):
     found = {}
     for device in range(256):
-        group, rank = key(*place_of(device))
+        group, rank = key(*device_at(device))
         found.setdefault(group, []).append((rank, device))
     return [[device for _, device in sorted(found[group])] for group in sorted(found)]
 
 
 def along_place(zl, x, y, c, t):
-    return ((c, zl, y, t), x) if c == 0 else ((c, zl, x, t), y)
+    place, other = squares(x, y, c)
+    return (c, zl, t, other), place
 
 
 def across_place(zl, x, y, c, t):
-    return ((c, zl, x, t), y) if c == 0 else ((c, zl, y, t), x)
+    place, other = squares(x, y, c)
+    return (c, zl, t, place), other
 
 
 def along_z(zl, x, y, c, t):
@@ -49,7 +64,8 @@
 
 
 def sharing_block(zl, x, y, c, t):
-    return ((c, x, t), 2 * y + zl) if c == 0 else ((c, y, t), 2 * x + zl)
+    place, other = squares(x, y, c)
+    return (c, t, place), 2 * other + zl
 
 
 def exchange(array, key):
@@ -111,10 +127,11 @@
             out[place, slab] = rows.astype(out.dtype)
 
 
-def newton_kernel(tokens_all, dev, newton_steps, total, out, mixed, gap, mixed_half):
+def newton_kernel(tokens_all, dev, newton_steps, total, out, mixed, gap, halves):
     dp, t = dev[0] // 4, dev[0] % 4
     core = dp % 2
-    place = jnp.where(core == 0, dp // 8 % 4, dp // 2 % 4)
+    x, y = dp // 8 % 4, dp // 2 % 4
+    place = jnp.where(core == 0, 2 * bit_a(x) + bit_a(y), 2 * bit_b(x) + bit_b(y))
     steps = newton_steps[core, place // 2, 2 * t + place % 2]
     for i, (row, col) in enumerate(PANELS):
         low = TILE * i
@@ -130,19 +147,25 @@
     norm_scale = jnp.sqrt(jnp.sum(factor * factor))
     mixed[...] = factor / norm_scale
 
-    def dot(a, b):
-        return jnp.dot(a.astype(jnp.bfloat16), b, preferred_element_type=jnp.float32)
+    def dot(rows):
+        return jnp.dot(halves[0:rows, :], halves[0:BLOCK, :], preferred_element_type=jnp.float32)
+
+    def last():
+        return jnp.dot(halves[BLOCK:, :], halves[0:BLOCK, :], preferred_element_type=jnp.float32)
 
     gap[...] = mixed[...]
-    power = 2.0
+    halves[0:BLOCK, :] = mixed[...].astype(jnp.bfloat16)
+    halves[BLOCK:, :] = mixed[...].astype(jnp.bfloat16)
+    mixed[...] = 2.0 * mixed[...] - dot(BLOCK)
     for turn in range(1, 4):
-        half = mixed[...].astype(jnp.bfloat16)
-        mixed_half[...] = half
-        mixed[...] = 2.0 * mixed[...] - dot(half, mixed_half[...])
-        mixed_half[...] = mixed[...].astype(jnp.bfloat16)
-        new_gap = 2.0 * gap[...] + power * mixed[...] - dot(gap[...], mixed_half[...])
+        halves[0:BLOCK, :] = mixed[...].astype(jnp.bfloat16)
+        products = dot(2 * BLOCK) if turn < 3 else None
+        step = products[BLOCK:] if turn < 3 else last()
+        new_gap = 2.0 * gap[...] + 2.0**turn * mixed[...] - step
         gap[...] = jnp.where(turn < steps, new_gap, gap[...])
-        power = 2.0 * power
+        if turn < 3:
+            mixed[...] = 2.0 * mixed[...] - products[0:BLOCK]
+            halves[BLOCK:, :] = gap[...].astype(jnp.bfloat16)
     reach = jnp.where(steps <= 1, 2.0, jnp.where(steps == 2, 4.0, jnp.where(steps == 3, 8.0, 16.0)))
     scale = 1.0 / norm_scale
     for i, (row, col) in enumerate(PANELS):
@@ -232,7 +255,7 @@
         scratch_shapes=[
             pltpu.VMEM((BLOCK, BLOCK), jnp.float32),
             pltpu.VMEM((BLOCK, BLOCK), jnp.float32),
-            pltpu.VMEM((BLOCK, BLOCK), half),
+            pltpu.VMEM((2 * BLOCK, BLOCK), half),
         ],
         compiler_params=PARAMS,
         name="newton",

time: 141 us -> 145 us (1.028)
  blocking collectives: 108 us -> 117 us
  starting transfers between devices: 11 us -> 5.58 us
    all_to_all x6, blocking collectives: 108 us -> 117 us  [exchange(): lax.all_to_all(array, AXES, 0, 0, axis_index_groups=groups_by(key), tiled...]
    ppermute x2, starting transfers between devices: 11 us -> 5.58 us  [to_other_core(): return lax.ppermute(array, 'dp', [(i, i ^ 1) for i in range(64)])]
where the time goes in v2:
time: 145 us
  blocking collectives  117 us (81%)
  Pallas kernels  19.9 us (14%)
  starting transfers between devices  5.58 us (4%)
    all_to_all x6, blocking collectives, exchange(): lax.all_to_all(array, AXES, 0, 0, axis_index_groups=groups_by(key), tiled...  117 us
    pallas_call x1, Pallas kernels, local(): pl.pallas_call(functools.partial(newton_kernel, tokens_all), out_shape=sh...  6.09 us
    pallas_call x2, Pallas kernels, apply(): pl.pallas_call(functools.partial(apply_kernel, side), out_shape=[shape(*d...  5.98 us
    ppermute x2, starting transfers between devices, to_other_core(): return lax.ppermute(array, 'dp', [(i, i ^ 1) for i in range(64)])  5.58 us
    pallas_call x1, Pallas kernels, local(): pl.pallas_call(gram_kernel, out_shape=shape(RING, SLABS, CHUNK, BLOCK), i...  4.92 us
  transfers between devices with their start and end apart: 2, of which 1 were waited for; matrix products, arithmetic and copies ran while one was open for 0% of the time, Pallas kernels for 2%

profile of v2, /device:TPU:1, one launch (start us, length us, event | category | flops | bytes accessed | tf_op | source)
XLA Modules:
  0.0 145.0 jit_solution(17193811494824619429)
XLA Ops:
  0.6 2.9 %pack.1 = (bf16[4,4,128,640]{3,2,1,0:T(8,128)(2,1)S(1)}, bf16[4,4,128,640]{3,2,1,0:T(8,128)(2,1)S(1)}) custom-call(s32[1]{0:T(128)} %bitcast.dev, bf16[2,2,128,5120]{3,2,1,0:T(8,128)(2,1)} %act.1), custom_call_target="tpu_custom_call" | custom-call | tf_op jit(solution)/shard_map/pack/pallas_call | solution.py:221
  3.5 3.3 %collective-permute-start = (bf16[4,4,128,640]{3,2,1,0:T(8,128)(2,1)S(1)}, bf16[4,4,128,640]{3,2,1,0:T(8,128)(2,1)S(1)}, u32[]{:S(2)}, u32[]{:S(2)}) collective-permute-start(bf16[4,4,128,640]{3,2,1,0:T(8,128)(2,1)S(1)} %get-tuple-element.7), channel_id=1, source_target_pairs={{0,4},{4,0},{8,12},{12,8},{16,20},{20,16},{24,28},{28,24},{32,36},... | collective-permute-start | bytes 7864328 | tf_op jit(solution)/shard_map/ppermute | solution.py:76
  6.9 23.9 %all_to_all.30.own = bf16[4,4,128,640]{3,2,1,0:T(8,128)(2,1)S(1)} all-to-all(bf16[4,4,128,640]{3,2,1,0:T(8,128)(2,1)S(1)} %get-tuple-element.6), channel_id=1, replica_groups={{0,8,32,40},{24,16,56,48},{96,104,64,72},{120,112,88,80},{1,9,33,41},{2..., dimensions={0} | all-to-all | bytes 5242880 | tf_op jit(solution)/shard_map/all_to_all | solution.py:72
  30.8 0.0 collective-permute-done
  30.8 22.9 %all_to_all.31.other = bf16[4,4,128,640]{3,2,1,0:T(8,128)(2,1)} all-to-all(bf16[4,4,128,640]{3,2,1,0:T(8,128)(2,1)S(1)} %collective-permute-done), channel_id=1, replica_groups={{0,8,32,40},{24,16,56,48},{96,104,64,72},{120,112,88,80},{1,9,33,41},{2..., dimensions={0} | all-to-all | bytes 5242880 | tf_op jit(solution)/shard_map/all_to_all | solution.py:72
  53.7 4.9 %gram.1 = bf16[4,4,96,640]{3,2,1,0:T(8,128)(2,1)S(1)} custom-call(bf16[4,4,128,640]{3,2,1,0:T(8,128)(2,1)S(1)} %all_to_all.30.own, bf16[4,4,128,640]{3,2,1,0:T(8,128)(2,1)} %all_to_all.31.other), custom_call_target="tpu_custom_call" | custom-call | tf_op jit(solution)/shard_map/gram/pallas_call | solution.py:234
  58.6 16.5 %all_to_all.32 = bf16[4,4,96,640]{3,2,1,0:T(8,128)(2,1)S(1)} all-to-all(bf16[4,4,96,640]{3,2,1,0:T(8,128)(2,1)S(1)} %gram.1), channel_id=1, replica_groups={{0,24,96,120},{8,16,104,112},{32,56,64,88},{40,48,72,80},{1,25,97,121},..., dimensions={0} | all-to-all | bytes 3932160 | tf_op jit(solution)/shard_map/all_to_all | solution.py:72
  75.1 0.5 reduce_sum.24
  75.6 0.0 copy-start.2
  75.6 22.8 %all_to_all.33 = bf16[8,48,640]{2,1,0:T(8,128)(2,1)S(1)} all-to-all(bf16[8,48,640]{2,1,0:T(8,128)(2,1)S(1)} %bitcast.4), channel_id=1, replica_groups={{0,128,1,129,2,130,3,131},{4,132,5,133,6,134,7,135},{8,136,9,137,10,138..., dimensions={0} | all-to-all | bytes 983040 | tf_op jit(solution)/shard_map/all_to_all | solution.py:72
  98.4 0.1 reduce_sum.25
  98.5 12.1 %all_to_all.34 = bf16[8,48,640]{2,1,0:T(8,128)(2,1)S(1)} all-to-all(bf16[8,48,640]{2,1,0:T(8,128)(2,1)S(1)} %broadcast_in_dim.2), channel_id=1, replica_groups={{0,128,24,152,96,224,120,248},{8,136,16,144,104,232,112,240},{32,160,56..., dimensions={0} | all-to-all | bytes 983040 | tf_op jit(solution)/shard_map/all_to_all | solution.py:72
  110.6 0.0 copy-done.2
  110.6 6.1 %newton.1 = bf16[4,384,640]{2,1,0:T(8,128)(2,1)S(1)} custom-call(s32[1]{0:T(128)} %bitcast.dev, s32[2,2,8]{2,1,0:T(2,128)S(1)} %copy-done.2, bf16[384,640]{1,0:T(8,128)(2,1)S(1)} %bitcast.3), custom_call_target="tpu_custom_call" | custom-call | tf_op jit(solution)/shard_map/newton/pallas_call | solution.py:250
  116.7 0.0 copy-start
  116.7 0.0 copy-start.1
  116.7 19.2 %all_to_all.35.blocks = bf16[4,384,640]{2,1,0:T(8,128)(2,1)S(1)} all-to-all(bf16[4,384,640]{2,1,0:T(8,128)(2,1)S(1)} %newton.1), channel_id=1, replica_groups={{0,8,32,40},{24,16,56,48},{96,104,64,72},{120,112,88,80},{1,9,33,41},{2..., dimensions={0} | all-to-all | bytes 3932160 | tf_op jit(solution)/shard_map/all_to_all | solution.py:72
  136.0 2.2 %collective-permute-start.1 = (bf16[4,384,640]{2,1,0:T(8,128)(2,1)S(1)}, bf16[4,384,640]{2,1,0:T(8,128)(2,1)S(1)}, u32[]{:S(2)}, u32[]{:S(2)}) collective-permute-start(bf16[4,384,640]{2,1,0:T(8,128)(2,1)S(1)} %all_to_all.35.blocks), channel_id=1, source_target_pairs={{0,4},{4,0},{8,12},{12,8},{16,20},{20,16},{24,28},{28,24},{32,36},... | collective-permute-start | bytes 5898248 | tf_op jit(solution)/shard_map/ppermute | solution.py:76
  138.2 0.0 copy-done
  138.2 0.0 copy-done.1
  138.2 3.0 %apply.2 = (bf16[2,240,1280]{2,1,0:T(8,128)(2,1)}, bf16[2,320,1280]{2,1,0:T(8,128)(2,1)}) custom-call(s32[1]{0:T(128)} %bitcast.dev, bf16[4,384,640]{2,1,0:T(8,128)(2,1)S(1)} %all_to_all.35.blocks, bf16[2,240,1280]{2,1,0:T(8,128)(2,1)S(1)} %copy-done.1, bf16[2,320,1280]{2,1,0:T(8,128)(2,1)S(1)} %copy-done), custom_call_target="tpu_custom_call" | custom-call | tf_op jit(solution)/shard_map/apply/pallas_call | solution.py:269
  141.2 0.6 collective-permute-done.1.blocks
  141.8 3.0 %apply.3 = (bf16[2,240,1280]{2,1,0:T(8,128)(2,1)}, bf16[2,320,1280]{2,1,0:T(8,128)(2,1)}) custom-call(s32[1]{0:T(128)} %bitcast.dev, bf16[4,384,640]{2,1,0:T(8,128)(2,1)S(1)} %collective-permute-done.1.blocks, bf16[2,240,1280]{2,1,0:T(8,128)(2,1)S(1)} %copy-done.1, bf16[2,320,1280]{2,1,0:T(8,128)(2,1)S(1)} %copy-done, ...), custom_call_target="tpu_custom_call", output_to_operand_aliasing={{0}: (4, {}), {1}: (5, {})} | custom-call | tf_op jit(solution)/shard_map/apply/pallas_call | solution.py:269
  (1 shorter events, 0.0 us)
Async XLA Ops:
  3.5 27.2 %collective-permute-start = (bf16[4,4,128,640]{3,2,1,0:T(8,128)(2,1)S(1)}, bf16[4,4,128,640]{3,2,1,0:T(8,128)(2,1)S(1)}, u32[]{:S(2)}, u32[]{:S(2)}) collective-permute-start(bf16[4,4,128,640]{3,2,1,0:T(8,128)(2,1)S(1)} %get-tuple-element.7), channel_id=1, source_target_pairs={{0,4},{4,0},{8,12},{12,8},{16,20},{20,16},{24,28},{28,24},{32,36},... | collective-permute-start | bytes 7864328 | tf_op jit(solution)/shard_map/ppermute | solution.py:76
  75.6 35.0 %copy-start.2 = (s32[2,2,8]{2,1,0:T(2,128)S(1)}, s32[2,2,8]{2,1,0:T(2,128)}, u32[]{:S(2)}) copy-start(s32[2,2,8]{2,1,0:T(2,128)} %newton_steps.1) | copy-start | bytes 388
  116.7 21.5 %copy-start = (bf16[2,320,1280]{2,1,0:T(8,128)(2,1)S(1)}, bf16[2,320,1280]{2,1,0:T(8,128)(2,1)}, u32[]{:S(2)}) copy-start(bf16[2,320,1280]{2,1,0:T(8,128)(2,1)} %grad_up.3) | copy-start | bytes 4915204
  116.7 21.5 %copy-start.1 = (bf16[2,240,1280]{2,1,0:T(8,128)(2,1)S(1)}, bf16[2,240,1280]{2,1,0:T(8,128)(2,1)}, u32[]{:S(2)}) copy-start(bf16[2,240,1280]{2,1,0:T(8,128)(2,1)} %grad_qkv.3) | copy-start | bytes 3686404
  136.0 5.8 %collective-permute-start.1 = (bf16[4,384,640]{2,1,0:T(8,128)(2,1)S(1)}, bf16[4,384,640]{2,1,0:T(8,128)(2,1)S(1)}, u32[]{:S(2)}, u32[]{:S(2)}) collective-permute-start(bf16[4,384,640]{2,1,0:T(8,128)(2,1)S(1)} %all_to_all.35.blocks), channel_id=1, source_target_pairs={{0,4},{4,0},{8,12},{12,8},{16,20},{20,16},{24,28},{28,24},{32,36},... | collective-permute-start | bytes 5898248 | tf_op jit(solution)/shard_map/ppermute | solution.py:76

commit v3 on v2

--- a/solution.py
+++ b/solution.py
@@ -49,16 +49,6 @@
     return [[device for _, device in sorted(found[group])] for group in sorted(found)]
 
 
-def along_place(zl, x, y, c, t):
-    place, other = squares(x, y, c)
-    return (c, zl, t, other), place
-
-
-def across_place(zl, x, y, c, t):
-    place, other = squares(x, y, c)
-    return (c, zl, t, place), other
-
-
 def along_z(zl, x, y, c, t):
     return (x, y, c), 2 * t + zl
 
@@ -76,41 +66,56 @@
     return lax.ppermute(array, "dp", [(i, i ^ 1) for i in range(64)])
 
 
-def pack_kernel(dev, act, own, sent, sem):
-    core = dev[0] // 4 % 2
+def in_square(array, flip, of_places):
+    pairs = []
+    for device in range(256):
+        zl, x, y, c, t = device_at(device)
+        if (c == 0) == of_places:
+            x2, y2 = x ^ 1, y ^ 1
+        else:
+            x2, y2 = 3 - x, 3 - y
+        x = x2 if flip & 2 else x
+        y = y2 if flip & 1 else y
+        pairs.append((device, (((zl * 4 + x) * 4 + y) * 2 + c) * 4 + t))
+    return lax.ppermute(array, AXES, pairs)
+
+
+def here(dev):
+    dp = dev[0] // 4
+    core, x, y = dp % 2, dp // 8 % 4, dp // 2 % 4
+    a, b = 2 * bit_a(x) + bit_a(y), 2 * bit_b(x) + bit_b(y)
+    return core, jnp.where(core == 0, a, b), jnp.where(core == 0, b, a)
+
+
+def pack_kernel(side, dev, act, *refs):
+    outs, sem = refs[:RING], refs[RING]
+    core, mine, across = here(dev)
     copies = []
-    for side, out in enumerate((sent, own)):
-        for place in range(RING):
-            for slab in range(SLABS):
-                start = (2 * slab + place % 2) * BLOCK
-                copies.append(
-                    pltpu.make_async_copy(
-                        act.at[core ^ (1 - side), place // 2, :, start : start + BLOCK],
-                        out.at[place, slab],
-                        sem.at[len(copies)],
-                    )
+    for flip in range(RING):
+        place = (across if side else mine) ^ flip
+        for slab in range(SLABS):
+            start = pl.multiple_of((2 * slab + place % 2) * BLOCK, TILE)
+            copies.append(
+                pltpu.make_async_copy(
+                    act.at[core ^ side, place // 2, :, pl.ds(start, BLOCK)],
+                    outs[flip].at[slab],
+                    sem.at[len(copies)],
                 )
-                copies[-1].start()
+            )
+            copies[-1].start()
     for copy in copies:
         copy.wait()
 
 
-def gram_kernel(own, other, out, tri):
-    count = own.shape[0] * own.shape[2]
+def gram_kernel(dev, *refs):
+    ins, outs, tri = refs[: 2 * RING], refs[2 * RING : 3 * RING], refs[3 * RING]
+    across = here(dev)[2]
     for slab in range(SLABS):
 
         def product(low, high):
-            def side(start, stop):
-                return jnp.concatenate(
-                    [
-                        ref[:, slab, :, start:stop].reshape(count, stop - start)
-                        for ref in (own, other)
-                    ]
-                )
-
             return lax.dot_general(
-                side(low, high),
-                side(low, BLOCK),
+                jnp.concatenate([ref[slab, :, low:high] for ref in ins]),
+                jnp.concatenate([ref[slab, :, low:] for ref in ins]),
                 (((0,), (0,)), ((), ())),
                 preferred_element_type=jnp.float32,
             )
@@ -122,16 +127,14 @@
         tri[256:384, 0:384] = middle[0:128]
         tri[256:384, 384:640] = middle[128:256, 128:]
         tri[128:256, 512:640] = product(512, 640)
-        for place in range(RING):
-            rows = tri[place * CHUNK : (place + 1) * CHUNK, :]
-            out[place, slab] = rows.astype(out.dtype)
+        for flip in range(RING):
+            start = pl.multiple_of((across ^ flip) * CHUNK, 32)
+            outs[flip][slab] = tri[pl.ds(start, CHUNK), :].astype(jnp.bfloat16)
 
 
 def newton_kernel(tokens_all, dev, newton_steps, total, out, mixed, gap, halves):
-    dp, t = dev[0] // 4, dev[0] % 4
-    core = dp % 2
-    x, y = dp // 8 % 4, dp // 2 % 4
-    place = jnp.where(core == 0, 2 * bit_a(x) + bit_a(y), 2 * bit_b(x) + bit_b(y))
+    t = dev[0] % 4
+    core, place, _ = here(dev)
     steps = newton_steps[core, place // 2, 2 * t + place % 2]
     for i, (row, col) in enumerate(PANELS):
         low = TILE * i
@@ -171,24 +174,32 @@
     for i, (row, col) in enumerate(PANELS):
         low = TILE * i
         value = (reach * eye[low : low + TILE, low:] - gap[low : low + TILE, low:]) * scale
-        for copy in range(RING):
-            out[copy, row : row + TILE, col : col + BLOCK - low] = value.astype(jnp.bfloat16)
-
-
-def apply_kernel(side, dev, blocks, grad_qkv, grad_up, *refs):
-    outs, ins_here, outs_here = refs[-8:-6], refs[-6:-4], refs[-4:-2]
-    whole, sem = refs[-2:]
-    layer = (dev[0] // 4 % 2) ^ side
+        out[row : row + TILE, col : col + BLOCK - low] = value.astype(jnp.bfloat16)
+
+
+def apply_kernel(side, dev, *refs):
+    ins, grads, outs = refs[:RING], refs[RING : RING + 2], refs[-10:-8]
+    ins_here, outs_here, blocks, whole, sem, block_sem = refs[-8:-6], refs[-6:-4], *refs[-4:]
+    core, mine, across = here(dev)
+    layer = core ^ side
+    arrivals = [
+        pltpu.make_async_copy(
+            ins[flip], blocks.at[(across if side else mine) ^ flip], block_sem.at[flip]
+        )
+        for flip in range(RING)
+    ]
     loads = [
-        pltpu.make_async_copy(grad.at[layer], here, sem.at[kind])
-        for kind, (grad, here) in enumerate(zip((grad_qkv, grad_up), ins_here))
+        pltpu.make_async_copy(grad.at[layer], place, sem.at[kind])
+        for kind, (grad, place) in enumerate(zip(grads, ins_here))
     ]
     stores = [
-        pltpu.make_async_copy(here, out.at[layer], sem.at[2 + kind])
-        for kind, (out, here) in enumerate(zip(outs, outs_here))
+        pltpu.make_async_copy(place, out.at[layer], sem.at[2 + kind])
+        for kind, (out, place) in enumerate(zip(outs, outs_here))
     ]
-    for load in loads:
-        load.start()
+    for copy in arrivals + loads:
+        copy.start()
+    for copy in arrivals:
+        copy.wait()
     for place in range(RING):
         kind, j = place // 2, place % 2
         for i, (row, col) in enumerate(PANELS):
@@ -218,30 +229,36 @@
     def shape(*dims):
         return jax.ShapeDtypeStruct(dims, half)
 
-    own, sent = pl.pallas_call(
-        pack_kernel,
-        out_shape=[shape(RING, SLABS, rows, BLOCK)] * 2,
-        in_specs=[SMEM, ANY],
-        out_specs=[ANY] * 2,
-        scratch_shapes=[pltpu.SemaphoreType.DMA((2 * RING * SLABS,))],
-        compiler_params=PARAMS,
-        name="pack",
-    )(dev, activations)
-    other = to_other_core(sent)
-    own = exchange(own, along_place)
-    other = exchange(other, along_place)
+    def pack(side):
+        return pl.pallas_call(
+            functools.partial(pack_kernel, side),
+            out_shape=[shape(SLABS, rows, BLOCK)] * RING,
+            in_specs=[SMEM, ANY],
+            out_specs=[ANY] * RING,
+            scratch_shapes=[pltpu.SemaphoreType.DMA((RING * SLABS,))],
+            compiler_params=PARAMS,
+            name="pack",
+        )(dev, activations)
+
+    def over_square(parts, of_places):
+        return [parts[0]] + [in_square(parts[flip], flip, of_places) for flip in (1, 2, 3)]
+
+    own = pack(0)
+    sent = pack(1)
+    own = over_square(own, True)
+    other = over_square([to_other_core(part) for part in sent], True)
 
     chunks = pl.pallas_call(
         gram_kernel,
-        out_shape=shape(RING, SLABS, CHUNK, BLOCK),
-        in_specs=[VMEM] * 2,
-        out_specs=VMEM,
+        out_shape=[shape(SLABS, CHUNK, BLOCK)] * RING,
+        in_specs=[SMEM] + [VMEM] * (2 * RING),
+        out_specs=[VMEM] * RING,
         scratch_shapes=[pltpu.VMEM((PACK, BLOCK), jnp.float32)],
         compiler_params=PARAMS,
         name="gram",
-    )(own, other)
-    chunks = exchange(chunks, across_place)
-    pieces = jnp.sum(chunks.astype(jnp.float32), axis=0).astype(half)
+    )(dev, *own, *other)
+    chunks = over_square(chunks, False)
+    pieces = sum(chunk.astype(jnp.float32) for chunk in chunks).astype(half)
     pieces = exchange(pieces.reshape(2 * SLABS, PIECE, BLOCK), along_z)
     piece = jnp.sum(pieces.astype(jnp.float32), axis=0).astype(half)
     members = jnp.broadcast_to(piece[None], (2 * RING, PIECE, BLOCK))
@@ -249,7 +266,7 @@
 
     inverse = pl.pallas_call(
         functools.partial(newton_kernel, tokens_all),
-        out_shape=shape(RING, PACK, BLOCK),
+        out_shape=shape(PACK, BLOCK),
         in_specs=[SMEM, SMEM, VMEM],
         out_specs=VMEM,
         scratch_shapes=[
@@ -260,24 +277,29 @@
         compiler_params=PARAMS,
         name="newton",
     )(dev, newton_steps, total)
-    mine = exchange(inverse, along_place)
-    others = to_other_core(mine)
+    mine = over_square([inverse] * RING, True)
+    others = [to_other_core(block) for block in mine]
 
     def apply(side, blocks, before):
         kinds = (grad_qkv.shape, grad_up.shape)
-        here = [pltpu.VMEM(dims[1:], half) for dims in kinds]
+        buffers = [pltpu.VMEM(dims[1:], half) for dims in kinds]
         return pl.pallas_call(
             functools.partial(apply_kernel, side),
             out_shape=[shape(*dims) for dims in kinds],
-            in_specs=[SMEM, VMEM] + [ANY] * (2 + len(before)),
+            in_specs=[SMEM] + [ANY] * (RING + 2 + len(before)),
             out_specs=[ANY] * 2,
-            input_output_aliases={4: 0, 5: 1} if before else {},
-            scratch_shapes=here
-            + here
-            + [pltpu.VMEM((RING, BLOCK, BLOCK), half), pltpu.SemaphoreType.DMA((4,))],
+            input_output_aliases={7: 0, 8: 1} if before else {},
+            scratch_shapes=buffers
+            + buffers
+            + [
+                pltpu.VMEM((RING, PACK, BLOCK), half),
+                pltpu.VMEM((RING, BLOCK, BLOCK), half),
+                pltpu.SemaphoreType.DMA((4,)),
+                pltpu.SemaphoreType.DMA((RING,)),
+            ],
             compiler_params=PARAMS,
             name="apply",
-        )(dev, blocks, grad_qkv, grad_up, *before)
+        )(dev, *blocks, grad_qkv, grad_up, *before)
 
     return tuple(apply(1, others, apply(0, mine, ())))
 

time: 145 us -> 134 us (0.924)
  blocking collectives: 117 us -> 28.6 us
  starting transfers between devices: 5.58 us -> 46 us
  waiting for transfers between devices: 0.59 us -> 34.2 us
  Pallas kernels: 19.9 us -> 23.2 us
    all_to_all x6 -> x2, blocking collectives: 117 us -> 28.6 us  [exchange(): lax.all_to_all(array, AXES, 0, 0, axis_index_groups=groups_by(key), tiled...]
    ppermute x0 -> x12, waiting for transfers between devices: none -> 34.2 us  [in_square(): return lax.ppermute(array, AXES, pairs)]
    ppermute x0 -> x12, starting transfers between devices: none -> 20.2 us  [in_square(): return lax.ppermute(array, AXES, pairs)]
    ppermute x2 -> x8, starting transfers between devices: 5.58 us -> 25.7 us  [to_other_core(): return lax.ppermute(array, 'dp', [(i, i ^ 1) for i in range(64)])]
    pallas_call x2, Pallas kernels: 5.98 us -> 8.59 us  [apply(): pl.pallas_call(functools.partial(apply_kernel, side), out_shape=[shape(*d...]
    pallas_call x2 -> x3, Pallas kernels: 7.82 us -> 8.55 us  [the longest x1 4.61 us: local(): pl.pallas_call(gram_kernel, out_shape=[shape(SLABS, CHUNK, BLOCK)] * RING...]
  transfers between devices with their start and end apart: 2 -> 20, of which waited for: 1 -> 8; matrix products, arithmetic and copies ran while one was open for 0% -> 0% of each run, Pallas kernels for 2% -> 5%
where the time goes in v3:
time: 134 us
  starting transfers between devices  46 us (34%)
  waiting for transfers between devices  34.2 us (26%)
  blocking collectives  28.6 us (21%)
  Pallas kernels  23.2 us (17%)
    ppermute x12, waiting for transfers between devices, in_square(): return lax.ppermute(array, AXES, pairs)  34.2 us
    all_to_all x2, blocking collectives, exchange(): lax.all_to_all(array, AXES, 0, 0, axis_index_groups=groups_by(key), tiled...  28.6 us
    ppermute x8, starting transfers between devices, to_other_core(): return lax.ppermute(array, 'dp', [(i, i ^ 1) for i in range(64)])  25.7 us
    ppermute x12, starting transfers between devices, in_square(): return lax.ppermute(array, AXES, pairs)  20.2 us
    pallas_call x2, Pallas kernels, apply(): pl.pallas_call(functools.partial(apply_kernel, side), out_shape=[shape(*d...  8.59 us
    pallas_call x1, Pallas kernels, local(): pl.pallas_call(functools.partial(newton_kernel, tokens_all), out_shape=sh...  6.08 us
    pallas_call x1, Pallas kernels, local(): pl.pallas_call(gram_kernel, out_shape=[shape(SLABS, CHUNK, BLOCK)] * RING...  4.61 us
    pallas_call x2, Pallas kernels, pack(): pl.pallas_call(functools.partial(pack_kernel, side), out_shape=[shape(SLA...  3.93 us
  transfers between devices with their start and end apart: 20, of which 8 were waited for; matrix products, arithmetic and copies ran while one was open for 0% of the time, Pallas kernels for 5%

profile of v3, /device:TPU:1, one launch (start us, length us, event | category | flops | bytes accessed | tf_op | source)
XLA Modules:
  0.0 134.2 jit_solution(9203014684790738969)
XLA Ops:
  0.6 2.0 %pack.3 = (bf16[4,128,640]{2,1,0:T(8,128)(2,1)S(1)}, bf16[4,128,640]{2,1,0:T(8,128)(2,1)S(1)}, bf16[4,128,640]{2,1,0:T(8,128)(2,1)S(1)}, bf16[4,128,640]{2,1,0:T(8,128)(2,1)S(1)}) custom-call(s32[1]{0:T(128)} %bitcast.dev, bf16[2,2,128,5120]{3,2,1,0:T(8,128)(2,1)} %act.3), custom_call_target="tpu_custom_call" | custom-call | tf_op jit(solution)/shard_map/pack/pallas_call | solution.py:233
  2.6 3.3 %collective-permute-start.3 = (bf16[4,128,640]{2,1,0:T(8,128)(2,1)S(1)}, bf16[4,128,640]{2,1,0:T(8,128)(2,1)S(1)}, u32[]{:S(2)}, u32[]{:S(2)}) collective-permute-start(bf16[4,128,640]{2,1,0:T(8,128)(2,1)S(1)} %get-tuple-element.20), channel_id=1, source_target_pairs={{0,4},{4,0},{8,12},{12,8},{16,20},{20,16},{24,28},{28,24},{32,36},... | collective-permute-start | bytes 1966088 | tf_op jit(solution)/shard_map/ppermute | solution.py:66
  6.0 0.1 collective-permute-start.4
  6.1 0.4 collective-permute-start.6
  6.5 0.1 collective-permute-start.8
  6.6 1.9 %pack.2 = (bf16[4,128,640]{2,1,0:T(8,128)(2,1)S(1)}, bf16[4,128,640]{2,1,0:T(8,128)(2,1)S(1)}, bf16[4,128,640]{2,1,0:T(8,128)(2,1)S(1)}, bf16[4,128,640]{2,1,0:T(8,128)(2,1)S(1)}) custom-call(s32[1]{0:T(128)} %bitcast.dev, bf16[2,2,128,5120]{3,2,1,0:T(8,128)(2,1)} %act.3), custom_call_target="tpu_custom_call" | custom-call | tf_op jit(solution)/shard_map/pack/pallas_call | solution.py:233
  8.5 1.1 collective-permute-start
  9.6 0.0 collective-permute-done.3.refs_4_
  9.6 2.5 %collective-permute-start.1 = (bf16[4,128,640]{2,1,0:T(8,128)(2,1)S(1)}, bf16[4,128,640]{2,1,0:T(8,128)(2,1)S(1)}, u32[]{:S(2)}, u32[]{:S(2)}) collective-permute-start(bf16[4,128,640]{2,1,0:T(8,128)(2,1)S(1)} %get-tuple-element.18), channel_id=1, source_target_pairs={{0,32},{1,33},{2,34},{3,35},{4,100},{5,101},{6,102},{7,103},{8,40}... | collective-permute-start | bytes 1966088 | tf_op jit(solution)/shard_map/ppermute | solution.py:80
  12.1 0.0 collective-permute-done.4
  12.1 1.6 %collective-permute-start.2 = (bf16[4,128,640]{2,1,0:T(8,128)(2,1)S(1)}, bf16[4,128,640]{2,1,0:T(8,128)(2,1)S(1)}, u32[]{:S(2)}, u32[]{:S(2)}) collective-permute-start(bf16[4,128,640]{2,1,0:T(8,128)(2,1)S(1)} %get-tuple-element.19), channel_id=1, source_target_pairs={{0,40},{1,41},{2,42},{3,43},{4,124},{5,125},{6,126},{7,127},{8,32}... | collective-permute-start | bytes 1966088 | tf_op jit(solution)/shard_map/ppermute | solution.py:80
  13.7 0.0 collective-permute-done.6
  13.7 1.0 collective-permute-start.5
  14.7 0.0 collective-permute-done.8
  14.7 2.5 %collective-permute-start.7 = (bf16[4,128,640]{2,1,0:T(8,128)(2,1)S(1)}, bf16[4,128,640]{2,1,0:T(8,128)(2,1)S(1)}, u32[]{:S(2)}, u32[]{:S(2)}) collective-permute-start(bf16[4,128,640]{2,1,0:T(8,128)(2,1)S(1)} %collective-permute-done.6), channel_id=1, source_target_pairs={{0,32},{1,33},{2,34},{3,35},{4,100},{5,101},{6,102},{7,103},{8,40}... | collective-permute-start | bytes 1966088 | tf_op jit(solution)/shard_map/ppermute | solution.py:80
  17.2 2.1 %collective-permute-done.refs_1_ = bf16[4,128,640]{2,1,0:T(8,128)(2,1)S(1)} collective-permute-done((bf16[4,128,640]{2,1,0:T(8,128)(2,1)S(1)}, bf16[4,128,640]{2,1,0:T(8,128)(2,1)S(1)}, u32[]{:S(2)}, u32[]{:S(2)}) %collective-permute-start) | collective-permute-done | bytes 655392 | tf_op jit(solution)/shard_map/ppermute | solution.py:80
  19.3 3.2 %collective-permute-start.9 = (bf16[4,128,640]{2,1,0:T(8,128)(2,1)S(1)}, bf16[4,128,640]{2,1,0:T(8,128)(2,1)S(1)}, u32[]{:S(2)}, u32[]{:S(2)}) collective-permute-start(bf16[4,128,640]{2,1,0:T(8,128)(2,1)S(1)} %collective-permute-done.8), channel_id=1, source_target_pairs={{0,40},{1,41},{2,42},{3,43},{4,124},{5,125},{6,126},{7,127},{8,32}... | collective-permute-start | bytes 1966088 | tf_op jit(solution)/shard_map/ppermute | solution.py:80
  22.5 0.0 collective-permute-done.1.refs_2_
  22.5 6.3 %collective-permute-done.2.refs_3_ = bf16[4,128,640]{2,1,0:T(8,128)(2,1)S(1)} collective-permute-done((bf16[4,128,640]{2,1,0:T(8,128)(2,1)S(1)}, bf16[4,128,640]{2,1,0:T(8,128)(2,1)S(1)}, u32[]{:S(2)}, u32[]{:S(2)}) %collective-permute-start.2) | collective-permute-done | bytes 655392 | tf_op jit(solution)/shard_map/ppermute | solution.py:80
  28.8 4.5 %collective-permute-done.5.refs_5_ = bf16[4,128,640]{2,1,0:T(8,128)(2,1)S(1)} collective-permute-done((bf16[4,128,640]{2,1,0:T(8,128)(2,1)S(1)}, bf16[4,128,640]{2,1,0:T(8,128)(2,1)S(1)}, u32[]{:S(2)}, u32[]{:S(2)}) %collective-permute-start.5) | collective-permute-done | bytes 655392 | tf_op jit(solution)/shard_map/ppermute | solution.py:80
  33.3 1.0 collective-permute-done.7.refs_6_
  34.3 0.0 copy-start.3
  34.3 8.4 %collective-permute-done.9.refs_7_ = bf16[4,128,640]{2,1,0:T(8,128)(2,1)S(1)} collective-permute-done((bf16[4,128,640]{2,1,0:T(8,128)(2,1)S(1)}, bf16[4,128,640]{2,1,0:T(8,128)(2,1)S(1)}, u32[]{:S(2)}, u32[]{:S(2)}) %collective-permute-start.9) | collective-permute-done | bytes 655392 | tf_op jit(solution)/shard_map/ppermute | solution.py:80
  42.8 0.0 copy-start.4
  42.8 0.0 copy-done.3
  42.8 0.8 copy-done.4
  43.6 4.6 %gram.1 = (bf16[4,96,640]{2,1,0:T(8,128)(2,1)S(1)}, bf16[4,96,640]{2,1,0:T(8,128)(2,1)S(1)}, bf16[4,96,640]{2,1,0:T(8,128)(2,1)S(1)}, bf16[4,96,640]{2,1,0:T(8,128)(2,1)S(1)}) custom-call(s32[1]{0:T(128)} %bitcast.dev, bf16[4,128,640]{2,1,0:T(8,128)(2,1)S(1)} %get-tuple-element.16.refs_0_, bf16[4,128,640]{2,1,0:T(8,128)(2,1)S(1)} %collective-permute-done.refs_1_, ...), custom_call_target="tpu_custom_call" | custom-call | tf_op jit(solution)/shard_map/gram/pallas_call | solution.py:251
  48.2 0.1 collective-permute-start.10
  48.3 0.1 collective-permute-start.11
  48.4 2.5 %collective-permute-start.12 = (bf16[4,96,640]{2,1,0:T(8,128)(2,1)S(1)}, bf16[4,96,640]{2,1,0:T(8,128)(2,1)S(1)}, u32[]{:S(2)}, u32[]{:S(2)}) collective-permute-start(bf16[4,96,640]{2,1,0:T(8,128)(2,1)S(1)} %get-tuple-element.27), channel_id=1, source_target_pairs={{0,120},{1,121},{2,122},{3,123},{4,44},{5,45},{6,46},{7,47},{8,112... | collective-permute-start | bytes 1474568 | tf_op jit(solution)/shard_map/ppermute | solution.py:80
  51.0 5.3 %collective-permute-done.10 = bf16[4,96,640]{2,1,0:T(8,128)(2,1)S(1)} collective-permute-done((bf16[4,96,640]{2,1,0:T(8,128)(2,1)S(1)}, bf16[4,96,640]{2,1,0:T(8,128)(2,1)S(1)}, u32[]{:S(2)}, u32[]{:S(2)}) %collective-permute-start.10) | collective-permute-done | bytes 491552 | tf_op jit(solution)/shard_map/ppermute | solution.py:80
  56.3 0.1 collective-permute-done.11
  56.4 6.3 %collective-permute-done.12 = bf16[4,96,640]{2,1,0:T(8,128)(2,1)S(1)} collective-permute-done((bf16[4,96,640]{2,1,0:T(8,128)(2,1)S(1)}, bf16[4,96,640]{2,1,0:T(8,128)(2,1)S(1)}, u32[]{:S(2)}, u32[]{:S(2)}) %collective-permute-start.12) | collective-permute-done | bytes 491552 | tf_op jit(solution)/shard_map/ppermute | solution.py:80
  62.7 0.2 add_convert_fusion
  63.0 0.0 copy-start.2
  63.0 19.0 %all_to_all.10 = bf16[8,48,640]{2,1,0:T(8,128)(2,1)S(1)} all-to-all(bf16[8,48,640]{2,1,0:T(8,128)(2,1)S(1)} %bitcast.4), channel_id=1, replica_groups={{0,128,1,129,2,130,3,131},{4,132,5,133,6,134,7,135},{8,136,9,137,10,138..., dimensions={0} | all-to-all | bytes 983040 | tf_op jit(solution)/shard_map/all_to_all | solution.py:62
  82.0 0.0 copy-start
  82.0 0.0 copy-start.1
  82.0 0.1 reduce_sum.12
  82.1 9.6 %all_to_all.11 = bf16[8,48,640]{2,1,0:T(8,128)(2,1)S(1)} all-to-all(bf16[8,48,640]{2,1,0:T(8,128)(2,1)S(1)} %broadcast_in_dim.2), channel_id=1, replica_groups={{0,128,24,152,96,224,120,248},{8,136,16,144,104,232,112,240},{32,160,56..., dimensions={0} | all-to-all | bytes 983040 | tf_op jit(solution)/shard_map/all_to_all | solution.py:62
  91.7 0.0 copy-done.2
  91.7 6.1 %newton.1.refs_0_ = bf16[384,640]{1,0:T(8,128)(2,1)S(1)} custom-call(s32[1]{0:T(128)} %bitcast.dev, s32[2,2,8]{2,1,0:T(2,128)S(1)} %copy-done.2, bf16[384,640]{1,0:T(8,128)(2,1)S(1)} %bitcast.3), custom_call_target="tpu_custom_call" | custom-call | tf_op jit(solution)/shard_map/newton/pallas_call | solution.py:267
  97.8 5.3 %collective-permute-start.18 = (bf16[384,640]{1,0:T(8,128)(2,1)S(1)}, bf16[384,640]{1,0:T(8,128)(2,1)S(1)}, u32[]{:S(2)}, u32[]{:S(2)}) collective-permute-start(bf16[384,640]{1,0:T(8,128)(2,1)S(1)} %newton.1.refs_0_), channel_id=1, source_target_pairs={{0,40},{1,41},{2,42},{3,43},{4,124},{5,125},{6,126},{7,127},{8,32}... | collective-permute-start | bytes 1474568 | tf_op jit(solution)/shard_map/ppermute | solution.py:80
  103.1 0.0 collective-permute-start.16
  103.1 0.4 collective-permute-start.14
  103.5 10.3 %collective-permute-start.13 = (bf16[384,640]{1,0:T(8,128)(2,1)S(1)}, bf16[384,640]{1,0:T(8,128)(2,1)S(1)}, u32[]{:S(2)}, u32[]{:S(2)}) collective-permute-start(bf16[384,640]{1,0:T(8,128)(2,1)S(1)} %newton.1.refs_0_), channel_id=1, source_target_pairs={{0,4},{4,0},{8,12},{12,8},{16,20},{20,16},{24,28},{28,24},{32,36},... | collective-permute-start | bytes 1474568 | tf_op jit(solution)/shard_map/ppermute | solution.py:66
  113.8 0.0 collective-permute-done.18.refs_3_
  113.8 6.3 %collective-permute-start.19 = (bf16[384,640]{1,0:T(8,128)(2,1)S(1)}, bf16[384,640]{1,0:T(8,128)(2,1)S(1)}, u32[]{:S(2)}, u32[]{:S(2)}) collective-permute-start(bf16[384,640]{1,0:T(8,128)(2,1)S(1)} %collective-permute-done.18.refs_3_), channel_id=1, source_target_pairs={{0,4},{4,0},{8,12},{12,8},{16,20},{20,16},{24,28},{28,24},{32,36},... | collective-permute-start | bytes 1474568 | tf_op jit(solution)/shard_map/ppermute | solution.py:66
  120.2 0.0 collective-permute-done.16.refs_2_
  120.2 2.3 %collective-permute-start.17 = (bf16[384,640]{1,0:T(8,128)(2,1)S(1)}, bf16[384,640]{1,0:T(8,128)(2,1)S(1)}, u32[]{:S(2)}, u32[]{:S(2)}) collective-permute-start(bf16[384,640]{1,0:T(8,128)(2,1)S(1)} %collective-permute-done.16.refs_2_), channel_id=1, source_target_pairs={{0,4},{4,0},{8,12},{12,8},{16,20},{20,16},{24,28},{28,24},{32,36},... | collective-permute-start | bytes 1474568 | tf_op jit(solution)/shard_map/ppermute | solution.py:66
  122.4 0.0 collective-permute-done.14.refs_1_
  122.4 2.9 %collective-permute-start.15 = (bf16[384,640]{1,0:T(8,128)(2,1)S(1)}, bf16[384,640]{1,0:T(8,128)(2,1)S(1)}, u32[]{:S(2)}, u32[]{:S(2)}) collective-permute-start(bf16[384,640]{1,0:T(8,128)(2,1)S(1)} %collective-permute-done.14.refs_1_), channel_id=1, source_target_pairs={{0,4},{4,0},{8,12},{12,8},{16,20},{20,16},{24,28},{28,24},{32,36},... | collective-permute-start | bytes 1474568 | tf_op jit(solution)/shard_map/ppermute | solution.py:66
  125.3 0.0 copy-done
  125.3 0.0 copy-done.1
  125.3 4.3 %apply.2 = (bf16[2,240,1280]{2,1,0:T(8,128)(2,1)}, bf16[2,320,1280]{2,1,0:T(8,128)(2,1)}) custom-call(s32[1]{0:T(128)} %bitcast.dev, bf16[384,640]{1,0:T(8,128)(2,1)S(1)} %newton.1.refs_0_, bf16[384,640]{1,0:T(8,128)(2,1)S(1)} %collective-permute-done.14.refs_1_, bf16[384,640]{1,0:T(8,128)(2,1)S(1)} %collective-permute-done.16.refs_2_, ...), custom_call_target="tpu_custom_call" | custom-call | tf_op jit(solution)/shard_map/apply/pallas_call | solution.py:286
  129.6 0.0 collective-permute-done.13.refs_0_
  129.6 0.0 collective-permute-done.19.refs_3_
  129.6 0.0 collective-permute-done.17.refs_2_
  129.6 0.0 collective-permute-done.15.refs_1_
  129.6 4.3 %apply.3 = (bf16[2,240,1280]{2,1,0:T(8,128)(2,1)}, bf16[2,320,1280]{2,1,0:T(8,128)(2,1)}) custom-call(s32[1]{0:T(128)} %bitcast.dev, bf16[384,640]{1,0:T(8,128)(2,1)S(1)} %collective-permute-done.13.refs_0_, bf16[384,640]{1,0:T(8,128)(2,1)S(1)} %collective-permute-done.15.refs_1_, ...), custom_call_target="tpu_custom_call", output_to_operand_aliasing={{0}: (7, {}), {1}: (8, {})} | custom-call | tf_op jit(solution)/shard_map/apply/pallas_call | solution.py:286
  (1 shorter events, 0.0 us)
Async XLA Ops:
  2.6 7.0 %collective-permute-start.3 = (bf16[4,128,640]{2,1,0:T(8,128)(2,1)S(1)}, bf16[4,128,640]{2,1,0:T(8,128)(2,1)S(1)}, u32[]{:S(2)}, u32[]{:S(2)}) collective-permute-start(bf16[4,128,640]{2,1,0:T(8,128)(2,1)S(1)} %get-tuple-element.20), channel_id=1, source_target_pairs={{0,4},{4,0},{8,12},{12,8},{16,20},{20,16},{24,28},{28,24},{32,36},... | collective-permute-start | bytes 1966088 | tf_op jit(solution)/shard_map/ppermute | solution.py:66
  6.0 6.1 %collective-permute-start.4 = (bf16[4,128,640]{2,1,0:T(8,128)(2,1)S(1)}, bf16[4,128,640]{2,1,0:T(8,128)(2,1)S(1)}, u32[]{:S(2)}, u32[]{:S(2)}) collective-permute-start(bf16[4,128,640]{2,1,0:T(8,128)(2,1)S(1)} %get-tuple-element.21), channel_id=1, source_target_pairs={{0,4},{4,0},{8,12},{12,8},{16,20},{20,16},{24,28},{28,24},{32,36},... | collective-permute-start | bytes 1966088 | tf_op jit(solution)/shard_map/ppermute | solution.py:66
  6.1 7.6 %collective-permute-start.6 = (bf16[4,128,640]{2,1,0:T(8,128)(2,1)S(1)}, bf16[4,128,640]{2,1,0:T(8,128)(2,1)S(1)}, u32[]{:S(2)}, u32[]{:S(2)}) collective-permute-start(bf16[4,128,640]{2,1,0:T(8,128)(2,1)S(1)} %get-tuple-element.22), channel_id=1, source_target_pairs={{0,4},{4,0},{8,12},{12,8},{16,20},{20,16},{24,28},{28,24},{32,36},... | collective-permute-start | bytes 1966088 | tf_op jit(solution)/shard_map/ppermute | solution.py:66
  6.5 8.2 %collective-permute-start.8 = (bf16[4,128,640]{2,1,0:T(8,128)(2,1)S(1)}, bf16[4,128,640]{2,1,0:T(8,128)(2,1)S(1)}, u32[]{:S(2)}, u32[]{:S(2)}) collective-permute-start(bf16[4,128,640]{2,1,0:T(8,128)(2,1)S(1)} %get-tuple-element.23), channel_id=1, source_target_pairs={{0,4},{4,0},{8,12},{12,8},{16,20},{20,16},{24,28},{28,24},{32,36},... | collective-permute-start | bytes 1966088 | tf_op jit(solution)/shard_map/ppermute | solution.py:66
  8.5 10.7 %collective-permute-start = (bf16[4,128,640]{2,1,0:T(8,128)(2,1)S(1)}, bf16[4,128,640]{2,1,0:T(8,128)(2,1)S(1)}, u32[]{:S(2)}, u32[]{:S(2)}) collective-permute-start(bf16[4,128,640]{2,1,0:T(8,128)(2,1)S(1)} %get-tuple-element.17), channel_id=1, source_target_pairs={{0,8},{1,9},{2,10},{3,11},{4,28},{5,29},{6,30},{7,31},{8,0},{9,1},... | collective-permute-start | bytes 1966088 | tf_op jit(solution)/shard_map/ppermute | solution.py:80
  9.6 12.8 %collective-permute-start.1 = (bf16[4,128,640]{2,1,0:T(8,128)(2,1)S(1)}, bf16[4,128,640]{2,1,0:T(8,128)(2,1)S(1)}, u32[]{:S(2)}, u32[]{:S(2)}) collective-permute-start(bf16[4,128,640]{2,1,0:T(8,128)(2,1)S(1)} %get-tuple-element.18), channel_id=1, source_target_pairs={{0,32},{1,33},{2,34},{3,35},{4,100},{5,101},{6,102},{7,103},{8,40}... | collective-permute-start | bytes 1966088 | tf_op jit(solution)/shard_map/ppermute | solution.py:80
  12.1 16.7 %collective-permute-start.2 = (bf16[4,128,640]{2,1,0:T(8,128)(2,1)S(1)}, bf16[4,128,640]{2,1,0:T(8,128)(2,1)S(1)}, u32[]{:S(2)}, u32[]{:S(2)}) collective-permute-start(bf16[4,128,640]{2,1,0:T(8,128)(2,1)S(1)} %get-tuple-element.19), channel_id=1, source_target_pairs={{0,40},{1,41},{2,42},{3,43},{4,124},{5,125},{6,126},{7,127},{8,32}... | collective-permute-start | bytes 1966088 | tf_op jit(solution)/shard_map/ppermute | solution.py:80
  13.7 19.6 %collective-permute-start.5 = (bf16[4,128,640]{2,1,0:T(8,128)(2,1)S(1)}, bf16[4,128,640]{2,1,0:T(8,128)(2,1)S(1)}, u32[]{:S(2)}, u32[]{:S(2)}) collective-permute-start(bf16[4,128,640]{2,1,0:T(8,128)(2,1)S(1)} %collective-permute-done.4), channel_id=1, source_target_pairs={{0,8},{1,9},{2,10},{3,11},{4,28},{5,29},{6,30},{7,31},{8,0},{9,1},... | collective-permute-start | bytes 1966088 | tf_op jit(solution)/shard_map/ppermute | solution.py:80
  14.7 19.7 %collective-permute-start.7 = (bf16[4,128,640]{2,1,0:T(8,128)(2,1)S(1)}, bf16[4,128,640]{2,1,0:T(8,128)(2,1)S(1)}, u32[]{:S(2)}, u32[]{:S(2)}) collective-permute-start(bf16[4,128,640]{2,1,0:T(8,128)(2,1)S(1)} %collective-permute-done.6), channel_id=1, source_target_pairs={{0,32},{1,33},{2,34},{3,35},{4,100},{5,101},{6,102},{7,103},{8,40}... | collective-permute-start | bytes 1966088 | tf_op jit(solution)/shard_map/ppermute | solution.py:80
  19.3 23.5 %collective-permute-start.9 = (bf16[4,128,640]{2,1,0:T(8,128)(2,1)S(1)}, bf16[4,128,640]{2,1,0:T(8,128)(2,1)S(1)}, u32[]{:S(2)}, u32[]{:S(2)}) collective-permute-start(bf16[4,128,640]{2,1,0:T(8,128)(2,1)S(1)} %collective-permute-done.8), channel_id=1, source_target_pairs={{0,40},{1,41},{2,42},{3,43},{4,124},{5,125},{6,126},{7,127},{8,32}... | collective-permute-start | bytes 1966088 | tf_op jit(solution)/shard_map/ppermute | solution.py:80
  34.3 8.4 %copy-start.3 = (bf16[4,128,640]{2,1,0:T(8,128)(2,1)}, bf16[4,128,640]{2,1,0:T(8,128)(2,1)S(1)}, u32[]{:S(2)}) copy-start(bf16[4,128,640]{2,1,0:T(8,128)(2,1)S(1)} %collective-permute-done.7.refs_6_) | copy-start | bytes 1966084
  42.8 0.8 copy-start.4
  48.2 8.1 %collective-permute-start.10 = (bf16[4,96,640]{2,1,0:T(8,128)(2,1)S(1)}, bf16[4,96,640]{2,1,0:T(8,128)(2,1)S(1)}, u32[]{:S(2)}, u32[]{:S(2)}) collective-permute-start(bf16[4,96,640]{2,1,0:T(8,128)(2,1)S(1)} %get-tuple-element.25), channel_id=1, source_target_pairs={{0,24},{1,25},{2,26},{3,27},{4,12},{5,13},{6,14},{7,15},{8,16},{9,... | collective-permute-start | bytes 1474568 | tf_op jit(solution)/shard_map/ppermute | solution.py:80
  48.3 8.1 %collective-permute-start.11 = (bf16[4,96,640]{2,1,0:T(8,128)(2,1)S(1)}, bf16[4,96,640]{2,1,0:T(8,128)(2,1)S(1)}, u32[]{:S(2)}, u32[]{:S(2)}) collective-permute-start(bf16[4,96,640]{2,1,0:T(8,128)(2,1)S(1)} %get-tuple-element.26), channel_id=1, source_target_pairs={{0,96},{1,97},{2,98},{3,99},{4,36},{5,37},{6,38},{7,39},{8,104},{9... | collective-permute-start | bytes 1474568 | tf_op jit(solution)/shard_map/ppermute | solution.py:80
  48.4 14.3 %collective-permute-start.12 = (bf16[4,96,640]{2,1,0:T(8,128)(2,1)S(1)}, bf16[4,96,640]{2,1,0:T(8,128)(2,1)S(1)}, u32[]{:S(2)}, u32[]{:S(2)}) collective-permute-start(bf16[4,96,640]{2,1,0:T(8,128)(2,1)S(1)} %get-tuple-element.27), channel_id=1, source_target_pairs={{0,120},{1,121},{2,122},{3,123},{4,44},{5,45},{6,46},{7,47},{8,112... | collective-permute-start | bytes 1474568 | tf_op jit(solution)/shard_map/ppermute | solution.py:80
  63.0 28.8 %copy-start.2 = (s32[2,2,8]{2,1,0:T(2,128)S(1)}, s32[2,2,8]{2,1,0:T(2,128)}, u32[]{:S(2)}) copy-start(s32[2,2,8]{2,1,0:T(2,128)} %newton_steps.1) | copy-start | bytes 388
  82.0 43.3 %copy-start = (bf16[2,320,1280]{2,1,0:T(8,128)(2,1)S(1)}, bf16[2,320,1280]{2,1,0:T(8,128)(2,1)}, u32[]{:S(2)}) copy-start(bf16[2,320,1280]{2,1,0:T(8,128)(2,1)} %refs_5_.3) | copy-start | bytes 4915204
  82.0 43.3 %copy-start.1 = (bf16[2,240,1280]{2,1,0:T(8,128)(2,1)S(1)}, bf16[2,240,1280]{2,1,0:T(8,128)(2,1)}, u32[]{:S(2)}) copy-start(bf16[2,240,1280]{2,1,0:T(8,128)(2,1)} %refs_4_.3) | copy-start | bytes 3686404
  97.8 16.0 %collective-permute-start.18 = (bf16[384,640]{1,0:T(8,128)(2,1)S(1)}, bf16[384,640]{1,0:T(8,128)(2,1)S(1)}, u32[]{:S(2)}, u32[]{:S(2)}) collective-permute-start(bf16[384,640]{1,0:T(8,128)(2,1)S(1)} %newton.1.refs_0_), channel_id=1, source_target_pairs={{0,40},{1,41},{2,42},{3,43},{4,124},{5,125},{6,126},{7,127},{8,32}... | collective-permute-start | bytes 1474568 | tf_op jit(solution)/shard_map/ppermute | solution.py:80
  103.1 17.0 %collective-permute-start.16 = (bf16[384,640]{1,0:T(8,128)(2,1)S(1)}, bf16[384,640]{1,0:T(8,128)(2,1)S(1)}, u32[]{:S(2)}, u32[]{:S(2)}) collective-permute-start(bf16[384,640]{1,0:T(8,128)(2,1)S(1)} %newton.1.refs_0_), channel_id=1, source_target_pairs={{0,32},{1,33},{2,34},{3,35},{4,100},{5,101},{6,102},{7,103},{8,40}... | collective-permute-start | bytes 1474568 | tf_op jit(solution)/shard_map/ppermute | solution.py:80
  103.1 19.3 %collective-permute-start.14 = (bf16[384,640]{1,0:T(8,128)(2,1)S(1)}, bf16[384,640]{1,0:T(8,128)(2,1)S(1)}, u32[]{:S(2)}, u32[]{:S(2)}) collective-permute-start(bf16[384,640]{1,0:T(8,128)(2,1)S(1)} %newton.1.refs_0_), channel_id=1, source_target_pairs={{0,8},{1,9},{2,10},{3,11},{4,28},{5,29},{6,30},{7,31},{8,0},{9,1},... | collective-permute-start | bytes 1474568 | tf_op jit(solution)/shard_map/ppermute | solution.py:80
  103.5 26.1 %collective-permute-start.13 = (bf16[384,640]{1,0:T(8,128)(2,1)S(1)}, bf16[384,640]{1,0:T(8,128)(2,1)S(1)}, u32[]{:S(2)}, u32[]{:S(2)}) collective-permute-start(bf16[384,640]{1,0:T(8,128)(2,1)S(1)} %newton.1.refs_0_), channel_id=1, source_target_pairs={{0,4},{4,0},{8,12},{12,8},{16,20},{20,16},{24,28},{28,24},{32,36},... | collective-permute-start | bytes 1474568 | tf_op jit(solution)/shard_map/ppermute | solution.py:66
  113.8 15.8 %collective-permute-start.19 = (bf16[384,640]{1,0:T(8,128)(2,1)S(1)}, bf16[384,640]{1,0:T(8,128)(2,1)S(1)}, u32[]{:S(2)}, u32[]{:S(2)}) collective-permute-start(bf16[384,640]{1,0:T(8,128)(2,1)S(1)} %collective-permute-done.18.refs_3_), channel_id=1, source_target_pairs={{0,4},{4,0},{8,12},{12,8},{16,20},{20,16},{24,28},{28,24},{32,36},... | collective-permute-start | bytes 1474568 | tf_op jit(solution)/shard_map/ppermute | solution.py:66
  120.2 9.5 %collective-permute-start.17 = (bf16[384,640]{1,0:T(8,128)(2,1)S(1)}, bf16[384,640]{1,0:T(8,128)(2,1)S(1)}, u32[]{:S(2)}, u32[]{:S(2)}) collective-permute-start(bf16[384,640]{1,0:T(8,128)(2,1)S(1)} %collective-permute-done.16.refs_2_), channel_id=1, source_target_pairs={{0,4},{4,0},{8,12},{12,8},{16,20},{20,16},{24,28},{28,24},{32,36},... | collective-permute-start | bytes 1474568 | tf_op jit(solution)/shard_map/ppermute | solution.py:66
  122.4 7.2 %collective-permute-start.15 = (bf16[384,640]{1,0:T(8,128)(2,1)S(1)}, bf16[384,640]{1,0:T(8,128)(2,1)S(1)}, u32[]{:S(2)}, u32[]{:S(2)}) collective-permute-start(bf16[384,640]{1,0:T(8,128)(2,1)S(1)} %collective-permute-done.14.refs_1_), channel_id=1, source_target_pairs={{0,4},{4,0},{8,12},{12,8},{16,20},{20,16},{24,28},{28,24},{32,36},... | collective-permute-start | bytes 1474568 | tf_op jit(solution)/shard_map/ppermute | solution.py:66

commit v4 on v3

v4 whole, which is shorter than its diff:
```python
import functools

import jax
import jax.numpy as jnp
from jax import lax
from jax.experimental import pallas as pl
from jax.experimental.pallas import tpu as pltpu
from jax.sharding import PartitionSpec as P

DAMPING = 0.05
BLOCK = 640
TILE = 128
PACK = 384
PANELS = ((0, 0), (128, 0), (256, 0), (256, 384), (128, 512))
RING = 4
SLABS = 4
CHUNK = PACK // RING
AXES = ("dp", "tensor")
PARAMS = pltpu.CompilerParams(vmem_limit_bytes=24 * 1024 * 1024)
SMEM = pl.BlockSpec(memory_space=pltpu.SMEM)
VMEM = pl.BlockSpec(memory_space=pltpu.VMEM)
ANY = pl.BlockSpec(memory_space=pl.ANY)


def bit_a(i):
    return (i + 1) // 2 % 2


def bit_b(i):
    return i // 2


def device_at(device):
    dp, t = device // 4, device % 4
    return dp // 32, dp // 8 % 4, dp // 2 % 4, dp % 2, t


def move(array, target):
    pairs = []
    for device in range(256):
        zl, x, y, c, t = target(*device_at(device))
        pairs.append((device, (((zl * 4 + x) * 4 + y) * 2 + c) * 4 + t))
    return lax.ppermute(array, AXES, pairs)


def to_other_core(array):
    return move(array, lambda zl, x, y, c, t: (zl, x, y, 1 - c, t))


def in_square(array, flip, of_places):
    def target(zl, x, y, c, t):
        x2, y2 = (x ^ 1, y ^ 1) if (c == 0) == of_places else (3 - x, 3 - y)
        return zl, x2 if flip & 2 else x, y2 if flip & 1 else y, c, t

    return move(array, target)


def to_slab(array, step):
    return move(array, lambda zl, x, y, c, t: (zl, x, y, c, t ^ 1 if c == step else 3 - t))


def to_z_neighbour(array):
    return move(array, lambda zl, x, y, c, t: (1 - zl, x, y, c, t))


def here(dev):
    dp = dev[0] // 4
    core, x, y = dp % 2, dp // 8 % 4, dp // 2 % 4
    a, b = 2 * bit_a(x) + bit_a(y), 2 * bit_b(x) + bit_b(y)
    return core, jnp.where(core == 0, a, b), jnp.where(core == 0, b, a)


def pack_kernel(dev, act, own_0, own_1, own_2, own_3, diagonal, rest, sem):
    core, mine, across = here(dev)
    t = dev[0] % 4
    copies = []
    for side, outs in (
        (1, (rest.at[0], rest.at[1], rest.at[2], diagonal)),
        (0, (own_0, own_1, own_2, own_3)),
    ):
        first = jnp.where(core == side, t ^ 1, 3 - t)
        second = jnp.where(core == side, 3 - t, t ^ 1)
        for flip, out in enumerate(outs):
            place = (across if side else mine) ^ flip
            for rank, slab in enumerate((t, second, first, t ^ 2)):
                start = pl.multiple_of((2 * slab + place % 2) * BLOCK, TILE)
                copies.append(
                    pltpu.make_async_copy(
                        act.at[core ^ side, place // 2, :, pl.ds(start, BLOCK)],
                        out.at[rank],
                        sem.at[len(copies)],
                    )
                )
                copies[-1].start()
    for copy in copies:
        copy.wait()


def gram_kernel(dev, *refs):
    ins, outs, tri = refs[: 2 * RING], refs[2 * RING : 3 * RING], refs[3 * RING]
    ins = [*ins[:-1], ins[-1].at[0]]
    across = here(dev)[2]
    for slab in range(SLABS):

        def product(low, high):
            return lax.dot_general(
                jnp.concatenate([ref[slab, :, low:high] for ref in ins]),
                jnp.concatenate([ref[slab, :, low:] for ref in ins]),
                (((0,), (0,)), ((), ())),
                preferred_element_type=jnp.float32,
            )

        top = product(0, 256)
        tri[0:128, :] = top[0:128]
        tri[128:256, 0:512] = top[128:256, 128:]
        middle = product(256, 512)
        tri[256:384, 0:384] = middle[0:128]
        tri[256:384, 384:640] = middle[128:256, 128:]
        tri[128:256, 512:640] = product(512, 640)
        for flip in range(RING):
            start = pl.multiple_of((across ^ flip) * CHUNK, 32)
            outs[flip][slab] = tri[pl.ds(start, CHUNK), :].astype(jnp.bfloat16)


def newton_kernel(tokens_all, dev, newton_steps, *refs):
    ins, (out, total, mixed, gap, halves) = refs[:RING], refs[RING:]
    t = dev[0] % 4
    core, place, across = here(dev)
    for flip in range(RING):
        start = pl.multiple_of((across ^ flip) * CHUNK, 32)
        total[pl.ds(start, CHUNK), :] = ins[3 - flip][...].astype(jnp.float32)
    steps = newton_steps[core, place // 2, 2 * t + place % 2]
    for i, (row, col) in enumerate(PANELS):
        low = TILE * i
        panel = total[row : row + TILE, col : col + BLOCK - low]
        mixed[low : low + TILE, low:] = panel
        if i < 4:
            mixed[low + TILE :, low : low + TILE] = panel[:, TILE:].T
    eye = (
        lax.broadcasted_iota(jnp.int32, (BLOCK, BLOCK), 0)
        == lax.broadcasted_iota(jnp.int32, (BLOCK, BLOCK), 1)
    ).astype(jnp.float32)
    factor = mixed[...] * (1.0 / tokens_all) + DAMPING * eye
    norm_scale = jnp.sqrt(jnp.sum(factor * factor))
    mixed[...] = factor / norm_scale

    def dot(rows):
        return jnp.dot(halves[0:rows, :], halves[0:BLOCK, :], preferred_element_type=jnp.float32)

    def last():
        return jnp.dot(halves[BLOCK:, :], halves[0:BLOCK, :], preferred_element_type=jnp.float32)

    gap[...] = mixed[...]
    halves[0:BLOCK, :] = mixed[...].astype(jnp.bfloat16)
    halves[BLOCK:, :] = mixed[...].astype(jnp.bfloat16)
    mixed[...] = 2.0 * mixed[...] - dot(BLOCK)
    for turn in range(1, 4):
        halves[0:BLOCK, :] = mixed[...].astype(jnp.bfloat16)
        products = dot(2 * BLOCK) if turn < 3 else None
        step = products[BLOCK:] if turn < 3 else last()
        new_gap = 2.0 * gap[...] + 2.0**turn * mixed[...] - step
        gap[...] = jnp.where(turn < steps, new_gap, gap[...])
        if turn < 3:
            mixed[...] = 2.0 * mixed[...] - products[0:BLOCK]
            halves[BLOCK:, :] = gap[...].astype(jnp.bfloat16)
    reach = jnp.where(steps <= 1, 2.0, jnp.where(steps == 2, 4.0, jnp.where(steps == 3, 8.0, 16.0)))
    scale = 1.0 / norm_scale
    for i, (row, col) in enumerate(PANELS):
        low = TILE * i
        value = (reach * eye[low : low + TILE, low:] - gap[low : low + TILE, low:]) * scale
        out[row : row + TILE, col : col + BLOCK - low] = value.astype(jnp.bfloat16)


def apply_kernel(side, dev, *refs):
    ins, grads, outs = refs[:RING], refs[RING : RING + 2], refs[-8:-6]
    ins_here, outs_here, whole, sem = refs[-6:-4], refs[-4:-2], refs[-2], refs[-1]
    core, mine, across = here(dev)
    layer = core ^ side
    mine = across if side else mine
    loads = [
        pltpu.make_async_copy(grad.at[layer], place, sem.at[kind])
        for kind, (grad, place) in enumerate(zip(grads, ins_here))
    ]
    stores = [
        pltpu.make_async_copy(place, out.at[layer], sem.at[2 + kind])
        for kind, (out, place) in enumerate(zip(outs, outs_here))
    ]
    for load in loads:
        load.start()

    def unfold(block, place):
        for i, (row, col) in enumerate(PANELS):
            low = TILE * i
            panel = block[row : row + TILE, col : col + BLOCK - low]
            whole[place, low : low + TILE, low:] = panel
            if i < 4:
                whole[place, low + TILE :, low : low + TILE] = panel[:, TILE:].T

    for flip in range(RING):
        unfold(ins[flip], mine ^ flip)
    for place in range(RING):
        kind, j = place // 2, place % 2
        if j == 0:
            loads[kind].wait()
        columns = slice(j * BLOCK, (j + 1) * BLOCK)
        outs_here[kind][:, columns] = jnp.dot(
            ins_here[kind][:, columns], whole[place], preferred_element_type=jnp.float32
        ).astype(jnp.bfloat16)
        if j == 1:
            stores[kind].start()
    for store in stores:
        store.wait()


def local(activations, grad_qkv, grad_up, newton_steps):
    half = jnp.bfloat16
    dev = (lax.axis_index("dp") * 4 + lax.axis_index("tensor")).astype(jnp.int32).reshape(1)
    rows = activations.shape[2]
    tokens_all = rows * 256

    def shape(*dims):
        return jax.ShapeDtypeStruct(dims, half)

    def over_square(parts, of_places):
        moved = {flip: in_square(parts[flip], flip, of_places) for flip in (3, 2, 1)}
        return [parts[0]] + [moved[flip] for flip in (1, 2, 3)]

    part = (SLABS, rows, BLOCK)
    *own, diagonal, rest = pl.pallas_call(
        pack_kernel,
        out_shape=[shape(*part)] * (RING + 1) + [shape(3, *part)],
        in_specs=[SMEM, ANY],
        out_specs=[ANY] * (RING + 2),
        scratch_shapes=[pltpu.SemaphoreType.DMA((2 * RING * SLABS,))],
        compiler_params=pltpu.CompilerParams(vmem_limit_bytes=48 * 1024 * 1024),
        name="pack",
    )(dev, activations)
    own = over_square(own, True)
    diagonal, rest = to_other_core(diagonal), to_other_core(rest)
    diagonal = in_square(diagonal, 3, True)
    others = [in_square(rest[flip], flip, True) for flip in (2, 1)]

    chunks = pl.pallas_call(
        gram_kernel,
        out_shape=[shape(SLABS, CHUNK, BLOCK)] * RING,
        in_specs=[SMEM] + [VMEM] * (2 * RING),
        out_specs=[VMEM] * RING,
        scratch_shapes=[pltpu.VMEM((PACK, BLOCK), jnp.float32)],
        compiler_params=PARAMS,
        name="gram",
    )(dev, *own[::-1], diagonal, *others, rest)
    chunks = over_square(chunks, False)

    def wide(array):
        return array.astype(jnp.float32)

    sums = sum(wide(chunk) for chunk in chunks[::-1])
    sums = sums[0:2] + wide(to_slab(sums[2:4].astype(half), 0))
    sums = sums[0] + wide(to_slab(sums[1].astype(half), 1))
    sums = sums + wide(to_z_neighbour(sums.astype(half)))
    members = over_square([sums.astype(half)] * RING, False)

    inverse = pl.pallas_call(
        functools.partial(newton_kernel, tokens_all),
        out_shape=shape(PACK, BLOCK),
        in_specs=[SMEM, SMEM] + [VMEM] * RING,
        out_specs=VMEM,
        scratch_shapes=[
            pltpu.VMEM((PACK, BLOCK), jnp.float32),
            pltpu.VMEM((BLOCK, BLOCK), jnp.float32),
            pltpu.VMEM((BLOCK, BLOCK), jnp.float32),
            pltpu.VMEM((2 * BLOCK, BLOCK), half),
        ],
        compiler_params=PARAMS,
        name="newton",
    )(dev, newton_steps, *members[::-1])
    mine = over_square([inverse] * RING, True)
    others = [to_other_core(block) for block in mine]

    def apply(side, blocks, before):
        kinds = (grad_qkv.shape, grad_up.shape)
        buffers = [pltpu.VMEM(dims[1:], half) for dims in kinds]
        return pl.pallas_call(
            functools.partial(apply_kernel, side),
            out_shape=[shape(*dims) for dims in kinds],
            in_specs=[SMEM] + [VMEM] * RING + [ANY] * (2 + len(before)),
            out_specs=[ANY] * 2,
            input_output_aliases={7: 0, 8: 1} if before else {},
            scratch_shapes=buffers
            + buffers
            + [
                pltpu.VMEM((RING, BLOCK, BLOCK), half),
                pltpu.SemaphoreType.DMA((4,)),
            ],
            compiler_params=PARAMS,
            name="apply",
        )(dev, *blocks, grad_qkv, grad_up, *before)

    return tuple(apply(1, others, apply(0, mine, ())))


def solution(mesh):
    placed = (
        P(None, None, ("dp", "tensor"), None),
        P(None, "dp", "tensor"),
        P(None, "dp", "tensor"),
        P(),
    )
    return jax.shard_map(
        local,
        mesh=mesh,
        in_specs=placed,
        out_specs=(P(None, "dp", "tensor"), P(None, "dp", "tensor")),
        check_vma=False,
    )
```

time: 134 us -> 127 us (0.948)
  blocking collectives: 28.6 us -> 0 us
  waiting for transfers between devices: 34.2 us -> 54.2 us
  starting transfers between devices: 46 us -> 51.6 us
  Pallas kernels: 23.2 us -> 19.3 us
    all_to_all x2 -> x0, blocking collectives: 28.6 us -> none  [exchange(): lax.all_to_all(array, AXES, 0, 0, axis_index_groups=groups_by(key), tiled...]
    ppermute x20 -> x24, waiting for transfers between devices: 34.2 us -> 54.2 us  [move(): return lax.ppermute(array, AXES, pairs)]
    ppermute x20 -> x24, starting transfers between devices: 46 us -> 51.6 us  [move(): return lax.ppermute(array, AXES, pairs)]
    pallas_call x2, Pallas kernels: 8.59 us -> 6.78 us  [apply(): pl.pallas_call(functools.partial(apply_kernel, side), out_shape=[shape(*d...]
    pallas_call x2 -> x1, Pallas kernels: 3.93 us -> 2.97 us  [local(): pl.pallas_call(pack_kernel, out_shape=[shape(*part)] * (RING + 1) + [shap...]
  transfers between devices with their start and end apart: 20 -> 24, of which waited for: 8 -> 14; matrix products, arithmetic and copies ran while one was open for 0% -> 0% of each run, Pallas kernels for 5% -> 3%
where the time goes in v4:
time: 127 us
  waiting for transfers between devices  54.2 us (43%)
  starting transfers between devices  51.6 us (41%)
  Pallas kernels  19.3 us (15%)
    ppermute x24, waiting for transfers between devices, move(): return lax.ppermute(array, AXES, pairs)  54.2 us
    ppermute x24, starting transfers between devices, move(): return lax.ppermute(array, AXES, pairs)  51.6 us
    pallas_call x2, Pallas kernels, apply(): pl.pallas_call(functools.partial(apply_kernel, side), out_shape=[shape(*d...  6.78 us
    pallas_call x1, Pallas kernels, local(): pl.pallas_call(functools.partial(newton_kernel, tokens_all), out_shape=sh...  6.18 us
    pallas_call x1, Pallas kernels, local(): pl.pallas_call(gram_kernel, out_shape=[shape(SLABS, CHUNK, BLOCK)] * RING...  3.39 us
    pallas_call x1, Pallas kernels, local(): pl.pallas_call(pack_kernel, out_shape=[shape(*part)] * (RING + 1) + [shap...  2.97 us
  transfers between devices with their start and end apart: 24, of which 14 were waited for; matrix products, arithmetic and copies ran while one was open for 0% of the time, Pallas kernels for 3%

profile of v4, /device:TPU:1, one launch (start us, length us, event | category | flops | bytes accessed | tf_op | source)
XLA Modules:
  0.0 126.6 jit_solution(11761442321187160637)
XLA Ops:
  0.6 3.0 %pack.1 = (bf16[4,128,640]{2,1,0:T(8,128)(2,1)S(1)}, bf16[4,128,640]{2,1,0:T(8,128)(2,1)S(1)}, bf16[4,128,640]{2,1,0:T(8,128)(2,1)S(1)}, bf16[4,128,640]{2,1,0:T...) custom-call(s32[1]{0:T(128)} %bitcast.dev, bf16[2,2,128,5120]{3,2,1,0:T(8,128)(2,1)} %act.1), custom_call_target="tpu_custom_call" | custom-call | tf_op jit(solution)/shard_map/pack/pallas_call | solution.py:229
  3.6 3.3 %collective-permute-start.5 = (bf16[3,4,128,640]{3,2,1,0:T(8,128)(2,1)S(1)}, bf16[3,4,128,640]{3,2,1,0:T(8,128)(2,1)S(1)}, u32[]{:S(2)}, u32[]{:S(2)}) collective-permute-start(bf16[3,4,128,640]{3,2,1,0:T(8,128)(2,1)S(1)} %get-tuple-element.19), channel_id=1, source_target_pairs={{0,4},{1,5},{2,6},{3,7},{4,0},{5,1},{6,2},{7,3},{8,12},{9,13},{10,... | collective-permute-start | bytes 5898248 | tf_op jit(solution)/shard_map/ppermute | solution.py:43
  6.9 0.1 collective-permute-start.3
  7.0 3.2 %collective-permute-start = (bf16[4,128,640]{2,1,0:T(8,128)(2,1)S(1)}, bf16[4,128,640]{2,1,0:T(8,128)(2,1)S(1)}, u32[]{:S(2)}, u32[]{:S(2)}) collective-permute-start(bf16[4,128,640]{2,1,0:T(8,128)(2,1)S(1)} %get-tuple-element.14), channel_id=1, source_target_pairs={{0,40},{1,41},{2,42},{3,43},{4,124},{5,125},{6,126},{7,127},{8,32}... | collective-permute-start | bytes 1966088 | tf_op jit(solution)/shard_map/ppermute | solution.py:43
  10.2 0.2 collective-permute-start.1
  10.4 1.7 %collective-permute-start.2 = (bf16[4,128,640]{2,1,0:T(8,128)(2,1)S(1)}, bf16[4,128,640]{2,1,0:T(8,128)(2,1)S(1)}, u32[]{:S(2)}, u32[]{:S(2)}) collective-permute-start(bf16[4,128,640]{2,1,0:T(8,128)(2,1)S(1)} %get-tuple-element.16), channel_id=1, source_target_pairs={{0,8},{1,9},{2,10},{3,11},{4,28},{5,29},{6,30},{7,31},{8,0},{9,1},... | collective-permute-start | bytes 1966088 | tf_op jit(solution)/shard_map/ppermute | solution.py:43
  12.1 0.0 collective-permute-done.3
  12.1 3.2 %collective-permute-start.4 = (bf16[4,128,640]{2,1,0:T(8,128)(2,1)S(1)}, bf16[4,128,640]{2,1,0:T(8,128)(2,1)S(1)}, u32[]{:S(2)}, u32[]{:S(2)}) collective-permute-start(bf16[4,128,640]{2,1,0:T(8,128)(2,1)S(1)} %collective-permute-done.3), channel_id=1, source_target_pairs={{0,40},{1,41},{2,42},{3,43},{4,124},{5,125},{6,126},{7,127},{8,32}... | collective-permute-start | bytes 1966088 | tf_op jit(solution)/shard_map/ppermute | solution.py:43
  15.3 0.0 collective-permute-done.5.refs_7_
  15.3 0.1 slice_bitcast_fusion
  15.4 0.1 collective-permute-start.7
  15.5 4.4 %collective-permute-done.refs_0_ = bf16[4,128,640]{2,1,0:T(8,128)(2,1)S(1)} collective-permute-done((bf16[4,128,640]{2,1,0:T(8,128)(2,1)S(1)}, bf16[4,128,640]{2,1,0:T(8,128)(2,1)S(1)}, u32[]{:S(2)}, u32[]{:S(2)}) %collective-permute-start) | collective-permute-done | bytes 655392 | tf_op jit(solution)/shard_map/ppermute | solution.py:43
  19.9 0.7 collective-permute-start.6
  20.6 4.8 %collective-permute-done.1.refs_1_ = bf16[4,128,640]{2,1,0:T(8,128)(2,1)S(1)} collective-permute-done((bf16[4,128,640]{2,1,0:T(8,128)(2,1)S(1)}, bf16[4,128,640]{2,1,0:T(8,128)(2,1)S(1)}, u32[]{:S(2)}, u32[]{:S(2)}) %collective-permute-start.1) | collective-permute-done | bytes 655392 | tf_op jit(solution)/shard_map/ppermute | solution.py:43
  25.5 1.5 %collective-permute-done.2.refs_2_ = bf16[4,128,640]{2,1,0:T(8,128)(2,1)S(1)} collective-permute-done((bf16[4,128,640]{2,1,0:T(8,128)(2,1)S(1)}, bf16[4,128,640]{2,1,0:T(8,128)(2,1)S(1)}, u32[]{:S(2)}, u32[]{:S(2)}) %collective-permute-start.2) | collective-permute-done | bytes 655392 | tf_op jit(solution)/shard_map/ppermute | solution.py:43
  27.0 7.0 %collective-permute-done.4.refs_4_ = bf16[4,128,640]{2,1,0:T(8,128)(2,1)S(1)} collective-permute-done((bf16[4,128,640]{2,1,0:T(8,128)(2,1)S(1)}, bf16[4,128,640]{2,1,0:T(8,128)(2,1)S(1)}, u32[]{:S(2)}, u32[]{:S(2)}) %collective-permute-start.4) | collective-permute-done | bytes 655392 | tf_op jit(solution)/shard_map/ppermute | solution.py:43
  34.0 6.9 %collective-permute-done.7.refs_6_ = bf16[4,128,640]{2,1,0:T(8,128)(2,1)S(1)} collective-permute-done((bf16[4,128,640]{2,1,0:T(8,128)(2,1)S(1)}, bf16[4,128,640]{2,1,0:T(8,128)(2,1)S(1)}, u32[]{:S(2)}, u32[]{:S(2)}) %collective-permute-start.7) | collective-permute-done | bytes 655392 | tf_op jit(solution)/shard_map/ppermute | solution.py:43
  40.9 0.0 collective-permute-done.6.refs_5_
  40.9 3.4 %gram.1 = (bf16[4,96,640]{2,1,0:T(8,128)(2,1)S(1)}, bf16[4,96,640]{2,1,0:T(8,128)(2,1)S(1)}, bf16[4,96,640]{2,1,0:T(8,128)(2,1)S(1)}, bf16[4,96,640]{2,1,0:T(8,128)(2,1)S(1)}) custom-call(s32[1]{0:T(128)} %bitcast.dev, bf16[4,128,640]{2,1,0:T(8,128)(2,1)S(1)} %collective-permute-done.refs_0_, bf16[4,128,640]{2,1,0:T(8,128)(2,1)S(1)} %collective-permute-done.1.refs_1_, ...), custom_call_target="tpu_custom_call" | custom-call | tf_op jit(solution)/shard_map/gram/pallas_call | solution.py:243
  44.3 0.1 collective-permute-start.8
  44.4 0.1 collective-permute-start.9
  44.5 2.5 %collective-permute-start.10 = (bf16[4,96,640]{2,1,0:T(8,128)(2,1)S(1)}, bf16[4,96,640]{2,1,0:T(8,128)(2,1)S(1)}, u32[]{:S(2)}, u32[]{:S(2)}) collective-permute-start(bf16[4,96,640]{2,1,0:T(8,128)(2,1)S(1)} %get-tuple-element.22), channel_id=1, source_target_pairs={{0,24},{1,25},{2,26},{3,27},{4,12},{5,13},{6,14},{7,15},{8,16},{9,... | collective-permute-start | bytes 1474568 | tf_op jit(solution)/shard_map/ppermute | solution.py:43
  47.0 6.3 %collective-permute-done.8 = bf16[4,96,640]{2,1,0:T(8,128)(2,1)S(1)} collective-permute-done((bf16[4,96,640]{2,1,0:T(8,128)(2,1)S(1)}, bf16[4,96,640]{2,1,0:T(8,128)(2,1)S(1)}, u32[]{:S(2)}, u32[]{:S(2)}) %collective-permute-start.8) | collective-permute-done | bytes 491552 | tf_op jit(solution)/shard_map/ppermute | solution.py:43
  53.3 2.7 %collective-permute-done.9 = bf16[4,96,640]{2,1,0:T(8,128)(2,1)S(1)} collective-permute-done((bf16[4,96,640]{2,1,0:T(8,128)(2,1)S(1)}, bf16[4,96,640]{2,1,0:T(8,128)(2,1)S(1)}, u32[]{:S(2)}, u32[]{:S(2)}) %collective-permute-start.9) | collective-permute-done | bytes 491552 | tf_op jit(solution)/shard_map/ppermute | solution.py:43
  56.0 2.5 %collective-permute-done.10 = bf16[4,96,640]{2,1,0:T(8,128)(2,1)S(1)} collective-permute-done((bf16[4,96,640]{2,1,0:T(8,128)(2,1)S(1)}, bf16[4,96,640]{2,1,0:T(8,128)(2,1)S(1)}, u32[]{:S(2)}, u32[]{:S(2)}) %collective-permute-start.10) | collective-permute-done | bytes 491552 | tf_op jit(solution)/shard_map/ppermute | solution.py:43
  58.5 0.2 convert_add_fusion
  58.7 0.0 copy-start.2
  58.8 0.0 copy-start
  58.8 0.0 copy-start.1
  58.8 4.8 %collective-permute-start.11 = (bf16[2,96,640]{2,1,0:T(8,128)(2,1)S(1)}, bf16[2,96,640]{2,1,0:T(8,128)(2,1)S(1)}, u32[]{:S(2)}, u32[]{:S(2)}) collective-permute-start(bf16[2,96,640]{2,1,0:T(8,128)(2,1)S(1)} %slice.46), channel_id=1, source_target_pairs={{0,1},{1,0},{2,3},{3,2},{4,7},{5,6},{6,5},{7,4},{8,9},{9,8},{10,11... | collective-permute-start | bytes 737288 | tf_op jit(solution)/shard_map/ppermute | solution.py:43
  63.6 5.8 %collective-permute-done.11 = bf16[2,96,640]{2,1,0:T(8,128)(2,1)S(1)} collective-permute-done((bf16[2,96,640]{2,1,0:T(8,128)(2,1)S(1)}, bf16[2,96,640]{2,1,0:T(8,128)(2,1)S(1)}, u32[]{:S(2)}, u32[]{:S(2)}) %collective-permute-start.11) | collective-permute-done | bytes 245792 | tf_op jit(solution)/shard_map/ppermute | solution.py:43
  69.4 0.1 slice_add_fusion
  69.5 1.7 %collective-permute-start.12 = (bf16[96,640]{1,0:T(8,128)(2,1)S(1)}, bf16[96,640]{1,0:T(8,128)(2,1)S(1)}, u32[]{:S(2)}, u32[]{:S(2)}) collective-permute-start(bf16[96,640]{1,0:T(8,128)(2,1)S(1)} %fusion.2), channel_id=1, source_target_pairs={{0,3},{1,2},{2,1},{3,0},{4,5},{5,4},{6,7},{7,6},{8,11},{9,10},{10,... | collective-permute-start | bytes 368648 | tf_op jit(solution)/shard_map/ppermute | solution.py:43
  71.2 4.3 %collective-permute-done.12 = bf16[96,640]{1,0:T(8,128)(2,1)S(1)} collective-permute-done((bf16[96,640]{1,0:T(8,128)(2,1)S(1)}, bf16[96,640]{1,0:T(8,128)(2,1)S(1)}, u32[]{:S(2)}, u32[]{:S(2)}) %collective-permute-start.12) | collective-permute-done | bytes 122912 | tf_op jit(solution)/shard_map/ppermute | solution.py:43
  75.5 0.1 collective-permute-start.13
  75.6 4.5 %collective-permute-done.13 = bf16[96,640]{1,0:T(8,128)(2,1)S(1)} collective-permute-done((bf16[96,640]{1,0:T(8,128)(2,1)S(1)}, bf16[96,640]{1,0:T(8,128)(2,1)S(1)}, u32[]{:S(2)}, u32[]{:S(2)}) %collective-permute-start.13) | collective-permute-done | bytes 122912 | tf_op jit(solution)/shard_map/ppermute | solution.py:43
  80.1 0.7 collective-permute-start.16
  80.8 0.0 collective-permute-start.15
  80.8 2.2 %collective-permute-start.14 = (bf16[96,640]{1,0:T(8,128)(2,1)S(1)}, bf16[96,640]{1,0:T(8,128)(2,1)S(1)}, u32[]{:S(2)}, u32[]{:S(2)}) collective-permute-start(bf16[96,640]{1,0:T(8,128)(2,1)S(1)} %add_convert_fusion.refs_3_), channel_id=1, source_target_pairs={{0,120},{1,121},{2,122},{3,123},{4,44},{5,45},{6,46},{7,47},{8,112... | collective-permute-start | bytes 368648 | tf_op jit(solution)/shard_map/ppermute | solution.py:43
  83.1 1.1 collective-permute-done.16.refs_2_
  84.1 0.4 collective-permute-done.15.refs_1_
  84.6 2.1 %collective-permute-done.14.refs_0_ = bf16[96,640]{1,0:T(8,128)(2,1)S(1)} collective-permute-done((bf16[96,640]{1,0:T(8,128)(2,1)S(1)}, bf16[96,640]{1,0:T(8,128)(2,1)S(1)}, u32[]{:S(2)}, u32[]{:S(2)}) %collective-permute-start.14) | collective-permute-done | bytes 122912 | tf_op jit(solution)/shard_map/ppermute | solution.py:43
  86.6 0.0 copy-done.2
  86.6 6.2 %newton.1.refs_0_ = bf16[384,640]{1,0:T(8,128)(2,1)S(1)} custom-call(s32[1]{0:T(128)} %bitcast.dev, s32[2,2,8]{2,1,0:T(2,128)S(1)} %copy-done.2, bf16[96,640]{1,0:T(8,128)(2,1)S(1)} %collective-permute-done.14.refs_0_, bf16[96,640]{1,0:T(8,128)(2,1)S(1)} %collective-permute-done.15.refs_1_, bf16[96,640]{1,0:T(8,128)(2,1)S(1)} %collective-permute-done.16.refs_2_, ...), custom_call_target="tpu_custom_call" | custom-call | tf_op jit(solution)/shard_map/newton/pallas_call | solution.py:263
  92.8 4.6 %collective-permute-start.22 = (bf16[384,640]{1,0:T(8,128)(2,1)S(1)}, bf16[384,640]{1,0:T(8,128)(2,1)S(1)}, u32[]{:S(2)}, u32[]{:S(2)}) collective-permute-start(bf16[384,640]{1,0:T(8,128)(2,1)S(1)} %newton.1.refs_0_), channel_id=1, source_target_pairs={{0,40},{1,41},{2,42},{3,43},{4,124},{5,125},{6,126},{7,127},{8,32}... | collective-permute-start | bytes 1474568 | tf_op jit(solution)/shard_map/ppermute | solution.py:43
  97.4 0.2 collective-permute-start.20
  97.6 0.4 collective-permute-start.18
  98.0 10.1 %collective-permute-start.17 = (bf16[384,640]{1,0:T(8,128)(2,1)S(1)}, bf16[384,640]{1,0:T(8,128)(2,1)S(1)}, u32[]{:S(2)}, u32[]{:S(2)}) collective-permute-start(bf16[384,640]{1,0:T(8,128)(2,1)S(1)} %newton.1.refs_0_), channel_id=1, source_target_pairs={{0,4},{1,5},{2,6},{3,7},{4,0},{5,1},{6,2},{7,3},{8,12},{9,13},{10,... | collective-permute-start | bytes 1474568 | tf_op jit(solution)/shard_map/ppermute | solution.py:43
  108.1 0.0 collective-permute-done.22.refs_3_
  108.1 6.3 %collective-permute-start.23 = (bf16[384,640]{1,0:T(8,128)(2,1)S(1)}, bf16[384,640]{1,0:T(8,128)(2,1)S(1)}, u32[]{:S(2)}, u32[]{:S(2)}) collective-permute-start(bf16[384,640]{1,0:T(8,128)(2,1)S(1)} %collective-permute-done.22.refs_3_), channel_id=1, source_target_pairs={{0,4},{1,5},{2,6},{3,7},{4,0},{5,1},{6,2},{7,3},{8,12},{9,13},{10,... | collective-permute-start | bytes 1474568 | tf_op jit(solution)/shard_map/ppermute | solution.py:43
  114.5 0.0 collective-permute-done.20.refs_2_
  114.5 1.8 %collective-permute-start.21 = (bf16[384,640]{1,0:T(8,128)(2,1)S(1)}, bf16[384,640]{1,0:T(8,128)(2,1)S(1)}, u32[]{:S(2)}, u32[]{:S(2)}) collective-permute-start(bf16[384,640]{1,0:T(8,128)(2,1)S(1)} %collective-permute-done.20.refs_2_), channel_id=1, source_target_pairs={{0,4},{1,5},{2,6},{3,7},{4,0},{5,1},{6,2},{7,3},{8,12},{9,13},{10,... | collective-permute-start | bytes 1474568 | tf_op jit(solution)/shard_map/ppermute | solution.py:43
  116.3 0.0 collective-permute-done.18.refs_1_
  116.3 3.3 %collective-permute-start.19 = (bf16[384,640]{1,0:T(8,128)(2,1)S(1)}, bf16[384,640]{1,0:T(8,128)(2,1)S(1)}, u32[]{:S(2)}, u32[]{:S(2)}) collective-permute-start(bf16[384,640]{1,0:T(8,128)(2,1)S(1)} %collective-permute-done.18.refs_1_), channel_id=1, source_target_pairs={{0,4},{1,5},{2,6},{3,7},{4,0},{5,1},{6,2},{7,3},{8,12},{9,13},{10,... | collective-permute-start | bytes 1474568 | tf_op jit(solution)/shard_map/ppermute | solution.py:43
  119.6 0.0 copy-done
  119.6 0.0 copy-done.1
  119.6 3.4 %apply.2 = (bf16[2,240,1280]{2,1,0:T(8,128)(2,1)}, bf16[2,320,1280]{2,1,0:T(8,128)(2,1)}) custom-call(s32[1]{0:T(128)} %bitcast.dev, bf16[384,640]{1,0:T(8,128)(2,1)S(1)} %newton.1.refs_0_, bf16[384,640]{1,0:T(8,128)(2,1)S(1)} %collective-permute-done.18.refs_1_, bf16[384,640]{1,0:T(8,128)(2,1)S(1)} %collective-permute-done.20.refs_2_, ...), custom_call_target="tpu_custom_call" | custom-call | tf_op jit(solution)/shard_map/apply/pallas_call | solution.py:283
  123.0 0.0 collective-permute-done.17.refs_0_
  123.0 0.0 collective-permute-done.23.refs_3_
  123.0 0.0 collective-permute-done.21.refs_2_
  123.0 0.0 collective-permute-done.19.refs_1_
  123.0 3.4 %apply.3 = (bf16[2,240,1280]{2,1,0:T(8,128)(2,1)}, bf16[2,320,1280]{2,1,0:T(8,128)(2,1)}) custom-call(s32[1]{0:T(128)} %bitcast.dev, bf16[384,640]{1,0:T(8,128)(2,1)S(1)} %collective-permute-done.17.refs_0_, bf16[384,640]{1,0:T(8,128)(2,1)S(1)} %collective-permute-done.19.refs_1_, ...), custom_call_target="tpu_custom_call", output_to_operand_aliasing={{0}: (7, {}), {1}: (8, {})} | custom-call | tf_op jit(solution)/shard_map/apply/pallas_call | solution.py:283
  (4 shorter events, 0.1 us)
Async XLA Ops:
  3.6 11.7 %collective-permute-start.5 = (bf16[3,4,128,640]{3,2,1,0:T(8,128)(2,1)S(1)}, bf16[3,4,128,640]{3,2,1,0:T(8,128)(2,1)S(1)}, u32[]{:S(2)}, u32[]{:S(2)}) collective-permute-start(bf16[3,4,128,640]{3,2,1,0:T(8,128)(2,1)S(1)} %get-tuple-element.19), channel_id=1, source_target_pairs={{0,4},{1,5},{2,6},{3,7},{4,0},{5,1},{6,2},{7,3},{8,12},{9,13},{10,... | collective-permute-start | bytes 5898248 | tf_op jit(solution)/shard_map/ppermute | solution.py:43
  6.9 5.2 %collective-permute-start.3 = (bf16[4,128,640]{2,1,0:T(8,128)(2,1)S(1)}, bf16[4,128,640]{2,1,0:T(8,128)(2,1)S(1)}, u32[]{:S(2)}, u32[]{:S(2)}) collective-permute-start(bf16[4,128,640]{2,1,0:T(8,128)(2,1)S(1)} %get-tuple-element.18), channel_id=1, source_target_pairs={{0,4},{1,5},{2,6},{3,7},{4,0},{5,1},{6,2},{7,3},{8,12},{9,13},{10,... | collective-permute-start | bytes 1966088 | tf_op jit(solution)/shard_map/ppermute | solution.py:43
  7.0 12.9 %collective-permute-start = (bf16[4,128,640]{2,1,0:T(8,128)(2,1)S(1)}, bf16[4,128,640]{2,1,0:T(8,128)(2,1)S(1)}, u32[]{:S(2)}, u32[]{:S(2)}) collective-permute-start(bf16[4,128,640]{2,1,0:T(8,128)(2,1)S(1)} %get-tuple-element.14), channel_id=1, source_target_pairs={{0,40},{1,41},{2,42},{3,43},{4,124},{5,125},{6,126},{7,127},{8,32}... | collective-permute-start | bytes 1966088 | tf_op jit(solution)/shard_map/ppermute | solution.py:43
  10.2 15.2 %collective-permute-start.1 = (bf16[4,128,640]{2,1,0:T(8,128)(2,1)S(1)}, bf16[4,128,640]{2,1,0:T(8,128)(2,1)S(1)}, u32[]{:S(2)}, u32[]{:S(2)}) collective-permute-start(bf16[4,128,640]{2,1,0:T(8,128)(2,1)S(1)} %get-tuple-element.15), channel_id=1, source_target_pairs={{0,32},{1,33},{2,34},{3,35},{4,100},{5,101},{6,102},{7,103},{8,40}... | collective-permute-start | bytes 1966088 | tf_op jit(solution)/shard_map/ppermute | solution.py:43
  10.4 16.5 %collective-permute-start.2 = (bf16[4,128,640]{2,1,0:T(8,128)(2,1)S(1)}, bf16[4,128,640]{2,1,0:T(8,128)(2,1)S(1)}, u32[]{:S(2)}, u32[]{:S(2)}) collective-permute-start(bf16[4,128,640]{2,1,0:T(8,128)(2,1)S(1)} %get-tuple-element.16), channel_id=1, source_target_pairs={{0,8},{1,9},{2,10},{3,11},{4,28},{5,29},{6,30},{7,31},{8,0},{9,1},... | collective-permute-start | bytes 1966088 | tf_op jit(solution)/shard_map/ppermute | solution.py:43
  12.1 21.9 %collective-permute-start.4 = (bf16[4,128,640]{2,1,0:T(8,128)(2,1)S(1)}, bf16[4,128,640]{2,1,0:T(8,128)(2,1)S(1)}, u32[]{:S(2)}, u32[]{:S(2)}) collective-permute-start(bf16[4,128,640]{2,1,0:T(8,128)(2,1)S(1)} %collective-permute-done.3), channel_id=1, source_target_pairs={{0,40},{1,41},{2,42},{3,43},{4,124},{5,125},{6,126},{7,127},{8,32}... | collective-permute-start | bytes 1966088 | tf_op jit(solution)/shard_map/ppermute | solution.py:43
  15.4 25.4 %collective-permute-start.7 = (bf16[4,128,640]{2,1,0:T(8,128)(2,1)S(1)}, bf16[4,128,640]{2,1,0:T(8,128)(2,1)S(1)}, u32[]{:S(2)}, u32[]{:S(2)}) collective-permute-start(bf16[4,128,640]{2,1,0:T(8,128)(2,1)S(1)} %get-tuple-element.26), channel_id=1, source_target_pairs={{0,8},{1,9},{2,10},{3,11},{4,28},{5,29},{6,30},{7,31},{8,0},{9,1},... | collective-permute-start | bytes 1966088 | tf_op jit(solution)/shard_map/ppermute | solution.py:43
  19.9 21.0 %collective-permute-start.6 = (bf16[4,128,640]{2,1,0:T(8,128)(2,1)S(1)}, bf16[4,128,640]{2,1,0:T(8,128)(2,1)S(1)}, u32[]{:S(2)}, u32[]{:S(2)}) collective-permute-start(bf16[4,128,640]{2,1,0:T(8,128)(2,1)S(1)} %get-tuple-element.27), channel_id=1, source_target_pairs={{0,32},{1,33},{2,34},{3,35},{4,100},{5,101},{6,102},{7,103},{8,40}... | collective-permute-start | bytes 1966088 | tf_op jit(solution)/shard_map/ppermute | solution.py:43
  44.3 9.0 %collective-permute-start.8 = (bf16[4,96,640]{2,1,0:T(8,128)(2,1)S(1)}, bf16[4,96,640]{2,1,0:T(8,128)(2,1)S(1)}, u32[]{:S(2)}, u32[]{:S(2)}) collective-permute-start(bf16[4,96,640]{2,1,0:T(8,128)(2,1)S(1)} %get-tuple-element.20), channel_id=1, source_target_pairs={{0,120},{1,121},{2,122},{3,123},{4,44},{5,45},{6,46},{7,47},{8,112... | collective-permute-start | bytes 1474568 | tf_op jit(solution)/shard_map/ppermute | solution.py:43
  44.4 11.6 %collective-permute-start.9 = (bf16[4,96,640]{2,1,0:T(8,128)(2,1)S(1)}, bf16[4,96,640]{2,1,0:T(8,128)(2,1)S(1)}, u32[]{:S(2)}, u32[]{:S(2)}) collective-permute-start(bf16[4,96,640]{2,1,0:T(8,128)(2,1)S(1)} %get-tuple-element.21), channel_id=1, source_target_pairs={{0,96},{1,97},{2,98},{3,99},{4,36},{5,37},{6,38},{7,39},{8,104},{9... | collective-permute-start | bytes 1474568 | tf_op jit(solution)/shard_map/ppermute | solution.py:43
  44.5 14.0 %collective-permute-start.10 = (bf16[4,96,640]{2,1,0:T(8,128)(2,1)S(1)}, bf16[4,96,640]{2,1,0:T(8,128)(2,1)S(1)}, u32[]{:S(2)}, u32[]{:S(2)}) collective-permute-start(bf16[4,96,640]{2,1,0:T(8,128)(2,1)S(1)} %get-tuple-element.22), channel_id=1, source_target_pairs={{0,24},{1,25},{2,26},{3,27},{4,12},{5,13},{6,14},{7,15},{8,16},{9,... | collective-permute-start | bytes 1474568 | tf_op jit(solution)/shard_map/ppermute | solution.py:43
  58.7 27.9 %copy-start.2 = (s32[2,2,8]{2,1,0:T(2,128)S(1)}, s32[2,2,8]{2,1,0:T(2,128)}, u32[]{:S(2)}) copy-start(s32[2,2,8]{2,1,0:T(2,128)} %newton_steps.1) | copy-start | bytes 388
  58.8 60.9 %copy-start = (bf16[2,320,1280]{2,1,0:T(8,128)(2,1)S(1)}, bf16[2,320,1280]{2,1,0:T(8,128)(2,1)}, u32[]{:S(2)}) copy-start(bf16[2,320,1280]{2,1,0:T(8,128)(2,1)} %refs_5_.3) | copy-start | bytes 4915204
  58.8 60.8 %copy-start.1 = (bf16[2,240,1280]{2,1,0:T(8,128)(2,1)S(1)}, bf16[2,240,1280]{2,1,0:T(8,128)(2,1)}, u32[]{:S(2)}) copy-start(bf16[2,240,1280]{2,1,0:T(8,128)(2,1)} %refs_4_.3) | copy-start | bytes 3686404
  58.8 10.6 %collective-permute-start.11 = (bf16[2,96,640]{2,1,0:T(8,128)(2,1)S(1)}, bf16[2,96,640]{2,1,0:T(8,128)(2,1)S(1)}, u32[]{:S(2)}, u32[]{:S(2)}) collective-permute-start(bf16[2,96,640]{2,1,0:T(8,128)(2,1)S(1)} %slice.46), channel_id=1, source_target_pairs={{0,1},{1,0},{2,3},{3,2},{4,7},{5,6},{6,5},{7,4},{8,9},{9,8},{10,11... | collective-permute-start | bytes 737288 | tf_op jit(solution)/shard_map/ppermute | solution.py:43
  69.5 6.0 %collective-permute-start.12 = (bf16[96,640]{1,0:T(8,128)(2,1)S(1)}, bf16[96,640]{1,0:T(8,128)(2,1)S(1)}, u32[]{:S(2)}, u32[]{:S(2)}) collective-permute-start(bf16[96,640]{1,0:T(8,128)(2,1)S(1)} %fusion.2), channel_id=1, source_target_pairs={{0,3},{1,2},{2,1},{3,0},{4,5},{5,4},{6,7},{7,6},{8,11},{9,10},{10,... | collective-permute-start | bytes 368648 | tf_op jit(solution)/shard_map/ppermute | solution.py:43
  75.5 4.6 %collective-permute-start.13 = (bf16[96,640]{1,0:T(8,128)(2,1)S(1)}, bf16[96,640]{1,0:T(8,128)(2,1)S(1)}, u32[]{:S(2)}, u32[]{:S(2)}) collective-permute-start(bf16[96,640]{1,0:T(8,128)(2,1)S(1)} %fusion.1), channel_id=1, source_target_pairs={{0,128},{1,129},{2,130},{3,131},{4,132},{5,133},{6,134},{7,135},{8... | collective-permute-start | bytes 368648 | tf_op jit(solution)/shard_map/ppermute | solution.py:43
  80.1 4.0 %collective-permute-start.16 = (bf16[96,640]{1,0:T(8,128)(2,1)S(1)}, bf16[96,640]{1,0:T(8,128)(2,1)S(1)}, u32[]{:S(2)}, u32[]{:S(2)}) collective-permute-start(bf16[96,640]{1,0:T(8,128)(2,1)S(1)} %add_convert_fusion.refs_3_), channel_id=1, source_target_pairs={{0,24},{1,25},{2,26},{3,27},{4,12},{5,13},{6,14},{7,15},{8,16},{9,... | collective-permute-start | bytes 368648 | tf_op jit(solution)/shard_map/ppermute | solution.py:43
  80.8 3.7 %collective-permute-start.15 = (bf16[96,640]{1,0:T(8,128)(2,1)S(1)}, bf16[96,640]{1,0:T(8,128)(2,1)S(1)}, u32[]{:S(2)}, u32[]{:S(2)}) collective-permute-start(bf16[96,640]{1,0:T(8,128)(2,1)S(1)} %add_convert_fusion.refs_3_), channel_id=1, source_target_pairs={{0,96},{1,97},{2,98},{3,99},{4,36},{5,37},{6,38},{7,39},{8,104},{9... | collective-permute-start | bytes 368648 | tf_op jit(solution)/shard_map/ppermute | solution.py:43
  80.8 5.8 %collective-permute-start.14 = (bf16[96,640]{1,0:T(8,128)(2,1)S(1)}, bf16[96,640]{1,0:T(8,128)(2,1)S(1)}, u32[]{:S(2)}, u32[]{:S(2)}) collective-permute-start(bf16[96,640]{1,0:T(8,128)(2,1)S(1)} %add_convert_fusion.refs_3_), channel_id=1, source_target_pairs={{0,120},{1,121},{2,122},{3,123},{4,44},{5,45},{6,46},{7,47},{8,112... | collective-permute-start | bytes 368648 | tf_op jit(solution)/shard_map/ppermute | solution.py:43
  92.8 15.3 %collective-permute-start.22 = (bf16[384,640]{1,0:T(8,128)(2,1)S(1)}, bf16[384,640]{1,0:T(8,128)(2,1)S(1)}, u32[]{:S(2)}, u32[]{:S(2)}) collective-permute-start(bf16[384,640]{1,0:T(8,128)(2,1)S(1)} %newton.1.refs_0_), channel_id=1, source_target_pairs={{0,40},{1,41},{2,42},{3,43},{4,124},{5,125},{6,126},{7,127},{8,32}... | collective-permute-start | bytes 1474568 | tf_op jit(solution)/shard_map/ppermute | solution.py:43
  97.4 17.1 %collective-permute-start.20 = (bf16[384,640]{1,0:T(8,128)(2,1)S(1)}, bf16[384,640]{1,0:T(8,128)(2,1)S(1)}, u32[]{:S(2)}, u32[]{:S(2)}) collective-permute-start(bf16[384,640]{1,0:T(8,128)(2,1)S(1)} %newton.1.refs_0_), channel_id=1, source_target_pairs={{0,32},{1,33},{2,34},{3,35},{4,100},{5,101},{6,102},{7,103},{8,40}... | collective-permute-start | bytes 1474568 | tf_op jit(solution)/shard_map/ppermute | solution.py:43
  97.6 18.7 %collective-permute-start.18 = (bf16[384,640]{1,0:T(8,128)(2,1)S(1)}, bf16[384,640]{1,0:T(8,128)(2,1)S(1)}, u32[]{:S(2)}, u32[]{:S(2)}) collective-permute-start(bf16[384,640]{1,0:T(8,128)(2,1)S(1)} %newton.1.refs_0_), channel_id=1, source_target_pairs={{0,8},{1,9},{2,10},{3,11},{4,28},{5,29},{6,30},{7,31},{8,0},{9,1},... | collective-permute-start | bytes 1474568 | tf_op jit(solution)/shard_map/ppermute | solution.py:43
  98.0 25.0 %collective-permute-start.17 = (bf16[384,640]{1,0:T(8,128)(2,1)S(1)}, bf16[384,640]{1,0:T(8,128)(2,1)S(1)}, u32[]{:S(2)}, u32[]{:S(2)}) collective-permute-start(bf16[384,640]{1,0:T(8,128)(2,1)S(1)} %newton.1.refs_0_), channel_id=1, source_target_pairs={{0,4},{1,5},{2,6},{3,7},{4,0},{5,1},{6,2},{7,3},{8,12},{9,13},{10,... | collective-permute-start | bytes 1474568 | tf_op jit(solution)/shard_map/ppermute | solution.py:43
  108.1 14.9 %collective-permute-start.23 = (bf16[384,640]{1,0:T(8,128)(2,1)S(1)}, bf16[384,640]{1,0:T(8,128)(2,1)S(1)}, u32[]{:S(2)}, u32[]{:S(2)}) collective-permute-start(bf16[384,640]{1,0:T(8,128)(2,1)S(1)} %collective-permute-done.22.refs_3_), channel_id=1, source_target_pairs={{0,4},{1,5},{2,6},{3,7},{4,0},{5,1},{6,2},{7,3},{8,12},{9,13},{10,... | collective-permute-start | bytes 1474568 | tf_op jit(solution)/shard_map/ppermute | solution.py:43
  114.5 8.6 %collective-permute-start.21 = (bf16[384,640]{1,0:T(8,128)(2,1)S(1)}, bf16[384,640]{1,0:T(8,128)(2,1)S(1)}, u32[]{:S(2)}, u32[]{:S(2)}) collective-permute-start(bf16[384,640]{1,0:T(8,128)(2,1)S(1)} %collective-permute-done.20.refs_2_), channel_id=1, source_target_pairs={{0,4},{1,5},{2,6},{3,7},{4,0},{5,1},{6,2},{7,3},{8,12},{9,13},{10,... | collective-permute-start | bytes 1474568 | tf_op jit(solution)/shard_map/ppermute | solution.py:43
  116.3 6.7 %collective-permute-start.19 = (bf16[384,640]{1,0:T(8,128)(2,1)S(1)}, bf16[384,640]{1,0:T(8,128)(2,1)S(1)}, u32[]{:S(2)}, u32[]{:S(2)}) collective-permute-start(bf16[384,640]{1,0:T(8,128)(2,1)S(1)} %collective-permute-done.18.refs_1_), channel_id=1, source_target_pairs={{0,4},{1,5},{2,6},{3,7},{4,0},{5,1},{6,2},{7,3},{8,12},{9,13},{10,... | collective-permute-start | bytes 1474568 | tf_op jit(solution)/shard_map/ppermute | solution.py:43

commit v5 on v4

--- a/solution.py
+++ b/solution.py
@@ -70,28 +70,28 @@
     return core, jnp.where(core == 0, a, b), jnp.where(core == 0, b, a)
 
 
-def pack_kernel(dev, act, own_0, own_1, own_2, own_3, diagonal, rest, sem):
+def pack_kernel(dev, act, *refs):
+    outs, sem = refs[:-1], refs[-1]
     core, mine, across = here(dev)
     t = dev[0] % 4
     copies = []
-    for side, outs in (
-        (1, (rest.at[0], rest.at[1], rest.at[2], diagonal)),
-        (0, (own_0, own_1, own_2, own_3)),
-    ):
-        first = jnp.where(core == side, t ^ 1, 3 - t)
-        second = jnp.where(core == side, 3 - t, t ^ 1)
-        for flip, out in enumerate(outs):
-            place = (across if side else mine) ^ flip
-            for rank, slab in enumerate((t, second, first, t ^ 2)):
-                start = pl.multiple_of((2 * slab + place % 2) * BLOCK, TILE)
-                copies.append(
-                    pltpu.make_async_copy(
-                        act.at[core ^ side, place // 2, :, pl.ds(start, BLOCK)],
-                        out.at[rank],
-                        sem.at[len(copies)],
+    for half in range(2):
+        *own, sent = outs[(RING + 1) * half : (RING + 1) * (half + 1)]
+        for side in (1, 0):
+            first = jnp.where(core == side, t ^ 1, 3 - t)
+            second = jnp.where(core == side, 3 - t, t ^ 1)
+            for flip in range(RING):
+                place = (across if side else mine) ^ flip
+                for rank, slab in enumerate((t, second) if half else (first, t ^ 2)):
+                    start = pl.multiple_of((2 * slab + place % 2) * BLOCK, TILE)
+                    copies.append(
+                        pltpu.make_async_copy(
+                            act.at[core ^ side, place // 2, :, pl.ds(start, BLOCK)],
+                            (sent.at[flip] if side else own[flip]).at[rank],
+                            sem.at[len(copies)],
+                        )
                     )
-                )
-                copies[-1].start()
+                    copies[-1].start()
     for copy in copies:
         copy.wait()
 
@@ -100,7 +100,7 @@
     ins, outs, tri = refs[: 2 * RING], refs[2 * RING : 3 * RING], refs[3 * RING]
     ins = [*ins[:-1], ins[-1].at[0]]
     across = here(dev)[2]
-    for slab in range(SLABS):
+    for slab in range(2):
 
         def product(low, high):
             return lax.dot_general(
@@ -128,21 +128,27 @@
     core, place, across = here(dev)
     for flip in range(RING):
         start = pl.multiple_of((across ^ flip) * CHUNK, 32)
-        total[pl.ds(start, CHUNK), :] = ins[3 - flip][...].astype(jnp.float32)
+        total[pl.ds(start, CHUNK), :] = ins[3 - flip][...]
     steps = newton_steps[core, place // 2, 2 * t + place % 2]
-    for i, (row, col) in enumerate(PANELS):
-        low = TILE * i
-        panel = total[row : row + TILE, col : col + BLOCK - low]
-        mixed[low : low + TILE, low:] = panel
-        if i < 4:
-            mixed[low + TILE :, low : low + TILE] = panel[:, TILE:].T
     eye = (
         lax.broadcasted_iota(jnp.int32, (BLOCK, BLOCK), 0)
         == lax.broadcasted_iota(jnp.int32, (BLOCK, BLOCK), 1)
     ).astype(jnp.float32)
-    factor = mixed[...] * (1.0 / tokens_all) + DAMPING * eye
-    norm_scale = jnp.sqrt(jnp.sum(factor * factor))
-    mixed[...] = factor / norm_scale
+    squares = jnp.zeros((TILE, TILE), jnp.float32)
+    for i, (row, col) in enumerate(PANELS):
+        low = TILE * i
+        panel = total[row : row + TILE, col : col + BLOCK - low]
+        for j in range(i, 5):
+            tile = panel[:, TILE * (j - i) : TILE * (j - i + 1)].astype(jnp.float32)
+            tile = tile * (1.0 / tokens_all)
+            if i == j:
+                tile = tile + DAMPING * eye[:TILE, :TILE]
+            mixed[low : low + TILE, TILE * j : TILE * (j + 1)] = tile
+            squares = squares + (1.0 if i == j else 2.0) * tile * tile
+            if i != j:
+                mixed[TILE * j : TILE * (j + 1), low : low + TILE] = tile.T
+    norm_scale = jnp.sqrt(jnp.sum(squares))
+    scale = 1.0 / norm_scale
 
     def dot(rows):
         return jnp.dot(halves[0:rows, :], halves[0:BLOCK, :], preferred_element_type=jnp.float32)
@@ -150,10 +156,11 @@
     def last():
         return jnp.dot(halves[BLOCK:, :], halves[0:BLOCK, :], preferred_element_type=jnp.float32)
 
-    gap[...] = mixed[...]
-    halves[0:BLOCK, :] = mixed[...].astype(jnp.bfloat16)
-    halves[BLOCK:, :] = mixed[...].astype(jnp.bfloat16)
-    mixed[...] = 2.0 * mixed[...] - dot(BLOCK)
+    start = mixed[...] * scale
+    gap[...] = start
+    halves[0:BLOCK, :] = start.astype(jnp.bfloat16)
+    halves[BLOCK:, :] = start.astype(jnp.bfloat16)
+    mixed[...] = 2.0 * gap[...] - dot(BLOCK)
     for turn in range(1, 4):
         halves[0:BLOCK, :] = mixed[...].astype(jnp.bfloat16)
         products = dot(2 * BLOCK) if turn < 3 else None
@@ -164,7 +171,6 @@
             mixed[...] = 2.0 * mixed[...] - products[0:BLOCK]
             halves[BLOCK:, :] = gap[...].astype(jnp.bfloat16)
     reach = jnp.where(steps <= 1, 2.0, jnp.where(steps == 2, 4.0, jnp.where(steps == 3, 8.0, 16.0)))
-    scale = 1.0 / norm_scale
     for i, (row, col) in enumerate(PANELS):
         low = TILE * i
         value = (reach * eye[low : low + TILE, low:] - gap[low : low + TILE, low:]) * scale
@@ -221,41 +227,42 @@
     def shape(*dims):
         return jax.ShapeDtypeStruct(dims, half)
 
+    def wide(array):
+        return array.astype(jnp.float32)
+
     def over_square(parts, of_places):
         moved = {flip: in_square(parts[flip], flip, of_places) for flip in (3, 2, 1)}
         return [parts[0]] + [moved[flip] for flip in (1, 2, 3)]
 
-    part = (SLABS, rows, BLOCK)
-    *own, diagonal, rest = pl.pallas_call(
+    part = (2, rows, BLOCK)
+    packed = pl.pallas_call(
         pack_kernel,
-        out_shape=[shape(*part)] * (RING + 1) + [shape(3, *part)],
+        out_shape=([shape(*part)] * RING + [shape(RING, *part)]) * 2,
         in_specs=[SMEM, ANY],
-        out_specs=[ANY] * (RING + 2),
-        scratch_shapes=[pltpu.SemaphoreType.DMA((2 * RING * SLABS,))],
+        out_specs=[ANY] * (2 * RING + 2),
+        scratch_shapes=[pltpu.SemaphoreType.DMA((4 * RING * 2,))],
         compiler_params=pltpu.CompilerParams(vmem_limit_bytes=48 * 1024 * 1024),
         name="pack",
     )(dev, activations)
-    own = over_square(own, True)
-    diagonal, rest = to_other_core(diagonal), to_other_core(rest)
-    diagonal = in_square(diagonal, 3, True)
-    others = [in_square(rest[flip], flip, True) for flip in (2, 1)]
-
-    chunks = pl.pallas_call(
-        gram_kernel,
-        out_shape=[shape(SLABS, CHUNK, BLOCK)] * RING,
-        in_specs=[SMEM] + [VMEM] * (2 * RING),
-        out_specs=[VMEM] * RING,
-        scratch_shapes=[pltpu.VMEM((PACK, BLOCK), jnp.float32)],
-        compiler_params=PARAMS,
-        name="gram",
-    )(dev, *own[::-1], diagonal, *others, rest)
-    chunks = over_square(chunks, False)
-
-    def wide(array):
-        return array.astype(jnp.float32)
-
-    sums = sum(wide(chunk) for chunk in chunks[::-1])
-    sums = sums[0:2] + wide(to_slab(sums[2:4].astype(half), 0))
+
+    def factors(own, sent):
+        received = to_other_core(sent)
+        own = over_square(own, True)
+        others = [in_square(received[flip], flip, True) for flip in (3, 2, 1)]
+        chunks = pl.pallas_call(
+            gram_kernel,
+            out_shape=[shape(2, CHUNK, BLOCK)] * RING,
+            in_specs=[SMEM] + [VMEM] * (2 * RING),
+            out_specs=[VMEM] * RING,
+            scratch_shapes=[pltpu.VMEM((PACK, BLOCK), jnp.float32)],
+            compiler_params=PARAMS,
+            name="gram",
+        )(dev, *own[::-1], *others, received)
+        chunks = over_square(chunks, False)
+        return sum(wide(chunk) for chunk in chunks[::-1])
+
+    leaving = to_slab(factors(packed[:RING], packed[RING]).astype(half), 0)
+    sums = factors(packed[RING + 1 : -1], packed[-1]) + wide(leaving)
     sums = sums[0] + wide(to_slab(sums[1].astype(half), 1))
     sums = sums + wide(to_z_neighbour(sums.astype(half)))
     members = over_square([sums.astype(half)] * RING, False)
@@ -266,7 +273,7 @@
         in_specs=[SMEM, SMEM] + [VMEM] * RING,
         out_specs=VMEM,
         scratch_shapes=[
-            pltpu.VMEM((PACK, BLOCK), jnp.float32),
+            pltpu.VMEM((PACK, BLOCK), half),
             pltpu.VMEM((BLOCK, BLOCK), jnp.float32),
             pltpu.VMEM((BLOCK, BLOCK), jnp.float32),
             pltpu.VMEM((2 * BLOCK, BLOCK), half),

time: 127 us -> 116 us (0.913)
  waiting for transfers between devices: 54.2 us -> 30.6 us
  starting transfers between devices: 51.6 us -> 64 us
    ppermute x24 -> x33, waiting for transfers between devices: 54.2 us -> 30.6 us  [move(): return lax.ppermute(array, AXES, pairs)]
    ppermute x24 -> x33, starting transfers between devices: 51.6 us -> 64 us  [move(): return lax.ppermute(array, AXES, pairs)]
    pallas_call x2 -> x3, Pallas kernels: 6.36 us -> 6.57 us  [the longest x2 3.59 us: factors(): pl.pallas_call(gram_kernel, out_shape=[shape(2, CHUNK, BLOCK)] * RING, in...]
  transfers between devices with their start and end apart: 24 -> 33, of which waited for: 14 -> 12; matrix products, arithmetic and copies ran while one was open for 0% -> 0% of each run, Pallas kernels for 3% -> 6%
where the time goes in v5:
time: 116 us
  starting transfers between devices  64 us (55%)
  waiting for transfers between devices  30.6 us (26%)
  Pallas kernels  19.3 us (17%)
    ppermute x33, starting transfers between devices, move(): return lax.ppermute(array, AXES, pairs)  64 us
    ppermute x33, waiting for transfers between devices, move(): return lax.ppermute(array, AXES, pairs)  30.6 us
    pallas_call x2, Pallas kernels, apply(): pl.pallas_call(functools.partial(apply_kernel, side), out_shape=[shape(*d...  6.83 us
    pallas_call x1, Pallas kernels, local(): pl.pallas_call(functools.partial(newton_kernel, tokens_all), out_shape=sh...  5.9 us
    pallas_call x2, Pallas kernels, factors(): pl.pallas_call(gram_kernel, out_shape=[shape(2, CHUNK, BLOCK)] * RING, in...  3.59 us
    pallas_call x1, Pallas kernels, local(): pl.pallas_call(pack_kernel, out_shape=([shape(*part)] * RING + [shape(RIN...  2.97 us
  transfers between devices with their start and end apart: 33, of which 12 were waited for; matrix products, arithmetic and copies ran while one was open for 0% of the time, Pallas kernels for 6%

profile of v5, /device:TPU:1, one launch (start us, length us, event | category | flops | bytes accessed | tf_op | source)
XLA Modules:
  0.0 115.6 jit_solution(2622226528497310073)
XLA Ops:
  0.6 3.0 %pack.1 = (bf16[2,128,640]{2,1,0:T(8,128)(2,1)S(1)}, bf16[2,128,640]{2,1,0:T(8,128)(2,1)S(1)}, bf16[2,128,640]{2,1,0:T(8,128)(2,1)S(1)}, bf16[2,128,640]{2,1,0:T...) custom-call(s32[1]{0:T(128)} %bitcast.dev, ...), custom_call_target="tpu_custom_call" | custom-call | tf_op jit(solution)/shard_map/pack/pallas_call | solution.py:238
  3.6 3.3 %collective-permute-start.13 = (bf16[4,2,128,640]{3,2,1,0:T(8,128)(2,1)S(1)}, bf16[4,2,128,640]{3,2,1,0:T(8,128)(2,1)S(1)}, u32[]{:S(2)}, u32[]{:S(2)}) collective-permute-start(bf16[4,2,128,640]{3,2,1,0:T(8,128)(2,1)S(1)} %get-tuple-element.35), channel_id=1, source_target_pairs={{0,4},{1,5},{2,6},{3,7},{4,0},{5,1},{6,2},{7,3},{8,12},{9,13},{10,... | collective-permute-start | bytes 3932168 | tf_op jit(solution)/shard_map/ppermute | solution.py:43
  6.9 0.1 collective-permute-start.3
  7.0 3.2 %collective-permute-start = (bf16[2,128,640]{2,1,0:T(8,128)(2,1)S(1)}, bf16[2,128,640]{2,1,0:T(8,128)(2,1)S(1)}, u32[]{:S(2)}, u32[]{:S(2)}) collective-permute-start(bf16[2,128,640]{2,1,0:T(8,128)(2,1)S(1)} %get-tuple-element.22), channel_id=1, source_target_pairs={{0,40},{1,41},{2,42},{3,43},{4,124},{5,125},{6,126},{7,127},{8,32}... | collective-permute-start | bytes 983048 | tf_op jit(solution)/shard_map/ppermute | solution.py:43
  10.2 1.6 %collective-permute-start.10 = (bf16[2,128,640]{2,1,0:T(8,128)(2,1)S(1)}, bf16[2,128,640]{2,1,0:T(8,128)(2,1)S(1)}, u32[]{:S(2)}, u32[]{:S(2)}) collective-permute-start(bf16[2,128,640]{2,1,0:T(8,128)(2,1)S(1)} %get-tuple-element.31), channel_id=1, source_target_pairs={{0,40},{1,41},{2,42},{3,43},{4,124},{5,125},{6,126},{7,127},{8,32}... | collective-permute-start | bytes 983048 | tf_op jit(solution)/shard_map/ppermute | solution.py:43
  11.8 0.7 collective-permute-start.11
  12.6 0.0 collective-permute-done.13.refs_7_
  12.6 2.7 %collective-permute-start.12 = (bf16[2,128,640]{2,1,0:T(8,128)(2,1)S(1)}, bf16[2,128,640]{2,1,0:T(8,128)(2,1)S(1)}, u32[]{:S(2)}, u32[]{:S(2)}) collective-permute-start(bf16[2,128,640]{2,1,0:T(8,128)(2,1)S(1)} %get-tuple-element.33), channel_id=1, source_target_pairs={{0,8},{1,9},{2,10},{3,11},{4,28},{5,29},{6,30},{7,31},{8,0},{9,1},... | collective-permute-start | bytes 983048 | tf_op jit(solution)/shard_map/ppermute | solution.py:43
  15.3 0.1 slice_bitcast_fusion
  15.4 0.9 collective-permute-done.refs_0_
  16.3 1.0 collective-permute-start.16
  17.3 2.6 %collective-permute-done.10.refs_0_ = bf16[2,128,640]{2,1,0:T(8,128)(2,1)S(1)} collective-permute-done((bf16[2,128,640]{2,1,0:T(8,128)(2,1)S(1)}, bf16[2,128,640]{2,1,0:T(8,128)(2,1)S(1)}, u32[]{:S(2)}, u32[]{:S(2)}) %collective-permute-start.10) | collective-permute-done | bytes 327712 | tf_op jit(solution)/shard_map/ppermute | solution.py:43
  19.9 0.7 collective-permute-start.15
  20.6 2.6 %collective-permute-start.14 = (bf16[2,128,640]{2,1,0:T(8,128)(2,1)S(1)}, bf16[2,128,640]{2,1,0:T(8,128)(2,1)S(1)}, u32[]{:S(2)}, u32[]{:S(2)}) collective-permute-start(bf16[2,128,640]{2,1,0:T(8,128)(2,1)S(1)} %get-tuple-element.47), channel_id=1, source_target_pairs={{0,40},{1,41},{2,42},{3,43},{4,124},{5,125},{6,126},{7,127},{8,32}... | collective-permute-start | bytes 983048 | tf_op jit(solution)/shard_map/ppermute | solution.py:43
  23.3 0.1 slice_bitcast_fusion.3
  23.4 0.0 collective-permute-done.11.refs_1_
  23.4 2.6 %collective-permute-start.1 = (bf16[2,128,640]{2,1,0:T(8,128)(2,1)S(1)}, bf16[2,128,640]{2,1,0:T(8,128)(2,1)S(1)}, u32[]{:S(2)}, u32[]{:S(2)}) collective-permute-start(bf16[2,128,640]{2,1,0:T(8,128)(2,1)S(1)} %get-tuple-element.23), channel_id=1, source_target_pairs={{0,32},{1,33},{2,34},{3,35},{4,100},{5,101},{6,102},{7,103},{8,40}... | collective-permute-start | bytes 983048 | tf_op jit(solution)/shard_map/ppermute | solution.py:43
  26.0 0.0 collective-permute-done.12.refs_2_
  26.0 0.0 collective-permute-start.2
  26.0 1.0 collective-permute-done.16.refs_6_
  27.0 1.7 %collective-permute-start.6 = (bf16[2,128,640]{2,1,0:T(8,128)(2,1)S(1)}, bf16[2,128,640]{2,1,0:T(8,128)(2,1)S(1)}, u32[]{:S(2)}, u32[]{:S(2)}) collective-permute-start(bf16[2,128,640]{2,1,0:T(8,128)(2,1)S(1)} %get-tuple-element.42), channel_id=1, source_target_pairs={{0,8},{1,9},{2,10},{3,11},{4,28},{5,29},{6,30},{7,31},{8,0},{9,1},... | collective-permute-start | bytes 983048 | tf_op jit(solution)/shard_map/ppermute | solution.py:43
  28.7 0.0 collective-permute-done.15.refs_5_
  28.7 1.8 %collective-permute-start.5 = (bf16[2,128,640]{2,1,0:T(8,128)(2,1)S(1)}, bf16[2,128,640]{2,1,0:T(8,128)(2,1)S(1)}, u32[]{:S(2)}, u32[]{:S(2)}) collective-permute-start(bf16[2,128,640]{2,1,0:T(8,128)(2,1)S(1)} %get-tuple-element.43), channel_id=1, source_target_pairs={{0,32},{1,33},{2,34},{3,35},{4,100},{5,101},{6,102},{7,103},{8,40}... | collective-permute-start | bytes 983048 | tf_op jit(solution)/shard_map/ppermute | solution.py:43
  30.4 0.9 collective-permute-done.14.refs_4_
  31.4 2.3 %collective-permute-start.4 = (bf16[2,128,640]{2,1,0:T(8,128)(2,1)S(1)}, bf16[2,128,640]{2,1,0:T(8,128)(2,1)S(1)}, u32[]{:S(2)}, u32[]{:S(2)}) collective-permute-start(bf16[2,128,640]{2,1,0:T(8,128)(2,1)S(1)} %get-tuple-element.44), channel_id=1, source_target_pairs={{0,40},{1,41},{2,42},{3,43},{4,124},{5,125},{6,126},{7,127},{8,32}... | collective-permute-start | bytes 983048 | tf_op jit(solution)/shard_map/ppermute | solution.py:43
  33.7 1.8 %gram.3 = (bf16[2,96,640]{2,1,0:T(8,128)(2,1)S(1)}, bf16[2,96,640]{2,1,0:T(8,128)(2,1)S(1)}, bf16[2,96,640]{2,1,0:T(8,128)(2,1)S(1)}, bf16[2,96,640]{2,1,0:T(8,128)(2,1)S(1)}) custom-call(s32[1]{0:T(128)} %bitcast.dev, bf16[2,128,640]{2,1,0:T(8,128)(2,1)S(1)} %collective-permute-done.10.refs_0_, bf16[2,128,640]{2,1,0:T(8,128)(2,1)S(1)} %collective-permute-done.11.refs_1_, ...), custom_call_target="tpu_custom_call" | custom-call | tf_op jit(solution)/shard_map/gram/pallas_call | solution.py:252
  35.5 0.0 collective-permute-done.1.refs_1_
  35.5 0.1 collective-permute-start.17
  35.6 0.1 collective-permute-start.18
  35.7 2.7 %collective-permute-done.6.refs_6_ = bf16[2,128,640]{2,1,0:T(8,128)(2,1)S(1)} collective-permute-done((bf16[2,128,640]{2,1,0:T(8,128)(2,1)S(1)}, bf16[2,128,640]{2,1,0:T(8,128)(2,1)S(1)}, u32[]{:S(2)}, u32[]{:S(2)}) %collective-permute-start.6) | collective-permute-done | bytes 327712 | tf_op jit(solution)/shard_map/ppermute | solution.py:43
  38.4 0.0 collective-permute-start.19
  38.4 0.0 collective-permute-done.5.refs_5_
  38.4 6.0 %collective-permute-done.4.refs_4_ = bf16[2,128,640]{2,1,0:T(8,128)(2,1)S(1)} collective-permute-done((bf16[2,128,640]{2,1,0:T(8,128)(2,1)S(1)}, bf16[2,128,640]{2,1,0:T(8,128)(2,1)S(1)}, u32[]{:S(2)}, u32[]{:S(2)}) %collective-permute-start.4) | collective-permute-done | bytes 327712 | tf_op jit(solution)/shard_map/ppermute | solution.py:43
  44.4 1.8 %gram.2 = (bf16[2,96,640]{2,1,0:T(8,128)(2,1)S(1)}, bf16[2,96,640]{2,1,0:T(8,128)(2,1)S(1)}, bf16[2,96,640]{2,1,0:T(8,128)(2,1)S(1)}, bf16[2,96,640]{2,1,0:T(8,128)(2,1)S(1)}) custom-call(s32[1]{0:T(128)} %bitcast.dev, bf16[2,128,640]{2,1,0:T(8,128)(2,1)S(1)} %collective-permute-done.refs_0_, bf16[2,128,640]{2,1,0:T(8,128)(2,1)S(1)} %collective-permute-done.1.refs_1_, ...), custom_call_target="tpu_custom_call" | custom-call | tf_op jit(solution)/shard_map/gram/pallas_call | solution.py:252
  46.2 0.1 collective-permute-start.7
  46.3 0.1 collective-permute-start.8
  46.5 2.5 %collective-permute-start.9 = (bf16[2,96,640]{2,1,0:T(8,128)(2,1)S(1)}, bf16[2,96,640]{2,1,0:T(8,128)(2,1)S(1)}, u32[]{:S(2)}, u32[]{:S(2)}) collective-permute-start(bf16[2,96,640]{2,1,0:T(8,128)(2,1)S(1)} %get-tuple-element.29), channel_id=1, source_target_pairs={{0,24},{1,25},{2,26},{3,27},{4,12},{5,13},{6,14},{7,15},{8,16},{9,... | collective-permute-start | bytes 737288 | tf_op jit(solution)/shard_map/ppermute | solution.py:43
  49.0 0.0 collective-permute-done.18
  49.0 0.0 collective-permute-done.19
  49.0 0.1 add_convert_fusion
  49.1 6.7 %collective-permute-start.20 = (bf16[2,96,640]{2,1,0:T(8,128)(2,1)S(1)}, bf16[2,96,640]{2,1,0:T(8,128)(2,1)S(1)}, u32[]{:S(2)}, u32[]{:S(2)}) collective-permute-start(bf16[2,96,640]{2,1,0:T(8,128)(2,1)S(1)} %add_convert_fusion), channel_id=1, source_target_pairs={{0,1},{1,0},{2,3},{3,2},{4,7},{5,6},{6,5},{7,4},{8,9},{9,8},{10,11... | collective-permute-start | bytes 737288 | tf_op jit(solution)/shard_map/ppermute | solution.py:43
  55.9 5.8 %collective-permute-done.20 = bf16[2,96,640]{2,1,0:T(8,128)(2,1)S(1)} collective-permute-done((bf16[2,96,640]{2,1,0:T(8,128)(2,1)S(1)}, bf16[2,96,640]{2,1,0:T(8,128)(2,1)S(1)}, u32[]{:S(2)}, u32[]{:S(2)}) %collective-permute-start.20) | collective-permute-done | bytes 245792 | tf_op jit(solution)/shard_map/ppermute | solution.py:43
  61.6 0.1 convert_add_fusion
  61.8 0.0 copy-start
  61.8 1.7 %collective-permute-start.21 = (bf16[96,640]{1,0:T(8,128)(2,1)S(1)}, bf16[96,640]{1,0:T(8,128)(2,1)S(1)}, u32[]{:S(2)}, u32[]{:S(2)}) collective-permute-start(bf16[96,640]{1,0:T(8,128)(2,1)S(1)} %fusion.2), channel_id=1, source_target_pairs={{0,3},{1,2},{2,1},{3,0},{4,5},{5,4},{6,7},{7,6},{8,11},{9,10},{10,... | collective-permute-start | bytes 368648 | tf_op jit(solution)/shard_map/ppermute | solution.py:43
  63.5 3.4 %collective-permute-done.21 = bf16[96,640]{1,0:T(8,128)(2,1)S(1)} collective-permute-done((bf16[96,640]{1,0:T(8,128)(2,1)S(1)}, bf16[96,640]{1,0:T(8,128)(2,1)S(1)}, u32[]{:S(2)}, u32[]{:S(2)}) %collective-permute-start.21) | collective-permute-done | bytes 122912 | tf_op jit(solution)/shard_map/ppermute | solution.py:43
  66.9 1.7 %collective-permute-start.22 = (bf16[96,640]{1,0:T(8,128)(2,1)S(1)}, bf16[96,640]{1,0:T(8,128)(2,1)S(1)}, u32[]{:S(2)}, u32[]{:S(2)}) collective-permute-start(bf16[96,640]{1,0:T(8,128)(2,1)S(1)} %fusion.1), channel_id=1, source_target_pairs={{0,128},{1,129},{2,130},{3,131},{4,132},{5,133},{6,134},{7,135},{8... | collective-permute-start | bytes 368648 | tf_op jit(solution)/shard_map/ppermute | solution.py:43
  68.6 3.7 %collective-permute-done.22 = bf16[96,640]{1,0:T(8,128)(2,1)S(1)} collective-permute-done((bf16[96,640]{1,0:T(8,128)(2,1)S(1)}, bf16[96,640]{1,0:T(8,128)(2,1)S(1)}, u32[]{:S(2)}, u32[]{:S(2)}) %collective-permute-start.22) | collective-permute-done | bytes 122912 | tf_op jit(solution)/shard_map/ppermute | solution.py:43
  72.4 0.1 collective-permute-start.25
  72.5 0.1 collective-permute-start.24
  72.6 2.5 %collective-permute-start.23 = (bf16[96,640]{1,0:T(8,128)(2,1)S(1)}, bf16[96,640]{1,0:T(8,128)(2,1)S(1)}, u32[]{:S(2)}, u32[]{:S(2)}) collective-permute-start(bf16[96,640]{1,0:T(8,128)(2,1)S(1)} %add_convert_fusion.1.refs_3_), channel_id=1, source_target_pairs={{0,120},{1,121},{2,122},{3,123},{4,44},{5,45},{6,46},{7,47},{8,112... | collective-permute-start | bytes 368648 | tf_op jit(solution)/shard_map/ppermute | solution.py:43
  75.1 1.1 collective-permute-done.25.refs_2_
  76.2 0.1 collective-permute-done.24.refs_1_
  76.3 2.4 %collective-permute-done.23.refs_0_ = bf16[96,640]{1,0:T(8,128)(2,1)S(1)} collective-permute-done((bf16[96,640]{1,0:T(8,128)(2,1)S(1)}, bf16[96,640]{1,0:T(8,128)(2,1)S(1)}, u32[]{:S(2)}, u32[]{:S(2)}) %collective-permute-start.23) | collective-permute-done | bytes 122912 | tf_op jit(solution)/shard_map/ppermute | solution.py:43
  78.7 5.9 %newton.1.refs_0_ = bf16[384,640]{1,0:T(8,128)(2,1)S(1)} custom-call(s32[1]{0:T(128)} %bitcast.dev, s32[2,2,8]{2,1,0:T(2,128)S(1)} %copy-done.2, bf16[96,640]{1,0:T(8,128)(2,1)S(1)} %collective-permute-done.23.refs_0_, bf16[96,640]{1,0:T(8,128)(2,1)S(1)} %collective-permute-done.24.refs_1_, bf16[96,640]{1,0:T(8,128)(2,1)S(1)} %collective-permute-done.25.refs_2_, ...), custom_call_target="tpu_custom_call" | custom-call | tf_op jit(solution)/shard_map/newton/pallas_call | solution.py:270
  84.6 1.1 collective-permute-start.31
  85.6 2.1 %collective-permute-start.29 = (bf16[384,640]{1,0:T(8,128)(2,1)S(1)}, bf16[384,640]{1,0:T(8,128)(2,1)S(1)}, u32[]{:S(2)}, u32[]{:S(2)}) collective-permute-start(bf16[384,640]{1,0:T(8,128)(2,1)S(1)} %newton.1.refs_0_), channel_id=1, source_target_pairs={{0,32},{1,33},{2,34},{3,35},{4,100},{5,101},{6,102},{7,103},{8,40}... | collective-permute-start | bytes 1474568 | tf_op jit(solution)/shard_map/ppermute | solution.py:43
  87.7 2.3 %collective-permute-start.27 = (bf16[384,640]{1,0:T(8,128)(2,1)S(1)}, bf16[384,640]{1,0:T(8,128)(2,1)S(1)}, u32[]{:S(2)}, u32[]{:S(2)}) collective-permute-start(bf16[384,640]{1,0:T(8,128)(2,1)S(1)} %newton.1.refs_0_), channel_id=1, source_target_pairs={{0,8},{1,9},{2,10},{3,11},{4,28},{5,29},{6,30},{7,31},{8,0},{9,1},... | collective-permute-start | bytes 1474568 | tf_op jit(solution)/shard_map/ppermute | solution.py:43
  90.0 6.6 %collective-permute-start.26 = (bf16[384,640]{1,0:T(8,128)(2,1)S(1)}, bf16[384,640]{1,0:T(8,128)(2,1)S(1)}, u32[]{:S(2)}, u32[]{:S(2)}) collective-permute-start(bf16[384,640]{1,0:T(8,128)(2,1)S(1)} %newton.1.refs_0_), channel_id=1, source_target_pairs={{0,4},{1,5},{2,6},{3,7},{4,0},{5,1},{6,2},{7,3},{8,12},{9,13},{10,... | collective-permute-start | bytes 1474568 | tf_op jit(solution)/shard_map/ppermute | solution.py:43
  96.7 6.3 %collective-permute-start.32 = (bf16[384,640]{1,0:T(8,128)(2,1)S(1)}, bf16[384,640]{1,0:T(8,128)(2,1)S(1)}, u32[]{:S(2)}, u32[]{:S(2)}) collective-permute-start(bf16[384,640]{1,0:T(8,128)(2,1)S(1)} %collective-permute-done.31.refs_3_), channel_id=1, source_target_pairs={{0,4},{1,5},{2,6},{3,7},{4,0},{5,1},{6,2},{7,3},{8,12},{9,13},{10,... | collective-permute-start | bytes 1474568 | tf_op jit(solution)/shard_map/ppermute | solution.py:43
  103.0 5.5 %collective-permute-start.30 = (bf16[384,640]{1,0:T(8,128)(2,1)S(1)}, bf16[384,640]{1,0:T(8,128)(2,1)S(1)}, u32[]{:S(2)}, u32[]{:S(2)}) collective-permute-start(bf16[384,640]{1,0:T(8,128)(2,1)S(1)} %collective-permute-done.29.refs_2_), channel_id=1, source_target_pairs={{0,4},{1,5},{2,6},{3,7},{4,0},{5,1},{6,2},{7,3},{8,12},{9,13},{10,... | collective-permute-start | bytes 1474568 | tf_op jit(solution)/shard_map/ppermute | solution.py:43
  108.5 0.0 collective-permute-start.28
  108.5 3.4 %apply.2 = (bf16[2,240,1280]{2,1,0:T(8,128)(2,1)}, bf16[2,320,1280]{2,1,0:T(8,128)(2,1)}) custom-call(s32[1]{0:T(128)} %bitcast.dev, bf16[384,640]{1,0:T(8,128)(2,1)S(1)} %newton.1.refs_0_, bf16[384,640]{1,0:T(8,128)(2,1)S(1)} %collective-permute-done.27.refs_1_, bf16[384,640]{1,0:T(8,128)(2,1)S(1)} %collective-permute-done.29.refs_2_, ...), custom_call_target="tpu_custom_call" | custom-call | tf_op jit(solution)/shard_map/apply/pallas_call | solution.py:290
  112.0 3.4 %apply.3 = (bf16[2,240,1280]{2,1,0:T(8,128)(2,1)}, bf16[2,320,1280]{2,1,0:T(8,128)(2,1)}) custom-call(s32[1]{0:T(128)} %bitcast.dev, bf16[384,640]{1,0:T(8,128)(2,1)S(1)} %collective-permute-done.26.refs_0_, bf16[384,640]{1,0:T(8,128)(2,1)S(1)} %collective-permute-done.28.refs_1_, ...), custom_call_target="tpu_custom_call", output_to_operand_aliasing={{0}: (7, {}), {1}: (8, {})} | custom-call | tf_op jit(solution)/shard_map/apply/pallas_call | solution.py:290
  (21 shorter events, 0.1 us)
Async XLA Ops:
  3.6 9.0 %collective-permute-start.13 = (bf16[4,2,128,640]{3,2,1,0:T(8,128)(2,1)S(1)}, bf16[4,2,128,640]{3,2,1,0:T(8,128)(2,1)S(1)}, u32[]{:S(2)}, u32[]{:S(2)}) collective-permute-start(bf16[4,2,128,640]{3,2,1,0:T(8,128)(2,1)S(1)} %get-tuple-element.35), channel_id=1, source_target_pairs={{0,4},{1,5},{2,6},{3,7},{4,0},{5,1},{6,2},{7,3},{8,12},{9,13},{10,... | collective-permute-start | bytes 3932168 | tf_op jit(solution)/shard_map/ppermute | solution.py:43
  6.9 13.7 %collective-permute-start.3 = (bf16[4,2,128,640]{3,2,1,0:T(8,128)(2,1)S(1)}, bf16[4,2,128,640]{3,2,1,0:T(8,128)(2,1)S(1)}, u32[]{:S(2)}, u32[]{:S(2)}) collective-permute-start(bf16[4,2,128,640]{3,2,1,0:T(8,128)(2,1)S(1)} %get-tuple-element.26), channel_id=1, source_target_pairs={{0,4},{1,5},{2,6},{3,7},{4,0},{5,1},{6,2},{7,3},{8,12},{9,13},{10,... | collective-permute-start | bytes 3932168 | tf_op jit(solution)/shard_map/ppermute | solution.py:43
  7.0 9.2 %collective-permute-start = (bf16[2,128,640]{2,1,0:T(8,128)(2,1)S(1)}, bf16[2,128,640]{2,1,0:T(8,128)(2,1)S(1)}, u32[]{:S(2)}, u32[]{:S(2)}) collective-permute-start(bf16[2,128,640]{2,1,0:T(8,128)(2,1)S(1)} %get-tuple-element.22), channel_id=1, source_target_pairs={{0,40},{1,41},{2,42},{3,43},{4,124},{5,125},{6,126},{7,127},{8,32}... | collective-permute-start | bytes 983048 | tf_op jit(solution)/shard_map/ppermute | solution.py:43
  10.2 9.7 %collective-permute-start.10 = (bf16[2,128,640]{2,1,0:T(8,128)(2,1)S(1)}, bf16[2,128,640]{2,1,0:T(8,128)(2,1)S(1)}, u32[]{:S(2)}, u32[]{:S(2)}) collective-permute-start(bf16[2,128,640]{2,1,0:T(8,128)(2,1)S(1)} %get-tuple-element.31), channel_id=1, source_target_pairs={{0,40},{1,41},{2,42},{3,43},{4,124},{5,125},{6,126},{7,127},{8,32}... | collective-permute-start | bytes 983048 | tf_op jit(solution)/shard_map/ppermute | solution.py:43
  11.8 11.6 %collective-permute-start.11 = (bf16[2,128,640]{2,1,0:T(8,128)(2,1)S(1)}, bf16[2,128,640]{2,1,0:T(8,128)(2,1)S(1)}, u32[]{:S(2)}, u32[]{:S(2)}) collective-permute-start(bf16[2,128,640]{2,1,0:T(8,128)(2,1)S(1)} %get-tuple-element.32), channel_id=1, source_target_pairs={{0,32},{1,33},{2,34},{3,35},{4,100},{5,101},{6,102},{7,103},{8,40}... | collective-permute-start | bytes 983048 | tf_op jit(solution)/shard_map/ppermute | solution.py:43
  12.6 13.4 %collective-permute-start.12 = (bf16[2,128,640]{2,1,0:T(8,128)(2,1)S(1)}, bf16[2,128,640]{2,1,0:T(8,128)(2,1)S(1)}, u32[]{:S(2)}, u32[]{:S(2)}) collective-permute-start(bf16[2,128,640]{2,1,0:T(8,128)(2,1)S(1)} %get-tuple-element.33), channel_id=1, source_target_pairs={{0,8},{1,9},{2,10},{3,11},{4,28},{5,29},{6,30},{7,31},{8,0},{9,1},... | collective-permute-start | bytes 983048 | tf_op jit(solution)/shard_map/ppermute | solution.py:43
  16.3 10.7 %collective-permute-start.16 = (bf16[2,128,640]{2,1,0:T(8,128)(2,1)S(1)}, bf16[2,128,640]{2,1,0:T(8,128)(2,1)S(1)}, u32[]{:S(2)}, u32[]{:S(2)}) collective-permute-start(bf16[2,128,640]{2,1,0:T(8,128)(2,1)S(1)} %get-tuple-element.45), channel_id=1, source_target_pairs={{0,8},{1,9},{2,10},{3,11},{4,28},{5,29},{6,30},{7,31},{8,0},{9,1},... | collective-permute-start | bytes 983048 | tf_op jit(solution)/shard_map/ppermute | solution.py:43
  19.9 8.8 %collective-permute-start.15 = (bf16[2,128,640]{2,1,0:T(8,128)(2,1)S(1)}, bf16[2,128,640]{2,1,0:T(8,128)(2,1)S(1)}, u32[]{:S(2)}, u32[]{:S(2)}) collective-permute-start(bf16[2,128,640]{2,1,0:T(8,128)(2,1)S(1)} %get-tuple-element.46), channel_id=1, source_target_pairs={{0,32},{1,33},{2,34},{3,35},{4,100},{5,101},{6,102},{7,103},{8,40}... | collective-permute-start | bytes 983048 | tf_op jit(solution)/shard_map/ppermute | solution.py:43
  20.6 10.7 %collective-permute-start.14 = (bf16[2,128,640]{2,1,0:T(8,128)(2,1)S(1)}, bf16[2,128,640]{2,1,0:T(8,128)(2,1)S(1)}, u32[]{:S(2)}, u32[]{:S(2)}) collective-permute-start(bf16[2,128,640]{2,1,0:T(8,128)(2,1)S(1)} %get-tuple-element.47), channel_id=1, source_target_pairs={{0,40},{1,41},{2,42},{3,43},{4,124},{5,125},{6,126},{7,127},{8,32}... | collective-permute-start | bytes 983048 | tf_op jit(solution)/shard_map/ppermute | solution.py:43
  23.4 12.1 %collective-permute-start.1 = (bf16[2,128,640]{2,1,0:T(8,128)(2,1)S(1)}, bf16[2,128,640]{2,1,0:T(8,128)(2,1)S(1)}, u32[]{:S(2)}, u32[]{:S(2)}) collective-permute-start(bf16[2,128,640]{2,1,0:T(8,128)(2,1)S(1)} %get-tuple-element.23), channel_id=1, source_target_pairs={{0,32},{1,33},{2,34},{3,35},{4,100},{5,101},{6,102},{7,103},{8,40}... | collective-permute-start | bytes 983048 | tf_op jit(solution)/shard_map/ppermute | solution.py:43
  26.0 9.6 %collective-permute-start.2 = (bf16[2,128,640]{2,1,0:T(8,128)(2,1)S(1)}, bf16[2,128,640]{2,1,0:T(8,128)(2,1)S(1)}, u32[]{:S(2)}, u32[]{:S(2)}) collective-permute-start(bf16[2,128,640]{2,1,0:T(8,128)(2,1)S(1)} %get-tuple-element.24), channel_id=1, source_target_pairs={{0,8},{1,9},{2,10},{3,11},{4,28},{5,29},{6,30},{7,31},{8,0},{9,1},... | collective-permute-start | bytes 983048 | tf_op jit(solution)/shard_map/ppermute | solution.py:43
  27.0 11.5 %collective-permute-start.6 = (bf16[2,128,640]{2,1,0:T(8,128)(2,1)S(1)}, bf16[2,128,640]{2,1,0:T(8,128)(2,1)S(1)}, u32[]{:S(2)}, u32[]{:S(2)}) collective-permute-start(bf16[2,128,640]{2,1,0:T(8,128)(2,1)S(1)} %get-tuple-element.42), channel_id=1, source_target_pairs={{0,8},{1,9},{2,10},{3,11},{4,28},{5,29},{6,30},{7,31},{8,0},{9,1},... | collective-permute-start | bytes 983048 | tf_op jit(solution)/shard_map/ppermute | solution.py:43
  28.7 9.8 %collective-permute-start.5 = (bf16[2,128,640]{2,1,0:T(8,128)(2,1)S(1)}, bf16[2,128,640]{2,1,0:T(8,128)(2,1)S(1)}, u32[]{:S(2)}, u32[]{:S(2)}) collective-permute-start(bf16[2,128,640]{2,1,0:T(8,128)(2,1)S(1)} %get-tuple-element.43), channel_id=1, source_target_pairs={{0,32},{1,33},{2,34},{3,35},{4,100},{5,101},{6,102},{7,103},{8,40}... | collective-permute-start | bytes 983048 | tf_op jit(solution)/shard_map/ppermute | solution.py:43
  31.4 13.1 %collective-permute-start.4 = (bf16[2,128,640]{2,1,0:T(8,128)(2,1)S(1)}, bf16[2,128,640]{2,1,0:T(8,128)(2,1)S(1)}, u32[]{:S(2)}, u32[]{:S(2)}) collective-permute-start(bf16[2,128,640]{2,1,0:T(8,128)(2,1)S(1)} %get-tuple-element.44), channel_id=1, source_target_pairs={{0,40},{1,41},{2,42},{3,43},{4,124},{5,125},{6,126},{7,127},{8,32}... | collective-permute-start | bytes 983048 | tf_op jit(solution)/shard_map/ppermute | solution.py:43
  35.5 11.0 %collective-permute-start.17 = (bf16[2,96,640]{2,1,0:T(8,128)(2,1)S(1)}, bf16[2,96,640]{2,1,0:T(8,128)(2,1)S(1)}, u32[]{:S(2)}, u32[]{:S(2)}) collective-permute-start(bf16[2,96,640]{2,1,0:T(8,128)(2,1)S(1)} %get-tuple-element.36), channel_id=1, source_target_pairs={{0,120},{1,121},{2,122},{3,123},{4,44},{5,45},{6,46},{7,47},{8,112... | collective-permute-start | bytes 737288 | tf_op jit(solution)/shard_map/ppermute | solution.py:43
  35.6 13.4 %collective-permute-start.18 = (bf16[2,96,640]{2,1,0:T(8,128)(2,1)S(1)}, bf16[2,96,640]{2,1,0:T(8,128)(2,1)S(1)}, u32[]{:S(2)}, u32[]{:S(2)}) collective-permute-start(bf16[2,96,640]{2,1,0:T(8,128)(2,1)S(1)} %get-tuple-element.37), channel_id=1, source_target_pairs={{0,96},{1,97},{2,98},{3,99},{4,36},{5,37},{6,38},{7,39},{8,104},{9... | collective-permute-start | bytes 737288 | tf_op jit(solution)/shard_map/ppermute | solution.py:43
  38.4 10.6 %collective-permute-start.19 = (bf16[2,96,640]{2,1,0:T(8,128)(2,1)S(1)}, bf16[2,96,640]{2,1,0:T(8,128)(2,1)S(1)}, u32[]{:S(2)}, u32[]{:S(2)}) collective-permute-start(bf16[2,96,640]{2,1,0:T(8,128)(2,1)S(1)} %get-tuple-element.38), channel_id=1, source_target_pairs={{0,24},{1,25},{2,26},{3,27},{4,12},{5,13},{6,14},{7,15},{8,16},{9,... | collective-permute-start | bytes 737288 | tf_op jit(solution)/shard_map/ppermute | solution.py:43
  46.2 9.6 %collective-permute-start.7 = (bf16[2,96,640]{2,1,0:T(8,128)(2,1)S(1)}, bf16[2,96,640]{2,1,0:T(8,128)(2,1)S(1)}, u32[]{:S(2)}, u32[]{:S(2)}) collective-permute-start(bf16[2,96,640]{2,1,0:T(8,128)(2,1)S(1)} %get-tuple-element.27), channel_id=1, source_target_pairs={{0,120},{1,121},{2,122},{3,123},{4,44},{5,45},{6,46},{7,47},{8,112... | collective-permute-start | bytes 737288 | tf_op jit(solution)/shard_map/ppermute | solution.py:43
  46.3 9.5 %collective-permute-start.8 = (bf16[2,96,640]{2,1,0:T(8,128)(2,1)S(1)}, bf16[2,96,640]{2,1,0:T(8,128)(2,1)S(1)}, u32[]{:S(2)}, u32[]{:S(2)}) collective-permute-start(bf16[2,96,640]{2,1,0:T(8,128)(2,1)S(1)} %get-tuple-element.28), channel_id=1, source_target_pairs={{0,96},{1,97},{2,98},{3,99},{4,36},{5,37},{6,38},{7,39},{8,104},{9... | collective-permute-start | bytes 737288 | tf_op jit(solution)/shard_map/ppermute | solution.py:43
  46.5 9.4 %collective-permute-start.9 = (bf16[2,96,640]{2,1,0:T(8,128)(2,1)S(1)}, bf16[2,96,640]{2,1,0:T(8,128)(2,1)S(1)}, u32[]{:S(2)}, u32[]{:S(2)}) collective-permute-start(bf16[2,96,640]{2,1,0:T(8,128)(2,1)S(1)} %get-tuple-element.29), channel_id=1, source_target_pairs={{0,24},{1,25},{2,26},{3,27},{4,12},{5,13},{6,14},{7,15},{8,16},{9,... | collective-permute-start | bytes 737288 | tf_op jit(solution)/shard_map/ppermute | solution.py:43
  49.1 12.5 %collective-permute-start.20 = (bf16[2,96,640]{2,1,0:T(8,128)(2,1)S(1)}, bf16[2,96,640]{2,1,0:T(8,128)(2,1)S(1)}, u32[]{:S(2)}, u32[]{:S(2)}) collective-permute-start(bf16[2,96,640]{2,1,0:T(8,128)(2,1)S(1)} %add_convert_fusion), channel_id=1, source_target_pairs={{0,1},{1,0},{2,3},{3,2},{4,7},{5,6},{6,5},{7,4},{8,9},{9,8},{10,11... | collective-permute-start | bytes 737288 | tf_op jit(solution)/shard_map/ppermute | solution.py:43
  61.6 17.1 %copy-start.2 = (s32[2,2,8]{2,1,0:T(2,128)S(1)}, s32[2,2,8]{2,1,0:T(2,128)}, u32[]{:S(2)}) copy-start(s32[2,2,8]{2,1,0:T(2,128)} %newton_steps.1) | copy-start | bytes 388
  61.6 46.9 %copy-start.1 = (bf16[2,240,1280]{2,1,0:T(8,128)(2,1)S(1)}, bf16[2,240,1280]{2,1,0:T(8,128)(2,1)}, u32[]{:S(2)}) copy-start(bf16[2,240,1280]{2,1,0:T(8,128)(2,1)} %refs_4_.3) | copy-start | bytes 3686404
  61.8 46.7 %copy-start = (bf16[2,320,1280]{2,1,0:T(8,128)(2,1)S(1)}, bf16[2,320,1280]{2,1,0:T(8,128)(2,1)}, u32[]{:S(2)}) copy-start(bf16[2,320,1280]{2,1,0:T(8,128)(2,1)} %refs_5_.3) | copy-start | bytes 4915204
  61.8 5.1 %collective-permute-start.21 = (bf16[96,640]{1,0:T(8,128)(2,1)S(1)}, bf16[96,640]{1,0:T(8,128)(2,1)S(1)}, u32[]{:S(2)}, u32[]{:S(2)}) collective-permute-start(bf16[96,640]{1,0:T(8,128)(2,1)S(1)} %fusion.2), channel_id=1, source_target_pairs={{0,3},{1,2},{2,1},{3,0},{4,5},{5,4},{6,7},{7,6},{8,11},{9,10},{10,... | collective-permute-start | bytes 368648 | tf_op jit(solution)/shard_map/ppermute | solution.py:43
  66.9 5.4 %collective-permute-start.22 = (bf16[96,640]{1,0:T(8,128)(2,1)S(1)}, bf16[96,640]{1,0:T(8,128)(2,1)S(1)}, u32[]{:S(2)}, u32[]{:S(2)}) collective-permute-start(bf16[96,640]{1,0:T(8,128)(2,1)S(1)} %fusion.1), channel_id=1, source_target_pairs={{0,128},{1,129},{2,130},{3,131},{4,132},{5,133},{6,134},{7,135},{8... | collective-permute-start | bytes 368648 | tf_op jit(solution)/shard_map/ppermute | solution.py:43
  72.4 3.8 %collective-permute-start.25 = (bf16[96,640]{1,0:T(8,128)(2,1)S(1)}, bf16[96,640]{1,0:T(8,128)(2,1)S(1)}, u32[]{:S(2)}, u32[]{:S(2)}) collective-permute-start(bf16[96,640]{1,0:T(8,128)(2,1)S(1)} %add_convert_fusion.1.refs_3_), channel_id=1, source_target_pairs={{0,24},{1,25},{2,26},{3,27},{4,12},{5,13},{6,14},{7,15},{8,16},{9,... | collective-permute-start | bytes 368648 | tf_op jit(solution)/shard_map/ppermute | solution.py:43
  72.5 3.8 %collective-permute-start.24 = (bf16[96,640]{1,0:T(8,128)(2,1)S(1)}, bf16[96,640]{1,0:T(8,128)(2,1)S(1)}, u32[]{:S(2)}, u32[]{:S(2)}) collective-permute-start(bf16[96,640]{1,0:T(8,128)(2,1)S(1)} %add_convert_fusion.1.refs_3_), channel_id=1, source_target_pairs={{0,96},{1,97},{2,98},{3,99},{4,36},{5,37},{6,38},{7,39},{8,104},{9... | collective-permute-start | bytes 368648 | tf_op jit(solution)/shard_map/ppermute | solution.py:43
  72.6 6.1 %collective-permute-start.23 = (bf16[96,640]{1,0:T(8,128)(2,1)S(1)}, bf16[96,640]{1,0:T(8,128)(2,1)S(1)}, u32[]{:S(2)}, u32[]{:S(2)}) collective-permute-start(bf16[96,640]{1,0:T(8,128)(2,1)S(1)} %add_convert_fusion.1.refs_3_), channel_id=1, source_target_pairs={{0,120},{1,121},{2,122},{3,123},{4,44},{5,45},{6,46},{7,47},{8,112... | collective-permute-start | bytes 368648 | tf_op jit(solution)/shard_map/ppermute | solution.py:43
  84.6 12.1 %collective-permute-start.31 = (bf16[384,640]{1,0:T(8,128)(2,1)S(1)}, bf16[384,640]{1,0:T(8,128)(2,1)S(1)}, u32[]{:S(2)}, u32[]{:S(2)}) collective-permute-start(bf16[384,640]{1,0:T(8,128)(2,1)S(1)} %newton.1.refs_0_), channel_id=1, source_target_pairs={{0,40},{1,41},{2,42},{3,43},{4,124},{5,125},{6,126},{7,127},{8,32}... | collective-permute-start | bytes 1474568 | tf_op jit(solution)/shard_map/ppermute | solution.py:43
  85.6 17.4 %collective-permute-start.29 = (bf16[384,640]{1,0:T(8,128)(2,1)S(1)}, bf16[384,640]{1,0:T(8,128)(2,1)S(1)}, u32[]{:S(2)}, u32[]{:S(2)}) collective-permute-start(bf16[384,640]{1,0:T(8,128)(2,1)S(1)} %newton.1.refs_0_), channel_id=1, source_target_pairs={{0,32},{1,33},{2,34},{3,35},{4,100},{5,101},{6,102},{7,103},{8,40}... | collective-permute-start | bytes 1474568 | tf_op jit(solution)/shard_map/ppermute | solution.py:43
  87.7 20.8 %collective-permute-start.27 = (bf16[384,640]{1,0:T(8,128)(2,1)S(1)}, bf16[384,640]{1,0:T(8,128)(2,1)S(1)}, u32[]{:S(2)}, u32[]{:S(2)}) collective-permute-start(bf16[384,640]{1,0:T(8,128)(2,1)S(1)} %newton.1.refs_0_), channel_id=1, source_target_pairs={{0,8},{1,9},{2,10},{3,11},{4,28},{5,29},{6,30},{7,31},{8,0},{9,1},... | collective-permute-start | bytes 1474568 | tf_op jit(solution)/shard_map/ppermute | solution.py:43
  90.0 21.9 %collective-permute-start.26 = (bf16[384,640]{1,0:T(8,128)(2,1)S(1)}, bf16[384,640]{1,0:T(8,128)(2,1)S(1)}, u32[]{:S(2)}, u32[]{:S(2)}) collective-permute-start(bf16[384,640]{1,0:T(8,128)(2,1)S(1)} %newton.1.refs_0_), channel_id=1, source_target_pairs={{0,4},{1,5},{2,6},{3,7},{4,0},{5,1},{6,2},{7,3},{8,12},{9,13},{10,... | collective-permute-start | bytes 1474568 | tf_op jit(solution)/shard_map/ppermute | solution.py:43
  96.7 15.3 %collective-permute-start.32 = (bf16[384,640]{1,0:T(8,128)(2,1)S(1)}, bf16[384,640]{1,0:T(8,128)(2,1)S(1)}, u32[]{:S(2)}, u32[]{:S(2)}) collective-permute-start(bf16[384,640]{1,0:T(8,128)(2,1)S(1)} %collective-permute-done.31.refs_3_), channel_id=1, source_target_pairs={{0,4},{1,5},{2,6},{3,7},{4,0},{5,1},{6,2},{7,3},{8,12},{9,13},{10,... | collective-permute-start | bytes 1474568 | tf_op jit(solution)/shard_map/ppermute | solution.py:43
  103.0 9.0 %collective-permute-start.30 = (bf16[384,640]{1,0:T(8,128)(2,1)S(1)}, bf16[384,640]{1,0:T(8,128)(2,1)S(1)}, u32[]{:S(2)}, u32[]{:S(2)}) collective-permute-start(bf16[384,640]{1,0:T(8,128)(2,1)S(1)} %collective-permute-done.29.refs_2_), channel_id=1, source_target_pairs={{0,4},{1,5},{2,6},{3,7},{4,0},{5,1},{6,2},{7,3},{8,12},{9,13},{10,... | collective-permute-start | bytes 1474568 | tf_op jit(solution)/shard_map/ppermute | solution.py:43
  108.5 3.5 %collective-permute-start.28 = (bf16[384,640]{1,0:T(8,128)(2,1)S(1)}, bf16[384,640]{1,0:T(8,128)(2,1)S(1)}, u32[]{:S(2)}, u32[]{:S(2)}) collective-permute-start(bf16[384,640]{1,0:T(8,128)(2,1)S(1)} %collective-permute-done.27.refs_1_), channel_id=1, source_target_pairs={{0,4},{1,5},{2,6},{3,7},{4,0},{5,1},{6,2},{7,3},{8,12},{9,13},{10,... | collective-permute-start | bytes 1474568 | tf_op jit(solution)/shard_map/ppermute | solution.py:43

commit v6 on v5

--- a/solution.py
+++ b/solution.py
@@ -123,7 +123,7 @@
 
 
 def newton_kernel(tokens_all, dev, newton_steps, *refs):
-    ins, (out, total, mixed, gap, halves) = refs[:RING], refs[RING:]
+    ins, (out, total, mixed, gap, mixed_half, gap_half) = refs[:RING], refs[RING:]
     t = dev[0] % 4
     core, place, across = here(dev)
     for flip in range(RING):
@@ -150,31 +150,44 @@
     norm_scale = jnp.sqrt(jnp.sum(squares))
     scale = 1.0 / norm_scale
 
-    def dot(rows):
-        return jnp.dot(halves[0:rows, :], halves[0:BLOCK, :], preferred_element_type=jnp.float32)
-
-    def last():
-        return jnp.dot(halves[BLOCK:, :], halves[0:BLOCK, :], preferred_element_type=jnp.float32)
-
-    start = mixed[...] * scale
-    gap[...] = start
-    halves[0:BLOCK, :] = start.astype(jnp.bfloat16)
-    halves[BLOCK:, :] = start.astype(jnp.bfloat16)
-    mixed[...] = 2.0 * gap[...] - dot(BLOCK)
-    for turn in range(1, 4):
-        halves[0:BLOCK, :] = mixed[...].astype(jnp.bfloat16)
-        products = dot(2 * BLOCK) if turn < 3 else None
-        step = products[BLOCK:] if turn < 3 else last()
-        new_gap = 2.0 * gap[...] + 2.0**turn * mixed[...] - step
-        gap[...] = jnp.where(turn < steps, new_gap, gap[...])
-        if turn < 3:
-            mixed[...] = 2.0 * mixed[...] - products[0:BLOCK]
-            halves[BLOCK:, :] = gap[...].astype(jnp.bfloat16)
+    def dot(a, b):
+        return jnp.dot(a, b, preferred_element_type=jnp.float32)
+
+    bands = (slice(0, 256), slice(256, 512), slice(512, 640))
+    for band in bands:
+        start = mixed[band, :] * scale
+        gap[band, :] = start
+        mixed_half[0, band, :] = start.astype(jnp.bfloat16)
+        gap_half[band, :] = start.astype(jnp.bfloat16)
+    for band in bands:
+        value = 2.0 * gap[band, :] - dot(mixed_half[0, band, :], mixed_half[0])
+        mixed[band, :] = value
+        mixed_half[1, band, :] = value.astype(jnp.bfloat16)
+    for turn in range(1, 3):
+        now = turn % 2
+        for band in bands:
+            old, old_gap = mixed[band, :], gap[band, :]
+            new = 2.0 * old - dot(mixed_half[now, band, :], mixed_half[now])
+            mixed[band, :] = new
+            mixed_half[1 - now, band, :] = new.astype(jnp.bfloat16)
+            new_gap = 2.0 * old_gap + 2.0**turn * old - dot(gap_half[band, :], mixed_half[now])
+            new_gap = jnp.where(turn < steps, new_gap, old_gap)
+            gap[band, :] = new_gap
+            gap_half[band, :] = new_gap.astype(jnp.bfloat16)
     reach = jnp.where(steps <= 1, 2.0, jnp.where(steps == 2, 4.0, jnp.where(steps == 3, 8.0, 16.0)))
-    for i, (row, col) in enumerate(PANELS):
-        low = TILE * i
-        value = (reach * eye[low : low + TILE, low:] - gap[low : low + TILE, low:]) * scale
-        out[row : row + TILE, col : col + BLOCK - low] = value.astype(jnp.bfloat16)
+    for band in bands:
+        begin = band.start
+        old_gap = gap[band, begin:]
+        new_gap = 2.0 * old_gap + 8.0 * mixed[band, begin:]
+        new_gap = new_gap - dot(gap_half[band, :], mixed_half[1, :, begin:])
+        value = reach * eye[band, begin:] - jnp.where(3 < steps, new_gap, old_gap)
+        value = (value * scale).astype(jnp.bfloat16)
+        for i in range(begin // TILE, band.stop // TILE):
+            row, col = PANELS[i]
+            low = TILE * i
+            out[row : row + TILE, col : col + BLOCK - low] = value[
+                low - begin : low - begin + TILE, low - begin :
+            ]
 
 
 def apply_kernel(side, dev, *refs):
@@ -199,8 +212,16 @@
             low = TILE * i
             panel = block[row : row + TILE, col : col + BLOCK - low]
             whole[place, low : low + TILE, low:] = panel
-            if i < 4:
-                whole[place, low + TILE :, low : low + TILE] = panel[:, TILE:].T
+            if i % 2 == 0 and i < 4:
+                whole[place, low + TILE : low + 2 * TILE, low : low + TILE] = panel[
+                    :, TILE : 2 * TILE
+                ].T
+
+    def dot(a, b):
+        return jnp.dot(a, b, preferred_element_type=jnp.float32)
+
+    def dot_transposed(a, b):
+        return lax.dot_general(a, b, (((1,), (1,)), ((), ())), preferred_element_type=jnp.float32)
 
     for flip in range(RING):
         unfold(ins[flip], mine ^ flip)
@@ -208,10 +229,23 @@
         kind, j = place // 2, place % 2
         if j == 0:
             loads[kind].wait()
-        columns = slice(j * BLOCK, (j + 1) * BLOCK)
-        outs_here[kind][:, columns] = jnp.dot(
-            ins_here[kind][:, columns], whole[place], preferred_element_type=jnp.float32
-        ).astype(jnp.bfloat16)
+        at = j * BLOCK
+        rows = ins_here[kind]
+        part_0, part_1 = rows[:, at : at + 256], rows[:, at + 256 : at + 512]
+        part_2, part_12 = rows[:, at + 512 : at + 640], rows[:, at + 256 : at + 640]
+        top = dot(part_0, whole[place, 0:256, :])
+        middle = dot(part_1, whole[place, 256:512, 256:])
+        low = dot(part_2, whole[place, 512:640, 512:])
+        left = top[:, 0:256] + dot_transposed(part_12, whole[place, 0:256, 256:])
+        centre = (
+            top[:, 256:512]
+            + middle[:, 0:256]
+            + dot_transposed(part_2, whole[place, 256:512, 512:])
+        )
+        right = top[:, 512:] + middle[:, 256:] + low
+        outs_here[kind][:, at : at + 256] = left.astype(jnp.bfloat16)
+        outs_here[kind][:, at + 256 : at + 512] = centre.astype(jnp.bfloat16)
+        outs_here[kind][:, at + 512 : at + 640] = right.astype(jnp.bfloat16)
         if j == 1:
             stores[kind].start()
     for store in stores:
@@ -276,7 +310,8 @@
             pltpu.VMEM((PACK, BLOCK), half),
             pltpu.VMEM((BLOCK, BLOCK), jnp.float32),
             pltpu.VMEM((BLOCK, BLOCK), jnp.float32),
-            pltpu.VMEM((2 * BLOCK, BLOCK), half),
+            pltpu.VMEM((2, BLOCK, BLOCK), half),
+            pltpu.VMEM((BLOCK, BLOCK), half),
         ],
         compiler_params=PARAMS,
         name="newton",

time: 116 us -> 115 us (level)
  no operation moved by 1% of the time
where the time goes in v6:
time: 115 us
  starting transfers between devices  64 us (56%)
  waiting for transfers between devices  30.6 us (27%)
  Pallas kernels  19.1 us (17%)
    ppermute x33, starting transfers between devices, move(): return lax.ppermute(array, AXES, pairs)  64 us
    ppermute x33, waiting for transfers between devices, move(): return lax.ppermute(array, AXES, pairs)  30.6 us
    pallas_call x2, Pallas kernels, apply(): pl.pallas_call(functools.partial(apply_kernel, side), out_shape=[shape(*d...  6.63 us
    pallas_call x1, Pallas kernels, local(): pl.pallas_call(functools.partial(newton_kernel, tokens_all), out_shape=sh...  5.87 us
    pallas_call x2, Pallas kernels, factors(): pl.pallas_call(gram_kernel, out_shape=[shape(2, CHUNK, BLOCK)] * RING, in...  3.59 us
    pallas_call x1, Pallas kernels, local(): pl.pallas_call(pack_kernel, out_shape=([shape(*part)] * RING + [shape(RIN...  2.97 us
  transfers between devices with their start and end apart: 33, of which 12 were waited for; matrix products, arithmetic and copies ran while one was open for 0% of the time, Pallas kernels for 6%

profile of v6, /device:TPU:1, one launch (start us, length us, event | category | flops | bytes accessed | tf_op | source)
XLA Modules:
  0.0 115.3 jit_solution(14180730845853862548)
XLA Ops:
  0.6 3.0 %pack.1 = (bf16[2,128,640]{2,1,0:T(8,128)(2,1)S(1)}, bf16[2,128,640]{2,1,0:T(8,128)(2,1)S(1)}, bf16[2,128,640]{2,1,0:T(8,128)(2,1)S(1)}, bf16[2,128,640]{2,1,0:T...) custom-call(s32[1]{0:T(128)} %bitcast.dev, ...), custom_call_target="tpu_custom_call" | custom-call | tf_op jit(solution)/shard_map/pack/pallas_call | solution.py:272
  3.6 3.3 %collective-permute-start.13 = (bf16[4,2,128,640]{3,2,1,0:T(8,128)(2,1)S(1)}, bf16[4,2,128,640]{3,2,1,0:T(8,128)(2,1)S(1)}, u32[]{:S(2)}, u32[]{:S(2)}) collective-permute-start(bf16[4,2,128,640]{3,2,1,0:T(8,128)(2,1)S(1)} %get-tuple-element.35), channel_id=1, source_target_pairs={{0,4},{1,5},{2,6},{3,7},{4,0},{5,1},{6,2},{7,3},{8,12},{9,13},{10,... | collective-permute-start | bytes 3932168 | tf_op jit(solution)/shard_map/ppermute | solution.py:43
  6.9 0.1 collective-permute-start.3
  7.0 3.2 %collective-permute-start = (bf16[2,128,640]{2,1,0:T(8,128)(2,1)S(1)}, bf16[2,128,640]{2,1,0:T(8,128)(2,1)S(1)}, u32[]{:S(2)}, u32[]{:S(2)}) collective-permute-start(bf16[2,128,640]{2,1,0:T(8,128)(2,1)S(1)} %get-tuple-element.22), channel_id=1, source_target_pairs={{0,40},{1,41},{2,42},{3,43},{4,124},{5,125},{6,126},{7,127},{8,32}... | collective-permute-start | bytes 983048 | tf_op jit(solution)/shard_map/ppermute | solution.py:43
  10.2 1.6 %collective-permute-start.10 = (bf16[2,128,640]{2,1,0:T(8,128)(2,1)S(1)}, bf16[2,128,640]{2,1,0:T(8,128)(2,1)S(1)}, u32[]{:S(2)}, u32[]{:S(2)}) collective-permute-start(bf16[2,128,640]{2,1,0:T(8,128)(2,1)S(1)} %get-tuple-element.31), channel_id=1, source_target_pairs={{0,40},{1,41},{2,42},{3,43},{4,124},{5,125},{6,126},{7,127},{8,32}... | collective-permute-start | bytes 983048 | tf_op jit(solution)/shard_map/ppermute | solution.py:43
  11.8 0.7 collective-permute-start.11
  12.6 0.0 collective-permute-done.13.refs_7_
  12.6 2.7 %collective-permute-start.12 = (bf16[2,128,640]{2,1,0:T(8,128)(2,1)S(1)}, bf16[2,128,640]{2,1,0:T(8,128)(2,1)S(1)}, u32[]{:S(2)}, u32[]{:S(2)}) collective-permute-start(bf16[2,128,640]{2,1,0:T(8,128)(2,1)S(1)} %get-tuple-element.33), channel_id=1, source_target_pairs={{0,8},{1,9},{2,10},{3,11},{4,28},{5,29},{6,30},{7,31},{8,0},{9,1},... | collective-permute-start | bytes 983048 | tf_op jit(solution)/shard_map/ppermute | solution.py:43
  15.3 0.1 slice_bitcast_fusion
  15.4 0.9 collective-permute-done.refs_0_
  16.3 1.0 collective-permute-start.16
  17.3 2.6 %collective-permute-done.10.refs_0_ = bf16[2,128,640]{2,1,0:T(8,128)(2,1)S(1)} collective-permute-done((bf16[2,128,640]{2,1,0:T(8,128)(2,1)S(1)}, bf16[2,128,640]{2,1,0:T(8,128)(2,1)S(1)}, u32[]{:S(2)}, u32[]{:S(2)}) %collective-permute-start.10) | collective-permute-done | bytes 327712 | tf_op jit(solution)/shard_map/ppermute | solution.py:43
  19.9 0.7 collective-permute-start.15
  20.6 0.0 collective-permute-done.3.refs_7_
  20.6 2.6 %collective-permute-start.14 = (bf16[2,128,640]{2,1,0:T(8,128)(2,1)S(1)}, bf16[2,128,640]{2,1,0:T(8,128)(2,1)S(1)}, u32[]{:S(2)}, u32[]{:S(2)}) collective-permute-start(bf16[2,128,640]{2,1,0:T(8,128)(2,1)S(1)} %get-tuple-element.47), channel_id=1, source_target_pairs={{0,40},{1,41},{2,42},{3,43},{4,124},{5,125},{6,126},{7,127},{8,32}... | collective-permute-start | bytes 983048 | tf_op jit(solution)/shard_map/ppermute | solution.py:43
  23.3 0.1 slice_bitcast_fusion.3
  23.4 2.6 %collective-permute-start.1 = (bf16[2,128,640]{2,1,0:T(8,128)(2,1)S(1)}, bf16[2,128,640]{2,1,0:T(8,128)(2,1)S(1)}, u32[]{:S(2)}, u32[]{:S(2)}) collective-permute-start(bf16[2,128,640]{2,1,0:T(8,128)(2,1)S(1)} %get-tuple-element.23), channel_id=1, source_target_pairs={{0,32},{1,33},{2,34},{3,35},{4,100},{5,101},{6,102},{7,103},{8,40}... | collective-permute-start | bytes 983048 | tf_op jit(solution)/shard_map/ppermute | solution.py:43
  26.0 0.0 collective-permute-done.12.refs_2_
  26.0 1.0 collective-permute-done.16.refs_6_
  27.0 1.7 %collective-permute-start.6 = (bf16[2,128,640]{2,1,0:T(8,128)(2,1)S(1)}, bf16[2,128,640]{2,1,0:T(8,128)(2,1)S(1)}, u32[]{:S(2)}, u32[]{:S(2)}) collective-permute-start(bf16[2,128,640]{2,1,0:T(8,128)(2,1)S(1)} %get-tuple-element.42), channel_id=1, source_target_pairs={{0,8},{1,9},{2,10},{3,11},{4,28},{5,29},{6,30},{7,31},{8,0},{9,1},... | collective-permute-start | bytes 983048 | tf_op jit(solution)/shard_map/ppermute | solution.py:43
  28.7 1.8 %collective-permute-start.5 = (bf16[2,128,640]{2,1,0:T(8,128)(2,1)S(1)}, bf16[2,128,640]{2,1,0:T(8,128)(2,1)S(1)}, u32[]{:S(2)}, u32[]{:S(2)}) collective-permute-start(bf16[2,128,640]{2,1,0:T(8,128)(2,1)S(1)} %get-tuple-element.43), channel_id=1, source_target_pairs={{0,32},{1,33},{2,34},{3,35},{4,100},{5,101},{6,102},{7,103},{8,40}... | collective-permute-start | bytes 983048 | tf_op jit(solution)/shard_map/ppermute | solution.py:43
  30.4 0.9 collective-permute-done.14.refs_4_
  31.4 2.3 %collective-permute-start.4 = (bf16[2,128,640]{2,1,0:T(8,128)(2,1)S(1)}, bf16[2,128,640]{2,1,0:T(8,128)(2,1)S(1)}, u32[]{:S(2)}, u32[]{:S(2)}) collective-permute-start(bf16[2,128,640]{2,1,0:T(8,128)(2,1)S(1)} %get-tuple-element.44), channel_id=1, source_target_pairs={{0,40},{1,41},{2,42},{3,43},{4,124},{5,125},{6,126},{7,127},{8,32}... | collective-permute-start | bytes 983048 | tf_op jit(solution)/shard_map/ppermute | solution.py:43
  33.7 1.8 %gram.3 = (bf16[2,96,640]{2,1,0:T(8,128)(2,1)S(1)}, bf16[2,96,640]{2,1,0:T(8,128)(2,1)S(1)}, bf16[2,96,640]{2,1,0:T(8,128)(2,1)S(1)}, bf16[2,96,640]{2,1,0:T(8,128)(2,1)S(1)}) custom-call(s32[1]{0:T(128)} %bitcast.dev, bf16[2,128,640]{2,1,0:T(8,128)(2,1)S(1)} %collective-permute-done.10.refs_0_, bf16[2,128,640]{2,1,0:T(8,128)(2,1)S(1)} %collective-permute-done.11.refs_1_, ...), custom_call_target="tpu_custom_call" | custom-call | tf_op jit(solution)/shard_map/gram/pallas_call | solution.py:286
  35.5 0.0 collective-permute-done.1.refs_1_
  35.5 0.1 collective-permute-start.17
  35.6 0.0 collective-permute-done.2.refs_2_
  35.6 0.1 collective-permute-start.18
  35.7 2.7 %collective-permute-done.6.refs_6_ = bf16[2,128,640]{2,1,0:T(8,128)(2,1)S(1)} collective-permute-done((bf16[2,128,640]{2,1,0:T(8,128)(2,1)S(1)}, bf16[2,128,640]{2,1,0:T(8,128)(2,1)S(1)}, u32[]{:S(2)}, u32[]{:S(2)}) %collective-permute-start.6) | collective-permute-done | bytes 327712 | tf_op jit(solution)/shard_map/ppermute | solution.py:43
  38.4 0.0 collective-permute-start.19
  38.4 6.0 %collective-permute-done.4.refs_4_ = bf16[2,128,640]{2,1,0:T(8,128)(2,1)S(1)} collective-permute-done((bf16[2,128,640]{2,1,0:T(8,128)(2,1)S(1)}, bf16[2,128,640]{2,1,0:T(8,128)(2,1)S(1)}, u32[]{:S(2)}, u32[]{:S(2)}) %collective-permute-start.4) | collective-permute-done | bytes 327712 | tf_op jit(solution)/shard_map/ppermute | solution.py:43
  44.4 1.8 %gram.2 = (bf16[2,96,640]{2,1,0:T(8,128)(2,1)S(1)}, bf16[2,96,640]{2,1,0:T(8,128)(2,1)S(1)}, bf16[2,96,640]{2,1,0:T(8,128)(2,1)S(1)}, bf16[2,96,640]{2,1,0:T(8,128)(2,1)S(1)}) custom-call(s32[1]{0:T(128)} %bitcast.dev, bf16[2,128,640]{2,1,0:T(8,128)(2,1)S(1)} %collective-permute-done.refs_0_, bf16[2,128,640]{2,1,0:T(8,128)(2,1)S(1)} %collective-permute-done.1.refs_1_, ...), custom_call_target="tpu_custom_call" | custom-call | tf_op jit(solution)/shard_map/gram/pallas_call | solution.py:286
  46.2 0.1 collective-permute-start.7
  46.3 0.1 collective-permute-start.8
  46.4 0.0 collective-permute-done.17
  46.5 2.5 %collective-permute-start.9 = (bf16[2,96,640]{2,1,0:T(8,128)(2,1)S(1)}, bf16[2,96,640]{2,1,0:T(8,128)(2,1)S(1)}, u32[]{:S(2)}, u32[]{:S(2)}) collective-permute-start(bf16[2,96,640]{2,1,0:T(8,128)(2,1)S(1)} %get-tuple-element.29), channel_id=1, source_target_pairs={{0,24},{1,25},{2,26},{3,27},{4,12},{5,13},{6,14},{7,15},{8,16},{9,... | collective-permute-start | bytes 737288 | tf_op jit(solution)/shard_map/ppermute | solution.py:43
  49.0 0.0 collective-permute-done.18
  49.0 0.0 collective-permute-done.19
  49.0 0.1 add_convert_fusion
  49.1 6.7 %collective-permute-start.20 = (bf16[2,96,640]{2,1,0:T(8,128)(2,1)S(1)}, bf16[2,96,640]{2,1,0:T(8,128)(2,1)S(1)}, u32[]{:S(2)}, u32[]{:S(2)}) collective-permute-start(bf16[2,96,640]{2,1,0:T(8,128)(2,1)S(1)} %add_convert_fusion), channel_id=1, source_target_pairs={{0,1},{1,0},{2,3},{3,2},{4,7},{5,6},{6,5},{7,4},{8,9},{9,8},{10,11... | collective-permute-start | bytes 737288 | tf_op jit(solution)/shard_map/ppermute | solution.py:43
  55.8 0.0 collective-permute-done.7
  55.9 5.8 %collective-permute-done.20 = bf16[2,96,640]{2,1,0:T(8,128)(2,1)S(1)} collective-permute-done((bf16[2,96,640]{2,1,0:T(8,128)(2,1)S(1)}, bf16[2,96,640]{2,1,0:T(8,128)(2,1)S(1)}, u32[]{:S(2)}, u32[]{:S(2)}) %collective-permute-start.20) | collective-permute-done | bytes 245792 | tf_op jit(solution)/shard_map/ppermute | solution.py:43
  61.6 0.1 convert_add_fusion
  61.8 0.0 copy-start
  61.8 1.7 %collective-permute-start.21 = (bf16[96,640]{1,0:T(8,128)(2,1)S(1)}, bf16[96,640]{1,0:T(8,128)(2,1)S(1)}, u32[]{:S(2)}, u32[]{:S(2)}) collective-permute-start(bf16[96,640]{1,0:T(8,128)(2,1)S(1)} %fusion.2), channel_id=1, source_target_pairs={{0,3},{1,2},{2,1},{3,0},{4,5},{5,4},{6,7},{7,6},{8,11},{9,10},{10,... | collective-permute-start | bytes 368648 | tf_op jit(solution)/shard_map/ppermute | solution.py:43
  63.5 3.4 %collective-permute-done.21 = bf16[96,640]{1,0:T(8,128)(2,1)S(1)} collective-permute-done((bf16[96,640]{1,0:T(8,128)(2,1)S(1)}, bf16[96,640]{1,0:T(8,128)(2,1)S(1)}, u32[]{:S(2)}, u32[]{:S(2)}) %collective-permute-start.21) | collective-permute-done | bytes 122912 | tf_op jit(solution)/shard_map/ppermute | solution.py:43
  66.9 1.7 %collective-permute-start.22 = (bf16[96,640]{1,0:T(8,128)(2,1)S(1)}, bf16[96,640]{1,0:T(8,128)(2,1)S(1)}, u32[]{:S(2)}, u32[]{:S(2)}) collective-permute-start(bf16[96,640]{1,0:T(8,128)(2,1)S(1)} %fusion.1), channel_id=1, source_target_pairs={{0,128},{1,129},{2,130},{3,131},{4,132},{5,133},{6,134},{7,135},{8... | collective-permute-start | bytes 368648 | tf_op jit(solution)/shard_map/ppermute | solution.py:43
  68.6 3.7 %collective-permute-done.22 = bf16[96,640]{1,0:T(8,128)(2,1)S(1)} collective-permute-done((bf16[96,640]{1,0:T(8,128)(2,1)S(1)}, bf16[96,640]{1,0:T(8,128)(2,1)S(1)}, u32[]{:S(2)}, u32[]{:S(2)}) %collective-permute-start.22) | collective-permute-done | bytes 122912 | tf_op jit(solution)/shard_map/ppermute | solution.py:43
  72.4 0.1 collective-permute-start.25
  72.5 0.1 collective-permute-start.24
  72.6 2.5 %collective-permute-start.23 = (bf16[96,640]{1,0:T(8,128)(2,1)S(1)}, bf16[96,640]{1,0:T(8,128)(2,1)S(1)}, u32[]{:S(2)}, u32[]{:S(2)}) collective-permute-start(bf16[96,640]{1,0:T(8,128)(2,1)S(1)} %add_convert_fusion.1.refs_3_), channel_id=1, source_target_pairs={{0,120},{1,121},{2,122},{3,123},{4,44},{5,45},{6,46},{7,47},{8,112... | collective-permute-start | bytes 368648 | tf_op jit(solution)/shard_map/ppermute | solution.py:43
  75.1 1.1 collective-permute-done.25.refs_2_
  76.2 0.1 collective-permute-done.24.refs_1_
  76.3 2.4 %collective-permute-done.23.refs_0_ = bf16[96,640]{1,0:T(8,128)(2,1)S(1)} collective-permute-done((bf16[96,640]{1,0:T(8,128)(2,1)S(1)}, bf16[96,640]{1,0:T(8,128)(2,1)S(1)}, u32[]{:S(2)}, u32[]{:S(2)}) %collective-permute-start.23) | collective-permute-done | bytes 122912 | tf_op jit(solution)/shard_map/ppermute | solution.py:43
  78.7 5.9 %newton.1.refs_0_ = bf16[384,640]{1,0:T(8,128)(2,1)S(1)} custom-call(s32[1]{0:T(128)} %bitcast.dev, s32[2,2,8]{2,1,0:T(2,128)S(1)} %copy-done.2, bf16[96,640]{1,0:T(8,128)(2,1)S(1)} %collective-permute-done.23.refs_0_, bf16[96,640]{1,0:T(8,128)(2,1)S(1)} %collective-permute-done.24.refs_1_, bf16[96,640]{1,0:T(8,128)(2,1)S(1)} %collective-permute-done.25.refs_2_, ...), custom_call_target="tpu_custom_call" | custom-call | tf_op jit(solution)/shard_map/newton/pallas_call | solution.py:304
  84.6 1.1 collective-permute-start.31
  85.6 2.1 %collective-permute-start.29 = (bf16[384,640]{1,0:T(8,128)(2,1)S(1)}, bf16[384,640]{1,0:T(8,128)(2,1)S(1)}, u32[]{:S(2)}, u32[]{:S(2)}) collective-permute-start(bf16[384,640]{1,0:T(8,128)(2,1)S(1)} %newton.1.refs_0_), channel_id=1, source_target_pairs={{0,32},{1,33},{2,34},{3,35},{4,100},{5,101},{6,102},{7,103},{8,40}... | collective-permute-start | bytes 1474568 | tf_op jit(solution)/shard_map/ppermute | solution.py:43
  87.7 2.3 %collective-permute-start.27 = (bf16[384,640]{1,0:T(8,128)(2,1)S(1)}, bf16[384,640]{1,0:T(8,128)(2,1)S(1)}, u32[]{:S(2)}, u32[]{:S(2)}) collective-permute-start(bf16[384,640]{1,0:T(8,128)(2,1)S(1)} %newton.1.refs_0_), channel_id=1, source_target_pairs={{0,8},{1,9},{2,10},{3,11},{4,28},{5,29},{6,30},{7,31},{8,0},{9,1},... | collective-permute-start | bytes 1474568 | tf_op jit(solution)/shard_map/ppermute | solution.py:43
  90.0 6.6 %collective-permute-start.26 = (bf16[384,640]{1,0:T(8,128)(2,1)S(1)}, bf16[384,640]{1,0:T(8,128)(2,1)S(1)}, u32[]{:S(2)}, u32[]{:S(2)}) collective-permute-start(bf16[384,640]{1,0:T(8,128)(2,1)S(1)} %newton.1.refs_0_), channel_id=1, source_target_pairs={{0,4},{1,5},{2,6},{3,7},{4,0},{5,1},{6,2},{7,3},{8,12},{9,13},{10,... | collective-permute-start | bytes 1474568 | tf_op jit(solution)/shard_map/ppermute | solution.py:43
  96.6 6.3 %collective-permute-start.32 = (bf16[384,640]{1,0:T(8,128)(2,1)S(1)}, bf16[384,640]{1,0:T(8,128)(2,1)S(1)}, u32[]{:S(2)}, u32[]{:S(2)}) collective-permute-start(bf16[384,640]{1,0:T(8,128)(2,1)S(1)} %collective-permute-done.31.refs_3_), channel_id=1, source_target_pairs={{0,4},{1,5},{2,6},{3,7},{4,0},{5,1},{6,2},{7,3},{8,12},{9,13},{10,... | collective-permute-start | bytes 1474568 | tf_op jit(solution)/shard_map/ppermute | solution.py:43
  103.0 5.5 %collective-permute-start.30 = (bf16[384,640]{1,0:T(8,128)(2,1)S(1)}, bf16[384,640]{1,0:T(8,128)(2,1)S(1)}, u32[]{:S(2)}, u32[]{:S(2)}) collective-permute-start(bf16[384,640]{1,0:T(8,128)(2,1)S(1)} %collective-permute-done.29.refs_2_), channel_id=1, source_target_pairs={{0,4},{1,5},{2,6},{3,7},{4,0},{5,1},{6,2},{7,3},{8,12},{9,13},{10,... | collective-permute-start | bytes 1474568 | tf_op jit(solution)/shard_map/ppermute | solution.py:43
  108.5 0.0 collective-permute-start.28
  108.5 3.3 %apply.2 = (bf16[2,240,1280]{2,1,0:T(8,128)(2,1)}, bf16[2,320,1280]{2,1,0:T(8,128)(2,1)}) custom-call(s32[1]{0:T(128)} %bitcast.dev, bf16[384,640]{1,0:T(8,128)(2,1)S(1)} %newton.1.refs_0_, bf16[384,640]{1,0:T(8,128)(2,1)S(1)} %collective-permute-done.27.refs_1_, bf16[384,640]{1,0:T(8,128)(2,1)S(1)} %collective-permute-done.29.refs_2_, ...), custom_call_target="tpu_custom_call" | custom-call | tf_op jit(solution)/shard_map/apply/pallas_call | solution.py:325
  111.8 3.3 %apply.3 = (bf16[2,240,1280]{2,1,0:T(8,128)(2,1)}, bf16[2,320,1280]{2,1,0:T(8,128)(2,1)}) custom-call(s32[1]{0:T(128)} %bitcast.dev, bf16[384,640]{1,0:T(8,128)(2,1)S(1)} %collective-permute-done.26.refs_0_, bf16[384,640]{1,0:T(8,128)(2,1)S(1)} %collective-permute-done.28.refs_1_, ...), custom_call_target="tpu_custom_call", output_to_operand_aliasing={{0}: (7, {}), {1}: (8, {})} | custom-call | tf_op jit(solution)/shard_map/apply/pallas_call | solution.py:325
  (21 shorter events, 0.1 us)
Async XLA Ops:
  3.6 9.0 %collective-permute-start.13 = (bf16[4,2,128,640]{3,2,1,0:T(8,128)(2,1)S(1)}, bf16[4,2,128,640]{3,2,1,0:T(8,128)(2,1)S(1)}, u32[]{:S(2)}, u32[]{:S(2)}) collective-permute-start(bf16[4,2,128,640]{3,2,1,0:T(8,128)(2,1)S(1)} %get-tuple-element.35), channel_id=1, source_target_pairs={{0,4},{1,5},{2,6},{3,7},{4,0},{5,1},{6,2},{7,3},{8,12},{9,13},{10,... | collective-permute-start | bytes 3932168 | tf_op jit(solution)/shard_map/ppermute | solution.py:43
  6.9 13.7 %collective-permute-start.3 = (bf16[4,2,128,640]{3,2,1,0:T(8,128)(2,1)S(1)}, bf16[4,2,128,640]{3,2,1,0:T(8,128)(2,1)S(1)}, u32[]{:S(2)}, u32[]{:S(2)}) collective-permute-start(bf16[4,2,128,640]{3,2,1,0:T(8,128)(2,1)S(1)} %get-tuple-element.26), channel_id=1, source_target_pairs={{0,4},{1,5},{2,6},{3,7},{4,0},{5,1},{6,2},{7,3},{8,12},{9,13},{10,... | collective-permute-start | bytes 3932168 | tf_op jit(solution)/shard_map/ppermute | solution.py:43
  7.0 9.2 %collective-permute-start = (bf16[2,128,640]{2,1,0:T(8,128)(2,1)S(1)}, bf16[2,128,640]{2,1,0:T(8,128)(2,1)S(1)}, u32[]{:S(2)}, u32[]{:S(2)}) collective-permute-start(bf16[2,128,640]{2,1,0:T(8,128)(2,1)S(1)} %get-tuple-element.22), channel_id=1, source_target_pairs={{0,40},{1,41},{2,42},{3,43},{4,124},{5,125},{6,126},{7,127},{8,32}... | collective-permute-start | bytes 983048 | tf_op jit(solution)/shard_map/ppermute | solution.py:43
  10.2 9.7 %collective-permute-start.10 = (bf16[2,128,640]{2,1,0:T(8,128)(2,1)S(1)}, bf16[2,128,640]{2,1,0:T(8,128)(2,1)S(1)}, u32[]{:S(2)}, u32[]{:S(2)}) collective-permute-start(bf16[2,128,640]{2,1,0:T(8,128)(2,1)S(1)} %get-tuple-element.31), channel_id=1, source_target_pairs={{0,40},{1,41},{2,42},{3,43},{4,124},{5,125},{6,126},{7,127},{8,32}... | collective-permute-start | bytes 983048 | tf_op jit(solution)/shard_map/ppermute | solution.py:43
  11.8 11.6 %collective-permute-start.11 = (bf16[2,128,640]{2,1,0:T(8,128)(2,1)S(1)}, bf16[2,128,640]{2,1,0:T(8,128)(2,1)S(1)}, u32[]{:S(2)}, u32[]{:S(2)}) collective-permute-start(bf16[2,128,640]{2,1,0:T(8,128)(2,1)S(1)} %get-tuple-element.32), channel_id=1, source_target_pairs={{0,32},{1,33},{2,34},{3,35},{4,100},{5,101},{6,102},{7,103},{8,40}... | collective-permute-start | bytes 983048 | tf_op jit(solution)/shard_map/ppermute | solution.py:43
  12.6 13.4 %collective-permute-start.12 = (bf16[2,128,640]{2,1,0:T(8,128)(2,1)S(1)}, bf16[2,128,640]{2,1,0:T(8,128)(2,1)S(1)}, u32[]{:S(2)}, u32[]{:S(2)}) collective-permute-start(bf16[2,128,640]{2,1,0:T(8,128)(2,1)S(1)} %get-tuple-element.33), channel_id=1, source_target_pairs={{0,8},{1,9},{2,10},{3,11},{4,28},{5,29},{6,30},{7,31},{8,0},{9,1},... | collective-permute-start | bytes 983048 | tf_op jit(solution)/shard_map/ppermute | solution.py:43
  16.3 10.7 %collective-permute-start.16 = (bf16[2,128,640]{2,1,0:T(8,128)(2,1)S(1)}, bf16[2,128,640]{2,1,0:T(8,128)(2,1)S(1)}, u32[]{:S(2)}, u32[]{:S(2)}) collective-permute-start(bf16[2,128,640]{2,1,0:T(8,128)(2,1)S(1)} %get-tuple-element.45), channel_id=1, source_target_pairs={{0,8},{1,9},{2,10},{3,11},{4,28},{5,29},{6,30},{7,31},{8,0},{9,1},... | collective-permute-start | bytes 983048 | tf_op jit(solution)/shard_map/ppermute | solution.py:43
  19.9 8.8 %collective-permute-start.15 = (bf16[2,128,640]{2,1,0:T(8,128)(2,1)S(1)}, bf16[2,128,640]{2,1,0:T(8,128)(2,1)S(1)}, u32[]{:S(2)}, u32[]{:S(2)}) collective-permute-start(bf16[2,128,640]{2,1,0:T(8,128)(2,1)S(1)} %get-tuple-element.46), channel_id=1, source_target_pairs={{0,32},{1,33},{2,34},{3,35},{4,100},{5,101},{6,102},{7,103},{8,40}... | collective-permute-start | bytes 983048 | tf_op jit(solution)/shard_map/ppermute | solution.py:43
  20.6 10.7 %collective-permute-start.14 = (bf16[2,128,640]{2,1,0:T(8,128)(2,1)S(1)}, bf16[2,128,640]{2,1,0:T(8,128)(2,1)S(1)}, u32[]{:S(2)}, u32[]{:S(2)}) collective-permute-start(bf16[2,128,640]{2,1,0:T(8,128)(2,1)S(1)} %get-tuple-element.47), channel_id=1, source_target_pairs={{0,40},{1,41},{2,42},{3,43},{4,124},{5,125},{6,126},{7,127},{8,32}... | collective-permute-start | bytes 983048 | tf_op jit(solution)/shard_map/ppermute | solution.py:43
  23.4 12.1 %collective-permute-start.1 = (bf16[2,128,640]{2,1,0:T(8,128)(2,1)S(1)}, bf16[2,128,640]{2,1,0:T(8,128)(2,1)S(1)}, u32[]{:S(2)}, u32[]{:S(2)}) collective-permute-start(bf16[2,128,640]{2,1,0:T(8,128)(2,1)S(1)} %get-tuple-element.23), channel_id=1, source_target_pairs={{0,32},{1,33},{2,34},{3,35},{4,100},{5,101},{6,102},{7,103},{8,40}... | collective-permute-start | bytes 983048 | tf_op jit(solution)/shard_map/ppermute | solution.py:43
  26.0 9.6 %collective-permute-start.2 = (bf16[2,128,640]{2,1,0:T(8,128)(2,1)S(1)}, bf16[2,128,640]{2,1,0:T(8,128)(2,1)S(1)}, u32[]{:S(2)}, u32[]{:S(2)}) collective-permute-start(bf16[2,128,640]{2,1,0:T(8,128)(2,1)S(1)} %get-tuple-element.24), channel_id=1, source_target_pairs={{0,8},{1,9},{2,10},{3,11},{4,28},{5,29},{6,30},{7,31},{8,0},{9,1},... | collective-permute-start | bytes 983048 | tf_op jit(solution)/shard_map/ppermute | solution.py:43
  27.0 11.5 %collective-permute-start.6 = (bf16[2,128,640]{2,1,0:T(8,128)(2,1)S(1)}, bf16[2,128,640]{2,1,0:T(8,128)(2,1)S(1)}, u32[]{:S(2)}, u32[]{:S(2)}) collective-permute-start(bf16[2,128,640]{2,1,0:T(8,128)(2,1)S(1)} %get-tuple-element.42), channel_id=1, source_target_pairs={{0,8},{1,9},{2,10},{3,11},{4,28},{5,29},{6,30},{7,31},{8,0},{9,1},... | collective-permute-start | bytes 983048 | tf_op jit(solution)/shard_map/ppermute | solution.py:43
  28.7 9.8 %collective-permute-start.5 = (bf16[2,128,640]{2,1,0:T(8,128)(2,1)S(1)}, bf16[2,128,640]{2,1,0:T(8,128)(2,1)S(1)}, u32[]{:S(2)}, u32[]{:S(2)}) collective-permute-start(bf16[2,128,640]{2,1,0:T(8,128)(2,1)S(1)} %get-tuple-element.43), channel_id=1, source_target_pairs={{0,32},{1,33},{2,34},{3,35},{4,100},{5,101},{6,102},{7,103},{8,40}... | collective-permute-start | bytes 983048 | tf_op jit(solution)/shard_map/ppermute | solution.py:43
  31.4 13.1 %collective-permute-start.4 = (bf16[2,128,640]{2,1,0:T(8,128)(2,1)S(1)}, bf16[2,128,640]{2,1,0:T(8,128)(2,1)S(1)}, u32[]{:S(2)}, u32[]{:S(2)}) collective-permute-start(bf16[2,128,640]{2,1,0:T(8,128)(2,1)S(1)} %get-tuple-element.44), channel_id=1, source_target_pairs={{0,40},{1,41},{2,42},{3,43},{4,124},{5,125},{6,126},{7,127},{8,32}... | collective-permute-start | bytes 983048 | tf_op jit(solution)/shard_map/ppermute | solution.py:43
  35.5 11.0 %collective-permute-start.17 = (bf16[2,96,640]{2,1,0:T(8,128)(2,1)S(1)}, bf16[2,96,640]{2,1,0:T(8,128)(2,1)S(1)}, u32[]{:S(2)}, u32[]{:S(2)}) collective-permute-start(bf16[2,96,640]{2,1,0:T(8,128)(2,1)S(1)} %get-tuple-element.36), channel_id=1, source_target_pairs={{0,120},{1,121},{2,122},{3,123},{4,44},{5,45},{6,46},{7,47},{8,112... | collective-permute-start | bytes 737288 | tf_op jit(solution)/shard_map/ppermute | solution.py:43
  35.6 13.4 %collective-permute-start.18 = (bf16[2,96,640]{2,1,0:T(8,128)(2,1)S(1)}, bf16[2,96,640]{2,1,0:T(8,128)(2,1)S(1)}, u32[]{:S(2)}, u32[]{:S(2)}) collective-permute-start(bf16[2,96,640]{2,1,0:T(8,128)(2,1)S(1)} %get-tuple-element.37), channel_id=1, source_target_pairs={{0,96},{1,97},{2,98},{3,99},{4,36},{5,37},{6,38},{7,39},{8,104},{9... | collective-permute-start | bytes 737288 | tf_op jit(solution)/shard_map/ppermute | solution.py:43
  38.4 10.6 %collective-permute-start.19 = (bf16[2,96,640]{2,1,0:T(8,128)(2,1)S(1)}, bf16[2,96,640]{2,1,0:T(8,128)(2,1)S(1)}, u32[]{:S(2)}, u32[]{:S(2)}) collective-permute-start(bf16[2,96,640]{2,1,0:T(8,128)(2,1)S(1)} %get-tuple-element.38), channel_id=1, source_target_pairs={{0,24},{1,25},{2,26},{3,27},{4,12},{5,13},{6,14},{7,15},{8,16},{9,... | collective-permute-start | bytes 737288 | tf_op jit(solution)/shard_map/ppermute | solution.py:43
  46.2 9.6 %collective-permute-start.7 = (bf16[2,96,640]{2,1,0:T(8,128)(2,1)S(1)}, bf16[2,96,640]{2,1,0:T(8,128)(2,1)S(1)}, u32[]{:S(2)}, u32[]{:S(2)}) collective-permute-start(bf16[2,96,640]{2,1,0:T(8,128)(2,1)S(1)} %get-tuple-element.27), channel_id=1, source_target_pairs={{0,120},{1,121},{2,122},{3,123},{4,44},{5,45},{6,46},{7,47},{8,112... | collective-permute-start | bytes 737288 | tf_op jit(solution)/shard_map/ppermute | solution.py:43
  46.3 9.5 %collective-permute-start.8 = (bf16[2,96,640]{2,1,0:T(8,128)(2,1)S(1)}, bf16[2,96,640]{2,1,0:T(8,128)(2,1)S(1)}, u32[]{:S(2)}, u32[]{:S(2)}) collective-permute-start(bf16[2,96,640]{2,1,0:T(8,128)(2,1)S(1)} %get-tuple-element.28), channel_id=1, source_target_pairs={{0,96},{1,97},{2,98},{3,99},{4,36},{5,37},{6,38},{7,39},{8,104},{9... | collective-permute-start | bytes 737288 | tf_op jit(solution)/shard_map/ppermute | solution.py:43
  46.5 9.4 %collective-permute-start.9 = (bf16[2,96,640]{2,1,0:T(8,128)(2,1)S(1)}, bf16[2,96,640]{2,1,0:T(8,128)(2,1)S(1)}, u32[]{:S(2)}, u32[]{:S(2)}) collective-permute-start(bf16[2,96,640]{2,1,0:T(8,128)(2,1)S(1)} %get-tuple-element.29), channel_id=1, source_target_pairs={{0,24},{1,25},{2,26},{3,27},{4,12},{5,13},{6,14},{7,15},{8,16},{9,... | collective-permute-start | bytes 737288 | tf_op jit(solution)/shard_map/ppermute | solution.py:43
  49.1 12.5 %collective-permute-start.20 = (bf16[2,96,640]{2,1,0:T(8,128)(2,1)S(1)}, bf16[2,96,640]{2,1,0:T(8,128)(2,1)S(1)}, u32[]{:S(2)}, u32[]{:S(2)}) collective-permute-start(bf16[2,96,640]{2,1,0:T(8,128)(2,1)S(1)} %add_convert_fusion), channel_id=1, source_target_pairs={{0,1},{1,0},{2,3},{3,2},{4,7},{5,6},{6,5},{7,4},{8,9},{9,8},{10,11... | collective-permute-start | bytes 737288 | tf_op jit(solution)/shard_map/ppermute | solution.py:43
  61.6 17.1 %copy-start.2 = (s32[2,2,8]{2,1,0:T(2,128)S(1)}, s32[2,2,8]{2,1,0:T(2,128)}, u32[]{:S(2)}) copy-start(s32[2,2,8]{2,1,0:T(2,128)} %newton_steps.1) | copy-start | bytes 388
  61.6 46.9 %copy-start.1 = (bf16[2,240,1280]{2,1,0:T(8,128)(2,1)S(1)}, bf16[2,240,1280]{2,1,0:T(8,128)(2,1)}, u32[]{:S(2)}) copy-start(bf16[2,240,1280]{2,1,0:T(8,128)(2,1)} %refs_4_.3) | copy-start | bytes 3686404
  61.8 46.7 %copy-start = (bf16[2,320,1280]{2,1,0:T(8,128)(2,1)S(1)}, bf16[2,320,1280]{2,1,0:T(8,128)(2,1)}, u32[]{:S(2)}) copy-start(bf16[2,320,1280]{2,1,0:T(8,128)(2,1)} %refs_5_.3) | copy-start | bytes 4915204
  61.8 5.1 %collective-permute-start.21 = (bf16[96,640]{1,0:T(8,128)(2,1)S(1)}, bf16[96,640]{1,0:T(8,128)(2,1)S(1)}, u32[]{:S(2)}, u32[]{:S(2)}) collective-permute-start(bf16[96,640]{1,0:T(8,128)(2,1)S(1)} %fusion.2), channel_id=1, source_target_pairs={{0,3},{1,2},{2,1},{3,0},{4,5},{5,4},{6,7},{7,6},{8,11},{9,10},{10,... | collective-permute-start | bytes 368648 | tf_op jit(solution)/shard_map/ppermute | solution.py:43
  66.9 5.4 %collective-permute-start.22 = (bf16[96,640]{1,0:T(8,128)(2,1)S(1)}, bf16[96,640]{1,0:T(8,128)(2,1)S(1)}, u32[]{:S(2)}, u32[]{:S(2)}) collective-permute-start(bf16[96,640]{1,0:T(8,128)(2,1)S(1)} %fusion.1), channel_id=1, source_target_pairs={{0,128},{1,129},{2,130},{3,131},{4,132},{5,133},{6,134},{7,135},{8... | collective-permute-start | bytes 368648 | tf_op jit(solution)/shard_map/ppermute | solution.py:43
  72.4 3.8 %collective-permute-start.25 = (bf16[96,640]{1,0:T(8,128)(2,1)S(1)}, bf16[96,640]{1,0:T(8,128)(2,1)S(1)}, u32[]{:S(2)}, u32[]{:S(2)}) collective-permute-start(bf16[96,640]{1,0:T(8,128)(2,1)S(1)} %add_convert_fusion.1.refs_3_), channel_id=1, source_target_pairs={{0,24},{1,25},{2,26},{3,27},{4,12},{5,13},{6,14},{7,15},{8,16},{9,... | collective-permute-start | bytes 368648 | tf_op jit(solution)/shard_map/ppermute | solution.py:43
  72.5 3.8 %collective-permute-start.24 = (bf16[96,640]{1,0:T(8,128)(2,1)S(1)}, bf16[96,640]{1,0:T(8,128)(2,1)S(1)}, u32[]{:S(2)}, u32[]{:S(2)}) collective-permute-start(bf16[96,640]{1,0:T(8,128)(2,1)S(1)} %add_convert_fusion.1.refs_3_), channel_id=1, source_target_pairs={{0,96},{1,97},{2,98},{3,99},{4,36},{5,37},{6,38},{7,39},{8,104},{9... | collective-permute-start | bytes 368648 | tf_op jit(solution)/shard_map/ppermute | solution.py:43
  72.6 6.1 %collective-permute-start.23 = (bf16[96,640]{1,0:T(8,128)(2,1)S(1)}, bf16[96,640]{1,0:T(8,128)(2,1)S(1)}, u32[]{:S(2)}, u32[]{:S(2)}) collective-permute-start(bf16[96,640]{1,0:T(8,128)(2,1)S(1)} %add_convert_fusion.1.refs_3_), channel_id=1, source_target_pairs={{0,120},{1,121},{2,122},{3,123},{4,44},{5,45},{6,46},{7,47},{8,112... | collective-permute-start | bytes 368648 | tf_op jit(solution)/shard_map/ppermute | solution.py:43
  84.6 12.1 %collective-permute-start.31 = (bf16[384,640]{1,0:T(8,128)(2,1)S(1)}, bf16[384,640]{1,0:T(8,128)(2,1)S(1)}, u32[]{:S(2)}, u32[]{:S(2)}) collective-permute-start(bf16[384,640]{1,0:T(8,128)(2,1)S(1)} %newton.1.refs_0_), channel_id=1, source_target_pairs={{0,40},{1,41},{2,42},{3,43},{4,124},{5,125},{6,126},{7,127},{8,32}... | collective-permute-start | bytes 1474568 | tf_op jit(solution)/shard_map/ppermute | solution.py:43
  85.6 17.4 %collective-permute-start.29 = (bf16[384,640]{1,0:T(8,128)(2,1)S(1)}, bf16[384,640]{1,0:T(8,128)(2,1)S(1)}, u32[]{:S(2)}, u32[]{:S(2)}) collective-permute-start(bf16[384,640]{1,0:T(8,128)(2,1)S(1)} %newton.1.refs_0_), channel_id=1, source_target_pairs={{0,32},{1,33},{2,34},{3,35},{4,100},{5,101},{6,102},{7,103},{8,40}... | collective-permute-start | bytes 1474568 | tf_op jit(solution)/shard_map/ppermute | solution.py:43
  87.7 20.8 %collective-permute-start.27 = (bf16[384,640]{1,0:T(8,128)(2,1)S(1)}, bf16[384,640]{1,0:T(8,128)(2,1)S(1)}, u32[]{:S(2)}, u32[]{:S(2)}) collective-permute-start(bf16[384,640]{1,0:T(8,128)(2,1)S(1)} %newton.1.refs_0_), channel_id=1, source_target_pairs={{0,8},{1,9},{2,10},{3,11},{4,28},{5,29},{6,30},{7,31},{8,0},{9,1},... | collective-permute-start | bytes 1474568 | tf_op jit(solution)/shard_map/ppermute | solution.py:43
  90.0 21.8 %collective-permute-start.26 = (bf16[384,640]{1,0:T(8,128)(2,1)S(1)}, bf16[384,640]{1,0:T(8,128)(2,1)S(1)}, u32[]{:S(2)}, u32[]{:S(2)}) collective-permute-start(bf16[384,640]{1,0:T(8,128)(2,1)S(1)} %newton.1.refs_0_), channel_id=1, source_target_pairs={{0,4},{1,5},{2,6},{3,7},{4,0},{5,1},{6,2},{7,3},{8,12},{9,13},{10,... | collective-permute-start | bytes 1474568 | tf_op jit(solution)/shard_map/ppermute | solution.py:43
  96.6 15.2 %collective-permute-start.32 = (bf16[384,640]{1,0:T(8,128)(2,1)S(1)}, bf16[384,640]{1,0:T(8,128)(2,1)S(1)}, u32[]{:S(2)}, u32[]{:S(2)}) collective-permute-start(bf16[384,640]{1,0:T(8,128)(2,1)S(1)} %collective-permute-done.31.refs_3_), channel_id=1, source_target_pairs={{0,4},{1,5},{2,6},{3,7},{4,0},{5,1},{6,2},{7,3},{8,12},{9,13},{10,... | collective-permute-start | bytes 1474568 | tf_op jit(solution)/shard_map/ppermute | solution.py:43
  103.0 8.9 %collective-permute-start.30 = (bf16[384,640]{1,0:T(8,128)(2,1)S(1)}, bf16[384,640]{1,0:T(8,128)(2,1)S(1)}, u32[]{:S(2)}, u32[]{:S(2)}) collective-permute-start(bf16[384,640]{1,0:T(8,128)(2,1)S(1)} %collective-permute-done.29.refs_2_), channel_id=1, source_target_pairs={{0,4},{1,5},{2,6},{3,7},{4,0},{5,1},{6,2},{7,3},{8,12},{9,13},{10,... | collective-permute-start | bytes 1474568 | tf_op jit(solution)/shard_map/ppermute | solution.py:43
  108.5 3.4 %collective-permute-start.28 = (bf16[384,640]{1,0:T(8,128)(2,1)S(1)}, bf16[384,640]{1,0:T(8,128)(2,1)S(1)}, u32[]{:S(2)}, u32[]{:S(2)}) collective-permute-start(bf16[384,640]{1,0:T(8,128)(2,1)S(1)} %collective-permute-done.27.refs_1_), channel_id=1, source_target_pairs={{0,4},{1,5},{2,6},{3,7},{4,0},{5,1},{6,2},{7,3},{8,12},{9,13},{10,... | collective-permute-start | bytes 1474568 | tf_op jit(solution)/shard_map/ppermute | solution.py:43

commit v7 on v6

--- a/solution.py
+++ b/solution.py
@@ -56,7 +56,19 @@
 
 
 def to_slab(array, step):
-    return move(array, lambda zl, x, y, c, t: (zl, x, y, c, t ^ 1 if c == step else 3 - t))
+    return move(array, lambda zl, x, y, c, t: (zl, x, y, c, 3 - t if c == step else t ^ 1))
+
+
+def gather_across(array):
+    found = {}
+    for device in range(256):
+        zl, x, y, c, t = device_at(device)
+        a, b = 2 * bit_a(x) + bit_a(y), 2 * bit_b(x) + bit_b(y)
+        place, across = (a, b) if c == 0 else (b, a)
+        found.setdefault((c, zl, t, place), {})[across] = device
+    groups = [[found[key][across] for across in range(RING)] for key in sorted(found)]
+    array = jnp.broadcast_to(array[None], (RING, *array.shape))
+    return lax.all_to_all(array, AXES, 0, 0, axis_index_groups=groups, tiled=True)
 
 
 def to_z_neighbour(array):
@@ -78,8 +90,8 @@
     for half in range(2):
         *own, sent = outs[(RING + 1) * half : (RING + 1) * (half + 1)]
         for side in (1, 0):
-            first = jnp.where(core == side, t ^ 1, 3 - t)
-            second = jnp.where(core == side, 3 - t, t ^ 1)
+            first = jnp.where(core == side, 3 - t, t ^ 1)
+            second = jnp.where(core == side, t ^ 1, 3 - t)
             for flip in range(RING):
                 place = (across if side else mine) ^ flip
                 for rank, slab in enumerate((t, second) if half else (first, t ^ 2)):
@@ -122,13 +134,11 @@
             outs[flip][slab] = tri[pl.ds(start, CHUNK), :].astype(jnp.bfloat16)
 
 
-def newton_kernel(tokens_all, dev, newton_steps, *refs):
-    ins, (out, total, mixed, gap, mixed_half, gap_half) = refs[:RING], refs[RING:]
+def newton_kernel(
+    tokens_all, dev, newton_steps, total, out, mixed, gap, mixed_half, gap_half
+):
     t = dev[0] % 4
-    core, place, across = here(dev)
-    for flip in range(RING):
-        start = pl.multiple_of((across ^ flip) * CHUNK, 32)
-        total[pl.ds(start, CHUNK), :] = ins[3 - flip][...]
+    core, place, _ = here(dev)
     steps = newton_steps[core, place // 2, 2 * t + place % 2]
     eye = (
         lax.broadcasted_iota(jnp.int32, (BLOCK, BLOCK), 0)
@@ -191,21 +201,12 @@
 
 
 def apply_kernel(side, dev, *refs):
-    ins, grads, outs = refs[:RING], refs[RING : RING + 2], refs[-8:-6]
-    ins_here, outs_here, whole, sem = refs[-6:-4], refs[-4:-2], refs[-2], refs[-1]
+    ins, grads, outs = refs[:RING], refs[RING : RING + 2], refs[-6:-4]
+    outs_here, whole, sem = refs[-4:-2], refs[-2], refs[-1]
     core, mine, across = here(dev)
     layer = core ^ side
     mine = across if side else mine
-    loads = [
-        pltpu.make_async_copy(grad.at[layer], place, sem.at[kind])
-        for kind, (grad, place) in enumerate(zip(grads, ins_here))
-    ]
-    stores = [
-        pltpu.make_async_copy(place, out.at[layer], sem.at[2 + kind])
-        for kind, (out, place) in enumerate(zip(outs, outs_here))
-    ]
-    for load in loads:
-        load.start()
+    stores = []
 
     def unfold(block, place):
         for i, (row, col) in enumerate(PANELS):
@@ -227,12 +228,13 @@
         unfold(ins[flip], mine ^ flip)
     for place in range(RING):
         kind, j = place // 2, place % 2
-        if j == 0:
-            loads[kind].wait()
         at = j * BLOCK
-        rows = ins_here[kind]
-        part_0, part_1 = rows[:, at : at + 256], rows[:, at + 256 : at + 512]
-        part_2, part_12 = rows[:, at + 512 : at + 640], rows[:, at + 256 : at + 640]
+
+        def columns(start, stop):
+            return grads[kind][layer, :, at + start : at + stop]
+
+        part_0, part_1 = columns(0, 256), columns(256, 512)
+        part_2, part_12 = columns(512, 640), columns(256, 640)
         top = dot(part_0, whole[place, 0:256, :])
         middle = dot(part_1, whole[place, 256:512, 256:])
         low = dot(part_2, whole[place, 512:640, 512:])
@@ -246,8 +248,13 @@
         outs_here[kind][:, at : at + 256] = left.astype(jnp.bfloat16)
         outs_here[kind][:, at + 256 : at + 512] = centre.astype(jnp.bfloat16)
         outs_here[kind][:, at + 512 : at + 640] = right.astype(jnp.bfloat16)
-        if j == 1:
-            stores[kind].start()
+        done = pl.ds(at, BLOCK)
+        stores.append(
+            pltpu.make_async_copy(
+                outs_here[kind].at[:, done], outs[kind].at[layer, :, done], sem.at[place]
+            )
+        )
+        stores[-1].start()
     for store in stores:
         store.wait()
 
@@ -299,15 +306,14 @@
     sums = factors(packed[RING + 1 : -1], packed[-1]) + wide(leaving)
     sums = sums[0] + wide(to_slab(sums[1].astype(half), 1))
     sums = sums + wide(to_z_neighbour(sums.astype(half)))
-    members = over_square([sums.astype(half)] * RING, False)
+    total = gather_across(sums.astype(half)).reshape(PACK, BLOCK)
 
     inverse = pl.pallas_call(
         functools.partial(newton_kernel, tokens_all),
         out_shape=shape(PACK, BLOCK),
-        in_specs=[SMEM, SMEM] + [VMEM] * RING,
+        in_specs=[SMEM, SMEM, VMEM],
         out_specs=VMEM,
         scratch_shapes=[
-            pltpu.VMEM((PACK, BLOCK), half),
             pltpu.VMEM((BLOCK, BLOCK), jnp.float32),
             pltpu.VMEM((BLOCK, BLOCK), jnp.float32),
             pltpu.VMEM((2, BLOCK, BLOCK), half),
@@ -315,7 +321,7 @@
         ],
         compiler_params=PARAMS,
         name="newton",
-    )(dev, newton_steps, *members[::-1])
+    )(dev, newton_steps, total)
     mine = over_square([inverse] * RING, True)
     others = [to_other_core(block) for block in mine]
 
@@ -325,11 +331,10 @@
         return pl.pallas_call(
             functools.partial(apply_kernel, side),
             out_shape=[shape(*dims) for dims in kinds],
-            in_specs=[SMEM] + [VMEM] * RING + [ANY] * (2 + len(before)),
+            in_specs=[SMEM] + [VMEM] * (RING + 2) + [ANY] * len(before),
             out_specs=[ANY] * 2,
             input_output_aliases={7: 0, 8: 1} if before else {},
             scratch_shapes=buffers
-            + buffers
             + [
                 pltpu.VMEM((RING, BLOCK, BLOCK), half),
                 pltpu.SemaphoreType.DMA((4,)),

time: 115 us -> 117 us (1.017)
  blocking collectives: 0 us -> 8.41 us
  starting transfers between devices: 64 us -> 60.3 us
  Pallas kernels: 19.1 us -> 17.5 us
    all_to_all x0 -> x1, blocking collectives: none -> 8.41 us  [gather_across(): lax.all_to_all(array, AXES, 0, 0, axis_index_groups=groups, tiled=True)]
    ppermute x33 -> x30, starting transfers between devices: 64 us -> 60.3 us  [move(): return lax.ppermute(array, AXES, pairs)]
    pallas_call x2, Pallas kernels: 6.63 us -> 5.18 us  [apply(): pl.pallas_call(functools.partial(apply_kernel, side), out_shape=[shape(*d...]
    ppermute x33 -> x30, waiting for transfers between devices: 30.6 us -> 29.5 us  [move(): return lax.ppermute(array, AXES, pairs)]
  transfers between devices with their start and end apart: 33 -> 30, of which waited for: 12 -> 10; matrix products, arithmetic and copies ran while one was open for 0% -> 0% of each run, Pallas kernels for 6% -> 5%
where the time goes in v7:
time: 117 us
  starting transfers between devices  60.3 us (52%)
  waiting for transfers between devices  29.5 us (25%)
  Pallas kernels  17.5 us (15%)
  blocking collectives  8.41 us (7%)
    ppermute x30, starting transfers between devices, move(): return lax.ppermute(array, AXES, pairs)  60.3 us
    ppermute x30, waiting for transfers between devices, move(): return lax.ppermute(array, AXES, pairs)  29.5 us
    all_to_all x1, blocking collectives, gather_across(): lax.all_to_all(array, AXES, 0, 0, axis_index_groups=groups, tiled=True)  8.41 us
    pallas_call x1, Pallas kernels, local(): pl.pallas_call(functools.partial(newton_kernel, tokens_all), out_shape=sh...  5.76 us
    pallas_call x2, Pallas kernels, apply(): pl.pallas_call(functools.partial(apply_kernel, side), out_shape=[shape(*d...  5.18 us
    pallas_call x2, Pallas kernels, factors(): pl.pallas_call(gram_kernel, out_shape=[shape(2, CHUNK, BLOCK)] * RING, in...  3.59 us
    pallas_call x1, Pallas kernels, local(): pl.pallas_call(pack_kernel, out_shape=([shape(*part)] * RING + [shape(RIN...  2.97 us
  transfers between devices with their start and end apart: 30, of which 10 were waited for; matrix products, arithmetic and copies ran while one was open for 0% of the time, Pallas kernels for 5%

profile of v7, /device:TPU:1, one launch (start us, length us, event | category | flops | bytes accessed | tf_op | source)
XLA Modules:
  0.0 117.3 jit_solution(13201863998949826974)
XLA Ops:
  0.6 3.0 %pack.1 = (bf16[2,128,640]{2,1,0:T(8,128)(2,1)S(1)}, bf16[2,128,640]{2,1,0:T(8,128)(2,1)S(1)}, bf16[2,128,640]{2,1,0:T(8,128)(2,1)S(1)}, bf16[2,128,640]{2,1,0:T...) custom-call(s32[1]{0:T(128)} %bitcast.dev, ...), custom_call_target="tpu_custom_call" | custom-call | tf_op jit(solution)/shard_map/pack/pallas_call | solution.py:279
  3.6 3.3 %collective-permute-start.13 = (bf16[4,2,128,640]{3,2,1,0:T(8,128)(2,1)S(1)}, bf16[4,2,128,640]{3,2,1,0:T(8,128)(2,1)S(1)}, u32[]{:S(2)}, u32[]{:S(2)}) collective-permute-start(bf16[4,2,128,640]{3,2,1,0:T(8,128)(2,1)S(1)} %get-tuple-element.35), channel_id=1, source_target_pairs={{0,4},{1,5},{2,6},{3,7},{4,0},{5,1},{6,2},{7,3},{8,12},{9,13},{10,... | collective-permute-start | bytes 3932168 | tf_op jit(solution)/shard_map/ppermute | solution.py:43
  6.9 0.1 collective-permute-start.3
  7.0 3.2 %collective-permute-start = (bf16[2,128,640]{2,1,0:T(8,128)(2,1)S(1)}, bf16[2,128,640]{2,1,0:T(8,128)(2,1)S(1)}, u32[]{:S(2)}, u32[]{:S(2)}) collective-permute-start(bf16[2,128,640]{2,1,0:T(8,128)(2,1)S(1)} %get-tuple-element.22), channel_id=1, source_target_pairs={{0,40},{1,41},{2,42},{3,43},{4,124},{5,125},{6,126},{7,127},{8,32}... | collective-permute-start | bytes 983048 | tf_op jit(solution)/shard_map/ppermute | solution.py:43
  10.2 1.6 %collective-permute-start.10 = (bf16[2,128,640]{2,1,0:T(8,128)(2,1)S(1)}, bf16[2,128,640]{2,1,0:T(8,128)(2,1)S(1)}, u32[]{:S(2)}, u32[]{:S(2)}) collective-permute-start(bf16[2,128,640]{2,1,0:T(8,128)(2,1)S(1)} %get-tuple-element.31), channel_id=1, source_target_pairs={{0,40},{1,41},{2,42},{3,43},{4,124},{5,125},{6,126},{7,127},{8,32}... | collective-permute-start | bytes 983048 | tf_op jit(solution)/shard_map/ppermute | solution.py:43
  11.8 0.7 collective-permute-start.11
  12.6 0.0 collective-permute-done.13.refs_7_
  12.6 2.7 %collective-permute-start.12 = (bf16[2,128,640]{2,1,0:T(8,128)(2,1)S(1)}, bf16[2,128,640]{2,1,0:T(8,128)(2,1)S(1)}, u32[]{:S(2)}, u32[]{:S(2)}) collective-permute-start(bf16[2,128,640]{2,1,0:T(8,128)(2,1)S(1)} %get-tuple-element.33), channel_id=1, source_target_pairs={{0,8},{1,9},{2,10},{3,11},{4,28},{5,29},{6,30},{7,31},{8,0},{9,1},... | collective-permute-start | bytes 983048 | tf_op jit(solution)/shard_map/ppermute | solution.py:43
  15.3 0.1 slice_bitcast_fusion
  15.4 0.9 collective-permute-done.refs_0_
  16.3 1.0 collective-permute-start.16
  17.3 2.6 %collective-permute-done.10.refs_0_ = bf16[2,128,640]{2,1,0:T(8,128)(2,1)S(1)} collective-permute-done((bf16[2,128,640]{2,1,0:T(8,128)(2,1)S(1)}, bf16[2,128,640]{2,1,0:T(8,128)(2,1)S(1)}, u32[]{:S(2)}, u32[]{:S(2)}) %collective-permute-start.10) | collective-permute-done | bytes 327712 | tf_op jit(solution)/shard_map/ppermute | solution.py:43
  19.9 0.7 collective-permute-start.15
  20.6 2.6 %collective-permute-start.14 = (bf16[2,128,640]{2,1,0:T(8,128)(2,1)S(1)}, bf16[2,128,640]{2,1,0:T(8,128)(2,1)S(1)}, u32[]{:S(2)}, u32[]{:S(2)}) collective-permute-start(bf16[2,128,640]{2,1,0:T(8,128)(2,1)S(1)} %get-tuple-element.47), channel_id=1, source_target_pairs={{0,40},{1,41},{2,42},{3,43},{4,124},{5,125},{6,126},{7,127},{8,32}... | collective-permute-start | bytes 983048 | tf_op jit(solution)/shard_map/ppermute | solution.py:43
  23.3 0.1 slice_bitcast_fusion.3
  23.4 0.0 collective-permute-done.11.refs_1_
  23.4 2.6 %collective-permute-start.1 = (bf16[2,128,640]{2,1,0:T(8,128)(2,1)S(1)}, bf16[2,128,640]{2,1,0:T(8,128)(2,1)S(1)}, u32[]{:S(2)}, u32[]{:S(2)}) collective-permute-start(bf16[2,128,640]{2,1,0:T(8,128)(2,1)S(1)} %get-tuple-element.23), channel_id=1, source_target_pairs={{0,32},{1,33},{2,34},{3,35},{4,100},{5,101},{6,102},{7,103},{8,40}... | collective-permute-start | bytes 983048 | tf_op jit(solution)/shard_map/ppermute | solution.py:43
  26.0 0.0 collective-permute-done.12.refs_2_
  26.0 0.0 collective-permute-start.2
  26.0 1.0 collective-permute-done.16.refs_6_
  27.0 1.7 %collective-permute-start.6 = (bf16[2,128,640]{2,1,0:T(8,128)(2,1)S(1)}, bf16[2,128,640]{2,1,0:T(8,128)(2,1)S(1)}, u32[]{:S(2)}, u32[]{:S(2)}) collective-permute-start(bf16[2,128,640]{2,1,0:T(8,128)(2,1)S(1)} %get-tuple-element.42), channel_id=1, source_target_pairs={{0,8},{1,9},{2,10},{3,11},{4,28},{5,29},{6,30},{7,31},{8,0},{9,1},... | collective-permute-start | bytes 983048 | tf_op jit(solution)/shard_map/ppermute | solution.py:43
  28.7 0.0 collective-permute-done.15.refs_5_
  28.7 1.8 %collective-permute-start.5 = (bf16[2,128,640]{2,1,0:T(8,128)(2,1)S(1)}, bf16[2,128,640]{2,1,0:T(8,128)(2,1)S(1)}, u32[]{:S(2)}, u32[]{:S(2)}) collective-permute-start(bf16[2,128,640]{2,1,0:T(8,128)(2,1)S(1)} %get-tuple-element.43), channel_id=1, source_target_pairs={{0,32},{1,33},{2,34},{3,35},{4,100},{5,101},{6,102},{7,103},{8,40}... | collective-permute-start | bytes 983048 | tf_op jit(solution)/shard_map/ppermute | solution.py:43
  30.4 0.9 collective-permute-done.14.refs_4_
  31.4 2.3 %collective-permute-start.4 = (bf16[2,128,640]{2,1,0:T(8,128)(2,1)S(1)}, bf16[2,128,640]{2,1,0:T(8,128)(2,1)S(1)}, u32[]{:S(2)}, u32[]{:S(2)}) collective-permute-start(bf16[2,128,640]{2,1,0:T(8,128)(2,1)S(1)} %get-tuple-element.44), channel_id=1, source_target_pairs={{0,40},{1,41},{2,42},{3,43},{4,124},{5,125},{6,126},{7,127},{8,32}... | collective-permute-start | bytes 983048 | tf_op jit(solution)/shard_map/ppermute | solution.py:43
  33.7 1.8 %gram.3 = (bf16[2,96,640]{2,1,0:T(8,128)(2,1)S(1)}, bf16[2,96,640]{2,1,0:T(8,128)(2,1)S(1)}, bf16[2,96,640]{2,1,0:T(8,128)(2,1)S(1)}, bf16[2,96,640]{2,1,0:T(8,128)(2,1)S(1)}) custom-call(s32[1]{0:T(128)} %bitcast.dev, bf16[2,128,640]{2,1,0:T(8,128)(2,1)S(1)} %collective-permute-done.10.refs_0_, bf16[2,128,640]{2,1,0:T(8,128)(2,1)S(1)} %collective-permute-done.11.refs_1_, ...), custom_call_target="tpu_custom_call" | custom-call | tf_op jit(solution)/shard_map/gram/pallas_call | solution.py:293
  35.5 0.0 collective-permute-done.1.refs_1_
  35.5 0.1 collective-permute-start.17
  35.6 0.1 collective-permute-start.18
  35.7 2.7 %collective-permute-done.6.refs_6_ = bf16[2,128,640]{2,1,0:T(8,128)(2,1)S(1)} collective-permute-done((bf16[2,128,640]{2,1,0:T(8,128)(2,1)S(1)}, bf16[2,128,640]{2,1,0:T(8,128)(2,1)S(1)}, u32[]{:S(2)}, u32[]{:S(2)}) %collective-permute-start.6) | collective-permute-done | bytes 327712 | tf_op jit(solution)/shard_map/ppermute | solution.py:43
  38.4 0.0 collective-permute-start.19
  38.4 6.0 %collective-permute-done.4.refs_4_ = bf16[2,128,640]{2,1,0:T(8,128)(2,1)S(1)} collective-permute-done((bf16[2,128,640]{2,1,0:T(8,128)(2,1)S(1)}, bf16[2,128,640]{2,1,0:T(8,128)(2,1)S(1)}, u32[]{:S(2)}, u32[]{:S(2)}) %collective-permute-start.4) | collective-permute-done | bytes 327712 | tf_op jit(solution)/shard_map/ppermute | solution.py:43
  44.4 1.8 %gram.2 = (bf16[2,96,640]{2,1,0:T(8,128)(2,1)S(1)}, bf16[2,96,640]{2,1,0:T(8,128)(2,1)S(1)}, bf16[2,96,640]{2,1,0:T(8,128)(2,1)S(1)}, bf16[2,96,640]{2,1,0:T(8,128)(2,1)S(1)}) custom-call(s32[1]{0:T(128)} %bitcast.dev, bf16[2,128,640]{2,1,0:T(8,128)(2,1)S(1)} %collective-permute-done.refs_0_, bf16[2,128,640]{2,1,0:T(8,128)(2,1)S(1)} %collective-permute-done.1.refs_1_, ...), custom_call_target="tpu_custom_call" | custom-call | tf_op jit(solution)/shard_map/gram/pallas_call | solution.py:293
  46.2 0.1 collective-permute-start.7
  46.3 0.1 collective-permute-start.8
  46.5 2.5 %collective-permute-start.9 = (bf16[2,96,640]{2,1,0:T(8,128)(2,1)S(1)}, bf16[2,96,640]{2,1,0:T(8,128)(2,1)S(1)}, u32[]{:S(2)}, u32[]{:S(2)}) collective-permute-start(bf16[2,96,640]{2,1,0:T(8,128)(2,1)S(1)} %get-tuple-element.29), channel_id=1, source_target_pairs={{0,24},{1,25},{2,26},{3,27},{4,12},{5,13},{6,14},{7,15},{8,16},{9,... | collective-permute-start | bytes 737288 | tf_op jit(solution)/shard_map/ppermute | solution.py:43
  49.0 0.0 collective-permute-done.18
  49.0 0.0 collective-permute-done.19
  49.0 0.1 add_convert_fusion
  49.1 3.7 %collective-permute-start.20 = (bf16[2,96,640]{2,1,0:T(8,128)(2,1)S(1)}, bf16[2,96,640]{2,1,0:T(8,128)(2,1)S(1)}, u32[]{:S(2)}, u32[]{:S(2)}) collective-permute-start(bf16[2,96,640]{2,1,0:T(8,128)(2,1)S(1)} %add_convert_fusion), channel_id=1, source_target_pairs={{0,3},{1,2},{2,1},{3,0},{4,5},{5,4},{6,7},{7,6},{8,11},{9,10},{10,... | collective-permute-start | bytes 737288 | tf_op jit(solution)/shard_map/ppermute | solution.py:43
  52.8 0.0 collective-permute-done.7
  52.8 0.0 collective-permute-done.8
  52.8 2.1 %collective-permute-done.9 = bf16[2,96,640]{2,1,0:T(8,128)(2,1)S(1)} collective-permute-done((bf16[2,96,640]{2,1,0:T(8,128)(2,1)S(1)}, bf16[2,96,640]{2,1,0:T(8,128)(2,1)S(1)}, u32[]{:S(2)}, u32[]{:S(2)}) %collective-permute-start.9) | collective-permute-done | bytes 245792 | tf_op jit(solution)/shard_map/ppermute | solution.py:43
  54.9 4.3 %collective-permute-done.20 = bf16[2,96,640]{2,1,0:T(8,128)(2,1)S(1)} collective-permute-done((bf16[2,96,640]{2,1,0:T(8,128)(2,1)S(1)}, bf16[2,96,640]{2,1,0:T(8,128)(2,1)S(1)}, u32[]{:S(2)}, u32[]{:S(2)}) %collective-permute-start.20) | collective-permute-done | bytes 245792 | tf_op jit(solution)/shard_map/ppermute | solution.py:43
  59.2 0.1 convert_add_fusion
  59.3 0.0 copy-start.2
  59.4 5.7 %collective-permute-start.21 = (bf16[96,640]{1,0:T(8,128)(2,1)S(1)}, bf16[96,640]{1,0:T(8,128)(2,1)S(1)}, u32[]{:S(2)}, u32[]{:S(2)}) collective-permute-start(bf16[96,640]{1,0:T(8,128)(2,1)S(1)} %fusion.2), channel_id=1, source_target_pairs={{0,1},{1,0},{2,3},{3,2},{4,7},{5,6},{6,5},{7,4},{8,9},{9,8},{10,11... | collective-permute-start | bytes 368648 | tf_op jit(solution)/shard_map/ppermute | solution.py:43
  65.0 3.6 %collective-permute-done.21 = bf16[96,640]{1,0:T(8,128)(2,1)S(1)} collective-permute-done((bf16[96,640]{1,0:T(8,128)(2,1)S(1)}, bf16[96,640]{1,0:T(8,128)(2,1)S(1)}, u32[]{:S(2)}, u32[]{:S(2)}) %collective-permute-start.21) | collective-permute-done | bytes 122912 | tf_op jit(solution)/shard_map/ppermute | solution.py:43
  68.7 0.1 collective-permute-start.22
  68.8 5.3 %collective-permute-done.22 = bf16[96,640]{1,0:T(8,128)(2,1)S(1)} collective-permute-done((bf16[96,640]{1,0:T(8,128)(2,1)S(1)}, bf16[96,640]{1,0:T(8,128)(2,1)S(1)}, u32[]{:S(2)}, u32[]{:S(2)}) %collective-permute-start.22) | collective-permute-done | bytes 122912 | tf_op jit(solution)/shard_map/ppermute | solution.py:43
  74.1 0.0 copy-start
  74.2 8.4 %all_to_all.5 = bf16[4,96,640]{2,1,0:T(8,128)(2,1)S(1)} all-to-all(bf16[4,96,640]{2,1,0:T(8,128)(2,1)S(1)} %broadcast_in_dim.2), channel_id=1, replica_groups={{0,24,96,120},{8,16,104,112},{32,56,64,88},{40,48,72,80},{1,25,97,121},..., dimensions={0} | all-to-all | bytes 983040 | tf_op jit(solution)/shard_map/all_to_all | solution.py:71
  82.6 5.8 %newton.1.refs_0_ = bf16[384,640]{1,0:T(8,128)(2,1)S(1)} custom-call(s32[1]{0:T(128)} %bitcast.dev, s32[2,2,8]{2,1,0:T(2,128)S(1)} %copy-done.2, bf16[384,640]{1,0:T(8,128)(2,1)S(1)} %bitcast.24), custom_call_target="tpu_custom_call" | custom-call | tf_op jit(solution)/shard_map/newton/pallas_call | solution.py:311
  88.4 0.1 collective-permute-start.28
  88.5 3.2 %collective-permute-start.26 = (bf16[384,640]{1,0:T(8,128)(2,1)S(1)}, bf16[384,640]{1,0:T(8,128)(2,1)S(1)}, u32[]{:S(2)}, u32[]{:S(2)}) collective-permute-start(bf16[384,640]{1,0:T(8,128)(2,1)S(1)} %newton.1.refs_0_), channel_id=1, source_target_pairs={{0,32},{1,33},{2,34},{3,35},{4,100},{5,101},{6,102},{7,103},{8,40}... | collective-permute-start | bytes 1474568 | tf_op jit(solution)/shard_map/ppermute | solution.py:43
  91.6 2.3 %collective-permute-start.24 = (bf16[384,640]{1,0:T(8,128)(2,1)S(1)}, bf16[384,640]{1,0:T(8,128)(2,1)S(1)}, u32[]{:S(2)}, u32[]{:S(2)}) collective-permute-start(bf16[384,640]{1,0:T(8,128)(2,1)S(1)} %newton.1.refs_0_), channel_id=1, source_target_pairs={{0,8},{1,9},{2,10},{3,11},{4,28},{5,29},{6,30},{7,31},{8,0},{9,1},... | collective-permute-start | bytes 1474568 | tf_op jit(solution)/shard_map/ppermute | solution.py:43
  93.9 5.9 %collective-permute-start.23 = (bf16[384,640]{1,0:T(8,128)(2,1)S(1)}, bf16[384,640]{1,0:T(8,128)(2,1)S(1)}, u32[]{:S(2)}, u32[]{:S(2)}) collective-permute-start(bf16[384,640]{1,0:T(8,128)(2,1)S(1)} %newton.1.refs_0_), channel_id=1, source_target_pairs={{0,4},{1,5},{2,6},{3,7},{4,0},{5,1},{6,2},{7,3},{8,12},{9,13},{10,... | collective-permute-start | bytes 1474568 | tf_op jit(solution)/shard_map/ppermute | solution.py:43
  99.8 0.0 collective-permute-done.28.refs_3_
  99.8 5.4 %collective-permute-start.29 = (bf16[384,640]{1,0:T(8,128)(2,1)S(1)}, bf16[384,640]{1,0:T(8,128)(2,1)S(1)}, u32[]{:S(2)}, u32[]{:S(2)}) collective-permute-start(bf16[384,640]{1,0:T(8,128)(2,1)S(1)} %collective-permute-done.28.refs_3_), channel_id=1, source_target_pairs={{0,4},{1,5},{2,6},{3,7},{4,0},{5,1},{6,2},{7,3},{8,12},{9,13},{10,... | collective-permute-start | bytes 1474568 | tf_op jit(solution)/shard_map/ppermute | solution.py:43
  105.2 0.0 collective-permute-done.26.refs_2_
  105.2 6.7 %collective-permute-start.27 = (bf16[384,640]{1,0:T(8,128)(2,1)S(1)}, bf16[384,640]{1,0:T(8,128)(2,1)S(1)}, u32[]{:S(2)}, u32[]{:S(2)}) collective-permute-start(bf16[384,640]{1,0:T(8,128)(2,1)S(1)} %collective-permute-done.26.refs_2_), channel_id=1, source_target_pairs={{0,4},{1,5},{2,6},{3,7},{4,0},{5,1},{6,2},{7,3},{8,12},{9,13},{10,... | collective-permute-start | bytes 1474568 | tf_op jit(solution)/shard_map/ppermute | solution.py:43
  111.9 0.0 collective-permute-start.25
  111.9 2.6 %apply.2 = (bf16[2,240,1280]{2,1,0:T(8,128)(2,1)}, bf16[2,320,1280]{2,1,0:T(8,128)(2,1)}) custom-call(s32[1]{0:T(128)} %bitcast.dev, bf16[384,640]{1,0:T(8,128)(2,1)S(1)} %newton.1.refs_0_, bf16[384,640]{1,0:T(8,128)(2,1)S(1)} %collective-permute-done.24.refs_1_, bf16[384,640]{1,0:T(8,128)(2,1)S(1)} %collective-permute-done.26.refs_2_, ...), custom_call_target="tpu_custom_call" | custom-call | tf_op jit(solution)/shard_map/apply/pallas_call | solution.py:331
  114.6 2.6 %apply.3 = (bf16[2,240,1280]{2,1,0:T(8,128)(2,1)}, bf16[2,320,1280]{2,1,0:T(8,128)(2,1)}) custom-call(s32[1]{0:T(128)} %bitcast.dev, bf16[384,640]{1,0:T(8,128)(2,1)S(1)} %collective-permute-done.23.refs_0_, bf16[384,640]{1,0:T(8,128)(2,1)S(1)} %collective-permute-done.25.refs_1_, ...), custom_call_target="tpu_custom_call", output_to_operand_aliasing={{0}: (7, {}), {1}: (8, {})} | custom-call | tf_op jit(solution)/shard_map/apply/pallas_call | solution.py:331
  (17 shorter events, 0.2 us)
Async XLA Ops:
  3.6 9.0 %collective-permute-start.13 = (bf16[4,2,128,640]{3,2,1,0:T(8,128)(2,1)S(1)}, bf16[4,2,128,640]{3,2,1,0:T(8,128)(2,1)S(1)}, u32[]{:S(2)}, u32[]{:S(2)}) collective-permute-start(bf16[4,2,128,640]{3,2,1,0:T(8,128)(2,1)S(1)} %get-tuple-element.35), channel_id=1, source_target_pairs={{0,4},{1,5},{2,6},{3,7},{4,0},{5,1},{6,2},{7,3},{8,12},{9,13},{10,... | collective-permute-start | bytes 3932168 | tf_op jit(solution)/shard_map/ppermute | solution.py:43
  6.9 13.7 %collective-permute-start.3 = (bf16[4,2,128,640]{3,2,1,0:T(8,128)(2,1)S(1)}, bf16[4,2,128,640]{3,2,1,0:T(8,128)(2,1)S(1)}, u32[]{:S(2)}, u32[]{:S(2)}) collective-permute-start(bf16[4,2,128,640]{3,2,1,0:T(8,128)(2,1)S(1)} %get-tuple-element.26), channel_id=1, source_target_pairs={{0,4},{1,5},{2,6},{3,7},{4,0},{5,1},{6,2},{7,3},{8,12},{9,13},{10,... | collective-permute-start | bytes 3932168 | tf_op jit(solution)/shard_map/ppermute | solution.py:43
  7.0 9.2 %collective-permute-start = (bf16[2,128,640]{2,1,0:T(8,128)(2,1)S(1)}, bf16[2,128,640]{2,1,0:T(8,128)(2,1)S(1)}, u32[]{:S(2)}, u32[]{:S(2)}) collective-permute-start(bf16[2,128,640]{2,1,0:T(8,128)(2,1)S(1)} %get-tuple-element.22), channel_id=1, source_target_pairs={{0,40},{1,41},{2,42},{3,43},{4,124},{5,125},{6,126},{7,127},{8,32}... | collective-permute-start | bytes 983048 | tf_op jit(solution)/shard_map/ppermute | solution.py:43
  10.2 9.7 %collective-permute-start.10 = (bf16[2,128,640]{2,1,0:T(8,128)(2,1)S(1)}, bf16[2,128,640]{2,1,0:T(8,128)(2,1)S(1)}, u32[]{:S(2)}, u32[]{:S(2)}) collective-permute-start(bf16[2,128,640]{2,1,0:T(8,128)(2,1)S(1)} %get-tuple-element.31), channel_id=1, source_target_pairs={{0,40},{1,41},{2,42},{3,43},{4,124},{5,125},{6,126},{7,127},{8,32}... | collective-permute-start | bytes 983048 | tf_op jit(solution)/shard_map/ppermute | solution.py:43
  11.8 11.6 %collective-permute-start.11 = (bf16[2,128,640]{2,1,0:T(8,128)(2,1)S(1)}, bf16[2,128,640]{2,1,0:T(8,128)(2,1)S(1)}, u32[]{:S(2)}, u32[]{:S(2)}) collective-permute-start(bf16[2,128,640]{2,1,0:T(8,128)(2,1)S(1)} %get-tuple-element.32), channel_id=1, source_target_pairs={{0,32},{1,33},{2,34},{3,35},{4,100},{5,101},{6,102},{7,103},{8,40}... | collective-permute-start | bytes 983048 | tf_op jit(solution)/shard_map/ppermute | solution.py:43
  12.6 13.4 %collective-permute-start.12 = (bf16[2,128,640]{2,1,0:T(8,128)(2,1)S(1)}, bf16[2,128,640]{2,1,0:T(8,128)(2,1)S(1)}, u32[]{:S(2)}, u32[]{:S(2)}) collective-permute-start(bf16[2,128,640]{2,1,0:T(8,128)(2,1)S(1)} %get-tuple-element.33), channel_id=1, source_target_pairs={{0,8},{1,9},{2,10},{3,11},{4,28},{5,29},{6,30},{7,31},{8,0},{9,1},... | collective-permute-start | bytes 983048 | tf_op jit(solution)/shard_map/ppermute | solution.py:43
  16.3 10.7 %collective-permute-start.16 = (bf16[2,128,640]{2,1,0:T(8,128)(2,1)S(1)}, bf16[2,128,640]{2,1,0:T(8,128)(2,1)S(1)}, u32[]{:S(2)}, u32[]{:S(2)}) collective-permute-start(bf16[2,128,640]{2,1,0:T(8,128)(2,1)S(1)} %get-tuple-element.45), channel_id=1, source_target_pairs={{0,8},{1,9},{2,10},{3,11},{4,28},{5,29},{6,30},{7,31},{8,0},{9,1},... | collective-permute-start | bytes 983048 | tf_op jit(solution)/shard_map/ppermute | solution.py:43
  19.9 8.8 %collective-permute-start.15 = (bf16[2,128,640]{2,1,0:T(8,128)(2,1)S(1)}, bf16[2,128,640]{2,1,0:T(8,128)(2,1)S(1)}, u32[]{:S(2)}, u32[]{:S(2)}) collective-permute-start(bf16[2,128,640]{2,1,0:T(8,128)(2,1)S(1)} %get-tuple-element.46), channel_id=1, source_target_pairs={{0,32},{1,33},{2,34},{3,35},{4,100},{5,101},{6,102},{7,103},{8,40}... | collective-permute-start | bytes 983048 | tf_op jit(solution)/shard_map/ppermute | solution.py:43
  20.6 10.7 %collective-permute-start.14 = (bf16[2,128,640]{2,1,0:T(8,128)(2,1)S(1)}, bf16[2,128,640]{2,1,0:T(8,128)(2,1)S(1)}, u32[]{:S(2)}, u32[]{:S(2)}) collective-permute-start(bf16[2,128,640]{2,1,0:T(8,128)(2,1)S(1)} %get-tuple-element.47), channel_id=1, source_target_pairs={{0,40},{1,41},{2,42},{3,43},{4,124},{5,125},{6,126},{7,127},{8,32}... | collective-permute-start | bytes 983048 | tf_op jit(solution)/shard_map/ppermute | solution.py:43
  23.4 12.1 %collective-permute-start.1 = (bf16[2,128,640]{2,1,0:T(8,128)(2,1)S(1)}, bf16[2,128,640]{2,1,0:T(8,128)(2,1)S(1)}, u32[]{:S(2)}, u32[]{:S(2)}) collective-permute-start(bf16[2,128,640]{2,1,0:T(8,128)(2,1)S(1)} %get-tuple-element.23), channel_id=1, source_target_pairs={{0,32},{1,33},{2,34},{3,35},{4,100},{5,101},{6,102},{7,103},{8,40}... | collective-permute-start | bytes 983048 | tf_op jit(solution)/shard_map/ppermute | solution.py:43
  26.0 9.6 %collective-permute-start.2 = (bf16[2,128,640]{2,1,0:T(8,128)(2,1)S(1)}, bf16[2,128,640]{2,1,0:T(8,128)(2,1)S(1)}, u32[]{:S(2)}, u32[]{:S(2)}) collective-permute-start(bf16[2,128,640]{2,1,0:T(8,128)(2,1)S(1)} %get-tuple-element.24), channel_id=1, source_target_pairs={{0,8},{1,9},{2,10},{3,11},{4,28},{5,29},{6,30},{7,31},{8,0},{9,1},... | collective-permute-start | bytes 983048 | tf_op jit(solution)/shard_map/ppermute | solution.py:43
  27.0 11.5 %collective-permute-start.6 = (bf16[2,128,640]{2,1,0:T(8,128)(2,1)S(1)}, bf16[2,128,640]{2,1,0:T(8,128)(2,1)S(1)}, u32[]{:S(2)}, u32[]{:S(2)}) collective-permute-start(bf16[2,128,640]{2,1,0:T(8,128)(2,1)S(1)} %get-tuple-element.42), channel_id=1, source_target_pairs={{0,8},{1,9},{2,10},{3,11},{4,28},{5,29},{6,30},{7,31},{8,0},{9,1},... | collective-permute-start | bytes 983048 | tf_op jit(solution)/shard_map/ppermute | solution.py:43
  28.7 9.8 %collective-permute-start.5 = (bf16[2,128,640]{2,1,0:T(8,128)(2,1)S(1)}, bf16[2,128,640]{2,1,0:T(8,128)(2,1)S(1)}, u32[]{:S(2)}, u32[]{:S(2)}) collective-permute-start(bf16[2,128,640]{2,1,0:T(8,128)(2,1)S(1)} %get-tuple-element.43), channel_id=1, source_target_pairs={{0,32},{1,33},{2,34},{3,35},{4,100},{5,101},{6,102},{7,103},{8,40}... | collective-permute-start | bytes 983048 | tf_op jit(solution)/shard_map/ppermute | solution.py:43
  31.4 13.1 %collective-permute-start.4 = (bf16[2,128,640]{2,1,0:T(8,128)(2,1)S(1)}, bf16[2,128,640]{2,1,0:T(8,128)(2,1)S(1)}, u32[]{:S(2)}, u32[]{:S(2)}) collective-permute-start(bf16[2,128,640]{2,1,0:T(8,128)(2,1)S(1)} %get-tuple-element.44), channel_id=1, source_target_pairs={{0,40},{1,41},{2,42},{3,43},{4,124},{5,125},{6,126},{7,127},{8,32}... | collective-permute-start | bytes 983048 | tf_op jit(solution)/shard_map/ppermute | solution.py:43
  35.5 11.0 %collective-permute-start.17 = (bf16[2,96,640]{2,1,0:T(8,128)(2,1)S(1)}, bf16[2,96,640]{2,1,0:T(8,128)(2,1)S(1)}, u32[]{:S(2)}, u32[]{:S(2)}) collective-permute-start(bf16[2,96,640]{2,1,0:T(8,128)(2,1)S(1)} %get-tuple-element.36), channel_id=1, source_target_pairs={{0,120},{1,121},{2,122},{3,123},{4,44},{5,45},{6,46},{7,47},{8,112... | collective-permute-start | bytes 737288 | tf_op jit(solution)/shard_map/ppermute | solution.py:43
  35.6 13.4 %collective-permute-start.18 = (bf16[2,96,640]{2,1,0:T(8,128)(2,1)S(1)}, bf16[2,96,640]{2,1,0:T(8,128)(2,1)S(1)}, u32[]{:S(2)}, u32[]{:S(2)}) collective-permute-start(bf16[2,96,640]{2,1,0:T(8,128)(2,1)S(1)} %get-tuple-element.37), channel_id=1, source_target_pairs={{0,96},{1,97},{2,98},{3,99},{4,36},{5,37},{6,38},{7,39},{8,104},{9... | collective-permute-start | bytes 737288 | tf_op jit(solution)/shard_map/ppermute | solution.py:43
  38.4 10.6 %collective-permute-start.19 = (bf16[2,96,640]{2,1,0:T(8,128)(2,1)S(1)}, bf16[2,96,640]{2,1,0:T(8,128)(2,1)S(1)}, u32[]{:S(2)}, u32[]{:S(2)}) collective-permute-start(bf16[2,96,640]{2,1,0:T(8,128)(2,1)S(1)} %get-tuple-element.38), channel_id=1, source_target_pairs={{0,24},{1,25},{2,26},{3,27},{4,12},{5,13},{6,14},{7,15},{8,16},{9,... | collective-permute-start | bytes 737288 | tf_op jit(solution)/shard_map/ppermute | solution.py:43
  46.2 6.6 %collective-permute-start.7 = (bf16[2,96,640]{2,1,0:T(8,128)(2,1)S(1)}, bf16[2,96,640]{2,1,0:T(8,128)(2,1)S(1)}, u32[]{:S(2)}, u32[]{:S(2)}) collective-permute-start(bf16[2,96,640]{2,1,0:T(8,128)(2,1)S(1)} %get-tuple-element.27), channel_id=1, source_target_pairs={{0,120},{1,121},{2,122},{3,123},{4,44},{5,45},{6,46},{7,47},{8,112... | collective-permute-start | bytes 737288 | tf_op jit(solution)/shard_map/ppermute | solution.py:43
  46.3 6.5 %collective-permute-start.8 = (bf16[2,96,640]{2,1,0:T(8,128)(2,1)S(1)}, bf16[2,96,640]{2,1,0:T(8,128)(2,1)S(1)}, u32[]{:S(2)}, u32[]{:S(2)}) collective-permute-start(bf16[2,96,640]{2,1,0:T(8,128)(2,1)S(1)} %get-tuple-element.28), channel_id=1, source_target_pairs={{0,96},{1,97},{2,98},{3,99},{4,36},{5,37},{6,38},{7,39},{8,104},{9... | collective-permute-start | bytes 737288 | tf_op jit(solution)/shard_map/ppermute | solution.py:43
  46.5 8.5 %collective-permute-start.9 = (bf16[2,96,640]{2,1,0:T(8,128)(2,1)S(1)}, bf16[2,96,640]{2,1,0:T(8,128)(2,1)S(1)}, u32[]{:S(2)}, u32[]{:S(2)}) collective-permute-start(bf16[2,96,640]{2,1,0:T(8,128)(2,1)S(1)} %get-tuple-element.29), channel_id=1, source_target_pairs={{0,24},{1,25},{2,26},{3,27},{4,12},{5,13},{6,14},{7,15},{8,16},{9,... | collective-permute-start | bytes 737288 | tf_op jit(solution)/shard_map/ppermute | solution.py:43
  49.1 10.0 %collective-permute-start.20 = (bf16[2,96,640]{2,1,0:T(8,128)(2,1)S(1)}, bf16[2,96,640]{2,1,0:T(8,128)(2,1)S(1)}, u32[]{:S(2)}, u32[]{:S(2)}) collective-permute-start(bf16[2,96,640]{2,1,0:T(8,128)(2,1)S(1)} %add_convert_fusion), channel_id=1, source_target_pairs={{0,3},{1,2},{2,1},{3,0},{4,5},{5,4},{6,7},{7,6},{8,11},{9,10},{10,... | collective-permute-start | bytes 737288 | tf_op jit(solution)/shard_map/ppermute | solution.py:43
  59.3 23.3 %copy-start.2 = (s32[2,2,8]{2,1,0:T(2,128)S(1)}, s32[2,2,8]{2,1,0:T(2,128)}, u32[]{:S(2)}) copy-start(s32[2,2,8]{2,1,0:T(2,128)} %newton_steps.1) | copy-start | bytes 388
  59.4 9.3 %collective-permute-start.21 = (bf16[96,640]{1,0:T(8,128)(2,1)S(1)}, bf16[96,640]{1,0:T(8,128)(2,1)S(1)}, u32[]{:S(2)}, u32[]{:S(2)}) collective-permute-start(bf16[96,640]{1,0:T(8,128)(2,1)S(1)} %fusion.2), channel_id=1, source_target_pairs={{0,1},{1,0},{2,3},{3,2},{4,7},{5,6},{6,5},{7,4},{8,9},{9,8},{10,11... | collective-permute-start | bytes 368648 | tf_op jit(solution)/shard_map/ppermute | solution.py:43
  68.7 5.4 %collective-permute-start.22 = (bf16[96,640]{1,0:T(8,128)(2,1)S(1)}, bf16[96,640]{1,0:T(8,128)(2,1)S(1)}, u32[]{:S(2)}, u32[]{:S(2)}) collective-permute-start(bf16[96,640]{1,0:T(8,128)(2,1)S(1)} %fusion.1), channel_id=1, source_target_pairs={{0,128},{1,129},{2,130},{3,131},{4,132},{5,133},{6,134},{7,135},{8... | collective-permute-start | bytes 368648 | tf_op jit(solution)/shard_map/ppermute | solution.py:43
  74.1 37.8 %copy-start.1 = (bf16[2,240,1280]{2,1,0:T(8,128)(2,1)S(1)}, bf16[2,240,1280]{2,1,0:T(8,128)(2,1)}, u32[]{:S(2)}) copy-start(bf16[2,240,1280]{2,1,0:T(8,128)(2,1)} %refs_4_.3) | copy-start | bytes 3686404
  74.1 37.8 %copy-start = (bf16[2,320,1280]{2,1,0:T(8,128)(2,1)S(1)}, bf16[2,320,1280]{2,1,0:T(8,128)(2,1)}, u32[]{:S(2)}) copy-start(bf16[2,320,1280]{2,1,0:T(8,128)(2,1)} %refs_5_.3) | copy-start | bytes 4915204
  88.4 11.4 %collective-permute-start.28 = (bf16[384,640]{1,0:T(8,128)(2,1)S(1)}, bf16[384,640]{1,0:T(8,128)(2,1)S(1)}, u32[]{:S(2)}, u32[]{:S(2)}) collective-permute-start(bf16[384,640]{1,0:T(8,128)(2,1)S(1)} %newton.1.refs_0_), channel_id=1, source_target_pairs={{0,40},{1,41},{2,42},{3,43},{4,124},{5,125},{6,126},{7,127},{8,32}... | collective-permute-start | bytes 1474568 | tf_op jit(solution)/shard_map/ppermute | solution.py:43
  88.5 16.7 %collective-permute-start.26 = (bf16[384,640]{1,0:T(8,128)(2,1)S(1)}, bf16[384,640]{1,0:T(8,128)(2,1)S(1)}, u32[]{:S(2)}, u32[]{:S(2)}) collective-permute-start(bf16[384,640]{1,0:T(8,128)(2,1)S(1)} %newton.1.refs_0_), channel_id=1, source_target_pairs={{0,32},{1,33},{2,34},{3,35},{4,100},{5,101},{6,102},{7,103},{8,40}... | collective-permute-start | bytes 1474568 | tf_op jit(solution)/shard_map/ppermute | solution.py:43
  91.6 20.3 %collective-permute-start.24 = (bf16[384,640]{1,0:T(8,128)(2,1)S(1)}, bf16[384,640]{1,0:T(8,128)(2,1)S(1)}, u32[]{:S(2)}, u32[]{:S(2)}) collective-permute-start(bf16[384,640]{1,0:T(8,128)(2,1)S(1)} %newton.1.refs_0_), channel_id=1, source_target_pairs={{0,8},{1,9},{2,10},{3,11},{4,28},{5,29},{6,30},{7,31},{8,0},{9,1},... | collective-permute-start | bytes 1474568 | tf_op jit(solution)/shard_map/ppermute | solution.py:43
  93.9 20.6 %collective-permute-start.23 = (bf16[384,640]{1,0:T(8,128)(2,1)S(1)}, bf16[384,640]{1,0:T(8,128)(2,1)S(1)}, u32[]{:S(2)}, u32[]{:S(2)}) collective-permute-start(bf16[384,640]{1,0:T(8,128)(2,1)S(1)} %newton.1.refs_0_), channel_id=1, source_target_pairs={{0,4},{1,5},{2,6},{3,7},{4,0},{5,1},{6,2},{7,3},{8,12},{9,13},{10,... | collective-permute-start | bytes 1474568 | tf_op jit(solution)/shard_map/ppermute | solution.py:43
  99.8 14.7 %collective-permute-start.29 = (bf16[384,640]{1,0:T(8,128)(2,1)S(1)}, bf16[384,640]{1,0:T(8,128)(2,1)S(1)}, u32[]{:S(2)}, u32[]{:S(2)}) collective-permute-start(bf16[384,640]{1,0:T(8,128)(2,1)S(1)} %collective-permute-done.28.refs_3_), channel_id=1, source_target_pairs={{0,4},{1,5},{2,6},{3,7},{4,0},{5,1},{6,2},{7,3},{8,12},{9,13},{10,... | collective-permute-start | bytes 1474568 | tf_op jit(solution)/shard_map/ppermute | solution.py:43
  105.2 9.4 %collective-permute-start.27 = (bf16[384,640]{1,0:T(8,128)(2,1)S(1)}, bf16[384,640]{1,0:T(8,128)(2,1)S(1)}, u32[]{:S(2)}, u32[]{:S(2)}) collective-permute-start(bf16[384,640]{1,0:T(8,128)(2,1)S(1)} %collective-permute-done.26.refs_2_), channel_id=1, source_target_pairs={{0,4},{1,5},{2,6},{3,7},{4,0},{5,1},{6,2},{7,3},{8,12},{9,13},{10,... | collective-permute-start | bytes 1474568 | tf_op jit(solution)/shard_map/ppermute | solution.py:43
  111.9 2.7 %collective-permute-start.25 = (bf16[384,640]{1,0:T(8,128)(2,1)S(1)}, bf16[384,640]{1,0:T(8,128)(2,1)S(1)}, u32[]{:S(2)}, u32[]{:S(2)}) collective-permute-start(bf16[384,640]{1,0:T(8,128)(2,1)S(1)} %collective-permute-done.24.refs_1_), channel_id=1, source_target_pairs={{0,4},{1,5},{2,6},{3,7},{4,0},{5,1},{6,2},{7,3},{8,12},{9,13},{10,... | collective-permute-start | bytes 1474568 | tf_op jit(solution)/shard_map/ppermute | solution.py:43

commit v8 on v7

--- a/solution.py
+++ b/solution.py
@@ -49,26 +49,14 @@
 
 def in_square(array, flip, of_places):
     def target(zl, x, y, c, t):
-        x2, y2 = (x ^ 1, y ^ 1) if (c == 0) == of_places else (3 - x, 3 - y)
+        x2, y2 = (x ^ 1, 3 - y) if (c == 0) == of_places else (3 - x, y ^ 1)
         return zl, x2 if flip & 2 else x, y2 if flip & 1 else y, c, t
 
     return move(array, target)
 
 
 def to_slab(array, step):
-    return move(array, lambda zl, x, y, c, t: (zl, x, y, c, 3 - t if c == step else t ^ 1))
-
-
-def gather_across(array):
-    found = {}
-    for device in range(256):
-        zl, x, y, c, t = device_at(device)
-        a, b = 2 * bit_a(x) + bit_a(y), 2 * bit_b(x) + bit_b(y)
-        place, across = (a, b) if c == 0 else (b, a)
-        found.setdefault((c, zl, t, place), {})[across] = device
-    groups = [[found[key][across] for across in range(RING)] for key in sorted(found)]
-    array = jnp.broadcast_to(array[None], (RING, *array.shape))
-    return lax.all_to_all(array, AXES, 0, 0, axis_index_groups=groups, tiled=True)
+    return move(array, lambda zl, x, y, c, t: (zl, x, y, c, t ^ 1 if c == step else 3 - t))
 
 
 def to_z_neighbour(array):
@@ -78,7 +66,7 @@
 def here(dev):
     dp = dev[0] // 4
     core, x, y = dp % 2, dp // 8 % 4, dp // 2 % 4
-    a, b = 2 * bit_a(x) + bit_a(y), 2 * bit_b(x) + bit_b(y)
+    a, b = 2 * bit_a(x) + bit_b(y), 2 * bit_b(x) + bit_a(y)
     return core, jnp.where(core == 0, a, b), jnp.where(core == 0, b, a)
 
 
@@ -90,8 +78,8 @@
     for half in range(2):
         *own, sent = outs[(RING + 1) * half : (RING + 1) * (half + 1)]
         for side in (1, 0):
-            first = jnp.where(core == side, 3 - t, t ^ 1)
-            second = jnp.where(core == side, t ^ 1, 3 - t)
+            first = jnp.where(core == side, t ^ 1, 3 - t)
+            second = jnp.where(core == side, 3 - t, t ^ 1)
             for flip in range(RING):
                 place = (across if side else mine) ^ flip
                 for rank, slab in enumerate((t, second) if half else (first, t ^ 2)):
@@ -134,11 +122,13 @@
             outs[flip][slab] = tri[pl.ds(start, CHUNK), :].astype(jnp.bfloat16)
 
 
-def newton_kernel(
-    tokens_all, dev, newton_steps, total, out, mixed, gap, mixed_half, gap_half
-):
+def newton_kernel(tokens_all, dev, newton_steps, *refs):
+    ins, (out, total, mixed, gap, mixed_half, gap_half) = refs[:RING], refs[RING:]
     t = dev[0] % 4
-    core, place, _ = here(dev)
+    core, place, across = here(dev)
+    for flip in range(RING):
+        start = pl.multiple_of((across ^ flip) * CHUNK, 32)
+        total[pl.ds(start, CHUNK), :] = ins[3 - flip][...]
     steps = newton_steps[core, place // 2, 2 * t + place % 2]
     eye = (
         lax.broadcasted_iota(jnp.int32, (BLOCK, BLOCK), 0)
@@ -306,14 +296,15 @@
     sums = factors(packed[RING + 1 : -1], packed[-1]) + wide(leaving)
     sums = sums[0] + wide(to_slab(sums[1].astype(half), 1))
     sums = sums + wide(to_z_neighbour(sums.astype(half)))
-    total = gather_across(sums.astype(half)).reshape(PACK, BLOCK)
+    members = over_square([sums.astype(half)] * RING, False)
 
     inverse = pl.pallas_call(
         functools.partial(newton_kernel, tokens_all),
         out_shape=shape(PACK, BLOCK),
-        in_specs=[SMEM, SMEM, VMEM],
+        in_specs=[SMEM, SMEM] + [VMEM] * RING,
         out_specs=VMEM,
         scratch_shapes=[
+            pltpu.VMEM((PACK, BLOCK), half),
             pltpu.VMEM((BLOCK, BLOCK), jnp.float32),
             pltpu.VMEM((BLOCK, BLOCK), jnp.float32),
             pltpu.VMEM((2, BLOCK, BLOCK), half),
@@ -321,7 +312,7 @@
         ],
         compiler_params=PARAMS,
         name="newton",
-    )(dev, newton_steps, total)
+    )(dev, newton_steps, *members[::-1])
     mine = over_square([inverse] * RING, True)
     others = [to_other_core(block) for block in mine]
 

time: 117 us -> 119 us (1.017)
  blocking collectives: 8.41 us -> 0 us
  starting transfers between devices: 60.3 us -> 68.3 us
  waiting for transfers between devices: 29.5 us -> 31.7 us
    all_to_all x1 -> x0, blocking collectives: 8.41 us -> none  [gather_across(): lax.all_to_all(array, AXES, 0, 0, axis_index_groups=groups, tiled=True)]
    ppermute x30 -> x33, starting transfers between devices: 60.3 us -> 68.3 us  [move(): return lax.ppermute(array, AXES, pairs)]
    ppermute x30 -> x33, waiting for transfers between devices: 29.5 us -> 31.7 us  [move(): return lax.ppermute(array, AXES, pairs)]
  transfers between devices with their start and end apart: 30 -> 33, of which waited for: 10 -> 15; matrix products, arithmetic and copies ran while one was open for 0% -> 0% of each run, Pallas kernels for 5% -> 5%
where the time goes in v8:
time: 119 us
  starting transfers between devices  68.3 us (57%)
  waiting for transfers between devices  31.7 us (27%)
  Pallas kernels  17.6 us (15%)
    ppermute x33, starting transfers between devices, move(): return lax.ppermute(array, AXES, pairs)  68.3 us
    ppermute x33, waiting for transfers between devices, move(): return lax.ppermute(array, AXES, pairs)  31.7 us
    pallas_call x1, Pallas kernels, local(): pl.pallas_call(functools.partial(newton_kernel, tokens_all), out_shape=sh...  5.87 us
    pallas_call x2, Pallas kernels, apply(): pl.pallas_call(functools.partial(apply_kernel, side), out_shape=[shape(*d...  5.18 us
    pallas_call x2, Pallas kernels, factors(): pl.pallas_call(gram_kernel, out_shape=[shape(2, CHUNK, BLOCK)] * RING, in...  3.59 us
    pallas_call x1, Pallas kernels, local(): pl.pallas_call(pack_kernel, out_shape=([shape(*part)] * RING + [shape(RIN...  2.97 us
  transfers between devices with their start and end apart: 33, of which 15 were waited for; matrix products, arithmetic and copies ran while one was open for 0% of the time, Pallas kernels for 5%

profile of v8, /device:TPU:1, one launch (start us, length us, event | category | flops | bytes accessed | tf_op | source)
XLA Modules:
  0.0 119.2 jit_solution(5953531904175699926)
XLA Ops:
  0.6 3.0 %pack.1 = (bf16[2,128,640]{2,1,0:T(8,128)(2,1)S(1)}, bf16[2,128,640]{2,1,0:T(8,128)(2,1)S(1)}, bf16[2,128,640]{2,1,0:T(8,128)(2,1)S(1)}, bf16[2,128,640]{2,1,0:T...) custom-call(s32[1]{0:T(128)} %bitcast.dev, ...), custom_call_target="tpu_custom_call" | custom-call | tf_op jit(solution)/shard_map/pack/pallas_call | solution.py:269
  3.6 3.3 %collective-permute-start.13 = (bf16[4,2,128,640]{3,2,1,0:T(8,128)(2,1)S(1)}, bf16[4,2,128,640]{3,2,1,0:T(8,128)(2,1)S(1)}, u32[]{:S(2)}, u32[]{:S(2)}) collective-permute-start(bf16[4,2,128,640]{3,2,1,0:T(8,128)(2,1)S(1)} %get-tuple-element.35), channel_id=1, source_target_pairs={{0,4},{1,5},{2,6},{3,7},{4,0},{5,1},{6,2},{7,3},{8,12},{9,13},{10,... | collective-permute-start | bytes 3932168 | tf_op jit(solution)/shard_map/ppermute | solution.py:43
  6.9 0.1 collective-permute-start.3
  7.0 1.8 %collective-permute-start = (bf16[2,128,640]{2,1,0:T(8,128)(2,1)S(1)}, bf16[2,128,640]{2,1,0:T(8,128)(2,1)S(1)}, u32[]{:S(2)}, u32[]{:S(2)}) collective-permute-start(bf16[2,128,640]{2,1,0:T(8,128)(2,1)S(1)} %get-tuple-element.22), channel_id=1, source_target_pairs={{0,56},{1,57},{2,58},{3,59},{4,108},{5,109},{6,110},{7,111},{8,48}... | collective-permute-start | bytes 983048 | tf_op jit(solution)/shard_map/ppermute | solution.py:43
  8.8 1.8 %collective-permute-start.10 = (bf16[2,128,640]{2,1,0:T(8,128)(2,1)S(1)}, bf16[2,128,640]{2,1,0:T(8,128)(2,1)S(1)}, u32[]{:S(2)}, u32[]{:S(2)}) collective-permute-start(bf16[2,128,640]{2,1,0:T(8,128)(2,1)S(1)} %get-tuple-element.31), channel_id=1, source_target_pairs={{0,56},{1,57},{2,58},{3,59},{4,108},{5,109},{6,110},{7,111},{8,48}... | collective-permute-start | bytes 983048 | tf_op jit(solution)/shard_map/ppermute | solution.py:43
  10.6 0.7 collective-permute-start.11
  11.4 0.0 collective-permute-done.13.refs_7_
  11.4 1.3 %collective-permute-start.12 = (bf16[2,128,640]{2,1,0:T(8,128)(2,1)S(1)}, bf16[2,128,640]{2,1,0:T(8,128)(2,1)S(1)}, u32[]{:S(2)}, u32[]{:S(2)}) collective-permute-start(bf16[2,128,640]{2,1,0:T(8,128)(2,1)S(1)} %get-tuple-element.33), channel_id=1, source_target_pairs={{0,24},{1,25},{2,26},{3,27},{4,12},{5,13},{6,14},{7,15},{8,16},{9,... | collective-permute-start | bytes 983048 | tf_op jit(solution)/shard_map/ppermute | solution.py:43
  12.7 0.1 slice_bitcast_fusion
  12.8 2.6 %collective-permute-done.refs_0_ = bf16[2,128,640]{2,1,0:T(8,128)(2,1)S(1)} collective-permute-done((bf16[2,128,640]{2,1,0:T(8,128)(2,1)S(1)}, bf16[2,128,640]{2,1,0:T(8,128)(2,1)S(1)}, u32[]{:S(2)}, u32[]{:S(2)}) %collective-permute-start) | collective-permute-done | bytes 327712 | tf_op jit(solution)/shard_map/ppermute | solution.py:43
  15.4 3.5 %collective-permute-done.10.refs_0_ = bf16[2,128,640]{2,1,0:T(8,128)(2,1)S(1)} collective-permute-done((bf16[2,128,640]{2,1,0:T(8,128)(2,1)S(1)}, bf16[2,128,640]{2,1,0:T(8,128)(2,1)S(1)}, u32[]{:S(2)}, u32[]{:S(2)}) %collective-permute-start.10) | collective-permute-done | bytes 327712 | tf_op jit(solution)/shard_map/ppermute | solution.py:43
  18.9 0.7 collective-permute-start.15
  19.7 1.0 collective-permute-start.14
  20.7 0.1 slice_bitcast_fusion.3
  20.7 0.1 collective-permute-done.11.refs_1_
  20.8 2.5 %collective-permute-start.1 = (bf16[2,128,640]{2,1,0:T(8,128)(2,1)S(1)}, bf16[2,128,640]{2,1,0:T(8,128)(2,1)S(1)}, u32[]{:S(2)}, u32[]{:S(2)}) collective-permute-start(bf16[2,128,640]{2,1,0:T(8,128)(2,1)S(1)} %get-tuple-element.23), channel_id=1, source_target_pairs={{0,32},{1,33},{2,34},{3,35},{4,100},{5,101},{6,102},{7,103},{8,40}... | collective-permute-start | bytes 983048 | tf_op jit(solution)/shard_map/ppermute | solution.py:43
  23.3 0.4 collective-permute-start.2
  23.7 2.2 %collective-permute-done.16.refs_6_ = bf16[2,128,640]{2,1,0:T(8,128)(2,1)S(1)} collective-permute-done((bf16[2,128,640]{2,1,0:T(8,128)(2,1)S(1)}, bf16[2,128,640]{2,1,0:T(8,128)(2,1)S(1)}, u32[]{:S(2)}, u32[]{:S(2)}) %collective-permute-start.16) | collective-permute-done | bytes 327712 | tf_op jit(solution)/shard_map/ppermute | solution.py:43
  25.9 0.0 collective-permute-start.6
  25.9 0.4 collective-permute-done.15.refs_5_
  26.4 1.4 %collective-permute-start.5 = (bf16[2,128,640]{2,1,0:T(8,128)(2,1)S(1)}, bf16[2,128,640]{2,1,0:T(8,128)(2,1)S(1)}, u32[]{:S(2)}, u32[]{:S(2)}) collective-permute-start(bf16[2,128,640]{2,1,0:T(8,128)(2,1)S(1)} %get-tuple-element.43), channel_id=1, source_target_pairs={{0,32},{1,33},{2,34},{3,35},{4,100},{5,101},{6,102},{7,103},{8,40}... | collective-permute-start | bytes 983048 | tf_op jit(solution)/shard_map/ppermute | solution.py:43
  27.8 1.7 %collective-permute-done.14.refs_4_ = bf16[2,128,640]{2,1,0:T(8,128)(2,1)S(1)} collective-permute-done((bf16[2,128,640]{2,1,0:T(8,128)(2,1)S(1)}, bf16[2,128,640]{2,1,0:T(8,128)(2,1)S(1)}, u32[]{:S(2)}, u32[]{:S(2)}) %collective-permute-start.14) | collective-permute-done | bytes 327712 | tf_op jit(solution)/shard_map/ppermute | solution.py:43
  29.5 1.8 %collective-permute-start.4 = (bf16[2,128,640]{2,1,0:T(8,128)(2,1)S(1)}, bf16[2,128,640]{2,1,0:T(8,128)(2,1)S(1)}, u32[]{:S(2)}, u32[]{:S(2)}) collective-permute-start(bf16[2,128,640]{2,1,0:T(8,128)(2,1)S(1)} %get-tuple-element.44), channel_id=1, source_target_pairs={{0,56},{1,57},{2,58},{3,59},{4,108},{5,109},{6,110},{7,111},{8,48}... | collective-permute-start | bytes 983048 | tf_op jit(solution)/shard_map/ppermute | solution.py:43
  31.3 1.8 %gram.3 = (bf16[2,96,640]{2,1,0:T(8,128)(2,1)S(1)}, bf16[2,96,640]{2,1,0:T(8,128)(2,1)S(1)}, bf16[2,96,640]{2,1,0:T(8,128)(2,1)S(1)}, bf16[2,96,640]{2,1,0:T(8,128)(2,1)S(1)}) custom-call(s32[1]{0:T(128)} %bitcast.dev, bf16[2,128,640]{2,1,0:T(8,128)(2,1)S(1)} %collective-permute-done.10.refs_0_, bf16[2,128,640]{2,1,0:T(8,128)(2,1)S(1)} %collective-permute-done.11.refs_1_, ...), custom_call_target="tpu_custom_call" | custom-call | tf_op jit(solution)/shard_map/gram/pallas_call | solution.py:283
  33.1 0.3 collective-permute-done.1.refs_1_
  33.4 0.1 collective-permute-start.17
  33.5 0.0 collective-permute-done.2.refs_2_
  33.5 3.6 %collective-permute-start.18 = (bf16[2,96,640]{2,1,0:T(8,128)(2,1)S(1)}, bf16[2,96,640]{2,1,0:T(8,128)(2,1)S(1)}, u32[]{:S(2)}, u32[]{:S(2)}) collective-permute-start(bf16[2,96,640]{2,1,0:T(8,128)(2,1)S(1)} %get-tuple-element.37), channel_id=1, source_target_pairs={{0,96},{1,97},{2,98},{3,99},{4,36},{5,37},{6,38},{7,39},{8,104},{9... | collective-permute-start | bytes 737288 | tf_op jit(solution)/shard_map/ppermute | solution.py:43
  37.1 0.0 collective-permute-done.6.refs_6_
  37.2 0.7 collective-permute-start.19
  37.8 2.2 %collective-permute-done.4.refs_4_ = bf16[2,128,640]{2,1,0:T(8,128)(2,1)S(1)} collective-permute-done((bf16[2,128,640]{2,1,0:T(8,128)(2,1)S(1)}, bf16[2,128,640]{2,1,0:T(8,128)(2,1)S(1)}, u32[]{:S(2)}, u32[]{:S(2)}) %collective-permute-start.4) | collective-permute-done | bytes 327712 | tf_op jit(solution)/shard_map/ppermute | solution.py:43
  40.0 1.8 %gram.2 = (bf16[2,96,640]{2,1,0:T(8,128)(2,1)S(1)}, bf16[2,96,640]{2,1,0:T(8,128)(2,1)S(1)}, bf16[2,96,640]{2,1,0:T(8,128)(2,1)S(1)}, bf16[2,96,640]{2,1,0:T(8,128)(2,1)S(1)}) custom-call(s32[1]{0:T(128)} %bitcast.dev, bf16[2,128,640]{2,1,0:T(8,128)(2,1)S(1)} %collective-permute-done.refs_0_, bf16[2,128,640]{2,1,0:T(8,128)(2,1)S(1)} %collective-permute-done.1.refs_1_, ...), custom_call_target="tpu_custom_call" | custom-call | tf_op jit(solution)/shard_map/gram/pallas_call | solution.py:283
  41.8 0.8 collective-permute-start.7
  42.7 3.2 %collective-permute-start.8 = (bf16[2,96,640]{2,1,0:T(8,128)(2,1)S(1)}, bf16[2,96,640]{2,1,0:T(8,128)(2,1)S(1)}, u32[]{:S(2)}, u32[]{:S(2)}) collective-permute-start(bf16[2,96,640]{2,1,0:T(8,128)(2,1)S(1)} %get-tuple-element.28), channel_id=1, source_target_pairs={{0,96},{1,97},{2,98},{3,99},{4,36},{5,37},{6,38},{7,39},{8,104},{9... | collective-permute-start | bytes 737288 | tf_op jit(solution)/shard_map/ppermute | solution.py:43
  45.9 0.0 collective-permute-done.17
  45.9 0.1 collective-permute-start.9
  46.0 0.0 collective-permute-done.18
  46.0 0.7 collective-permute-done.19
  46.7 0.1 add_convert_fusion
  46.8 6.1 %collective-permute-start.20 = (bf16[2,96,640]{2,1,0:T(8,128)(2,1)S(1)}, bf16[2,96,640]{2,1,0:T(8,128)(2,1)S(1)}, u32[]{:S(2)}, u32[]{:S(2)}) collective-permute-start(bf16[2,96,640]{2,1,0:T(8,128)(2,1)S(1)} %add_convert_fusion), channel_id=1, source_target_pairs={{0,1},{1,0},{2,3},{3,2},{4,7},{5,6},{6,5},{7,4},{8,9},{9,8},{10,11... | collective-permute-start | bytes 737288 | tf_op jit(solution)/shard_map/ppermute | solution.py:43
  52.9 0.0 collective-permute-done.8
  53.0 0.0 collective-permute-done.9
  53.0 5.8 %collective-permute-done.20 = bf16[2,96,640]{2,1,0:T(8,128)(2,1)S(1)} collective-permute-done((bf16[2,96,640]{2,1,0:T(8,128)(2,1)S(1)}, bf16[2,96,640]{2,1,0:T(8,128)(2,1)S(1)}, u32[]{:S(2)}, u32[]{:S(2)}) %collective-permute-start.20) | collective-permute-done | bytes 245792 | tf_op jit(solution)/shard_map/ppermute | solution.py:43
  58.7 0.1 convert_add_fusion
  58.9 0.0 copy-start
  58.9 1.8 %collective-permute-start.21 = (bf16[96,640]{1,0:T(8,128)(2,1)S(1)}, bf16[96,640]{1,0:T(8,128)(2,1)S(1)}, u32[]{:S(2)}, u32[]{:S(2)}) collective-permute-start(bf16[96,640]{1,0:T(8,128)(2,1)S(1)} %fusion.2), channel_id=1, source_target_pairs={{0,3},{1,2},{2,1},{3,0},{4,5},{5,4},{6,7},{7,6},{8,11},{9,10},{10,... | collective-permute-start | bytes 368648 | tf_op jit(solution)/shard_map/ppermute | solution.py:43
  60.7 5.0 %collective-permute-done.21 = bf16[96,640]{1,0:T(8,128)(2,1)S(1)} collective-permute-done((bf16[96,640]{1,0:T(8,128)(2,1)S(1)}, bf16[96,640]{1,0:T(8,128)(2,1)S(1)}, u32[]{:S(2)}, u32[]{:S(2)}) %collective-permute-start.21) | collective-permute-done | bytes 122912 | tf_op jit(solution)/shard_map/ppermute | solution.py:43
  65.7 0.2 collective-permute-start.22
  66.0 3.6 %collective-permute-done.22 = bf16[96,640]{1,0:T(8,128)(2,1)S(1)} collective-permute-done((bf16[96,640]{1,0:T(8,128)(2,1)S(1)}, bf16[96,640]{1,0:T(8,128)(2,1)S(1)}, u32[]{:S(2)}, u32[]{:S(2)}) %collective-permute-start.22) | collective-permute-done | bytes 122912 | tf_op jit(solution)/shard_map/ppermute | solution.py:43
  69.6 1.4 %collective-permute-start.25 = (bf16[96,640]{1,0:T(8,128)(2,1)S(1)}, bf16[96,640]{1,0:T(8,128)(2,1)S(1)}, u32[]{:S(2)}, u32[]{:S(2)}) collective-permute-start(bf16[96,640]{1,0:T(8,128)(2,1)S(1)} %add_convert_fusion.1.refs_3_), channel_id=1, source_target_pairs={{0,8},{1,9},{2,10},{3,11},{4,28},{5,29},{6,30},{7,31},{8,0},{9,1},... | collective-permute-start | bytes 368648 | tf_op jit(solution)/shard_map/ppermute | solution.py:43
  71.0 2.5 %collective-permute-start.23 = (bf16[96,640]{1,0:T(8,128)(2,1)S(1)}, bf16[96,640]{1,0:T(8,128)(2,1)S(1)}, u32[]{:S(2)}, u32[]{:S(2)}) collective-permute-start(bf16[96,640]{1,0:T(8,128)(2,1)S(1)} %add_convert_fusion.1.refs_3_), channel_id=1, source_target_pairs={{0,104},{1,105},{2,106},{3,107},{4,60},{5,61},{6,62},{7,63},{8,96}... | collective-permute-start | bytes 368648 | tf_op jit(solution)/shard_map/ppermute | solution.py:43
  73.6 1.1 collective-permute-done.25.refs_2_
  74.6 0.1 collective-permute-done.24.refs_1_
  74.8 2.4 %collective-permute-done.23.refs_0_ = bf16[96,640]{1,0:T(8,128)(2,1)S(1)} collective-permute-done((bf16[96,640]{1,0:T(8,128)(2,1)S(1)}, bf16[96,640]{1,0:T(8,128)(2,1)S(1)}, u32[]{:S(2)}, u32[]{:S(2)}) %collective-permute-start.23) | collective-permute-done | bytes 122912 | tf_op jit(solution)/shard_map/ppermute | solution.py:43
  77.1 5.9 %newton.1.refs_0_ = bf16[384,640]{1,0:T(8,128)(2,1)S(1)} custom-call(s32[1]{0:T(128)} %bitcast.dev, s32[2,2,8]{2,1,0:T(2,128)S(1)} %copy-done.2, bf16[96,640]{1,0:T(8,128)(2,1)S(1)} %collective-permute-done.23.refs_0_, bf16[96,640]{1,0:T(8,128)(2,1)S(1)} %collective-permute-done.24.refs_1_, bf16[96,640]{1,0:T(8,128)(2,1)S(1)} %collective-permute-done.25.refs_2_, ...), custom_call_target="tpu_custom_call" | custom-call | tf_op jit(solution)/shard_map/newton/pallas_call | solution.py:301
  83.0 2.1 %collective-permute-start.31 = (bf16[384,640]{1,0:T(8,128)(2,1)S(1)}, bf16[384,640]{1,0:T(8,128)(2,1)S(1)}, u32[]{:S(2)}, u32[]{:S(2)}) collective-permute-start(bf16[384,640]{1,0:T(8,128)(2,1)S(1)} %newton.1.refs_0_), channel_id=1, source_target_pairs={{0,56},{1,57},{2,58},{3,59},{4,108},{5,109},{6,110},{7,111},{8,48}... | collective-permute-start | bytes 1474568 | tf_op jit(solution)/shard_map/ppermute | solution.py:43
  85.1 1.3 %collective-permute-start.29 = (bf16[384,640]{1,0:T(8,128)(2,1)S(1)}, bf16[384,640]{1,0:T(8,128)(2,1)S(1)}, u32[]{:S(2)}, u32[]{:S(2)}) collective-permute-start(bf16[384,640]{1,0:T(8,128)(2,1)S(1)} %newton.1.refs_0_), channel_id=1, source_target_pairs={{0,32},{1,33},{2,34},{3,35},{4,100},{5,101},{6,102},{7,103},{8,40}... | collective-permute-start | bytes 1474568 | tf_op jit(solution)/shard_map/ppermute | solution.py:43
  86.4 1.1 collective-permute-start.27
  87.5 14.8 %collective-permute-start.26 = (bf16[384,640]{1,0:T(8,128)(2,1)S(1)}, bf16[384,640]{1,0:T(8,128)(2,1)S(1)}, u32[]{:S(2)}, u32[]{:S(2)}) collective-permute-start(bf16[384,640]{1,0:T(8,128)(2,1)S(1)} %newton.1.refs_0_), channel_id=1, source_target_pairs={{0,4},{1,5},{2,6},{3,7},{4,0},{5,1},{6,2},{7,3},{8,12},{9,13},{10,... | collective-permute-start | bytes 1474568 | tf_op jit(solution)/shard_map/ppermute | solution.py:43
  102.2 6.3 %collective-permute-start.32 = (bf16[384,640]{1,0:T(8,128)(2,1)S(1)}, bf16[384,640]{1,0:T(8,128)(2,1)S(1)}, u32[]{:S(2)}, u32[]{:S(2)}) collective-permute-start(bf16[384,640]{1,0:T(8,128)(2,1)S(1)} %collective-permute-done.31.refs_3_), channel_id=1, source_target_pairs={{0,4},{1,5},{2,6},{3,7},{4,0},{5,1},{6,2},{7,3},{8,12},{9,13},{10,... | collective-permute-start | bytes 1474568 | tf_op jit(solution)/shard_map/ppermute | solution.py:43
  108.6 0.6 collective-permute-start.30
  109.2 4.5 %collective-permute-start.28 = (bf16[384,640]{1,0:T(8,128)(2,1)S(1)}, bf16[384,640]{1,0:T(8,128)(2,1)S(1)}, u32[]{:S(2)}, u32[]{:S(2)}) collective-permute-start(bf16[384,640]{1,0:T(8,128)(2,1)S(1)} %collective-permute-done.27.refs_1_), channel_id=1, source_target_pairs={{0,4},{1,5},{2,6},{3,7},{4,0},{5,1},{6,2},{7,3},{8,12},{9,13},{10,... | collective-permute-start | bytes 1474568 | tf_op jit(solution)/shard_map/ppermute | solution.py:43
  113.8 2.6 %apply.2 = (bf16[2,240,1280]{2,1,0:T(8,128)(2,1)}, bf16[2,320,1280]{2,1,0:T(8,128)(2,1)}) custom-call(s32[1]{0:T(128)} %bitcast.dev, bf16[384,640]{1,0:T(8,128)(2,1)S(1)} %newton.1.refs_0_, bf16[384,640]{1,0:T(8,128)(2,1)S(1)} %collective-permute-done.27.refs_1_, bf16[384,640]{1,0:T(8,128)(2,1)S(1)} %collective-permute-done.29.refs_2_, ...), custom_call_target="tpu_custom_call" | custom-call | tf_op jit(solution)/shard_map/apply/pallas_call | solution.py:322
  116.4 2.6 %apply.3 = (bf16[2,240,1280]{2,1,0:T(8,128)(2,1)}, bf16[2,320,1280]{2,1,0:T(8,128)(2,1)}) custom-call(s32[1]{0:T(128)} %bitcast.dev, bf16[384,640]{1,0:T(8,128)(2,1)S(1)} %collective-permute-done.26.refs_0_, bf16[384,640]{1,0:T(8,128)(2,1)S(1)} %collective-permute-done.28.refs_1_, ...), custom_call_target="tpu_custom_call", output_to_operand_aliasing={{0}: (7, {}), {1}: (8, {})} | custom-call | tf_op jit(solution)/shard_map/apply/pallas_call | solution.py:322
  (21 shorter events, 0.1 us)
Async XLA Ops:
  3.6 7.8 %collective-permute-start.13 = (bf16[4,2,128,640]{3,2,1,0:T(8,128)(2,1)S(1)}, bf16[4,2,128,640]{3,2,1,0:T(8,128)(2,1)S(1)}, u32[]{:S(2)}, u32[]{:S(2)}) collective-permute-start(bf16[4,2,128,640]{3,2,1,0:T(8,128)(2,1)S(1)} %get-tuple-element.35), channel_id=1, source_target_pairs={{0,4},{1,5},{2,6},{3,7},{4,0},{5,1},{6,2},{7,3},{8,12},{9,13},{10,... | collective-permute-start | bytes 3932168 | tf_op jit(solution)/shard_map/ppermute | solution.py:43
  6.9 12.7 %collective-permute-start.3 = (bf16[4,2,128,640]{3,2,1,0:T(8,128)(2,1)S(1)}, bf16[4,2,128,640]{3,2,1,0:T(8,128)(2,1)S(1)}, u32[]{:S(2)}, u32[]{:S(2)}) collective-permute-start(bf16[4,2,128,640]{3,2,1,0:T(8,128)(2,1)S(1)} %get-tuple-element.26), channel_id=1, source_target_pairs={{0,4},{1,5},{2,6},{3,7},{4,0},{5,1},{6,2},{7,3},{8,12},{9,13},{10,... | collective-permute-start | bytes 3932168 | tf_op jit(solution)/shard_map/ppermute | solution.py:43
  7.0 8.3 %collective-permute-start = (bf16[2,128,640]{2,1,0:T(8,128)(2,1)S(1)}, bf16[2,128,640]{2,1,0:T(8,128)(2,1)S(1)}, u32[]{:S(2)}, u32[]{:S(2)}) collective-permute-start(bf16[2,128,640]{2,1,0:T(8,128)(2,1)S(1)} %get-tuple-element.22), channel_id=1, source_target_pairs={{0,56},{1,57},{2,58},{3,59},{4,108},{5,109},{6,110},{7,111},{8,48}... | collective-permute-start | bytes 983048 | tf_op jit(solution)/shard_map/ppermute | solution.py:43
  8.8 10.1 %collective-permute-start.10 = (bf16[2,128,640]{2,1,0:T(8,128)(2,1)S(1)}, bf16[2,128,640]{2,1,0:T(8,128)(2,1)S(1)}, u32[]{:S(2)}, u32[]{:S(2)}) collective-permute-start(bf16[2,128,640]{2,1,0:T(8,128)(2,1)S(1)} %get-tuple-element.31), channel_id=1, source_target_pairs={{0,56},{1,57},{2,58},{3,59},{4,108},{5,109},{6,110},{7,111},{8,48}... | collective-permute-start | bytes 983048 | tf_op jit(solution)/shard_map/ppermute | solution.py:43
  10.6 10.2 %collective-permute-start.11 = (bf16[2,128,640]{2,1,0:T(8,128)(2,1)S(1)}, bf16[2,128,640]{2,1,0:T(8,128)(2,1)S(1)}, u32[]{:S(2)}, u32[]{:S(2)}) collective-permute-start(bf16[2,128,640]{2,1,0:T(8,128)(2,1)S(1)} %get-tuple-element.32), channel_id=1, source_target_pairs={{0,32},{1,33},{2,34},{3,35},{4,100},{5,101},{6,102},{7,103},{8,40}... | collective-permute-start | bytes 983048 | tf_op jit(solution)/shard_map/ppermute | solution.py:43
  11.4 12.0 %collective-permute-start.12 = (bf16[2,128,640]{2,1,0:T(8,128)(2,1)S(1)}, bf16[2,128,640]{2,1,0:T(8,128)(2,1)S(1)}, u32[]{:S(2)}, u32[]{:S(2)}) collective-permute-start(bf16[2,128,640]{2,1,0:T(8,128)(2,1)S(1)} %get-tuple-element.33), channel_id=1, source_target_pairs={{0,24},{1,25},{2,26},{3,27},{4,12},{5,13},{6,14},{7,15},{8,16},{9,... | collective-permute-start | bytes 983048 | tf_op jit(solution)/shard_map/ppermute | solution.py:43
  15.4 10.5 %collective-permute-start.16 = (bf16[2,128,640]{2,1,0:T(8,128)(2,1)S(1)}, bf16[2,128,640]{2,1,0:T(8,128)(2,1)S(1)}, u32[]{:S(2)}, u32[]{:S(2)}) collective-permute-start(bf16[2,128,640]{2,1,0:T(8,128)(2,1)S(1)} %get-tuple-element.45), channel_id=1, source_target_pairs={{0,24},{1,25},{2,26},{3,27},{4,12},{5,13},{6,14},{7,15},{8,16},{9,... | collective-permute-start | bytes 983048 | tf_op jit(solution)/shard_map/ppermute | solution.py:43
  18.9 7.4 %collective-permute-start.15 = (bf16[2,128,640]{2,1,0:T(8,128)(2,1)S(1)}, bf16[2,128,640]{2,1,0:T(8,128)(2,1)S(1)}, u32[]{:S(2)}, u32[]{:S(2)}) collective-permute-start(bf16[2,128,640]{2,1,0:T(8,128)(2,1)S(1)} %get-tuple-element.46), channel_id=1, source_target_pairs={{0,32},{1,33},{2,34},{3,35},{4,100},{5,101},{6,102},{7,103},{8,40}... | collective-permute-start | bytes 983048 | tf_op jit(solution)/shard_map/ppermute | solution.py:43
  19.7 9.8 %collective-permute-start.14 = (bf16[2,128,640]{2,1,0:T(8,128)(2,1)S(1)}, bf16[2,128,640]{2,1,0:T(8,128)(2,1)S(1)}, u32[]{:S(2)}, u32[]{:S(2)}) collective-permute-start(bf16[2,128,640]{2,1,0:T(8,128)(2,1)S(1)} %get-tuple-element.47), channel_id=1, source_target_pairs={{0,56},{1,57},{2,58},{3,59},{4,108},{5,109},{6,110},{7,111},{8,48}... | collective-permute-start | bytes 983048 | tf_op jit(solution)/shard_map/ppermute | solution.py:43
  20.8 12.6 %collective-permute-start.1 = (bf16[2,128,640]{2,1,0:T(8,128)(2,1)S(1)}, bf16[2,128,640]{2,1,0:T(8,128)(2,1)S(1)}, u32[]{:S(2)}, u32[]{:S(2)}) collective-permute-start(bf16[2,128,640]{2,1,0:T(8,128)(2,1)S(1)} %get-tuple-element.23), channel_id=1, source_target_pairs={{0,32},{1,33},{2,34},{3,35},{4,100},{5,101},{6,102},{7,103},{8,40}... | collective-permute-start | bytes 983048 | tf_op jit(solution)/shard_map/ppermute | solution.py:43
  23.3 10.2 %collective-permute-start.2 = (bf16[2,128,640]{2,1,0:T(8,128)(2,1)S(1)}, bf16[2,128,640]{2,1,0:T(8,128)(2,1)S(1)}, u32[]{:S(2)}, u32[]{:S(2)}) collective-permute-start(bf16[2,128,640]{2,1,0:T(8,128)(2,1)S(1)} %get-tuple-element.24), channel_id=1, source_target_pairs={{0,24},{1,25},{2,26},{3,27},{4,12},{5,13},{6,14},{7,15},{8,16},{9,... | collective-permute-start | bytes 983048 | tf_op jit(solution)/shard_map/ppermute | solution.py:43
  25.9 11.2 %collective-permute-start.6 = (bf16[2,128,640]{2,1,0:T(8,128)(2,1)S(1)}, bf16[2,128,640]{2,1,0:T(8,128)(2,1)S(1)}, u32[]{:S(2)}, u32[]{:S(2)}) collective-permute-start(bf16[2,128,640]{2,1,0:T(8,128)(2,1)S(1)} %get-tuple-element.42), channel_id=1, source_target_pairs={{0,24},{1,25},{2,26},{3,27},{4,12},{5,13},{6,14},{7,15},{8,16},{9,... | collective-permute-start | bytes 983048 | tf_op jit(solution)/shard_map/ppermute | solution.py:43
  26.4 11.5 %collective-permute-start.5 = (bf16[2,128,640]{2,1,0:T(8,128)(2,1)S(1)}, bf16[2,128,640]{2,1,0:T(8,128)(2,1)S(1)}, u32[]{:S(2)}, u32[]{:S(2)}) collective-permute-start(bf16[2,128,640]{2,1,0:T(8,128)(2,1)S(1)} %get-tuple-element.43), channel_id=1, source_target_pairs={{0,32},{1,33},{2,34},{3,35},{4,100},{5,101},{6,102},{7,103},{8,40}... | collective-permute-start | bytes 983048 | tf_op jit(solution)/shard_map/ppermute | solution.py:43
  29.5 10.5 %collective-permute-start.4 = (bf16[2,128,640]{2,1,0:T(8,128)(2,1)S(1)}, bf16[2,128,640]{2,1,0:T(8,128)(2,1)S(1)}, u32[]{:S(2)}, u32[]{:S(2)}) collective-permute-start(bf16[2,128,640]{2,1,0:T(8,128)(2,1)S(1)} %get-tuple-element.44), channel_id=1, source_target_pairs={{0,56},{1,57},{2,58},{3,59},{4,108},{5,109},{6,110},{7,111},{8,48}... | collective-permute-start | bytes 983048 | tf_op jit(solution)/shard_map/ppermute | solution.py:43
  33.4 12.5 %collective-permute-start.17 = (bf16[2,96,640]{2,1,0:T(8,128)(2,1)S(1)}, bf16[2,96,640]{2,1,0:T(8,128)(2,1)S(1)}, u32[]{:S(2)}, u32[]{:S(2)}) collective-permute-start(bf16[2,96,640]{2,1,0:T(8,128)(2,1)S(1)} %get-tuple-element.36), channel_id=1, source_target_pairs={{0,104},{1,105},{2,106},{3,107},{4,60},{5,61},{6,62},{7,63},{8,96}... | collective-permute-start | bytes 737288 | tf_op jit(solution)/shard_map/ppermute | solution.py:43
  33.5 12.5 %collective-permute-start.18 = (bf16[2,96,640]{2,1,0:T(8,128)(2,1)S(1)}, bf16[2,96,640]{2,1,0:T(8,128)(2,1)S(1)}, u32[]{:S(2)}, u32[]{:S(2)}) collective-permute-start(bf16[2,96,640]{2,1,0:T(8,128)(2,1)S(1)} %get-tuple-element.37), channel_id=1, source_target_pairs={{0,96},{1,97},{2,98},{3,99},{4,36},{5,37},{6,38},{7,39},{8,104},{9... | collective-permute-start | bytes 737288 | tf_op jit(solution)/shard_map/ppermute | solution.py:43
  37.2 9.6 %collective-permute-start.19 = (bf16[2,96,640]{2,1,0:T(8,128)(2,1)S(1)}, bf16[2,96,640]{2,1,0:T(8,128)(2,1)S(1)}, u32[]{:S(2)}, u32[]{:S(2)}) collective-permute-start(bf16[2,96,640]{2,1,0:T(8,128)(2,1)S(1)} %get-tuple-element.38), channel_id=1, source_target_pairs={{0,8},{1,9},{2,10},{3,11},{4,28},{5,29},{6,30},{7,31},{8,0},{9,1},... | collective-permute-start | bytes 737288 | tf_op jit(solution)/shard_map/ppermute | solution.py:43
  41.8 11.1 %collective-permute-start.7 = (bf16[2,96,640]{2,1,0:T(8,128)(2,1)S(1)}, bf16[2,96,640]{2,1,0:T(8,128)(2,1)S(1)}, u32[]{:S(2)}, u32[]{:S(2)}) collective-permute-start(bf16[2,96,640]{2,1,0:T(8,128)(2,1)S(1)} %get-tuple-element.27), channel_id=1, source_target_pairs={{0,104},{1,105},{2,106},{3,107},{4,60},{5,61},{6,62},{7,63},{8,96}... | collective-permute-start | bytes 737288 | tf_op jit(solution)/shard_map/ppermute | solution.py:43
  42.7 10.3 %collective-permute-start.8 = (bf16[2,96,640]{2,1,0:T(8,128)(2,1)S(1)}, bf16[2,96,640]{2,1,0:T(8,128)(2,1)S(1)}, u32[]{:S(2)}, u32[]{:S(2)}) collective-permute-start(bf16[2,96,640]{2,1,0:T(8,128)(2,1)S(1)} %get-tuple-element.28), channel_id=1, source_target_pairs={{0,96},{1,97},{2,98},{3,99},{4,36},{5,37},{6,38},{7,39},{8,104},{9... | collective-permute-start | bytes 737288 | tf_op jit(solution)/shard_map/ppermute | solution.py:43
  45.9 7.1 %collective-permute-start.9 = (bf16[2,96,640]{2,1,0:T(8,128)(2,1)S(1)}, bf16[2,96,640]{2,1,0:T(8,128)(2,1)S(1)}, u32[]{:S(2)}, u32[]{:S(2)}) collective-permute-start(bf16[2,96,640]{2,1,0:T(8,128)(2,1)S(1)} %get-tuple-element.29), channel_id=1, source_target_pairs={{0,8},{1,9},{2,10},{3,11},{4,28},{5,29},{6,30},{7,31},{8,0},{9,1},... | collective-permute-start | bytes 737288 | tf_op jit(solution)/shard_map/ppermute | solution.py:43
  46.8 11.9 %collective-permute-start.20 = (bf16[2,96,640]{2,1,0:T(8,128)(2,1)S(1)}, bf16[2,96,640]{2,1,0:T(8,128)(2,1)S(1)}, u32[]{:S(2)}, u32[]{:S(2)}) collective-permute-start(bf16[2,96,640]{2,1,0:T(8,128)(2,1)S(1)} %add_convert_fusion), channel_id=1, source_target_pairs={{0,1},{1,0},{2,3},{3,2},{4,7},{5,6},{6,5},{7,4},{8,9},{9,8},{10,11... | collective-permute-start | bytes 737288 | tf_op jit(solution)/shard_map/ppermute | solution.py:43
  58.7 18.4 %copy-start.2 = (s32[2,2,8]{2,1,0:T(2,128)S(1)}, s32[2,2,8]{2,1,0:T(2,128)}, u32[]{:S(2)}) copy-start(s32[2,2,8]{2,1,0:T(2,128)} %newton_steps.1) | copy-start | bytes 388
  58.7 55.0 %copy-start.1 = (bf16[2,240,1280]{2,1,0:T(8,128)(2,1)S(1)}, bf16[2,240,1280]{2,1,0:T(8,128)(2,1)}, u32[]{:S(2)}) copy-start(bf16[2,240,1280]{2,1,0:T(8,128)(2,1)} %refs_4_.3) | copy-start | bytes 3686404
  58.9 54.9 %copy-start = (bf16[2,320,1280]{2,1,0:T(8,128)(2,1)S(1)}, bf16[2,320,1280]{2,1,0:T(8,128)(2,1)}, u32[]{:S(2)}) copy-start(bf16[2,320,1280]{2,1,0:T(8,128)(2,1)} %refs_5_.3) | copy-start | bytes 4915204
  58.9 6.8 %collective-permute-start.21 = (bf16[96,640]{1,0:T(8,128)(2,1)S(1)}, bf16[96,640]{1,0:T(8,128)(2,1)S(1)}, u32[]{:S(2)}, u32[]{:S(2)}) collective-permute-start(bf16[96,640]{1,0:T(8,128)(2,1)S(1)} %fusion.2), channel_id=1, source_target_pairs={{0,3},{1,2},{2,1},{3,0},{4,5},{5,4},{6,7},{7,6},{8,11},{9,10},{10,... | collective-permute-start | bytes 368648 | tf_op jit(solution)/shard_map/ppermute | solution.py:43
  65.7 3.8 %collective-permute-start.22 = (bf16[96,640]{1,0:T(8,128)(2,1)S(1)}, bf16[96,640]{1,0:T(8,128)(2,1)S(1)}, u32[]{:S(2)}, u32[]{:S(2)}) collective-permute-start(bf16[96,640]{1,0:T(8,128)(2,1)S(1)} %fusion.1), channel_id=1, source_target_pairs={{0,128},{1,129},{2,130},{3,131},{4,132},{5,133},{6,134},{7,135},{8... | collective-permute-start | bytes 368648 | tf_op jit(solution)/shard_map/ppermute | solution.py:43
  69.6 5.0 %collective-permute-start.25 = (bf16[96,640]{1,0:T(8,128)(2,1)S(1)}, bf16[96,640]{1,0:T(8,128)(2,1)S(1)}, u32[]{:S(2)}, u32[]{:S(2)}) collective-permute-start(bf16[96,640]{1,0:T(8,128)(2,1)S(1)} %add_convert_fusion.1.refs_3_), channel_id=1, source_target_pairs={{0,8},{1,9},{2,10},{3,11},{4,28},{5,29},{6,30},{7,31},{8,0},{9,1},... | collective-permute-start | bytes 368648 | tf_op jit(solution)/shard_map/ppermute | solution.py:43
  71.0 3.7 %collective-permute-start.24 = (bf16[96,640]{1,0:T(8,128)(2,1)S(1)}, bf16[96,640]{1,0:T(8,128)(2,1)S(1)}, u32[]{:S(2)}, u32[]{:S(2)}) collective-permute-start(bf16[96,640]{1,0:T(8,128)(2,1)S(1)} %add_convert_fusion.1.refs_3_), channel_id=1, source_target_pairs={{0,96},{1,97},{2,98},{3,99},{4,36},{5,37},{6,38},{7,39},{8,104},{9... | collective-permute-start | bytes 368648 | tf_op jit(solution)/shard_map/ppermute | solution.py:43
  71.0 6.1 %collective-permute-start.23 = (bf16[96,640]{1,0:T(8,128)(2,1)S(1)}, bf16[96,640]{1,0:T(8,128)(2,1)S(1)}, u32[]{:S(2)}, u32[]{:S(2)}) collective-permute-start(bf16[96,640]{1,0:T(8,128)(2,1)S(1)} %add_convert_fusion.1.refs_3_), channel_id=1, source_target_pairs={{0,104},{1,105},{2,106},{3,107},{4,60},{5,61},{6,62},{7,63},{8,96}... | collective-permute-start | bytes 368648 | tf_op jit(solution)/shard_map/ppermute | solution.py:43
  83.0 19.2 %collective-permute-start.31 = (bf16[384,640]{1,0:T(8,128)(2,1)S(1)}, bf16[384,640]{1,0:T(8,128)(2,1)S(1)}, u32[]{:S(2)}, u32[]{:S(2)}) collective-permute-start(bf16[384,640]{1,0:T(8,128)(2,1)S(1)} %newton.1.refs_0_), channel_id=1, source_target_pairs={{0,56},{1,57},{2,58},{3,59},{4,108},{5,109},{6,110},{7,111},{8,48}... | collective-permute-start | bytes 1474568 | tf_op jit(solution)/shard_map/ppermute | solution.py:43
  85.1 23.5 %collective-permute-start.29 = (bf16[384,640]{1,0:T(8,128)(2,1)S(1)}, bf16[384,640]{1,0:T(8,128)(2,1)S(1)}, u32[]{:S(2)}, u32[]{:S(2)}) collective-permute-start(bf16[384,640]{1,0:T(8,128)(2,1)S(1)} %newton.1.refs_0_), channel_id=1, source_target_pairs={{0,32},{1,33},{2,34},{3,35},{4,100},{5,101},{6,102},{7,103},{8,40}... | collective-permute-start | bytes 1474568 | tf_op jit(solution)/shard_map/ppermute | solution.py:43
  86.4 22.8 %collective-permute-start.27 = (bf16[384,640]{1,0:T(8,128)(2,1)S(1)}, bf16[384,640]{1,0:T(8,128)(2,1)S(1)}, u32[]{:S(2)}, u32[]{:S(2)}) collective-permute-start(bf16[384,640]{1,0:T(8,128)(2,1)S(1)} %newton.1.refs_0_), channel_id=1, source_target_pairs={{0,24},{1,25},{2,26},{3,27},{4,12},{5,13},{6,14},{7,15},{8,16},{9,... | collective-permute-start | bytes 1474568 | tf_op jit(solution)/shard_map/ppermute | solution.py:43
  87.5 28.9 %collective-permute-start.26 = (bf16[384,640]{1,0:T(8,128)(2,1)S(1)}, bf16[384,640]{1,0:T(8,128)(2,1)S(1)}, u32[]{:S(2)}, u32[]{:S(2)}) collective-permute-start(bf16[384,640]{1,0:T(8,128)(2,1)S(1)} %newton.1.refs_0_), channel_id=1, source_target_pairs={{0,4},{1,5},{2,6},{3,7},{4,0},{5,1},{6,2},{7,3},{8,12},{9,13},{10,... | collective-permute-start | bytes 1474568 | tf_op jit(solution)/shard_map/ppermute | solution.py:43
  102.2 14.1 %collective-permute-start.32 = (bf16[384,640]{1,0:T(8,128)(2,1)S(1)}, bf16[384,640]{1,0:T(8,128)(2,1)S(1)}, u32[]{:S(2)}, u32[]{:S(2)}) collective-permute-start(bf16[384,640]{1,0:T(8,128)(2,1)S(1)} %collective-permute-done.31.refs_3_), channel_id=1, source_target_pairs={{0,4},{1,5},{2,6},{3,7},{4,0},{5,1},{6,2},{7,3},{8,12},{9,13},{10,... | collective-permute-start | bytes 1474568 | tf_op jit(solution)/shard_map/ppermute | solution.py:43
  108.6 7.8 %collective-permute-start.30 = (bf16[384,640]{1,0:T(8,128)(2,1)S(1)}, bf16[384,640]{1,0:T(8,128)(2,1)S(1)}, u32[]{:S(2)}, u32[]{:S(2)}) collective-permute-start(bf16[384,640]{1,0:T(8,128)(2,1)S(1)} %collective-permute-done.29.refs_2_), channel_id=1, source_target_pairs={{0,4},{1,5},{2,6},{3,7},{4,0},{5,1},{6,2},{7,3},{8,12},{9,13},{10,... | collective-permute-start | bytes 1474568 | tf_op jit(solution)/shard_map/ppermute | solution.py:43
  109.2 7.2 %collective-permute-start.28 = (bf16[384,640]{1,0:T(8,128)(2,1)S(1)}, bf16[384,640]{1,0:T(8,128)(2,1)S(1)}, u32[]{:S(2)}, u32[]{:S(2)}) collective-permute-start(bf16[384,640]{1,0:T(8,128)(2,1)S(1)} %collective-permute-done.27.refs_1_), channel_id=1, source_target_pairs={{0,4},{1,5},{2,6},{3,7},{4,0},{5,1},{6,2},{7,3},{8,12},{9,13},{10,... | collective-permute-start | bytes 1474568 | tf_op jit(solution)/shard_map/ppermute | solution.py:43

commit v9 on v8

--- a/solution.py
+++ b/solution.py
@@ -49,7 +49,7 @@
 
 def in_square(array, flip, of_places):
     def target(zl, x, y, c, t):
-        x2, y2 = (x ^ 1, 3 - y) if (c == 0) == of_places else (3 - x, y ^ 1)
+        x2, y2 = (x ^ 1, y ^ 1) if (c == 0) == of_places else (3 - x, 3 - y)
         return zl, x2 if flip & 2 else x, y2 if flip & 1 else y, c, t
 
     return move(array, target)
@@ -66,7 +66,7 @@
 def here(dev):
     dp = dev[0] // 4
     core, x, y = dp % 2, dp // 8 % 4, dp // 2 % 4
-    a, b = 2 * bit_a(x) + bit_b(y), 2 * bit_b(x) + bit_a(y)
+    a, b = 2 * bit_a(x) + bit_a(y), 2 * bit_b(x) + bit_b(y)
     return core, jnp.where(core == 0, a, b), jnp.where(core == 0, b, a)
 
 
@@ -145,7 +145,7 @@
                 tile = tile + DAMPING * eye[:TILE, :TILE]
             mixed[low : low + TILE, TILE * j : TILE * (j + 1)] = tile
             squares = squares + (1.0 if i == j else 2.0) * tile * tile
-            if i != j:
+            if (i, j) in ((0, 1), (2, 3)):
                 mixed[TILE * j : TILE * (j + 1), low : low + TILE] = tile.T
     norm_scale = jnp.sqrt(jnp.sum(squares))
     scale = 1.0 / norm_scale
@@ -154,32 +154,41 @@
         return jnp.dot(a, b, preferred_element_type=jnp.float32)
 
     bands = (slice(0, 256), slice(256, 512), slice(512, 640))
+
+    def keep(whole, band, value):
+        value = value.astype(jnp.bfloat16)
+        whole[band, band.start :] = value
+        if band.stop < BLOCK:
+            whole[band.stop :, band] = value[:, band.stop - band.start :].T
+
     for band in bands:
-        start = mixed[band, :] * scale
-        gap[band, :] = start
-        mixed_half[0, band, :] = start.astype(jnp.bfloat16)
-        gap_half[band, :] = start.astype(jnp.bfloat16)
+        start = mixed[band, band.start :] * scale
+        gap[band, band.start :] = start
+        keep(mixed_half.at[0], band, start)
+        keep(gap_half.at[1], band, start)
     for band in bands:
-        value = 2.0 * gap[band, :] - dot(mixed_half[0, band, :], mixed_half[0])
-        mixed[band, :] = value
-        mixed_half[1, band, :] = value.astype(jnp.bfloat16)
+        right = slice(band.start, BLOCK)
+        value = 2.0 * gap[band, right] - dot(mixed_half[0, band, :], mixed_half[0, :, right])
+        mixed[band, right] = value
+        keep(mixed_half.at[1], band, value)
     for turn in range(1, 3):
         now = turn % 2
         for band in bands:
-            old, old_gap = mixed[band, :], gap[band, :]
-            new = 2.0 * old - dot(mixed_half[now, band, :], mixed_half[now])
-            mixed[band, :] = new
-            mixed_half[1 - now, band, :] = new.astype(jnp.bfloat16)
-            new_gap = 2.0 * old_gap + 2.0**turn * old - dot(gap_half[band, :], mixed_half[now])
+            right = slice(band.start, BLOCK)
+            old, old_gap, operand = mixed[band, right], gap[band, right], mixed_half[now, :, right]
+            new = 2.0 * old - dot(mixed_half[now, band, :], operand)
+            mixed[band, right] = new
+            keep(mixed_half.at[1 - now], band, new)
+            new_gap = 2.0 * old_gap + 2.0**turn * old - dot(gap_half[now, band, :], operand)
             new_gap = jnp.where(turn < steps, new_gap, old_gap)
-            gap[band, :] = new_gap
-            gap_half[band, :] = new_gap.astype(jnp.bfloat16)
+            gap[band, right] = new_gap
+            keep(gap_half.at[1 - now], band, new_gap)
     reach = jnp.where(steps <= 1, 2.0, jnp.where(steps == 2, 4.0, jnp.where(steps == 3, 8.0, 16.0)))
     for band in bands:
         begin = band.start
         old_gap = gap[band, begin:]
         new_gap = 2.0 * old_gap + 8.0 * mixed[band, begin:]
-        new_gap = new_gap - dot(gap_half[band, :], mixed_half[1, :, begin:])
+        new_gap = new_gap - dot(gap_half[1, band, :], mixed_half[1, :, begin:])
         value = reach * eye[band, begin:] - jnp.where(3 < steps, new_gap, old_gap)
         value = (value * scale).astype(jnp.bfloat16)
         for i in range(begin // TILE, band.stop // TILE):
@@ -308,7 +317,7 @@
             pltpu.VMEM((BLOCK, BLOCK), jnp.float32),
             pltpu.VMEM((BLOCK, BLOCK), jnp.float32),
             pltpu.VMEM((2, BLOCK, BLOCK), half),
-            pltpu.VMEM((BLOCK, BLOCK), half),
+            pltpu.VMEM((2, BLOCK, BLOCK), half),
         ],
         compiler_params=PARAMS,
         name="newton",

time: 119 us -> 114 us (0.958); the launches traced: 119 us -> 113 us
  starting transfers between devices: 68.3 us -> 63.8 us
  Pallas kernels: 17.6 us -> 16.4 us
    ppermute x33, starting transfers between devices: 68.3 us -> 63.8 us  [move(): return lax.ppermute(array, AXES, pairs)]
  transfers between devices with their start and end apart: 33 -> 33, of which waited for: 15 -> 12; matrix products, arithmetic and copies ran while one was open for 0% -> 0% of each run, Pallas kernels for 5% -> 5%
where the time goes in v9:
time: 114 us; the launch traced here: 113 us
  starting transfers between devices  63.8 us (56%)
  waiting for transfers between devices  30.6 us (27%)
  Pallas kernels  16.4 us (14%)
    ppermute x33, starting transfers between devices, move(): return lax.ppermute(array, AXES, pairs)  63.8 us
    ppermute x33, waiting for transfers between devices, move(): return lax.ppermute(array, AXES, pairs)  30.6 us
    pallas_call x2, Pallas kernels, apply(): pl.pallas_call(functools.partial(apply_kernel, side), out_shape=[shape(*d...  5.18 us
    pallas_call x1, Pallas kernels, local(): pl.pallas_call(functools.partial(newton_kernel, tokens_all), out_shape=sh...  4.69 us
    pallas_call x2, Pallas kernels, factors(): pl.pallas_call(gram_kernel, out_shape=[shape(2, CHUNK, BLOCK)] * RING, in...  3.59 us
    pallas_call x1, Pallas kernels, local(): pl.pallas_call(pack_kernel, out_shape=([shape(*part)] * RING + [shape(RIN...  2.97 us
  transfers between devices with their start and end apart: 33, of which 12 were waited for; matrix products, arithmetic and copies ran while one was open for 0% of the time, Pallas kernels for 5%

profile of v9, /device:TPU:1, one launch (start us, length us, event | category | flops | bytes accessed | tf_op | source)
XLA Modules:
  0.0 112.5 jit_solution(17948898327239922443)
XLA Ops:
  0.6 3.0 %pack.1 = (bf16[2,128,640]{2,1,0:T(8,128)(2,1)S(1)}, bf16[2,128,640]{2,1,0:T(8,128)(2,1)S(1)}, bf16[2,128,640]{2,1,0:T(8,128)(2,1)S(1)}, bf16[2,128,640]{2,1,0:T...) custom-call(s32[1]{0:T(128)} %bitcast.dev, ...), custom_call_target="tpu_custom_call" | custom-call | tf_op jit(solution)/shard_map/pack/pallas_call | solution.py:278
  3.6 3.3 %collective-permute-start.13 = (bf16[4,2,128,640]{3,2,1,0:T(8,128)(2,1)S(1)}, bf16[4,2,128,640]{3,2,1,0:T(8,128)(2,1)S(1)}, u32[]{:S(2)}, u32[]{:S(2)}) collective-permute-start(bf16[4,2,128,640]{3,2,1,0:T(8,128)(2,1)S(1)} %get-tuple-element.35), channel_id=1, source_target_pairs={{0,4},{1,5},{2,6},{3,7},{4,0},{5,1},{6,2},{7,3},{8,12},{9,13},{10,... | collective-permute-start | bytes 3932168 | tf_op jit(solution)/shard_map/ppermute | solution.py:43
  6.9 0.1 collective-permute-start.3
  7.0 3.2 %collective-permute-start = (bf16[2,128,640]{2,1,0:T(8,128)(2,1)S(1)}, bf16[2,128,640]{2,1,0:T(8,128)(2,1)S(1)}, u32[]{:S(2)}, u32[]{:S(2)}) collective-permute-start(bf16[2,128,640]{2,1,0:T(8,128)(2,1)S(1)} %get-tuple-element.22), channel_id=1, source_target_pairs={{0,40},{1,41},{2,42},{3,43},{4,124},{5,125},{6,126},{7,127},{8,32}... | collective-permute-start | bytes 983048 | tf_op jit(solution)/shard_map/ppermute | solution.py:43
  10.2 1.6 %collective-permute-start.10 = (bf16[2,128,640]{2,1,0:T(8,128)(2,1)S(1)}, bf16[2,128,640]{2,1,0:T(8,128)(2,1)S(1)}, u32[]{:S(2)}, u32[]{:S(2)}) collective-permute-start(bf16[2,128,640]{2,1,0:T(8,128)(2,1)S(1)} %get-tuple-element.31), channel_id=1, source_target_pairs={{0,40},{1,41},{2,42},{3,43},{4,124},{5,125},{6,126},{7,127},{8,32}... | collective-permute-start | bytes 983048 | tf_op jit(solution)/shard_map/ppermute | solution.py:43
  11.8 0.7 collective-permute-start.11
  12.6 0.0 collective-permute-done.13.refs_7_
  12.6 2.7 %collective-permute-start.12 = (bf16[2,128,640]{2,1,0:T(8,128)(2,1)S(1)}, bf16[2,128,640]{2,1,0:T(8,128)(2,1)S(1)}, u32[]{:S(2)}, u32[]{:S(2)}) collective-permute-start(bf16[2,128,640]{2,1,0:T(8,128)(2,1)S(1)} %get-tuple-element.33), channel_id=1, source_target_pairs={{0,8},{1,9},{2,10},{3,11},{4,28},{5,29},{6,30},{7,31},{8,0},{9,1},... | collective-permute-start | bytes 983048 | tf_op jit(solution)/shard_map/ppermute | solution.py:43
  15.3 0.1 slice_bitcast_fusion
  15.4 0.9 collective-permute-done.refs_0_
  16.3 1.0 collective-permute-start.16
  17.3 2.6 %collective-permute-done.10.refs_0_ = bf16[2,128,640]{2,1,0:T(8,128)(2,1)S(1)} collective-permute-done((bf16[2,128,640]{2,1,0:T(8,128)(2,1)S(1)}, bf16[2,128,640]{2,1,0:T(8,128)(2,1)S(1)}, u32[]{:S(2)}, u32[]{:S(2)}) %collective-permute-start.10) | collective-permute-done | bytes 327712 | tf_op jit(solution)/shard_map/ppermute | solution.py:43
  19.9 0.7 collective-permute-start.15
  20.6 2.6 %collective-permute-start.14 = (bf16[2,128,640]{2,1,0:T(8,128)(2,1)S(1)}, bf16[2,128,640]{2,1,0:T(8,128)(2,1)S(1)}, u32[]{:S(2)}, u32[]{:S(2)}) collective-permute-start(bf16[2,128,640]{2,1,0:T(8,128)(2,1)S(1)} %get-tuple-element.47), channel_id=1, source_target_pairs={{0,40},{1,41},{2,42},{3,43},{4,124},{5,125},{6,126},{7,127},{8,32}... | collective-permute-start | bytes 983048 | tf_op jit(solution)/shard_map/ppermute | solution.py:43
  23.3 0.1 slice_bitcast_fusion.3
  23.4 0.0 collective-permute-done.11.refs_1_
  23.4 2.6 %collective-permute-start.1 = (bf16[2,128,640]{2,1,0:T(8,128)(2,1)S(1)}, bf16[2,128,640]{2,1,0:T(8,128)(2,1)S(1)}, u32[]{:S(2)}, u32[]{:S(2)}) collective-permute-start(bf16[2,128,640]{2,1,0:T(8,128)(2,1)S(1)} %get-tuple-element.23), channel_id=1, source_target_pairs={{0,32},{1,33},{2,34},{3,35},{4,100},{5,101},{6,102},{7,103},{8,40}... | collective-permute-start | bytes 983048 | tf_op jit(solution)/shard_map/ppermute | solution.py:43
  26.0 0.0 collective-permute-done.12.refs_2_
  26.0 0.0 collective-permute-start.2
  26.0 1.0 collective-permute-done.16.refs_6_
  27.0 1.7 %collective-permute-start.6 = (bf16[2,128,640]{2,1,0:T(8,128)(2,1)S(1)}, bf16[2,128,640]{2,1,0:T(8,128)(2,1)S(1)}, u32[]{:S(2)}, u32[]{:S(2)}) collective-permute-start(bf16[2,128,640]{2,1,0:T(8,128)(2,1)S(1)} %get-tuple-element.42), channel_id=1, source_target_pairs={{0,8},{1,9},{2,10},{3,11},{4,28},{5,29},{6,30},{7,31},{8,0},{9,1},... | collective-permute-start | bytes 983048 | tf_op jit(solution)/shard_map/ppermute | solution.py:43
  28.7 0.0 collective-permute-done.15.refs_5_
  28.7 1.8 %collective-permute-start.5 = (bf16[2,128,640]{2,1,0:T(8,128)(2,1)S(1)}, bf16[2,128,640]{2,1,0:T(8,128)(2,1)S(1)}, u32[]{:S(2)}, u32[]{:S(2)}) collective-permute-start(bf16[2,128,640]{2,1,0:T(8,128)(2,1)S(1)} %get-tuple-element.43), channel_id=1, source_target_pairs={{0,32},{1,33},{2,34},{3,35},{4,100},{5,101},{6,102},{7,103},{8,40}... | collective-permute-start | bytes 983048 | tf_op jit(solution)/shard_map/ppermute | solution.py:43
  30.4 0.9 collective-permute-done.14.refs_4_
  31.4 2.3 %collective-permute-start.4 = (bf16[2,128,640]{2,1,0:T(8,128)(2,1)S(1)}, bf16[2,128,640]{2,1,0:T(8,128)(2,1)S(1)}, u32[]{:S(2)}, u32[]{:S(2)}) collective-permute-start(bf16[2,128,640]{2,1,0:T(8,128)(2,1)S(1)} %get-tuple-element.44), channel_id=1, source_target_pairs={{0,40},{1,41},{2,42},{3,43},{4,124},{5,125},{6,126},{7,127},{8,32}... | collective-permute-start | bytes 983048 | tf_op jit(solution)/shard_map/ppermute | solution.py:43
  33.7 1.8 %gram.3 = (bf16[2,96,640]{2,1,0:T(8,128)(2,1)S(1)}, bf16[2,96,640]{2,1,0:T(8,128)(2,1)S(1)}, bf16[2,96,640]{2,1,0:T(8,128)(2,1)S(1)}, bf16[2,96,640]{2,1,0:T(8,128)(2,1)S(1)}) custom-call(s32[1]{0:T(128)} %bitcast.dev, bf16[2,128,640]{2,1,0:T(8,128)(2,1)S(1)} %collective-permute-done.10.refs_0_, bf16[2,128,640]{2,1,0:T(8,128)(2,1)S(1)} %collective-permute-done.11.refs_1_, ...), custom_call_target="tpu_custom_call" | custom-call | tf_op jit(solution)/shard_map/gram/pallas_call | solution.py:292
  35.5 0.0 collective-permute-done.1.refs_1_
  35.5 0.1 collective-permute-start.17
  35.6 0.1 collective-permute-start.18
  35.7 2.7 %collective-permute-done.6.refs_6_ = bf16[2,128,640]{2,1,0:T(8,128)(2,1)S(1)} collective-permute-done((bf16[2,128,640]{2,1,0:T(8,128)(2,1)S(1)}, bf16[2,128,640]{2,1,0:T(8,128)(2,1)S(1)}, u32[]{:S(2)}, u32[]{:S(2)}) %collective-permute-start.6) | collective-permute-done | bytes 327712 | tf_op jit(solution)/shard_map/ppermute | solution.py:43
  38.4 0.0 collective-permute-start.19
  38.4 6.0 %collective-permute-done.4.refs_4_ = bf16[2,128,640]{2,1,0:T(8,128)(2,1)S(1)} collective-permute-done((bf16[2,128,640]{2,1,0:T(8,128)(2,1)S(1)}, bf16[2,128,640]{2,1,0:T(8,128)(2,1)S(1)}, u32[]{:S(2)}, u32[]{:S(2)}) %collective-permute-start.4) | collective-permute-done | bytes 327712 | tf_op jit(solution)/shard_map/ppermute | solution.py:43
  44.4 1.8 %gram.2 = (bf16[2,96,640]{2,1,0:T(8,128)(2,1)S(1)}, bf16[2,96,640]{2,1,0:T(8,128)(2,1)S(1)}, bf16[2,96,640]{2,1,0:T(8,128)(2,1)S(1)}, bf16[2,96,640]{2,1,0:T(8,128)(2,1)S(1)}) custom-call(s32[1]{0:T(128)} %bitcast.dev, bf16[2,128,640]{2,1,0:T(8,128)(2,1)S(1)} %collective-permute-done.refs_0_, bf16[2,128,640]{2,1,0:T(8,128)(2,1)S(1)} %collective-permute-done.1.refs_1_, ...), custom_call_target="tpu_custom_call" | custom-call | tf_op jit(solution)/shard_map/gram/pallas_call | solution.py:292
  46.2 0.1 collective-permute-start.7
  46.3 0.1 collective-permute-start.8
  46.5 2.5 %collective-permute-start.9 = (bf16[2,96,640]{2,1,0:T(8,128)(2,1)S(1)}, bf16[2,96,640]{2,1,0:T(8,128)(2,1)S(1)}, u32[]{:S(2)}, u32[]{:S(2)}) collective-permute-start(bf16[2,96,640]{2,1,0:T(8,128)(2,1)S(1)} %get-tuple-element.29), channel_id=1, source_target_pairs={{0,24},{1,25},{2,26},{3,27},{4,12},{5,13},{6,14},{7,15},{8,16},{9,... | collective-permute-start | bytes 737288 | tf_op jit(solution)/shard_map/ppermute | solution.py:43
  49.0 0.0 collective-permute-done.18
  49.0 0.0 collective-permute-done.19
  49.0 0.1 add_convert_fusion
  49.1 6.7 %collective-permute-start.20 = (bf16[2,96,640]{2,1,0:T(8,128)(2,1)S(1)}, bf16[2,96,640]{2,1,0:T(8,128)(2,1)S(1)}, u32[]{:S(2)}, u32[]{:S(2)}) collective-permute-start(bf16[2,96,640]{2,1,0:T(8,128)(2,1)S(1)} %add_convert_fusion), channel_id=1, source_target_pairs={{0,1},{1,0},{2,3},{3,2},{4,7},{5,6},{6,5},{7,4},{8,9},{9,8},{10,11... | collective-permute-start | bytes 737288 | tf_op jit(solution)/shard_map/ppermute | solution.py:43
  55.8 0.0 collective-permute-done.7
  55.9 5.8 %collective-permute-done.20 = bf16[2,96,640]{2,1,0:T(8,128)(2,1)S(1)} collective-permute-done((bf16[2,96,640]{2,1,0:T(8,128)(2,1)S(1)}, bf16[2,96,640]{2,1,0:T(8,128)(2,1)S(1)}, u32[]{:S(2)}, u32[]{:S(2)}) %collective-permute-start.20) | collective-permute-done | bytes 245792 | tf_op jit(solution)/shard_map/ppermute | solution.py:43
  61.6 0.1 convert_add_fusion
  61.8 0.0 copy-start
  61.8 1.7 %collective-permute-start.21 = (bf16[96,640]{1,0:T(8,128)(2,1)S(1)}, bf16[96,640]{1,0:T(8,128)(2,1)S(1)}, u32[]{:S(2)}, u32[]{:S(2)}) collective-permute-start(bf16[96,640]{1,0:T(8,128)(2,1)S(1)} %fusion.2), channel_id=1, source_target_pairs={{0,3},{1,2},{2,1},{3,0},{4,5},{5,4},{6,7},{7,6},{8,11},{9,10},{10,... | collective-permute-start | bytes 368648 | tf_op jit(solution)/shard_map/ppermute | solution.py:43
  63.5 3.4 %collective-permute-done.21 = bf16[96,640]{1,0:T(8,128)(2,1)S(1)} collective-permute-done((bf16[96,640]{1,0:T(8,128)(2,1)S(1)}, bf16[96,640]{1,0:T(8,128)(2,1)S(1)}, u32[]{:S(2)}, u32[]{:S(2)}) %collective-permute-start.21) | collective-permute-done | bytes 122912 | tf_op jit(solution)/shard_map/ppermute | solution.py:43
  66.9 1.7 %collective-permute-start.22 = (bf16[96,640]{1,0:T(8,128)(2,1)S(1)}, bf16[96,640]{1,0:T(8,128)(2,1)S(1)}, u32[]{:S(2)}, u32[]{:S(2)}) collective-permute-start(bf16[96,640]{1,0:T(8,128)(2,1)S(1)} %fusion.1), channel_id=1, source_target_pairs={{0,128},{1,129},{2,130},{3,131},{4,132},{5,133},{6,134},{7,135},{8... | collective-permute-start | bytes 368648 | tf_op jit(solution)/shard_map/ppermute | solution.py:43
  68.6 3.7 %collective-permute-done.22 = bf16[96,640]{1,0:T(8,128)(2,1)S(1)} collective-permute-done((bf16[96,640]{1,0:T(8,128)(2,1)S(1)}, bf16[96,640]{1,0:T(8,128)(2,1)S(1)}, u32[]{:S(2)}, u32[]{:S(2)}) %collective-permute-start.22) | collective-permute-done | bytes 122912 | tf_op jit(solution)/shard_map/ppermute | solution.py:43
  72.4 0.1 collective-permute-start.25
  72.5 0.1 collective-permute-start.24
  72.6 2.5 %collective-permute-start.23 = (bf16[96,640]{1,0:T(8,128)(2,1)S(1)}, bf16[96,640]{1,0:T(8,128)(2,1)S(1)}, u32[]{:S(2)}, u32[]{:S(2)}) collective-permute-start(bf16[96,640]{1,0:T(8,128)(2,1)S(1)} %add_convert_fusion.1.refs_3_), channel_id=1, source_target_pairs={{0,120},{1,121},{2,122},{3,123},{4,44},{5,45},{6,46},{7,47},{8,112... | collective-permute-start | bytes 368648 | tf_op jit(solution)/shard_map/ppermute | solution.py:43
  75.1 1.1 collective-permute-done.25.refs_2_
  76.2 0.1 collective-permute-done.24.refs_1_
  76.3 2.4 %collective-permute-done.23.refs_0_ = bf16[96,640]{1,0:T(8,128)(2,1)S(1)} collective-permute-done((bf16[96,640]{1,0:T(8,128)(2,1)S(1)}, bf16[96,640]{1,0:T(8,128)(2,1)S(1)}, u32[]{:S(2)}, u32[]{:S(2)}) %collective-permute-start.23) | collective-permute-done | bytes 122912 | tf_op jit(solution)/shard_map/ppermute | solution.py:43
  78.7 4.7 %newton.1.refs_0_ = bf16[384,640]{1,0:T(8,128)(2,1)S(1)} custom-call(s32[1]{0:T(128)} %bitcast.dev, s32[2,2,8]{2,1,0:T(2,128)S(1)} %copy-done.2, bf16[96,640]{1,0:T(8,128)(2,1)S(1)} %collective-permute-done.23.refs_0_, bf16[96,640]{1,0:T(8,128)(2,1)S(1)} %collective-permute-done.24.refs_1_, bf16[96,640]{1,0:T(8,128)(2,1)S(1)} %collective-permute-done.25.refs_2_, ...), custom_call_target="tpu_custom_call" | custom-call | tf_op jit(solution)/shard_map/newton/pallas_call | solution.py:310
  83.4 0.8 collective-permute-start.31
  84.2 2.1 %collective-permute-start.29 = (bf16[384,640]{1,0:T(8,128)(2,1)S(1)}, bf16[384,640]{1,0:T(8,128)(2,1)S(1)}, u32[]{:S(2)}, u32[]{:S(2)}) collective-permute-start(bf16[384,640]{1,0:T(8,128)(2,1)S(1)} %newton.1.refs_0_), channel_id=1, source_target_pairs={{0,32},{1,33},{2,34},{3,35},{4,100},{5,101},{6,102},{7,103},{8,40}... | collective-permute-start | bytes 1474568 | tf_op jit(solution)/shard_map/ppermute | solution.py:43
  86.3 2.3 %collective-permute-start.27 = (bf16[384,640]{1,0:T(8,128)(2,1)S(1)}, bf16[384,640]{1,0:T(8,128)(2,1)S(1)}, u32[]{:S(2)}, u32[]{:S(2)}) collective-permute-start(bf16[384,640]{1,0:T(8,128)(2,1)S(1)} %newton.1.refs_0_), channel_id=1, source_target_pairs={{0,8},{1,9},{2,10},{3,11},{4,28},{5,29},{6,30},{7,31},{8,0},{9,1},... | collective-permute-start | bytes 1474568 | tf_op jit(solution)/shard_map/ppermute | solution.py:43
  88.6 6.6 %collective-permute-start.26 = (bf16[384,640]{1,0:T(8,128)(2,1)S(1)}, bf16[384,640]{1,0:T(8,128)(2,1)S(1)}, u32[]{:S(2)}, u32[]{:S(2)}) collective-permute-start(bf16[384,640]{1,0:T(8,128)(2,1)S(1)} %newton.1.refs_0_), channel_id=1, source_target_pairs={{0,4},{1,5},{2,6},{3,7},{4,0},{5,1},{6,2},{7,3},{8,12},{9,13},{10,... | collective-permute-start | bytes 1474568 | tf_op jit(solution)/shard_map/ppermute | solution.py:43
  95.2 6.3 %collective-permute-start.32 = (bf16[384,640]{1,0:T(8,128)(2,1)S(1)}, bf16[384,640]{1,0:T(8,128)(2,1)S(1)}, u32[]{:S(2)}, u32[]{:S(2)}) collective-permute-start(bf16[384,640]{1,0:T(8,128)(2,1)S(1)} %collective-permute-done.31.refs_3_), channel_id=1, source_target_pairs={{0,4},{1,5},{2,6},{3,7},{4,0},{5,1},{6,2},{7,3},{8,12},{9,13},{10,... | collective-permute-start | bytes 1474568 | tf_op jit(solution)/shard_map/ppermute | solution.py:43
  101.6 5.5 %collective-permute-start.30 = (bf16[384,640]{1,0:T(8,128)(2,1)S(1)}, bf16[384,640]{1,0:T(8,128)(2,1)S(1)}, u32[]{:S(2)}, u32[]{:S(2)}) collective-permute-start(bf16[384,640]{1,0:T(8,128)(2,1)S(1)} %collective-permute-done.29.refs_2_), channel_id=1, source_target_pairs={{0,4},{1,5},{2,6},{3,7},{4,0},{5,1},{6,2},{7,3},{8,12},{9,13},{10,... | collective-permute-start | bytes 1474568 | tf_op jit(solution)/shard_map/ppermute | solution.py:43
  107.1 0.0 collective-permute-start.28
  107.1 2.6 %apply.2 = (bf16[2,240,1280]{2,1,0:T(8,128)(2,1)}, bf16[2,320,1280]{2,1,0:T(8,128)(2,1)}) custom-call(s32[1]{0:T(128)} %bitcast.dev, bf16[384,640]{1,0:T(8,128)(2,1)S(1)} %newton.1.refs_0_, bf16[384,640]{1,0:T(8,128)(2,1)S(1)} %collective-permute-done.27.refs_1_, bf16[384,640]{1,0:T(8,128)(2,1)S(1)} %collective-permute-done.29.refs_2_, ...), custom_call_target="tpu_custom_call" | custom-call | tf_op jit(solution)/shard_map/apply/pallas_call | solution.py:331
  109.7 2.6 %apply.3 = (bf16[2,240,1280]{2,1,0:T(8,128)(2,1)}, bf16[2,320,1280]{2,1,0:T(8,128)(2,1)}) custom-call(s32[1]{0:T(128)} %bitcast.dev, bf16[384,640]{1,0:T(8,128)(2,1)S(1)} %collective-permute-done.26.refs_0_, bf16[384,640]{1,0:T(8,128)(2,1)S(1)} %collective-permute-done.28.refs_1_, ...), custom_call_target="tpu_custom_call", output_to_operand_aliasing={{0}: (7, {}), {1}: (8, {})} | custom-call | tf_op jit(solution)/shard_map/apply/pallas_call | solution.py:331
  (21 shorter events, 0.1 us)
Async XLA Ops:
  3.6 9.0 %collective-permute-start.13 = (bf16[4,2,128,640]{3,2,1,0:T(8,128)(2,1)S(1)}, bf16[4,2,128,640]{3,2,1,0:T(8,128)(2,1)S(1)}, u32[]{:S(2)}, u32[]{:S(2)}) collective-permute-start(bf16[4,2,128,640]{3,2,1,0:T(8,128)(2,1)S(1)} %get-tuple-element.35), channel_id=1, source_target_pairs={{0,4},{1,5},{2,6},{3,7},{4,0},{5,1},{6,2},{7,3},{8,12},{9,13},{10,... | collective-permute-start | bytes 3932168 | tf_op jit(solution)/shard_map/ppermute | solution.py:43
  6.9 13.7 %collective-permute-start.3 = (bf16[4,2,128,640]{3,2,1,0:T(8,128)(2,1)S(1)}, bf16[4,2,128,640]{3,2,1,0:T(8,128)(2,1)S(1)}, u32[]{:S(2)}, u32[]{:S(2)}) collective-permute-start(bf16[4,2,128,640]{3,2,1,0:T(8,128)(2,1)S(1)} %get-tuple-element.26), channel_id=1, source_target_pairs={{0,4},{1,5},{2,6},{3,7},{4,0},{5,1},{6,2},{7,3},{8,12},{9,13},{10,... | collective-permute-start | bytes 3932168 | tf_op jit(solution)/shard_map/ppermute | solution.py:43
  7.0 9.2 %collective-permute-start = (bf16[2,128,640]{2,1,0:T(8,128)(2,1)S(1)}, bf16[2,128,640]{2,1,0:T(8,128)(2,1)S(1)}, u32[]{:S(2)}, u32[]{:S(2)}) collective-permute-start(bf16[2,128,640]{2,1,0:T(8,128)(2,1)S(1)} %get-tuple-element.22), channel_id=1, source_target_pairs={{0,40},{1,41},{2,42},{3,43},{4,124},{5,125},{6,126},{7,127},{8,32}... | collective-permute-start | bytes 983048 | tf_op jit(solution)/shard_map/ppermute | solution.py:43
  10.2 9.7 %collective-permute-start.10 = (bf16[2,128,640]{2,1,0:T(8,128)(2,1)S(1)}, bf16[2,128,640]{2,1,0:T(8,128)(2,1)S(1)}, u32[]{:S(2)}, u32[]{:S(2)}) collective-permute-start(bf16[2,128,640]{2,1,0:T(8,128)(2,1)S(1)} %get-tuple-element.31), channel_id=1, source_target_pairs={{0,40},{1,41},{2,42},{3,43},{4,124},{5,125},{6,126},{7,127},{8,32}... | collective-permute-start | bytes 983048 | tf_op jit(solution)/shard_map/ppermute | solution.py:43
  11.8 11.6 %collective-permute-start.11 = (bf16[2,128,640]{2,1,0:T(8,128)(2,1)S(1)}, bf16[2,128,640]{2,1,0:T(8,128)(2,1)S(1)}, u32[]{:S(2)}, u32[]{:S(2)}) collective-permute-start(bf16[2,128,640]{2,1,0:T(8,128)(2,1)S(1)} %get-tuple-element.32), channel_id=1, source_target_pairs={{0,32},{1,33},{2,34},{3,35},{4,100},{5,101},{6,102},{7,103},{8,40}... | collective-permute-start | bytes 983048 | tf_op jit(solution)/shard_map/ppermute | solution.py:43
  12.6 13.4 %collective-permute-start.12 = (bf16[2,128,640]{2,1,0:T(8,128)(2,1)S(1)}, bf16[2,128,640]{2,1,0:T(8,128)(2,1)S(1)}, u32[]{:S(2)}, u32[]{:S(2)}) collective-permute-start(bf16[2,128,640]{2,1,0:T(8,128)(2,1)S(1)} %get-tuple-element.33), channel_id=1, source_target_pairs={{0,8},{1,9},{2,10},{3,11},{4,28},{5,29},{6,30},{7,31},{8,0},{9,1},... | collective-permute-start | bytes 983048 | tf_op jit(solution)/shard_map/ppermute | solution.py:43
  16.3 10.7 %collective-permute-start.16 = (bf16[2,128,640]{2,1,0:T(8,128)(2,1)S(1)}, bf16[2,128,640]{2,1,0:T(8,128)(2,1)S(1)}, u32[]{:S(2)}, u32[]{:S(2)}) collective-permute-start(bf16[2,128,640]{2,1,0:T(8,128)(2,1)S(1)} %get-tuple-element.45), channel_id=1, source_target_pairs={{0,8},{1,9},{2,10},{3,11},{4,28},{5,29},{6,30},{7,31},{8,0},{9,1},... | collective-permute-start | bytes 983048 | tf_op jit(solution)/shard_map/ppermute | solution.py:43
  19.9 8.8 %collective-permute-start.15 = (bf16[2,128,640]{2,1,0:T(8,128)(2,1)S(1)}, bf16[2,128,640]{2,1,0:T(8,128)(2,1)S(1)}, u32[]{:S(2)}, u32[]{:S(2)}) collective-permute-start(bf16[2,128,640]{2,1,0:T(8,128)(2,1)S(1)} %get-tuple-element.46), channel_id=1, source_target_pairs={{0,32},{1,33},{2,34},{3,35},{4,100},{5,101},{6,102},{7,103},{8,40}... | collective-permute-start | bytes 983048 | tf_op jit(solution)/shard_map/ppermute | solution.py:43
  20.6 10.7 %collective-permute-start.14 = (bf16[2,128,640]{2,1,0:T(8,128)(2,1)S(1)}, bf16[2,128,640]{2,1,0:T(8,128)(2,1)S(1)}, u32[]{:S(2)}, u32[]{:S(2)}) collective-permute-start(bf16[2,128,640]{2,1,0:T(8,128)(2,1)S(1)} %get-tuple-element.47), channel_id=1, source_target_pairs={{0,40},{1,41},{2,42},{3,43},{4,124},{5,125},{6,126},{7,127},{8,32}... | collective-permute-start | bytes 983048 | tf_op jit(solution)/shard_map/ppermute | solution.py:43
  23.4 12.1 %collective-permute-start.1 = (bf16[2,128,640]{2,1,0:T(8,128)(2,1)S(1)}, bf16[2,128,640]{2,1,0:T(8,128)(2,1)S(1)}, u32[]{:S(2)}, u32[]{:S(2)}) collective-permute-start(bf16[2,128,640]{2,1,0:T(8,128)(2,1)S(1)} %get-tuple-element.23), channel_id=1, source_target_pairs={{0,32},{1,33},{2,34},{3,35},{4,100},{5,101},{6,102},{7,103},{8,40}... | collective-permute-start | bytes 983048 | tf_op jit(solution)/shard_map/ppermute | solution.py:43
  26.0 9.6 %collective-permute-start.2 = (bf16[2,128,640]{2,1,0:T(8,128)(2,1)S(1)}, bf16[2,128,640]{2,1,0:T(8,128)(2,1)S(1)}, u32[]{:S(2)}, u32[]{:S(2)}) collective-permute-start(bf16[2,128,640]{2,1,0:T(8,128)(2,1)S(1)} %get-tuple-element.24), channel_id=1, source_target_pairs={{0,8},{1,9},{2,10},{3,11},{4,28},{5,29},{6,30},{7,31},{8,0},{9,1},... | collective-permute-start | bytes 983048 | tf_op jit(solution)/shard_map/ppermute | solution.py:43
  27.0 11.5 %collective-permute-start.6 = (bf16[2,128,640]{2,1,0:T(8,128)(2,1)S(1)}, bf16[2,128,640]{2,1,0:T(8,128)(2,1)S(1)}, u32[]{:S(2)}, u32[]{:S(2)}) collective-permute-start(bf16[2,128,640]{2,1,0:T(8,128)(2,1)S(1)} %get-tuple-element.42), channel_id=1, source_target_pairs={{0,8},{1,9},{2,10},{3,11},{4,28},{5,29},{6,30},{7,31},{8,0},{9,1},... | collective-permute-start | bytes 983048 | tf_op jit(solution)/shard_map/ppermute | solution.py:43
  28.7 9.8 %collective-permute-start.5 = (bf16[2,128,640]{2,1,0:T(8,128)(2,1)S(1)}, bf16[2,128,640]{2,1,0:T(8,128)(2,1)S(1)}, u32[]{:S(2)}, u32[]{:S(2)}) collective-permute-start(bf16[2,128,640]{2,1,0:T(8,128)(2,1)S(1)} %get-tuple-element.43), channel_id=1, source_target_pairs={{0,32},{1,33},{2,34},{3,35},{4,100},{5,101},{6,102},{7,103},{8,40}... | collective-permute-start | bytes 983048 | tf_op jit(solution)/shard_map/ppermute | solution.py:43
  31.4 13.1 %collective-permute-start.4 = (bf16[2,128,640]{2,1,0:T(8,128)(2,1)S(1)}, bf16[2,128,640]{2,1,0:T(8,128)(2,1)S(1)}, u32[]{:S(2)}, u32[]{:S(2)}) collective-permute-start(bf16[2,128,640]{2,1,0:T(8,128)(2,1)S(1)} %get-tuple-element.44), channel_id=1, source_target_pairs={{0,40},{1,41},{2,42},{3,43},{4,124},{5,125},{6,126},{7,127},{8,32}... | collective-permute-start | bytes 983048 | tf_op jit(solution)/shard_map/ppermute | solution.py:43
  35.5 11.0 %collective-permute-start.17 = (bf16[2,96,640]{2,1,0:T(8,128)(2,1)S(1)}, bf16[2,96,640]{2,1,0:T(8,128)(2,1)S(1)}, u32[]{:S(2)}, u32[]{:S(2)}) collective-permute-start(bf16[2,96,640]{2,1,0:T(8,128)(2,1)S(1)} %get-tuple-element.36), channel_id=1, source_target_pairs={{0,120},{1,121},{2,122},{3,123},{4,44},{5,45},{6,46},{7,47},{8,112... | collective-permute-start | bytes 737288 | tf_op jit(solution)/shard_map/ppermute | solution.py:43
  35.6 13.4 %collective-permute-start.18 = (bf16[2,96,640]{2,1,0:T(8,128)(2,1)S(1)}, bf16[2,96,640]{2,1,0:T(8,128)(2,1)S(1)}, u32[]{:S(2)}, u32[]{:S(2)}) collective-permute-start(bf16[2,96,640]{2,1,0:T(8,128)(2,1)S(1)} %get-tuple-element.37), channel_id=1, source_target_pairs={{0,96},{1,97},{2,98},{3,99},{4,36},{5,37},{6,38},{7,39},{8,104},{9... | collective-permute-start | bytes 737288 | tf_op jit(solution)/shard_map/ppermute | solution.py:43
  38.4 10.6 %collective-permute-start.19 = (bf16[2,96,640]{2,1,0:T(8,128)(2,1)S(1)}, bf16[2,96,640]{2,1,0:T(8,128)(2,1)S(1)}, u32[]{:S(2)}, u32[]{:S(2)}) collective-permute-start(bf16[2,96,640]{2,1,0:T(8,128)(2,1)S(1)} %get-tuple-element.38), channel_id=1, source_target_pairs={{0,24},{1,25},{2,26},{3,27},{4,12},{5,13},{6,14},{7,15},{8,16},{9,... | collective-permute-start | bytes 737288 | tf_op jit(solution)/shard_map/ppermute | solution.py:43
  46.2 9.6 %collective-permute-start.7 = (bf16[2,96,640]{2,1,0:T(8,128)(2,1)S(1)}, bf16[2,96,640]{2,1,0:T(8,128)(2,1)S(1)}, u32[]{:S(2)}, u32[]{:S(2)}) collective-permute-start(bf16[2,96,640]{2,1,0:T(8,128)(2,1)S(1)} %get-tuple-element.27), channel_id=1, source_target_pairs={{0,120},{1,121},{2,122},{3,123},{4,44},{5,45},{6,46},{7,47},{8,112... | collective-permute-start | bytes 737288 | tf_op jit(solution)/shard_map/ppermute | solution.py:43
  46.3 9.5 %collective-permute-start.8 = (bf16[2,96,640]{2,1,0:T(8,128)(2,1)S(1)}, bf16[2,96,640]{2,1,0:T(8,128)(2,1)S(1)}, u32[]{:S(2)}, u32[]{:S(2)}) collective-permute-start(bf16[2,96,640]{2,1,0:T(8,128)(2,1)S(1)} %get-tuple-element.28), channel_id=1, source_target_pairs={{0,96},{1,97},{2,98},{3,99},{4,36},{5,37},{6,38},{7,39},{8,104},{9... | collective-permute-start | bytes 737288 | tf_op jit(solution)/shard_map/ppermute | solution.py:43
  46.5 9.4 %collective-permute-start.9 = (bf16[2,96,640]{2,1,0:T(8,128)(2,1)S(1)}, bf16[2,96,640]{2,1,0:T(8,128)(2,1)S(1)}, u32[]{:S(2)}, u32[]{:S(2)}) collective-permute-start(bf16[2,96,640]{2,1,0:T(8,128)(2,1)S(1)} %get-tuple-element.29), channel_id=1, source_target_pairs={{0,24},{1,25},{2,26},{3,27},{4,12},{5,13},{6,14},{7,15},{8,16},{9,... | collective-permute-start | bytes 737288 | tf_op jit(solution)/shard_map/ppermute | solution.py:43
  49.1 12.5 %collective-permute-start.20 = (bf16[2,96,640]{2,1,0:T(8,128)(2,1)S(1)}, bf16[2,96,640]{2,1,0:T(8,128)(2,1)S(1)}, u32[]{:S(2)}, u32[]{:S(2)}) collective-permute-start(bf16[2,96,640]{2,1,0:T(8,128)(2,1)S(1)} %add_convert_fusion), channel_id=1, source_target_pairs={{0,1},{1,0},{2,3},{3,2},{4,7},{5,6},{6,5},{7,4},{8,9},{9,8},{10,11... | collective-permute-start | bytes 737288 | tf_op jit(solution)/shard_map/ppermute | solution.py:43
  61.6 17.1 %copy-start.2 = (s32[2,2,8]{2,1,0:T(2,128)S(1)}, s32[2,2,8]{2,1,0:T(2,128)}, u32[]{:S(2)}) copy-start(s32[2,2,8]{2,1,0:T(2,128)} %newton_steps.1) | copy-start | bytes 388
  61.6 45.5 %copy-start.1 = (bf16[2,240,1280]{2,1,0:T(8,128)(2,1)S(1)}, bf16[2,240,1280]{2,1,0:T(8,128)(2,1)}, u32[]{:S(2)}) copy-start(bf16[2,240,1280]{2,1,0:T(8,128)(2,1)} %refs_4_.3) | copy-start | bytes 3686404
  61.8 45.3 %copy-start = (bf16[2,320,1280]{2,1,0:T(8,128)(2,1)S(1)}, bf16[2,320,1280]{2,1,0:T(8,128)(2,1)}, u32[]{:S(2)}) copy-start(bf16[2,320,1280]{2,1,0:T(8,128)(2,1)} %refs_5_.3) | copy-start | bytes 4915204
  61.8 5.1 %collective-permute-start.21 = (bf16[96,640]{1,0:T(8,128)(2,1)S(1)}, bf16[96,640]{1,0:T(8,128)(2,1)S(1)}, u32[]{:S(2)}, u32[]{:S(2)}) collective-permute-start(bf16[96,640]{1,0:T(8,128)(2,1)S(1)} %fusion.2), channel_id=1, source_target_pairs={{0,3},{1,2},{2,1},{3,0},{4,5},{5,4},{6,7},{7,6},{8,11},{9,10},{10,... | collective-permute-start | bytes 368648 | tf_op jit(solution)/shard_map/ppermute | solution.py:43
  66.9 5.4 %collective-permute-start.22 = (bf16[96,640]{1,0:T(8,128)(2,1)S(1)}, bf16[96,640]{1,0:T(8,128)(2,1)S(1)}, u32[]{:S(2)}, u32[]{:S(2)}) collective-permute-start(bf16[96,640]{1,0:T(8,128)(2,1)S(1)} %fusion.1), channel_id=1, source_target_pairs={{0,128},{1,129},{2,130},{3,131},{4,132},{5,133},{6,134},{7,135},{8... | collective-permute-start | bytes 368648 | tf_op jit(solution)/shard_map/ppermute | solution.py:43
  72.4 3.8 %collective-permute-start.25 = (bf16[96,640]{1,0:T(8,128)(2,1)S(1)}, bf16[96,640]{1,0:T(8,128)(2,1)S(1)}, u32[]{:S(2)}, u32[]{:S(2)}) collective-permute-start(bf16[96,640]{1,0:T(8,128)(2,1)S(1)} %add_convert_fusion.1.refs_3_), channel_id=1, source_target_pairs={{0,24},{1,25},{2,26},{3,27},{4,12},{5,13},{6,14},{7,15},{8,16},{9,... | collective-permute-start | bytes 368648 | tf_op jit(solution)/shard_map/ppermute | solution.py:43
  72.5 3.8 %collective-permute-start.24 = (bf16[96,640]{1,0:T(8,128)(2,1)S(1)}, bf16[96,640]{1,0:T(8,128)(2,1)S(1)}, u32[]{:S(2)}, u32[]{:S(2)}) collective-permute-start(bf16[96,640]{1,0:T(8,128)(2,1)S(1)} %add_convert_fusion.1.refs_3_), channel_id=1, source_target_pairs={{0,96},{1,97},{2,98},{3,99},{4,36},{5,37},{6,38},{7,39},{8,104},{9... | collective-permute-start | bytes 368648 | tf_op jit(solution)/shard_map/ppermute | solution.py:43
  72.6 6.1 %collective-permute-start.23 = (bf16[96,640]{1,0:T(8,128)(2,1)S(1)}, bf16[96,640]{1,0:T(8,128)(2,1)S(1)}, u32[]{:S(2)}, u32[]{:S(2)}) collective-permute-start(bf16[96,640]{1,0:T(8,128)(2,1)S(1)} %add_convert_fusion.1.refs_3_), channel_id=1, source_target_pairs={{0,120},{1,121},{2,122},{3,123},{4,44},{5,45},{6,46},{7,47},{8,112... | collective-permute-start | bytes 368648 | tf_op jit(solution)/shard_map/ppermute | solution.py:43
  83.4 11.9 %collective-permute-start.31 = (bf16[384,640]{1,0:T(8,128)(2,1)S(1)}, bf16[384,640]{1,0:T(8,128)(2,1)S(1)}, u32[]{:S(2)}, u32[]{:S(2)}) collective-permute-start(bf16[384,640]{1,0:T(8,128)(2,1)S(1)} %newton.1.refs_0_), channel_id=1, source_target_pairs={{0,40},{1,41},{2,42},{3,43},{4,124},{5,125},{6,126},{7,127},{8,32}... | collective-permute-start | bytes 1474568 | tf_op jit(solution)/shard_map/ppermute | solution.py:43
  84.2 17.4 %collective-permute-start.29 = (bf16[384,640]{1,0:T(8,128)(2,1)S(1)}, bf16[384,640]{1,0:T(8,128)(2,1)S(1)}, u32[]{:S(2)}, u32[]{:S(2)}) collective-permute-start(bf16[384,640]{1,0:T(8,128)(2,1)S(1)} %newton.1.refs_0_), channel_id=1, source_target_pairs={{0,32},{1,33},{2,34},{3,35},{4,100},{5,101},{6,102},{7,103},{8,40}... | collective-permute-start | bytes 1474568 | tf_op jit(solution)/shard_map/ppermute | solution.py:43
  86.3 20.8 %collective-permute-start.27 = (bf16[384,640]{1,0:T(8,128)(2,1)S(1)}, bf16[384,640]{1,0:T(8,128)(2,1)S(1)}, u32[]{:S(2)}, u32[]{:S(2)}) collective-permute-start(bf16[384,640]{1,0:T(8,128)(2,1)S(1)} %newton.1.refs_0_), channel_id=1, source_target_pairs={{0,8},{1,9},{2,10},{3,11},{4,28},{5,29},{6,30},{7,31},{8,0},{9,1},... | collective-permute-start | bytes 1474568 | tf_op jit(solution)/shard_map/ppermute | solution.py:43
  88.6 21.1 %collective-permute-start.26 = (bf16[384,640]{1,0:T(8,128)(2,1)S(1)}, bf16[384,640]{1,0:T(8,128)(2,1)S(1)}, u32[]{:S(2)}, u32[]{:S(2)}) collective-permute-start(bf16[384,640]{1,0:T(8,128)(2,1)S(1)} %newton.1.refs_0_), channel_id=1, source_target_pairs={{0,4},{1,5},{2,6},{3,7},{4,0},{5,1},{6,2},{7,3},{8,12},{9,13},{10,... | collective-permute-start | bytes 1474568 | tf_op jit(solution)/shard_map/ppermute | solution.py:43
  95.2 14.5 %collective-permute-start.32 = (bf16[384,640]{1,0:T(8,128)(2,1)S(1)}, bf16[384,640]{1,0:T(8,128)(2,1)S(1)}, u32[]{:S(2)}, u32[]{:S(2)}) collective-permute-start(bf16[384,640]{1,0:T(8,128)(2,1)S(1)} %collective-permute-done.31.refs_3_), channel_id=1, source_target_pairs={{0,4},{1,5},{2,6},{3,7},{4,0},{5,1},{6,2},{7,3},{8,12},{9,13},{10,... | collective-permute-start | bytes 1474568 | tf_op jit(solution)/shard_map/ppermute | solution.py:43
  101.6 8.1 %collective-permute-start.30 = (bf16[384,640]{1,0:T(8,128)(2,1)S(1)}, bf16[384,640]{1,0:T(8,128)(2,1)S(1)}, u32[]{:S(2)}, u32[]{:S(2)}) collective-permute-start(bf16[384,640]{1,0:T(8,128)(2,1)S(1)} %collective-permute-done.29.refs_2_), channel_id=1, source_target_pairs={{0,4},{1,5},{2,6},{3,7},{4,0},{5,1},{6,2},{7,3},{8,12},{9,13},{10,... | collective-permute-start | bytes 1474568 | tf_op jit(solution)/shard_map/ppermute | solution.py:43
  107.1 2.7 %collective-permute-start.28 = (bf16[384,640]{1,0:T(8,128)(2,1)S(1)}, bf16[384,640]{1,0:T(8,128)(2,1)S(1)}, u32[]{:S(2)}, u32[]{:S(2)}) collective-permute-start(bf16[384,640]{1,0:T(8,128)(2,1)S(1)} %collective-permute-done.27.refs_1_), channel_id=1, source_target_pairs={{0,4},{1,5},{2,6},{3,7},{4,0},{5,1},{6,2},{7,3},{8,12},{9,13},{10,... | collective-permute-start | bytes 1474568 | tf_op jit(solution)/shard_map/ppermute | solution.py:43

commit v10 on v9

--- a/solution.py
+++ b/solution.py
@@ -57,6 +57,13 @@
 
 def to_slab(array, step):
     return move(array, lambda zl, x, y, c, t: (zl, x, y, c, t ^ 1 if c == step else 3 - t))
+
+
+def to_slab_and_neighbour(array):
+    def target(zl, x, y, c, t):
+        return 1 - zl, x, y, c, t ^ 1 if c == 1 else 3 - t
+
+    return move(array, target)
 
 
 def to_z_neighbour(array):
@@ -303,8 +310,9 @@
 
     leaving = to_slab(factors(packed[:RING], packed[RING]).astype(half), 0)
     sums = factors(packed[RING + 1 : -1], packed[-1]) + wide(leaving)
-    sums = sums[0] + wide(to_slab(sums[1].astype(half), 1))
-    sums = sums + wide(to_z_neighbour(sums.astype(half)))
+    stays, leaves = sums[0].astype(half), sums[1].astype(half)
+    arrived = [to_slab_and_neighbour(leaves), to_slab(leaves, 1), to_z_neighbour(stays)]
+    sums = sums[0] + sum(wide(array) for array in arrived)
     members = over_square([sums.astype(half)] * RING, False)
 
     inverse = pl.pallas_call(

time: 114 us -> 112 us (0.982); the launches traced: 113 us -> 112 us
    ppermute x33 -> x34, waiting for transfers between devices: 30.6 us -> 29.6 us  [move(): return lax.ppermute(array, AXES, pairs)]
    ppermute x33 -> x34, starting transfers between devices: 63.8 us -> 64.6 us  [move(): return lax.ppermute(array, AXES, pairs)]
  transfers between devices with their start and end apart: 33 -> 34, of which waited for: 12 -> 13; matrix products, arithmetic and copies ran while one was open for 0% -> 0% of each run, Pallas kernels for 5% -> 6%
where the time goes in v10:
time: 112 us
  starting transfers between devices  64.6 us (58%)
  waiting for transfers between devices  29.6 us (26%)
  Pallas kernels  16.4 us (15%)
    ppermute x34, starting transfers between devices, move(): return lax.ppermute(array, AXES, pairs)  64.6 us
    ppermute x34, waiting for transfers between devices, move(): return lax.ppermute(array, AXES, pairs)  29.6 us
    pallas_call x2, Pallas kernels, apply(): pl.pallas_call(functools.partial(apply_kernel, side), out_shape=[shape(*d...  5.18 us
    pallas_call x1, Pallas kernels, local(): pl.pallas_call(functools.partial(newton_kernel, tokens_all), out_shape=sh...  4.7 us
    pallas_call x2, Pallas kernels, factors(): pl.pallas_call(gram_kernel, out_shape=[shape(2, CHUNK, BLOCK)] * RING, in...  3.59 us
    pallas_call x1, Pallas kernels, local(): pl.pallas_call(pack_kernel, out_shape=([shape(*part)] * RING + [shape(RIN...  2.97 us
  transfers between devices with their start and end apart: 34, of which 13 were waited for; matrix products, arithmetic and copies ran while one was open for 0% of the time, Pallas kernels for 6%

profile of v10, /device:TPU:1, one launch (start us, length us, event | category | flops | bytes accessed | tf_op | source)
XLA Modules:
  0.0 112.3 jit_solution(10373043991947300331)
XLA Ops:
  0.6 3.0 %pack.1 = (bf16[2,128,640]{2,1,0:T(8,128)(2,1)S(1)}, bf16[2,128,640]{2,1,0:T(8,128)(2,1)S(1)}, bf16[2,128,640]{2,1,0:T(8,128)(2,1)S(1)}, bf16[2,128,640]{2,1,0:T...) custom-call(s32[1]{0:T(128)} %bitcast.dev, ...), custom_call_target="tpu_custom_call" | custom-call | tf_op jit(solution)/shard_map/pack/pallas_call | solution.py:285
  3.6 3.3 %collective-permute-start.13 = (bf16[4,2,128,640]{3,2,1,0:T(8,128)(2,1)S(1)}, bf16[4,2,128,640]{3,2,1,0:T(8,128)(2,1)S(1)}, u32[]{:S(2)}, u32[]{:S(2)}) collective-permute-start(bf16[4,2,128,640]{3,2,1,0:T(8,128)(2,1)S(1)} %get-tuple-element.35), channel_id=1, source_target_pairs={{0,4},{1,5},{2,6},{3,7},{4,0},{5,1},{6,2},{7,3},{8,12},{9,13},{10,... | collective-permute-start | bytes 3932168 | tf_op jit(solution)/shard_map/ppermute | solution.py:43
  6.9 0.1 collective-permute-start.3
  7.0 3.2 %collective-permute-start = (bf16[2,128,640]{2,1,0:T(8,128)(2,1)S(1)}, bf16[2,128,640]{2,1,0:T(8,128)(2,1)S(1)}, u32[]{:S(2)}, u32[]{:S(2)}) collective-permute-start(bf16[2,128,640]{2,1,0:T(8,128)(2,1)S(1)} %get-tuple-element.22), channel_id=1, source_target_pairs={{0,40},{1,41},{2,42},{3,43},{4,124},{5,125},{6,126},{7,127},{8,32}... | collective-permute-start | bytes 983048 | tf_op jit(solution)/shard_map/ppermute | solution.py:43
  10.2 1.6 %collective-permute-start.10 = (bf16[2,128,640]{2,1,0:T(8,128)(2,1)S(1)}, bf16[2,128,640]{2,1,0:T(8,128)(2,1)S(1)}, u32[]{:S(2)}, u32[]{:S(2)}) collective-permute-start(bf16[2,128,640]{2,1,0:T(8,128)(2,1)S(1)} %get-tuple-element.31), channel_id=1, source_target_pairs={{0,40},{1,41},{2,42},{3,43},{4,124},{5,125},{6,126},{7,127},{8,32}... | collective-permute-start | bytes 983048 | tf_op jit(solution)/shard_map/ppermute | solution.py:43
  11.8 0.7 collective-permute-start.11
  12.6 0.0 collective-permute-done.13.refs_7_
  12.6 2.7 %collective-permute-start.12 = (bf16[2,128,640]{2,1,0:T(8,128)(2,1)S(1)}, bf16[2,128,640]{2,1,0:T(8,128)(2,1)S(1)}, u32[]{:S(2)}, u32[]{:S(2)}) collective-permute-start(bf16[2,128,640]{2,1,0:T(8,128)(2,1)S(1)} %get-tuple-element.33), channel_id=1, source_target_pairs={{0,8},{1,9},{2,10},{3,11},{4,28},{5,29},{6,30},{7,31},{8,0},{9,1},... | collective-permute-start | bytes 983048 | tf_op jit(solution)/shard_map/ppermute | solution.py:43
  15.3 0.1 slice_bitcast_fusion
  15.4 0.9 collective-permute-done.refs_0_
  16.3 1.0 collective-permute-start.16
  17.3 2.6 %collective-permute-done.10.refs_0_ = bf16[2,128,640]{2,1,0:T(8,128)(2,1)S(1)} collective-permute-done((bf16[2,128,640]{2,1,0:T(8,128)(2,1)S(1)}, bf16[2,128,640]{2,1,0:T(8,128)(2,1)S(1)}, u32[]{:S(2)}, u32[]{:S(2)}) %collective-permute-start.10) | collective-permute-done | bytes 327712 | tf_op jit(solution)/shard_map/ppermute | solution.py:43
  19.9 0.7 collective-permute-start.15
  20.6 2.6 %collective-permute-start.14 = (bf16[2,128,640]{2,1,0:T(8,128)(2,1)S(1)}, bf16[2,128,640]{2,1,0:T(8,128)(2,1)S(1)}, u32[]{:S(2)}, u32[]{:S(2)}) collective-permute-start(bf16[2,128,640]{2,1,0:T(8,128)(2,1)S(1)} %get-tuple-element.47), channel_id=1, source_target_pairs={{0,40},{1,41},{2,42},{3,43},{4,124},{5,125},{6,126},{7,127},{8,32}... | collective-permute-start | bytes 983048 | tf_op jit(solution)/shard_map/ppermute | solution.py:43
  23.3 0.1 slice_bitcast_fusion.3
  23.4 0.0 collective-permute-done.11.refs_1_
  23.4 2.6 %collective-permute-start.1 = (bf16[2,128,640]{2,1,0:T(8,128)(2,1)S(1)}, bf16[2,128,640]{2,1,0:T(8,128)(2,1)S(1)}, u32[]{:S(2)}, u32[]{:S(2)}) collective-permute-start(bf16[2,128,640]{2,1,0:T(8,128)(2,1)S(1)} %get-tuple-element.23), channel_id=1, source_target_pairs={{0,32},{1,33},{2,34},{3,35},{4,100},{5,101},{6,102},{7,103},{8,40}... | collective-permute-start | bytes 983048 | tf_op jit(solution)/shard_map/ppermute | solution.py:43
  26.0 0.0 collective-permute-done.12.refs_2_
  26.0 0.0 collective-permute-start.2
  26.0 1.0 collective-permute-done.16.refs_6_
  27.0 1.7 %collective-permute-start.6 = (bf16[2,128,640]{2,1,0:T(8,128)(2,1)S(1)}, bf16[2,128,640]{2,1,0:T(8,128)(2,1)S(1)}, u32[]{:S(2)}, u32[]{:S(2)}) collective-permute-start(bf16[2,128,640]{2,1,0:T(8,128)(2,1)S(1)} %get-tuple-element.42), channel_id=1, source_target_pairs={{0,8},{1,9},{2,10},{3,11},{4,28},{5,29},{6,30},{7,31},{8,0},{9,1},... | collective-permute-start | bytes 983048 | tf_op jit(solution)/shard_map/ppermute | solution.py:43
  28.7 0.0 collective-permute-done.15.refs_5_
  28.7 1.8 %collective-permute-start.5 = (bf16[2,128,640]{2,1,0:T(8,128)(2,1)S(1)}, bf16[2,128,640]{2,1,0:T(8,128)(2,1)S(1)}, u32[]{:S(2)}, u32[]{:S(2)}) collective-permute-start(bf16[2,128,640]{2,1,0:T(8,128)(2,1)S(1)} %get-tuple-element.43), channel_id=1, source_target_pairs={{0,32},{1,33},{2,34},{3,35},{4,100},{5,101},{6,102},{7,103},{8,40}... | collective-permute-start | bytes 983048 | tf_op jit(solution)/shard_map/ppermute | solution.py:43
  30.4 0.9 collective-permute-done.14.refs_4_
  31.4 2.3 %collective-permute-start.4 = (bf16[2,128,640]{2,1,0:T(8,128)(2,1)S(1)}, bf16[2,128,640]{2,1,0:T(8,128)(2,1)S(1)}, u32[]{:S(2)}, u32[]{:S(2)}) collective-permute-start(bf16[2,128,640]{2,1,0:T(8,128)(2,1)S(1)} %get-tuple-element.44), channel_id=1, source_target_pairs={{0,40},{1,41},{2,42},{3,43},{4,124},{5,125},{6,126},{7,127},{8,32}... | collective-permute-start | bytes 983048 | tf_op jit(solution)/shard_map/ppermute | solution.py:43
  33.7 1.8 %gram.3 = (bf16[2,96,640]{2,1,0:T(8,128)(2,1)S(1)}, bf16[2,96,640]{2,1,0:T(8,128)(2,1)S(1)}, bf16[2,96,640]{2,1,0:T(8,128)(2,1)S(1)}, bf16[2,96,640]{2,1,0:T(8,128)(2,1)S(1)}) custom-call(s32[1]{0:T(128)} %bitcast.dev, bf16[2,128,640]{2,1,0:T(8,128)(2,1)S(1)} %collective-permute-done.10.refs_0_, bf16[2,128,640]{2,1,0:T(8,128)(2,1)S(1)} %collective-permute-done.11.refs_1_, ...), custom_call_target="tpu_custom_call" | custom-call | tf_op jit(solution)/shard_map/gram/pallas_call | solution.py:299
  35.5 0.0 collective-permute-done.1.refs_1_
  35.5 0.1 collective-permute-start.17
  35.6 0.1 collective-permute-start.18
  35.7 2.7 %collective-permute-done.6.refs_6_ = bf16[2,128,640]{2,1,0:T(8,128)(2,1)S(1)} collective-permute-done((bf16[2,128,640]{2,1,0:T(8,128)(2,1)S(1)}, bf16[2,128,640]{2,1,0:T(8,128)(2,1)S(1)}, u32[]{:S(2)}, u32[]{:S(2)}) %collective-permute-start.6) | collective-permute-done | bytes 327712 | tf_op jit(solution)/shard_map/ppermute | solution.py:43
  38.4 0.0 collective-permute-start.19
  38.4 6.0 %collective-permute-done.4.refs_4_ = bf16[2,128,640]{2,1,0:T(8,128)(2,1)S(1)} collective-permute-done((bf16[2,128,640]{2,1,0:T(8,128)(2,1)S(1)}, bf16[2,128,640]{2,1,0:T(8,128)(2,1)S(1)}, u32[]{:S(2)}, u32[]{:S(2)}) %collective-permute-start.4) | collective-permute-done | bytes 327712 | tf_op jit(solution)/shard_map/ppermute | solution.py:43
  44.4 1.8 %gram.2 = (bf16[2,96,640]{2,1,0:T(8,128)(2,1)S(1)}, bf16[2,96,640]{2,1,0:T(8,128)(2,1)S(1)}, bf16[2,96,640]{2,1,0:T(8,128)(2,1)S(1)}, bf16[2,96,640]{2,1,0:T(8,128)(2,1)S(1)}) custom-call(s32[1]{0:T(128)} %bitcast.dev, bf16[2,128,640]{2,1,0:T(8,128)(2,1)S(1)} %collective-permute-done.refs_0_, bf16[2,128,640]{2,1,0:T(8,128)(2,1)S(1)} %collective-permute-done.1.refs_1_, ...), custom_call_target="tpu_custom_call" | custom-call | tf_op jit(solution)/shard_map/gram/pallas_call | solution.py:299
  46.2 0.1 collective-permute-start.7
  46.3 0.1 collective-permute-start.8
  46.5 2.5 %collective-permute-start.9 = (bf16[2,96,640]{2,1,0:T(8,128)(2,1)S(1)}, bf16[2,96,640]{2,1,0:T(8,128)(2,1)S(1)}, u32[]{:S(2)}, u32[]{:S(2)}) collective-permute-start(bf16[2,96,640]{2,1,0:T(8,128)(2,1)S(1)} %get-tuple-element.29), channel_id=1, source_target_pairs={{0,24},{1,25},{2,26},{3,27},{4,12},{5,13},{6,14},{7,15},{8,16},{9,... | collective-permute-start | bytes 737288 | tf_op jit(solution)/shard_map/ppermute | solution.py:43
  49.0 0.1 add_convert_fusion
  49.1 6.7 %collective-permute-start.20 = (bf16[2,96,640]{2,1,0:T(8,128)(2,1)S(1)}, bf16[2,96,640]{2,1,0:T(8,128)(2,1)S(1)}, u32[]{:S(2)}, u32[]{:S(2)}) collective-permute-start(bf16[2,96,640]{2,1,0:T(8,128)(2,1)S(1)} %add_convert_fusion), channel_id=1, source_target_pairs={{0,1},{1,0},{2,3},{3,2},{4,7},{5,6},{6,5},{7,4},{8,9},{9,8},{10,11... | collective-permute-start | bytes 737288 | tf_op jit(solution)/shard_map/ppermute | solution.py:43
  55.9 5.8 %collective-permute-done.20 = bf16[2,96,640]{2,1,0:T(8,128)(2,1)S(1)} collective-permute-done((bf16[2,96,640]{2,1,0:T(8,128)(2,1)S(1)}, bf16[2,96,640]{2,1,0:T(8,128)(2,1)S(1)}, u32[]{:S(2)}, u32[]{:S(2)}) %collective-permute-start.20) | collective-permute-done | bytes 245792 | tf_op jit(solution)/shard_map/ppermute | solution.py:43
  61.6 0.1 convert_add_fusion
  61.8 0.0 copy-start
  61.8 1.3 %collective-permute-start.23 = (bf16[96,640]{1,0:T(8,128)(2,1)S(1)}, bf16[96,640]{1,0:T(8,128)(2,1)S(1)}, u32[]{:S(2)}, u32[]{:S(2)}) collective-permute-start(bf16[96,640]{1,0:T(8,128)(2,1)S(1)} %get-tuple-element.49), channel_id=1, source_target_pairs={{0,128},{1,129},{2,130},{3,131},{4,132},{5,133},{6,134},{7,135},{8... | collective-permute-start | bytes 368648 | tf_op jit(solution)/shard_map/ppermute | solution.py:43
  63.1 0.5 collective-permute-start.22
  63.6 1.8 %collective-permute-start.21 = (bf16[96,640]{1,0:T(8,128)(2,1)S(1)}, bf16[96,640]{1,0:T(8,128)(2,1)S(1)}, u32[]{:S(2)}, u32[]{:S(2)}) collective-permute-start(bf16[96,640]{1,0:T(8,128)(2,1)S(1)} %get-tuple-element.48), channel_id=1, source_target_pairs={{0,131},{1,130},{2,129},{3,128},{4,133},{5,132},{6,135},{7,134},{8... | collective-permute-start | bytes 368648 | tf_op jit(solution)/shard_map/ppermute | solution.py:43
  65.5 0.8 collective-permute-done.23
  66.3 2.2 %collective-permute-done.22 = bf16[96,640]{1,0:T(8,128)(2,1)S(1)} collective-permute-done((bf16[96,640]{1,0:T(8,128)(2,1)S(1)}, bf16[96,640]{1,0:T(8,128)(2,1)S(1)}, u32[]{:S(2)}, u32[]{:S(2)}) %collective-permute-start.22) | collective-permute-done | bytes 122912 | tf_op jit(solution)/shard_map/ppermute | solution.py:43
  68.5 2.8 %collective-permute-done.21 = bf16[96,640]{1,0:T(8,128)(2,1)S(1)} collective-permute-done((bf16[96,640]{1,0:T(8,128)(2,1)S(1)}, bf16[96,640]{1,0:T(8,128)(2,1)S(1)}, u32[]{:S(2)}, u32[]{:S(2)}) %collective-permute-start.21) | collective-permute-done | bytes 122912 | tf_op jit(solution)/shard_map/ppermute | solution.py:43
  71.3 0.1 add_convert_fusion.1.refs_3_
  71.3 1.4 %collective-permute-start.26 = (bf16[96,640]{1,0:T(8,128)(2,1)S(1)}, bf16[96,640]{1,0:T(8,128)(2,1)S(1)}, u32[]{:S(2)}, u32[]{:S(2)}) collective-permute-start(bf16[96,640]{1,0:T(8,128)(2,1)S(1)} %add_convert_fusion.1.refs_3_), channel_id=1, source_target_pairs={{0,24},{1,25},{2,26},{3,27},{4,12},{5,13},{6,14},{7,15},{8,16},{9,... | collective-permute-start | bytes 368648 | tf_op jit(solution)/shard_map/ppermute | solution.py:43
  72.7 0.0 collective-permute-start.25
  72.8 1.3 %collective-permute-start.24 = (bf16[96,640]{1,0:T(8,128)(2,1)S(1)}, bf16[96,640]{1,0:T(8,128)(2,1)S(1)}, u32[]{:S(2)}, u32[]{:S(2)}) collective-permute-start(bf16[96,640]{1,0:T(8,128)(2,1)S(1)} %add_convert_fusion.1.refs_3_), channel_id=1, source_target_pairs={{0,120},{1,121},{2,122},{3,123},{4,44},{5,45},{6,46},{7,47},{8,112... | collective-permute-start | bytes 368648 | tf_op jit(solution)/shard_map/ppermute | solution.py:43
  74.1 1.1 collective-permute-done.26.refs_2_
  75.1 1.3 %collective-permute-done.25.refs_1_ = bf16[96,640]{1,0:T(8,128)(2,1)S(1)} collective-permute-done((bf16[96,640]{1,0:T(8,128)(2,1)S(1)}, bf16[96,640]{1,0:T(8,128)(2,1)S(1)}, u32[]{:S(2)}, u32[]{:S(2)}) %collective-permute-start.25) | collective-permute-done | bytes 122912 | tf_op jit(solution)/shard_map/ppermute | solution.py:43
  76.5 1.5 %collective-permute-done.24.refs_0_ = bf16[96,640]{1,0:T(8,128)(2,1)S(1)} collective-permute-done((bf16[96,640]{1,0:T(8,128)(2,1)S(1)}, bf16[96,640]{1,0:T(8,128)(2,1)S(1)}, u32[]{:S(2)}, u32[]{:S(2)}) %collective-permute-start.24) | collective-permute-done | bytes 122912 | tf_op jit(solution)/shard_map/ppermute | solution.py:43
  77.9 4.7 %newton.1.refs_0_ = bf16[384,640]{1,0:T(8,128)(2,1)S(1)} custom-call(s32[1]{0:T(128)} %bitcast.dev, s32[2,2,8]{2,1,0:T(2,128)S(1)} %copy-done.2, bf16[96,640]{1,0:T(8,128)(2,1)S(1)} %collective-permute-done.24.refs_0_, bf16[96,640]{1,0:T(8,128)(2,1)S(1)} %collective-permute-done.25.refs_1_, bf16[96,640]{1,0:T(8,128)(2,1)S(1)} %collective-permute-done.26.refs_2_, ...), custom_call_target="tpu_custom_call" | custom-call | tf_op jit(solution)/shard_map/newton/pallas_call | solution.py:318
  82.6 0.2 collective-permute-start.32
  82.8 3.3 %collective-permute-start.30 = (bf16[384,640]{1,0:T(8,128)(2,1)S(1)}, bf16[384,640]{1,0:T(8,128)(2,1)S(1)}, u32[]{:S(2)}, u32[]{:S(2)}) collective-permute-start(bf16[384,640]{1,0:T(8,128)(2,1)S(1)} %newton.1.refs_0_), channel_id=1, source_target_pairs={{0,32},{1,33},{2,34},{3,35},{4,100},{5,101},{6,102},{7,103},{8,40}... | collective-permute-start | bytes 1474568 | tf_op jit(solution)/shard_map/ppermute | solution.py:43
  86.2 2.1 %collective-permute-start.28 = (bf16[384,640]{1,0:T(8,128)(2,1)S(1)}, bf16[384,640]{1,0:T(8,128)(2,1)S(1)}, u32[]{:S(2)}, u32[]{:S(2)}) collective-permute-start(bf16[384,640]{1,0:T(8,128)(2,1)S(1)} %newton.1.refs_0_), channel_id=1, source_target_pairs={{0,8},{1,9},{2,10},{3,11},{4,28},{5,29},{6,30},{7,31},{8,0},{9,1},... | collective-permute-start | bytes 1474568 | tf_op jit(solution)/shard_map/ppermute | solution.py:43
  88.2 7.1 %collective-permute-start.27 = (bf16[384,640]{1,0:T(8,128)(2,1)S(1)}, bf16[384,640]{1,0:T(8,128)(2,1)S(1)}, u32[]{:S(2)}, u32[]{:S(2)}) collective-permute-start(bf16[384,640]{1,0:T(8,128)(2,1)S(1)} %newton.1.refs_0_), channel_id=1, source_target_pairs={{0,4},{1,5},{2,6},{3,7},{4,0},{5,1},{6,2},{7,3},{8,12},{9,13},{10,... | collective-permute-start | bytes 1474568 | tf_op jit(solution)/shard_map/ppermute | solution.py:43
  95.4 6.3 %collective-permute-start.33 = (bf16[384,640]{1,0:T(8,128)(2,1)S(1)}, bf16[384,640]{1,0:T(8,128)(2,1)S(1)}, u32[]{:S(2)}, u32[]{:S(2)}) collective-permute-start(bf16[384,640]{1,0:T(8,128)(2,1)S(1)} %collective-permute-done.32.refs_3_), channel_id=1, source_target_pairs={{0,4},{1,5},{2,6},{3,7},{4,0},{5,1},{6,2},{7,3},{8,12},{9,13},{10,... | collective-permute-start | bytes 1474568 | tf_op jit(solution)/shard_map/ppermute | solution.py:43
  101.7 4.6 %collective-permute-start.31 = (bf16[384,640]{1,0:T(8,128)(2,1)S(1)}, bf16[384,640]{1,0:T(8,128)(2,1)S(1)}, u32[]{:S(2)}, u32[]{:S(2)}) collective-permute-start(bf16[384,640]{1,0:T(8,128)(2,1)S(1)} %collective-permute-done.30.refs_2_), channel_id=1, source_target_pairs={{0,4},{1,5},{2,6},{3,7},{4,0},{5,1},{6,2},{7,3},{8,12},{9,13},{10,... | collective-permute-start | bytes 1474568 | tf_op jit(solution)/shard_map/ppermute | solution.py:43
  106.3 0.6 collective-permute-start.29
  106.9 2.6 %apply.2 = (bf16[2,240,1280]{2,1,0:T(8,128)(2,1)}, bf16[2,320,1280]{2,1,0:T(8,128)(2,1)}) custom-call(s32[1]{0:T(128)} %bitcast.dev, bf16[384,640]{1,0:T(8,128)(2,1)S(1)} %newton.1.refs_0_, bf16[384,640]{1,0:T(8,128)(2,1)S(1)} %collective-permute-done.28.refs_1_, bf16[384,640]{1,0:T(8,128)(2,1)S(1)} %collective-permute-done.30.refs_2_, ...), custom_call_target="tpu_custom_call" | custom-call | tf_op jit(solution)/shard_map/apply/pallas_call | solution.py:339
  109.5 2.6 %apply.3 = (bf16[2,240,1280]{2,1,0:T(8,128)(2,1)}, bf16[2,320,1280]{2,1,0:T(8,128)(2,1)}) custom-call(s32[1]{0:T(128)} %bitcast.dev, bf16[384,640]{1,0:T(8,128)(2,1)S(1)} %collective-permute-done.27.refs_0_, bf16[384,640]{1,0:T(8,128)(2,1)S(1)} %collective-permute-done.29.refs_1_, ...), custom_call_target="tpu_custom_call", output_to_operand_aliasing={{0}: (7, {}), {1}: (8, {})} | custom-call | tf_op jit(solution)/shard_map/apply/pallas_call | solution.py:339
  (22 shorter events, 0.1 us)
Async XLA Ops:
  3.6 9.0 %collective-permute-start.13 = (bf16[4,2,128,640]{3,2,1,0:T(8,128)(2,1)S(1)}, bf16[4,2,128,640]{3,2,1,0:T(8,128)(2,1)S(1)}, u32[]{:S(2)}, u32[]{:S(2)}) collective-permute-start(bf16[4,2,128,640]{3,2,1,0:T(8,128)(2,1)S(1)} %get-tuple-element.35), channel_id=1, source_target_pairs={{0,4},{1,5},{2,6},{3,7},{4,0},{5,1},{6,2},{7,3},{8,12},{9,13},{10,... | collective-permute-start | bytes 3932168 | tf_op jit(solution)/shard_map/ppermute | solution.py:43
  6.9 13.7 %collective-permute-start.3 = (bf16[4,2,128,640]{3,2,1,0:T(8,128)(2,1)S(1)}, bf16[4,2,128,640]{3,2,1,0:T(8,128)(2,1)S(1)}, u32[]{:S(2)}, u32[]{:S(2)}) collective-permute-start(bf16[4,2,128,640]{3,2,1,0:T(8,128)(2,1)S(1)} %get-tuple-element.26), channel_id=1, source_target_pairs={{0,4},{1,5},{2,6},{3,7},{4,0},{5,1},{6,2},{7,3},{8,12},{9,13},{10,... | collective-permute-start | bytes 3932168 | tf_op jit(solution)/shard_map/ppermute | solution.py:43
  7.0 9.2 %collective-permute-start = (bf16[2,128,640]{2,1,0:T(8,128)(2,1)S(1)}, bf16[2,128,640]{2,1,0:T(8,128)(2,1)S(1)}, u32[]{:S(2)}, u32[]{:S(2)}) collective-permute-start(bf16[2,128,640]{2,1,0:T(8,128)(2,1)S(1)} %get-tuple-element.22), channel_id=1, source_target_pairs={{0,40},{1,41},{2,42},{3,43},{4,124},{5,125},{6,126},{7,127},{8,32}... | collective-permute-start | bytes 983048 | tf_op jit(solution)/shard_map/ppermute | solution.py:43
  10.2 9.7 %collective-permute-start.10 = (bf16[2,128,640]{2,1,0:T(8,128)(2,1)S(1)}, bf16[2,128,640]{2,1,0:T(8,128)(2,1)S(1)}, u32[]{:S(2)}, u32[]{:S(2)}) collective-permute-start(bf16[2,128,640]{2,1,0:T(8,128)(2,1)S(1)} %get-tuple-element.31), channel_id=1, source_target_pairs={{0,40},{1,41},{2,42},{3,43},{4,124},{5,125},{6,126},{7,127},{8,32}... | collective-permute-start | bytes 983048 | tf_op jit(solution)/shard_map/ppermute | solution.py:43
  11.8 11.6 %collective-permute-start.11 = (bf16[2,128,640]{2,1,0:T(8,128)(2,1)S(1)}, bf16[2,128,640]{2,1,0:T(8,128)(2,1)S(1)}, u32[]{:S(2)}, u32[]{:S(2)}) collective-permute-start(bf16[2,128,640]{2,1,0:T(8,128)(2,1)S(1)} %get-tuple-element.32), channel_id=1, source_target_pairs={{0,32},{1,33},{2,34},{3,35},{4,100},{5,101},{6,102},{7,103},{8,40}... | collective-permute-start | bytes 983048 | tf_op jit(solution)/shard_map/ppermute | solution.py:43
  12.6 13.4 %collective-permute-start.12 = (bf16[2,128,640]{2,1,0:T(8,128)(2,1)S(1)}, bf16[2,128,640]{2,1,0:T(8,128)(2,1)S(1)}, u32[]{:S(2)}, u32[]{:S(2)}) collective-permute-start(bf16[2,128,640]{2,1,0:T(8,128)(2,1)S(1)} %get-tuple-element.33), channel_id=1, source_target_pairs={{0,8},{1,9},{2,10},{3,11},{4,28},{5,29},{6,30},{7,31},{8,0},{9,1},... | collective-permute-start | bytes 983048 | tf_op jit(solution)/shard_map/ppermute | solution.py:43
  16.3 10.7 %collective-permute-start.16 = (bf16[2,128,640]{2,1,0:T(8,128)(2,1)S(1)}, bf16[2,128,640]{2,1,0:T(8,128)(2,1)S(1)}, u32[]{:S(2)}, u32[]{:S(2)}) collective-permute-start(bf16[2,128,640]{2,1,0:T(8,128)(2,1)S(1)} %get-tuple-element.45), channel_id=1, source_target_pairs={{0,8},{1,9},{2,10},{3,11},{4,28},{5,29},{6,30},{7,31},{8,0},{9,1},... | collective-permute-start | bytes 983048 | tf_op jit(solution)/shard_map/ppermute | solution.py:43
  19.9 8.8 %collective-permute-start.15 = (bf16[2,128,640]{2,1,0:T(8,128)(2,1)S(1)}, bf16[2,128,640]{2,1,0:T(8,128)(2,1)S(1)}, u32[]{:S(2)}, u32[]{:S(2)}) collective-permute-start(bf16[2,128,640]{2,1,0:T(8,128)(2,1)S(1)} %get-tuple-element.46), channel_id=1, source_target_pairs={{0,32},{1,33},{2,34},{3,35},{4,100},{5,101},{6,102},{7,103},{8,40}... | collective-permute-start | bytes 983048 | tf_op jit(solution)/shard_map/ppermute | solution.py:43
  20.6 10.7 %collective-permute-start.14 = (bf16[2,128,640]{2,1,0:T(8,128)(2,1)S(1)}, bf16[2,128,640]{2,1,0:T(8,128)(2,1)S(1)}, u32[]{:S(2)}, u32[]{:S(2)}) collective-permute-start(bf16[2,128,640]{2,1,0:T(8,128)(2,1)S(1)} %get-tuple-element.47), channel_id=1, source_target_pairs={{0,40},{1,41},{2,42},{3,43},{4,124},{5,125},{6,126},{7,127},{8,32}... | collective-permute-start | bytes 983048 | tf_op jit(solution)/shard_map/ppermute | solution.py:43
  23.4 12.1 %collective-permute-start.1 = (bf16[2,128,640]{2,1,0:T(8,128)(2,1)S(1)}, bf16[2,128,640]{2,1,0:T(8,128)(2,1)S(1)}, u32[]{:S(2)}, u32[]{:S(2)}) collective-permute-start(bf16[2,128,640]{2,1,0:T(8,128)(2,1)S(1)} %get-tuple-element.23), channel_id=1, source_target_pairs={{0,32},{1,33},{2,34},{3,35},{4,100},{5,101},{6,102},{7,103},{8,40}... | collective-permute-start | bytes 983048 | tf_op jit(solution)/shard_map/ppermute | solution.py:43
  26.0 9.6 %collective-permute-start.2 = (bf16[2,128,640]{2,1,0:T(8,128)(2,1)S(1)}, bf16[2,128,640]{2,1,0:T(8,128)(2,1)S(1)}, u32[]{:S(2)}, u32[]{:S(2)}) collective-permute-start(bf16[2,128,640]{2,1,0:T(8,128)(2,1)S(1)} %get-tuple-element.24), channel_id=1, source_target_pairs={{0,8},{1,9},{2,10},{3,11},{4,28},{5,29},{6,30},{7,31},{8,0},{9,1},... | collective-permute-start | bytes 983048 | tf_op jit(solution)/shard_map/ppermute | solution.py:43
  27.0 11.5 %collective-permute-start.6 = (bf16[2,128,640]{2,1,0:T(8,128)(2,1)S(1)}, bf16[2,128,640]{2,1,0:T(8,128)(2,1)S(1)}, u32[]{:S(2)}, u32[]{:S(2)}) collective-permute-start(bf16[2,128,640]{2,1,0:T(8,128)(2,1)S(1)} %get-tuple-element.42), channel_id=1, source_target_pairs={{0,8},{1,9},{2,10},{3,11},{4,28},{5,29},{6,30},{7,31},{8,0},{9,1},... | collective-permute-start | bytes 983048 | tf_op jit(solution)/shard_map/ppermute | solution.py:43
  28.7 9.8 %collective-permute-start.5 = (bf16[2,128,640]{2,1,0:T(8,128)(2,1)S(1)}, bf16[2,128,640]{2,1,0:T(8,128)(2,1)S(1)}, u32[]{:S(2)}, u32[]{:S(2)}) collective-permute-start(bf16[2,128,640]{2,1,0:T(8,128)(2,1)S(1)} %get-tuple-element.43), channel_id=1, source_target_pairs={{0,32},{1,33},{2,34},{3,35},{4,100},{5,101},{6,102},{7,103},{8,40}... | collective-permute-start | bytes 983048 | tf_op jit(solution)/shard_map/ppermute | solution.py:43
  31.4 13.1 %collective-permute-start.4 = (bf16[2,128,640]{2,1,0:T(8,128)(2,1)S(1)}, bf16[2,128,640]{2,1,0:T(8,128)(2,1)S(1)}, u32[]{:S(2)}, u32[]{:S(2)}) collective-permute-start(bf16[2,128,640]{2,1,0:T(8,128)(2,1)S(1)} %get-tuple-element.44), channel_id=1, source_target_pairs={{0,40},{1,41},{2,42},{3,43},{4,124},{5,125},{6,126},{7,127},{8,32}... | collective-permute-start | bytes 983048 | tf_op jit(solution)/shard_map/ppermute | solution.py:43
  35.5 11.0 %collective-permute-start.17 = (bf16[2,96,640]{2,1,0:T(8,128)(2,1)S(1)}, bf16[2,96,640]{2,1,0:T(8,128)(2,1)S(1)}, u32[]{:S(2)}, u32[]{:S(2)}) collective-permute-start(bf16[2,96,640]{2,1,0:T(8,128)(2,1)S(1)} %get-tuple-element.36), channel_id=1, source_target_pairs={{0,120},{1,121},{2,122},{3,123},{4,44},{5,45},{6,46},{7,47},{8,112... | collective-permute-start | bytes 737288 | tf_op jit(solution)/shard_map/ppermute | solution.py:43
  35.6 13.4 %collective-permute-start.18 = (bf16[2,96,640]{2,1,0:T(8,128)(2,1)S(1)}, bf16[2,96,640]{2,1,0:T(8,128)(2,1)S(1)}, u32[]{:S(2)}, u32[]{:S(2)}) collective-permute-start(bf16[2,96,640]{2,1,0:T(8,128)(2,1)S(1)} %get-tuple-element.37), channel_id=1, source_target_pairs={{0,96},{1,97},{2,98},{3,99},{4,36},{5,37},{6,38},{7,39},{8,104},{9... | collective-permute-start | bytes 737288 | tf_op jit(solution)/shard_map/ppermute | solution.py:43
  38.4 10.6 %collective-permute-start.19 = (bf16[2,96,640]{2,1,0:T(8,128)(2,1)S(1)}, bf16[2,96,640]{2,1,0:T(8,128)(2,1)S(1)}, u32[]{:S(2)}, u32[]{:S(2)}) collective-permute-start(bf16[2,96,640]{2,1,0:T(8,128)(2,1)S(1)} %get-tuple-element.38), channel_id=1, source_target_pairs={{0,24},{1,25},{2,26},{3,27},{4,12},{5,13},{6,14},{7,15},{8,16},{9,... | collective-permute-start | bytes 737288 | tf_op jit(solution)/shard_map/ppermute | solution.py:43
  46.2 9.6 %collective-permute-start.7 = (bf16[2,96,640]{2,1,0:T(8,128)(2,1)S(1)}, bf16[2,96,640]{2,1,0:T(8,128)(2,1)S(1)}, u32[]{:S(2)}, u32[]{:S(2)}) collective-permute-start(bf16[2,96,640]{2,1,0:T(8,128)(2,1)S(1)} %get-tuple-element.27), channel_id=1, source_target_pairs={{0,120},{1,121},{2,122},{3,123},{4,44},{5,45},{6,46},{7,47},{8,112... | collective-permute-start | bytes 737288 | tf_op jit(solution)/shard_map/ppermute | solution.py:43
  46.3 9.5 %collective-permute-start.8 = (bf16[2,96,640]{2,1,0:T(8,128)(2,1)S(1)}, bf16[2,96,640]{2,1,0:T(8,128)(2,1)S(1)}, u32[]{:S(2)}, u32[]{:S(2)}) collective-permute-start(bf16[2,96,640]{2,1,0:T(8,128)(2,1)S(1)} %get-tuple-element.28), channel_id=1, source_target_pairs={{0,96},{1,97},{2,98},{3,99},{4,36},{5,37},{6,38},{7,39},{8,104},{9... | collective-permute-start | bytes 737288 | tf_op jit(solution)/shard_map/ppermute | solution.py:43
  46.5 9.4 %collective-permute-start.9 = (bf16[2,96,640]{2,1,0:T(8,128)(2,1)S(1)}, bf16[2,96,640]{2,1,0:T(8,128)(2,1)S(1)}, u32[]{:S(2)}, u32[]{:S(2)}) collective-permute-start(bf16[2,96,640]{2,1,0:T(8,128)(2,1)S(1)} %get-tuple-element.29), channel_id=1, source_target_pairs={{0,24},{1,25},{2,26},{3,27},{4,12},{5,13},{6,14},{7,15},{8,16},{9,... | collective-permute-start | bytes 737288 | tf_op jit(solution)/shard_map/ppermute | solution.py:43
  49.1 12.5 %collective-permute-start.20 = (bf16[2,96,640]{2,1,0:T(8,128)(2,1)S(1)}, bf16[2,96,640]{2,1,0:T(8,128)(2,1)S(1)}, u32[]{:S(2)}, u32[]{:S(2)}) collective-permute-start(bf16[2,96,640]{2,1,0:T(8,128)(2,1)S(1)} %add_convert_fusion), channel_id=1, source_target_pairs={{0,1},{1,0},{2,3},{3,2},{4,7},{5,6},{6,5},{7,4},{8,9},{9,8},{10,11... | collective-permute-start | bytes 737288 | tf_op jit(solution)/shard_map/ppermute | solution.py:43
  61.6 16.3 %copy-start.2 = (s32[2,2,8]{2,1,0:T(2,128)S(1)}, s32[2,2,8]{2,1,0:T(2,128)}, u32[]{:S(2)}) copy-start(s32[2,2,8]{2,1,0:T(2,128)} %newton_steps.1) | copy-start | bytes 388
  61.6 45.2 %copy-start.1 = (bf16[2,240,1280]{2,1,0:T(8,128)(2,1)S(1)}, bf16[2,240,1280]{2,1,0:T(8,128)(2,1)}, u32[]{:S(2)}) copy-start(bf16[2,240,1280]{2,1,0:T(8,128)(2,1)} %refs_4_.3) | copy-start | bytes 3686404
  61.8 45.1 %copy-start = (bf16[2,320,1280]{2,1,0:T(8,128)(2,1)S(1)}, bf16[2,320,1280]{2,1,0:T(8,128)(2,1)}, u32[]{:S(2)}) copy-start(bf16[2,320,1280]{2,1,0:T(8,128)(2,1)} %refs_5_.3) | copy-start | bytes 4915204
  61.8 4.5 %collective-permute-start.23 = (bf16[96,640]{1,0:T(8,128)(2,1)S(1)}, bf16[96,640]{1,0:T(8,128)(2,1)S(1)}, u32[]{:S(2)}, u32[]{:S(2)}) collective-permute-start(bf16[96,640]{1,0:T(8,128)(2,1)S(1)} %get-tuple-element.49), channel_id=1, source_target_pairs={{0,128},{1,129},{2,130},{3,131},{4,132},{5,133},{6,134},{7,135},{8... | collective-permute-start | bytes 368648 | tf_op jit(solution)/shard_map/ppermute | solution.py:43
  63.1 5.3 %collective-permute-start.22 = (bf16[96,640]{1,0:T(8,128)(2,1)S(1)}, bf16[96,640]{1,0:T(8,128)(2,1)S(1)}, u32[]{:S(2)}, u32[]{:S(2)}) collective-permute-start(bf16[96,640]{1,0:T(8,128)(2,1)S(1)} %get-tuple-element.48), channel_id=1, source_target_pairs={{0,3},{1,2},{2,1},{3,0},{4,5},{5,4},{6,7},{7,6},{8,11},{9,10},{10,... | collective-permute-start | bytes 368648 | tf_op jit(solution)/shard_map/ppermute | solution.py:43
  63.6 7.6 %collective-permute-start.21 = (bf16[96,640]{1,0:T(8,128)(2,1)S(1)}, bf16[96,640]{1,0:T(8,128)(2,1)S(1)}, u32[]{:S(2)}, u32[]{:S(2)}) collective-permute-start(bf16[96,640]{1,0:T(8,128)(2,1)S(1)} %get-tuple-element.48), channel_id=1, source_target_pairs={{0,131},{1,130},{2,129},{3,128},{4,133},{5,132},{6,135},{7,134},{8... | collective-permute-start | bytes 368648 | tf_op jit(solution)/shard_map/ppermute | solution.py:43
  71.3 3.8 %collective-permute-start.26 = (bf16[96,640]{1,0:T(8,128)(2,1)S(1)}, bf16[96,640]{1,0:T(8,128)(2,1)S(1)}, u32[]{:S(2)}, u32[]{:S(2)}) collective-permute-start(bf16[96,640]{1,0:T(8,128)(2,1)S(1)} %add_convert_fusion.1.refs_3_), channel_id=1, source_target_pairs={{0,24},{1,25},{2,26},{3,27},{4,12},{5,13},{6,14},{7,15},{8,16},{9,... | collective-permute-start | bytes 368648 | tf_op jit(solution)/shard_map/ppermute | solution.py:43
  72.7 3.7 %collective-permute-start.25 = (bf16[96,640]{1,0:T(8,128)(2,1)S(1)}, bf16[96,640]{1,0:T(8,128)(2,1)S(1)}, u32[]{:S(2)}, u32[]{:S(2)}) collective-permute-start(bf16[96,640]{1,0:T(8,128)(2,1)S(1)} %add_convert_fusion.1.refs_3_), channel_id=1, source_target_pairs={{0,96},{1,97},{2,98},{3,99},{4,36},{5,37},{6,38},{7,39},{8,104},{9... | collective-permute-start | bytes 368648 | tf_op jit(solution)/shard_map/ppermute | solution.py:43
  72.8 5.2 %collective-permute-start.24 = (bf16[96,640]{1,0:T(8,128)(2,1)S(1)}, bf16[96,640]{1,0:T(8,128)(2,1)S(1)}, u32[]{:S(2)}, u32[]{:S(2)}) collective-permute-start(bf16[96,640]{1,0:T(8,128)(2,1)S(1)} %add_convert_fusion.1.refs_3_), channel_id=1, source_target_pairs={{0,120},{1,121},{2,122},{3,123},{4,44},{5,45},{6,46},{7,47},{8,112... | collective-permute-start | bytes 368648 | tf_op jit(solution)/shard_map/ppermute | solution.py:43
  82.6 12.7 %collective-permute-start.32 = (bf16[384,640]{1,0:T(8,128)(2,1)S(1)}, bf16[384,640]{1,0:T(8,128)(2,1)S(1)}, u32[]{:S(2)}, u32[]{:S(2)}) collective-permute-start(bf16[384,640]{1,0:T(8,128)(2,1)S(1)} %newton.1.refs_0_), channel_id=1, source_target_pairs={{0,40},{1,41},{2,42},{3,43},{4,124},{5,125},{6,126},{7,127},{8,32}... | collective-permute-start | bytes 1474568 | tf_op jit(solution)/shard_map/ppermute | solution.py:43
  82.8 18.9 %collective-permute-start.30 = (bf16[384,640]{1,0:T(8,128)(2,1)S(1)}, bf16[384,640]{1,0:T(8,128)(2,1)S(1)}, u32[]{:S(2)}, u32[]{:S(2)}) collective-permute-start(bf16[384,640]{1,0:T(8,128)(2,1)S(1)} %newton.1.refs_0_), channel_id=1, source_target_pairs={{0,32},{1,33},{2,34},{3,35},{4,100},{5,101},{6,102},{7,103},{8,40}... | collective-permute-start | bytes 1474568 | tf_op jit(solution)/shard_map/ppermute | solution.py:43
  86.2 20.1 %collective-permute-start.28 = (bf16[384,640]{1,0:T(8,128)(2,1)S(1)}, bf16[384,640]{1,0:T(8,128)(2,1)S(1)}, u32[]{:S(2)}, u32[]{:S(2)}) collective-permute-start(bf16[384,640]{1,0:T(8,128)(2,1)S(1)} %newton.1.refs_0_), channel_id=1, source_target_pairs={{0,8},{1,9},{2,10},{3,11},{4,28},{5,29},{6,30},{7,31},{8,0},{9,1},... | collective-permute-start | bytes 1474568 | tf_op jit(solution)/shard_map/ppermute | solution.py:43
  88.2 21.2 %collective-permute-start.27 = (bf16[384,640]{1,0:T(8,128)(2,1)S(1)}, bf16[384,640]{1,0:T(8,128)(2,1)S(1)}, u32[]{:S(2)}, u32[]{:S(2)}) collective-permute-start(bf16[384,640]{1,0:T(8,128)(2,1)S(1)} %newton.1.refs_0_), channel_id=1, source_target_pairs={{0,4},{1,5},{2,6},{3,7},{4,0},{5,1},{6,2},{7,3},{8,12},{9,13},{10,... | collective-permute-start | bytes 1474568 | tf_op jit(solution)/shard_map/ppermute | solution.py:43
  95.4 14.1 %collective-permute-start.33 = (bf16[384,640]{1,0:T(8,128)(2,1)S(1)}, bf16[384,640]{1,0:T(8,128)(2,1)S(1)}, u32[]{:S(2)}, u32[]{:S(2)}) collective-permute-start(bf16[384,640]{1,0:T(8,128)(2,1)S(1)} %collective-permute-done.32.refs_3_), channel_id=1, source_target_pairs={{0,4},{1,5},{2,6},{3,7},{4,0},{5,1},{6,2},{7,3},{8,12},{9,13},{10,... | collective-permute-start | bytes 1474568 | tf_op jit(solution)/shard_map/ppermute | solution.py:43
  101.7 7.8 %collective-permute-start.31 = (bf16[384,640]{1,0:T(8,128)(2,1)S(1)}, bf16[384,640]{1,0:T(8,128)(2,1)S(1)}, u32[]{:S(2)}, u32[]{:S(2)}) collective-permute-start(bf16[384,640]{1,0:T(8,128)(2,1)S(1)} %collective-permute-done.30.refs_2_), channel_id=1, source_target_pairs={{0,4},{1,5},{2,6},{3,7},{4,0},{5,1},{6,2},{7,3},{8,12},{9,13},{10,... | collective-permute-start | bytes 1474568 | tf_op jit(solution)/shard_map/ppermute | solution.py:43
  106.3 3.2 %collective-permute-start.29 = (bf16[384,640]{1,0:T(8,128)(2,1)S(1)}, bf16[384,640]{1,0:T(8,128)(2,1)S(1)}, u32[]{:S(2)}, u32[]{:S(2)}) collective-permute-start(bf16[384,640]{1,0:T(8,128)(2,1)S(1)} %collective-permute-done.28.refs_1_), channel_id=1, source_target_pairs={{0,4},{1,5},{2,6},{3,7},{4,0},{5,1},{6,2},{7,3},{8,12},{9,13},{10,... | collective-permute-start | bytes 1474568 | tf_op jit(solution)/shard_map/ppermute | solution.py:43
